TPU v7x, 128 devices: a whole 4x4x4 slice. The times are simulated.
128 devices in a mesh: section: 2 (over x_hi), ctx: 16 (over x_lo, z, core), tp: 4 (over y).
Axes of the slice: x: 4 (x_hi: 2, x_lo: 2; x = x_hi * 2 + x_lo), y: 4, z: 4, core: 2. Of those that a mesh axis runs over, the one named last changes fastest.
Arguments:
- tokens: bfloat16 [2, 1024, 4096], P(None, 'ctx', 'tp'), may hold values from -6 to 6
- norm_gain: bfloat16 [2, 4096], P('section'), may hold values from 0.099609375 to 1.8984375
- query_weight: bfloat16 [2, 4096, 4096], P('section', None, 'tp'), may hold values from -1 to 1
- key_weight: bfloat16 [2, 4096, 1024], P('section', None, 'tp'), may hold values from -1 to 1
- value_weight: bfloat16 [2, 4096, 1024], P('section', None, 'tp'), may hold values from -0.1875 to 0.1875
- output_weight: bfloat16 [2, 4096, 4096], P('section', 'tp'), may hold values from -0.1875 to 0.1875
Outputs:
- layer_outputs: bfloat16 [2, 2, 1024, 4096], P('section', None, 'ctx', 'tp')
All inputs are finite; a program needn't handle non-finite values.
Results may differ from a plain program's by a relative error of at most 0.02.
Values may be sent and summed in bfloat16 or wider, within the bound.
No kernel may reach another device: no remote copies, remote signals or barrier semaphores. Data moves between devices by JAX's collectives and lax.ppermute only.
A program may use at most 128 MiB of HBM per device.

v0:
```python
import jax
import jax.numpy as jnp
from jax import lax
from jax.sharding import PartitionSpec as P

HS = 128


def from_behind(block, axis, distance):
    devices = range(lax.axis_size(axis))
    route = [(i - distance, i) for i in devices if i - distance in devices]
    return lax.ppermute(block, axis, route)


def rotate(values, cosine, sine):
    half = values.shape[-1] // 2
    first = values[..., :half]
    second = values[..., half:]
    cos_b = cosine[:, None, :]
    sin_b = sine[:, None, :]
    return jnp.concatenate(
        [first * cos_b - second * sin_b, second * cos_b + first * sin_b], axis=-1
    )


def fold_keys(carry, pieces, query, query_pos):
    best, total, acc = carry
    keys, values = pieces
    rows = keys.shape[0]
    kv_heads = query.shape[1]
    head_size = query.shape[3]
    keys = keys.reshape(rows, kv_heads, head_size)
    values = values.reshape(rows, kv_heads, head_size)
    scores = jnp.einsum(
        "qgjd,kgd->gjqk", query, keys, preferred_element_type=jnp.float32
    ) * head_size ** (-0.5)
    key_pos = lax.iota(jnp.int32, rows)
    allowed = key_pos[None, :] <= query_pos[:, None]
    masked = jnp.where(allowed, scores, -1e30)
    new_best = jnp.maximum(best, jnp.max(masked, axis=-1))
    weights = jnp.where(allowed, jnp.exp(masked - new_best[..., None]), 0.0)
    total = jnp.sum(weights, axis=-1)
    acc = jnp.einsum(
        "gjqk,kgd->gjqd", weights.astype(jnp.bfloat16), values, preferred_element_type=jnp.float32
    )
    return (new_best, total, acc)


def attend_block(whole, gain, w_query, w_key, w_value, w_out, cosine, sine, query_pos):
    count = whole.shape[0]
    kv_local = w_key.shape[1] // HS
    q_local = w_query.shape[1] // HS
    group = q_local // kv_local
    state = whole.astype(jnp.float32)
    normed = (
        state
        * lax.rsqrt(jnp.mean(state * state, axis=-1, keepdims=True) + 1e-05)
        * gain.astype(jnp.float32)
    ).astype(jnp.bfloat16)
    query = rotate(
        jnp.dot(normed, w_query, preferred_element_type=jnp.float32).reshape(count, q_local, HS),
        cosine,
        sine,
    ).astype(jnp.bfloat16)
    keys = (
        rotate(
            jnp.dot(normed, w_key, preferred_element_type=jnp.float32).reshape(count, kv_local, HS),
            cosine,
            sine,
        )
        .astype(jnp.bfloat16)
        .reshape(count, kv_local * HS)
    )
    values = jnp.dot(normed, w_value, preferred_element_type=jnp.float32).astype(jnp.bfloat16)
    query = query.reshape(count, kv_local, group, HS)
    start_carry = (
        jnp.full((kv_local, group, count), -1e30, jnp.float32),
        jnp.zeros((kv_local, group, count), jnp.float32),
        jnp.zeros((kv_local, group, count, HS), jnp.float32),
    )
    best, total, acc = fold_keys(
        start_carry,
        (
            lax.all_gather(keys, "ctx", axis=0, tiled=True),
            lax.all_gather(values, "ctx", axis=0, tiled=True),
        ),
        query,
        query_pos,
    )
    attended = (acc / total[..., None]).astype(jnp.bfloat16)
    attended = jnp.transpose(attended, (2, 0, 1, 3)).reshape(count, q_local * HS)
    return jnp.dot(attended, w_out, preferred_element_type=jnp.float32)


def per_device(tokens, norm_gain, query_weight, key_weight, value_weight, output_weight):
    section_rank = lax.axis_index("section")
    ctx_rank = lax.axis_index("ctx")
    segments = tokens.shape[0]
    count = tokens.shape[1]
    width = tokens.shape[2]
    query_pos = ctx_rank * count + lax.iota(jnp.int32, count)
    pairs = lax.iota(jnp.int32, HS // 2).astype(jnp.float32)
    freqs = jnp.power(jnp.float32(500000.0), -2.0 * pairs / HS)
    angle = query_pos.astype(jnp.float32)[:, None] * freqs[None, :]
    cosine = jnp.cos(angle)
    sine = jnp.sin(angle)
    gain = norm_gain[0]
    w_query = query_weight[0]
    w_key = key_weight[0]
    w_value = value_weight[0]
    w_out = output_weight[0]
    results = []
    received = jnp.zeros((count, width), jnp.bfloat16)
    for tick in range(segments + 1):
        own = tokens[min(tick, segments - 1)]
        slice_in = jnp.where(section_rank == 0, own, received)
        whole = lax.all_gather(slice_in, "tp", axis=1, tiled=True)
        partial_value = attend_block(
            whole, gain, w_query, w_key, w_value, w_out, cosine, sine, query_pos
        )
        summed = lax.psum_scatter(
            partial_value.astype(jnp.bfloat16), "tp", scatter_dimension=1, tiled=True
        ).astype(jnp.float32)
        result = (slice_in.astype(jnp.float32) + summed).astype(jnp.bfloat16)
        results.append(result)
        if tick < segments:
            received = from_behind(result, "section", 1)
    stacked = jnp.stack(results)
    mine = lax.dynamic_slice_in_dim(stacked, section_rank, segments, 0)
    return mine[None]


def solution(mesh):
    return jax.shard_map(
        per_device,
        mesh=mesh,
        in_specs=(
            P(None, "ctx", "tp"),
            P("section", None),
            P("section", None, "tp"),
            P("section", None, "tp"),
            P("section", None, "tp"),
            P("section", "tp", None),
        ),
        out_specs=P("section", None, "ctx", "tp"),
        check_vma=False,
    )
```

profile of v0, /device:TPU:1, one launch (start us, length us, event | category | flops | bytes accessed | tf_op | source)
XLA Modules:
  0.0 327.1 jit_solution(248189623028631327)
XLA Ops:
  6.6 0.9 mul.307
  7.5 0.1 iota_compare_fusion
  7.6 0.9 slice_select_fusion
  8.5 12.6 %all-gather = bf16[1,64,4096]{2,1,0:T(8,128)(2,1)S(1)} all-gather(bf16[1,64,1024]{2,1,0:T(8,128)(2,1)S(1)} %slice_select_fusion), channel_id=2, replica_groups=mesh['section'=2,'ctx'=16,'tp'=4] {'tp'}, dimensions={2}, use_global_device_ids=true | all-gather | bytes 655360 | tf_op jit(solution)/shard_map/all_gather | solution.py:117
  21.1 0.2 fusion.51
  21.3 0.5 fusion.36
  21.9 24.4 %all_gather.29 = bf16[1024,256]{1,0:T(8,128)(2,1)S(1)} all-gather(bf16[64,256]{1,0:T(8,128)(2,1)S(1)} %fusion.36), channel_id=1, replica_groups=mesh['section'=2,'ctx'=16,'tp'=4] {'ctx'}, dimensions={0}, use_global_device_ids=true | all-gather | bytes 557056 | tf_op jit(solution)/shard_map/all_gather | solution.py:85
  46.2 1.0 reshape.163
  47.2 4.1 %copy.55 = bf16[256,4096]{1,0:T(8,128)(2,1)} copy(bf16[256,4096]{0,1:T(8,128)(2,1)} %bitcast.185) | data formatting | bytes 4194304 | tf_op jit(solution)/shard_map/dot_general | solution.py:67
  51.3 2.4 fusion.82
  53.6 0.2 multiply_cosine_fusion
  53.8 0.1 subtract_convert_fusion.5
  53.9 0.1 copy_bitcast_fusion.2
  54.0 17.7 %all_gather.28 = bf16[1024,256]{1,0:T(8,128)(2,1)S(1)} all-gather(bf16[64,256]{1,0:T(8,128)(2,1)S(1)} %copy_bitcast_fusion.2), channel_id=1, replica_groups=mesh['section'=2,'ctx'=16,'tp'=4] {'ctx'}, dimensions={0}, use_global_device_ids=true | all-gather | bytes 557056 | tf_op jit(solution)/shard_map/all_gather | solution.py:84
  71.7 1.0 copy.18
  72.7 11.3 %copy.56 = bf16[1024,4096]{1,0:T(8,128)(2,1)} copy(bf16[1024,4096]{0,1:T(8,128)(2,1)} %bitcast.184) | data formatting | bytes 16777216 | tf_op jit(solution)/shard_map/dot_general | solution.py:61
  84.0 6.1 %fusion.80 = f32[64,8,128]{2,0,1:T(8,128)S(1)} fusion(bf16[8,128,4096]{2,1,0:T(8,128)(2,1)} %bitcast.178, bf16[1,64,4096]{2,1,0:T(8,128)(2,1)S(1)} %all-gather, f32[4096]{0:T(1024)S(1)} %bitcast.191, f32[64]{0:T(128)S(1)} %add_rsqrt_fusion.2), kind=kOutput, calls=%fused_computation.80 | convolution fusion | flops 537919488 | bytes 9191680 | tf_op jit(solution)/shard_map/dot_general | solution.py:61
  90.1 0.2 subtract_convert_fusion.2
  90.3 0.6 fusion.21
  90.9 0.7 fusion.24
  91.6 0.8 fusion.33
  92.5 0.1 copy.22
  92.7 5.8 %fusion.6 = bf16[64,4096]{1,0:T(8,128)(2,1)} fusion(bf16[64,1024]{1,0:T(8,128)(2,1)S(1)} %reshape.164, bf16[1,1024,4096]{2,1,0:T(8,128)(2,1)} %param.11), kind=kOutput, calls=%fused_computation.6 | convolution fusion | flops 537133056 | bytes 9043968 | tf_op jit(solution)/shard_map/dot_general | solution.py:92
  98.5 19.1 %reduce-scatter.4.cloned.1.call-done = bf16[64,1024]{1,0:T(8,128)(2,1)} async-done(((bf16[64,4096]{1,0:T(8,128)(2,1)}), bf16[64,1024]{1,0:T(8,128)(2,1)}) %reduce-scatter.4.cloned.1.call-update) | async-done | bytes 131088 | tf_op jit(solution)/shard_map/reduce_scatter | solution.py:121
  117.6 0.9 fusion.87
  118.6 4.8 %collective-permute-start = (bf16[64,1024]{1,0:T(8,128)(2,1)S(1)}, bf16[64,1024]{1,0:T(8,128)(2,1)S(1)}, u32[]{:S(2)}, u32[]{:S(2)}) collective-permute-start(bf16[64,1024]{1,0:T(8,128)(2,1)S(1)} %fusion.87), channel_id=1, source_target_pairs={{0,64},{1,65},{2,66},{3,67},{4,68},{5,69},{6,70},{7,71},{8,72},{9,... | collective-permute-start | bytes 393224 | tf_op jit(solution)/shard_map/ppermute | solution.py:12
  123.4 1.9 collective-permute-done
  125.3 11.1 %all_gather.30 = bf16[64,4096]{1,0:T(8,128)(2,1)S(1)} all-gather(bf16[64,1024]{1,0:T(8,128)(2,1)S(1)} %bitcast_select_fusion.4), channel_id=1, replica_groups=mesh['section'=2,'ctx'=16,'tp'=4] {'tp'}, dimensions={1}, use_global_device_ids=true | all-gather | bytes 655360 | tf_op jit(solution)/shard_map/all_gather | solution.py:117
  136.4 0.2 fusion.45
  136.6 1.1 fusion.39
  137.8 0.8 fusion.77
  138.5 6.1 %fusion.75 = f32[64,8,128]{2,0,1:T(8,128)S(1)} fusion(bf16[8,128,4096]{2,1,0:T(8,128)(2,1)} %bitcast.179, bf16[64,4096]{1,0:T(8,128)(2,1)S(1)} %all_gather.30, f32[64]{0:T(128)S(1)} %add_rsqrt_fusion.1, f32[4096]{0:T(1024)S(1)} %bitcast.194), kind=kOutput, calls=%fused_computation.75 | convolution fusion | flops 537919488 | bytes 9191680 | tf_op jit(solution)/shard_map/dot_general | solution.py:61
  144.6 0.8 subtract_convert_fusion.1
  145.6 25.2 %all_gather.31 = bf16[1024,256]{1,0:T(8,128)(2,1)S(1)} all-gather(bf16[64,256]{1,0:T(8,128)(2,1)S(1)} %copy_bitcast_fusion.1), channel_id=1, replica_groups=mesh['section'=2,'ctx'=16,'tp'=4] {'ctx'}, dimensions={0}, use_global_device_ids=true | all-gather | bytes 557056 | tf_op jit(solution)/shard_map/all_gather | solution.py:84
  170.8 0.2 copy.25
  171.0 18.0 %all_gather.32 = bf16[1024,256]{1,0:T(8,128)(2,1)S(1)} all-gather(bf16[64,256]{1,0:T(8,128)(2,1)} %fusion.39), channel_id=1, replica_groups=mesh['section'=2,'ctx'=16,'tp'=4] {'ctx'}, dimensions={0}, use_global_device_ids=true | all-gather | bytes 557056 | tf_op jit(solution)/shard_map/all_gather | solution.py:85
  189.0 1.0 reshape.166
  189.9 1.6 fusion.22
  191.5 0.7 fusion.26
  192.2 0.8 fusion.34
  193.0 0.1 copy.29
  193.2 5.8 %fusion.9 = bf16[64,4096]{1,0:T(8,128)(2,1)} fusion(bf16[64,1024]{1,0:T(8,128)(2,1)S(1)} %reshape.167, bf16[1,1024,4096]{2,1,0:T(8,128)(2,1)} %param.11), kind=kOutput, calls=%fused_computation.7 | convolution fusion | flops 537133056 | bytes 9043968 | tf_op jit(solution)/shard_map/dot_general | solution.py:92
  199.1 19.2 %reduce-scatter.6.cloned.1.call-done = bf16[64,1024]{1,0:T(8,128)(2,1)} async-done(((bf16[64,4096]{1,0:T(8,128)(2,1)}), bf16[64,1024]{1,0:T(8,128)(2,1)}) %reduce-scatter.6.cloned.1.call-update) | async-done | bytes 131088 | tf_op jit(solution)/shard_map/reduce_scatter | solution.py:121
  218.3 0.9 add_convert_fusion.2
  219.2 4.6 %collective-permute-start.1 = (bf16[64,1024]{1,0:T(8,128)(2,1)S(1)}, bf16[64,1024]{1,0:T(8,128)(2,1)S(1)}, u32[]{:S(2)}, u32[]{:S(2)}) collective-permute-start(bf16[64,1024]{1,0:T(8,128)(2,1)S(1)} %add_convert_fusion.2), channel_id=1, source_target_pairs={{0,64},{1,65},{2,66},{3,67},{4,68},{5,69},{6,70},{7,71},{8,72},{9,... | collective-permute-start | bytes 393224 | tf_op jit(solution)/shard_map/ppermute | solution.py:12
  223.8 1.9 collective-permute-done.1
  225.8 11.1 %all_gather.33 = bf16[64,4096]{1,0:T(8,128)(2,1)S(1)} all-gather(bf16[64,1024]{1,0:T(8,128)(2,1)S(1)} %bitcast_select_fusion.3), channel_id=1, replica_groups=mesh['section'=2,'ctx'=16,'tp'=4] {'tp'}, dimensions={1}, use_global_device_ids=true | all-gather | bytes 655360 | tf_op jit(solution)/shard_map/all_gather | solution.py:117
  236.8 0.2 fusion.48
  237.1 6.2 %fusion.70 = f32[64,8,128]{2,0,1:T(8,128)S(1)} fusion(bf16[8,128,4096]{2,1,0:T(8,128)(2,1)} %bitcast.180, bf16[64,4096]{1,0:T(8,128)(2,1)S(1)} %all_gather.33, f32[64]{0:T(128)S(1)} %add_rsqrt_fusion, f32[4096]{0:T(1024)S(1)} %bitcast.195), kind=kOutput, calls=%fused_computation.70 | convolution fusion | flops 537919488 | bytes 9191680 | tf_op jit(solution)/shard_map/dot_general | solution.py:61
  243.3 0.8 fusion.72
  244.1 1.1 fusion.42
  245.3 0.9 subtract_convert_fusion
  246.2 25.1 %all_gather.34 = bf16[1024,256]{1,0:T(8,128)(2,1)S(1)} all-gather(bf16[64,256]{1,0:T(8,128)(2,1)S(1)} %copy_bitcast_fusion), channel_id=1, replica_groups=mesh['section'=2,'ctx'=16,'tp'=4] {'ctx'}, dimensions={0}, use_global_device_ids=true | all-gather | bytes 557056 | tf_op jit(solution)/shard_map/all_gather | solution.py:84
  271.3 0.2 copy.32
  271.5 18.0 %all_gather.35 = bf16[1024,256]{1,0:T(8,128)(2,1)S(1)} all-gather(bf16[64,256]{1,0:T(8,128)(2,1)} %fusion.42), channel_id=1, replica_groups=mesh['section'=2,'ctx'=16,'tp'=4] {'ctx'}, dimensions={0}, use_global_device_ids=true | all-gather | bytes 557056 | tf_op jit(solution)/shard_map/all_gather | solution.py:85
  289.5 0.9 reshape.169
  290.4 1.6 fusion.23
  292.1 0.7 fusion.28
  292.8 0.8 fusion.35
  293.6 0.1 copy.36
  293.8 5.8 %fusion.12 = bf16[64,4096]{1,0:T(8,128)(2,1)} fusion(bf16[64,1024]{1,0:T(8,128)(2,1)S(1)} %reshape.170, bf16[1,1024,4096]{2,1,0:T(8,128)(2,1)} %param.11), kind=kOutput, calls=%fused_computation.8 | convolution fusion | flops 537133056 | bytes 9043968 | tf_op jit(solution)/shard_map/dot_general | solution.py:92
  299.6 19.2 %reduce-scatter.8.cloned.1.call-done = bf16[64,1024]{1,0:T(8,128)(2,1)} async-done(((bf16[64,4096]{1,0:T(8,128)(2,1)}), bf16[64,1024]{1,0:T(8,128)(2,1)}) %reduce-scatter.8.cloned.1.call-update) | async-done | bytes 131088 | tf_op jit(solution)/shard_map/reduce_scatter | solution.py:121
  318.8 0.9 fusion.88
  319.7 0.9 fusion.86
  (46 shorter events, 0.8 us)
Async XLA Ops:
  6.5 14.8 %copy-start = (bf16[1,4096,256]{2,1,0:T(8,128)(2,1)S(1)}, bf16[1,4096,256]{2,1,0:T(8,128)(2,1)}, u32[]{:S(2)}) copy-start(bf16[1,4096,256]{2,1,0:T(8,128)(2,1)} %param.10) | copy-start | bytes 6291460
  6.5 111.1 %reduce-scatter.4.cloned.1.call-start = ((), (), s32[]{:S(2)}) async-start(), calls=%async_computation.3 | async-start | bytes 655360 | tf_op jit(solution)/shard_map/reduce_scatter | solution.py:121
  84.0 6.3 %copy-start.3 = (bf16[1024,256]{0,1:T(8,128)(2,1)S(1)}, bf16[1024,256]{0,1:T(8,128)(2,1)}, u32[]{:S(2)}) copy-start(bf16[1024,256]{0,1:T(8,128)(2,1)} %copy.18) | copy-start | bytes 1572868
  90.3 1.4 copy-start.6
  92.6 25.0 %copy-start.4 = (bf16[2,64,1024]{2,1,0:T(8,128)(2,1)S(1)}, bf16[2,64,1024]{2,1,0:T(8,128)(2,1)}, u32[]{:S(2)}) copy-start(bf16[2,64,1024]{2,1,0:T(8,128)(2,1)} %param.6) | copy-start | bytes 786436
  98.5 119.8 %reduce-scatter.6.cloned.1.call-start = ((), (), s32[]{:S(2)}) async-start(), calls=%async_computation.4 | async-start | bytes 655360 | tf_op jit(solution)/shard_map/reduce_scatter | solution.py:121
  118.6 19.2 %copy-start.9 = (bf16[64,1024]{1,0:T(8,128)(2,1)}, bf16[64,1024]{1,0:T(8,128)(2,1)S(1)}, u32[]{:S(2)}) copy-start(bf16[64,1024]{1,0:T(8,128)(2,1)S(1)} %fusion.87) | copy-start | bytes 393220
  118.6 19.2 %copy-start.1 = (bf16[256,4096]{1,0:T(8,128)(2,1)S(1)}, bf16[256,4096]{1,0:T(8,128)(2,1)}, u32[]{:S(2)}) copy-start(bf16[256,4096]{1,0:T(8,128)(2,1)} %copy.55) | copy-start | bytes 6291460
  118.6 6.7 %collective-permute-start = (bf16[64,1024]{1,0:T(8,128)(2,1)S(1)}, bf16[64,1024]{1,0:T(8,128)(2,1)S(1)}, u32[]{:S(2)}, u32[]{:S(2)}) collective-permute-start(bf16[64,1024]{1,0:T(8,128)(2,1)S(1)} %fusion.87), channel_id=1, source_target_pairs={{0,64},{1,65},{2,66},{3,67},{4,68},{5,69},{6,70},{7,71},{8,72},{9,... | collective-permute-start | bytes 393224 | tf_op jit(solution)/shard_map/ppermute | solution.py:12
  189.9 2.3 copy-start.8
  193.2 32.6 %copy-start.5 = (bf16[2,64,1024]{2,1,0:T(8,128)(2,1)S(1)}, bf16[2,64,1024]{2,1,0:T(8,128)(2,1)}, u32[]{:S(2)}) copy-start(bf16[2,64,1024]{2,1,0:T(8,128)(2,1)} %param.6) | copy-start | bytes 786436
  199.1 119.7 %reduce-scatter.8.cloned.1.call-start = ((), (), s32[]{:S(2)}) async-start(), calls=%async_computation.5 | async-start | bytes 655360 | tf_op jit(solution)/shard_map/reduce_scatter | solution.py:121
  219.2 6.5 %collective-permute-start.1 = (bf16[64,1024]{1,0:T(8,128)(2,1)S(1)}, bf16[64,1024]{1,0:T(8,128)(2,1)S(1)}, u32[]{:S(2)}, u32[]{:S(2)}) collective-permute-start(bf16[64,1024]{1,0:T(8,128)(2,1)S(1)} %add_convert_fusion.2), channel_id=1, source_target_pairs={{0,64},{1,65},{2,66},{3,67},{4,68},{5,69},{6,70},{7,71},{8,72},{9,... | collective-permute-start | bytes 393224 | tf_op jit(solution)/shard_map/ppermute | solution.py:12
  237.1 6.2 %copy-start.2 = (bf16[256,4096]{1,0:T(8,128)(2,1)S(1)}, bf16[256,4096]{1,0:T(8,128)(2,1)}, u32[]{:S(2)}) copy-start(bf16[256,4096]{1,0:T(8,128)(2,1)} %copy.55) | copy-start | bytes 6291460
  290.4 2.4 copy-start.7
  293.8 26.0 %copy-start.10 = (bf16[64,1024]{1,0:T(8,128)(2,1)S(1)}, bf16[64,1024]{1,0:T(8,128)(2,1)}, u32[]{:S(2)}) copy-start(bf16[64,1024]{1,0:T(8,128)(2,1)} %copy-done.9) | copy-start | bytes 393220
Sparse Core Ops, SparseCore 0:
  98.6 18.9 reduce-scatter.3
  199.2 19.0 reduce-scatter.5
  299.7 19.0 reduce-scatter.7
where the time goes:
time: 329 us; the launch traced here: 327 us
  blocking collectives  163 us (50%)
  waiting for transfers between devices  61.3 us (19%)
  matrix products  48.8 us (15%)
  local copies, waits for them, and re-layouts  20.2 us (6%)
  between operations  13.4 us (4%)
  other arithmetic  11 us (3%)
  starting transfers between devices  9.45 us (3%)
    all_gather x3, blocking collectives, attend_block(): lax.all_gather(keys, 'ctx', axis=0, tiled=True)  68 us
    all_gather x3, blocking collectives, attend_block(): lax.all_gather(values, 'ctx', axis=0, tiled=True)  60.3 us
    reduce_scatter x3, waiting for transfers between devices, per_device(): lax.psum_scatter(partial_value.astype(jnp.bfloat16), 'tp', scatter_dimens...  57.4 us
    all_gather x3, blocking collectives, per_device(): whole = lax.all_gather(slice_in, 'tp', axis=1, tiled=True)  34.7 us
    dot_general x3, matrix products, attend_block(): jnp.dot(normed, w_query, preferred_element_type=jnp.float32)  18.4 us
    dot_general x3, matrix products, attend_block(): return jnp.dot(attended, w_out, preferred_element_type=jnp.float32)  17.4 us
    dot_general x1, local copies, waits for them, and re-layouts, attend_block(): jnp.dot(normed, w_query, preferred_element_type=jnp.float32)  11.3 us
    ppermute x2, starting transfers between devices, from_behind(): return lax.ppermute(block, axis, route)  9.37 us
  transfers between devices with their start and end apart: 5, of which 5 were waited for; matrix products, arithmetic and copies ran while one was open for 0% of the time, Pallas kernels for 0%

commit v1 on v0

v1 whole, which is shorter than its diff:
```python
import math
import jax
import jax.numpy as jnp
from jax import lax
from jax.experimental import pallas as pl
from jax.experimental.pallas import tpu as pltpu
from jax.sharding import PartitionSpec as P

HS = 128
EPS = 1e-05
KT = 256
NT = 256
CTX_AND_TP = ("ctx", "tp")


def shift_tp(block, n_tp, by):
    return lax.ppermute(block, "tp", [(i, (i + by) % n_tp) for i in range(n_tp)])


def cross_tp(block, n_ctx, n_tp, by):
    route = []
    for c in range(n_ctx):
        for t in range(n_tp):
            to = (c ^ (n_ctx // 2)) * n_tp + (t + by) % n_tp
            route.append((c * n_tp + t, to))
    return lax.ppermute(block, CTX_AND_TP, route)


def shift_z(block, n_ctx, by):
    half = n_ctx // 2
    route = [(c, c // half * half + (c % half + 2 * by) % half) for c in range(n_ctx)]
    return lax.ppermute(block, "ctx", route)


def other_core(block, n_ctx):
    return lax.ppermute(block, "ctx", [(c, c ^ 1) for c in range(n_ctx)])


def qkv_kernel(src_ref, *refs, first, last, q_cols, kv_cols):
    refs = list(refs)
    xa, xb, gain, wq, wk, wv = refs[:6]
    refs = refs[6:]
    acc_in = ss_in = cos = sin = None
    if not first:
        acc_in, ss_in = refs[:2]
        refs = refs[2:]
    if last:
        cos, sin, q_out, kv_out, acc, ss = refs
    else:
        acc, ss = refs
    step = pl.program_id(0)

    @pl.when(step == 0)
    def _():
        if first:
            acc[...] = jnp.zeros_like(acc)
            ss[...] = jnp.zeros_like(ss)
        else:
            acc[...] = acc_in[...]
            ss[...] = ss_in[...]

    x = jnp.concatenate([xa[...], xb[...]], axis=0).astype(jnp.float32)
    ss[...] += jnp.sum(x * x, axis=-1, keepdims=True)
    g = gain[...].astype(jnp.float32)
    scaled = (x * g).astype(jnp.bfloat16)
    acc[:, :q_cols] += jnp.dot(scaled, wq[0], preferred_element_type=jnp.float32)
    acc[:, q_cols : q_cols + kv_cols] += jnp.dot(
        scaled, wk[0], preferred_element_type=jnp.float32
    )
    acc[:, q_cols + kv_cols :] += jnp.dot(scaled, wv[0], preferred_element_type=jnp.float32)

    if last:

        @pl.when(step == pl.num_programs(0) - 1)
        def _():
            width = 4096.0
            r = lax.rsqrt(ss[...] / width + EPS)
            c = cos[...]
            s = sin[...]
            for h in range(q_cols // HS):
                u = acc[:, h * HS : (h + 1) * HS] * r
                q_out[:, h * HS : (h + 1) * HS] = (
                    u * c + pltpu.roll(u, HS // 2, 1) * s
                ).astype(jnp.bfloat16)
            for h in range(kv_cols // HS):
                lo = q_cols + h * HS
                u = acc[:, lo : lo + HS] * r
                kv_out[:, h * HS : (h + 1) * HS] = (
                    u * c + pltpu.roll(u, HS // 2, 1) * s
                ).astype(jnp.bfloat16)
            kv_out[:, kv_cols:] = (acc[:, q_cols + kv_cols :] * r).astype(jnp.bfloat16)


def qkv_part(src, xa, xb, halves, gain, wq, wk, wv, carry, rope):
    half = xa.shape[0] if halves is None else xa.shape[0] // 2
    width = xa.shape[1]
    rows = 2 * half
    q_cols = wq.shape[2]
    kv_cols = wk.shape[2]
    cols = q_cols + 2 * kv_cols
    steps = width // KT
    first, last = carry is None, rope is not None
    b_block = 0 if halves is None else 1
    in_specs = [
        pl.BlockSpec((half, KT), lambda k, s: (0, k)),
        pl.BlockSpec((half, KT), lambda k, s: (b_block, k)),
        pl.BlockSpec((1, KT), lambda k, s: (0, s[0] * steps + k)),
        pl.BlockSpec((1, KT, q_cols), lambda k, s: (0, s[0] * steps + k, 0)),
        pl.BlockSpec((1, KT, kv_cols), lambda k, s: (0, s[0] * steps + k, 0)),
        pl.BlockSpec((1, KT, kv_cols), lambda k, s: (0, s[0] * steps + k, 0)),
    ]
    operands = [xa, xb, gain, wq, wk, wv]
    acc_spec = pl.BlockSpec((rows, cols), lambda k, s: (0, 0))
    ss_spec = pl.BlockSpec((rows, 1), lambda k, s: (0, 0))
    if not first:
        in_specs += [acc_spec, ss_spec]
        operands += list(carry)
    scratch = []
    if last:
        in_specs += [pl.BlockSpec((rows, HS), lambda k, s: (0, 0))] * 2
        operands += list(rope)
        out_shape = [
            jax.ShapeDtypeStruct((rows, q_cols), jnp.bfloat16),
            jax.ShapeDtypeStruct((rows, 2 * kv_cols), jnp.bfloat16),
        ]
        out_specs = [
            pl.BlockSpec((rows, q_cols), lambda k, s: (0, 0)),
            pl.BlockSpec((rows, 2 * kv_cols), lambda k, s: (0, 0)),
        ]
        scratch = [pltpu.VMEM((rows, cols), jnp.float32), pltpu.VMEM((rows, 1), jnp.float32)]
    else:
        out_shape = [
            jax.ShapeDtypeStruct((rows, cols), jnp.float32),
            jax.ShapeDtypeStruct((rows, 1), jnp.float32),
        ]
        out_specs = [acc_spec, ss_spec]

    def body(src_ref, *refs):
        qkv_kernel(src_ref, *refs, first=first, last=last, q_cols=q_cols, kv_cols=kv_cols)

    return pl.pallas_call(
        body,
        grid_spec=pltpu.PrefetchScalarGridSpec(
            num_scalar_prefetch=1,
            grid=(steps,),
            in_specs=in_specs,
            out_specs=out_specs,
            scratch_shapes=scratch,
        ),
        out_shape=out_shape,
        compiler_params=pltpu.CompilerParams(vmem_limit_bytes=24 * 1024 * 1024),
        cost_estimate=pl.CostEstimate(
            flops=2 * rows * width * cols, bytes_accessed=2 * width * cols, transcendentals=0
        ),
        name="qkv_last" if last else "qkv_part",
    )(src, *operands)


def attend_kernel(q, qpos, kpos, *refs, kv_heads, group):
    *blocks, out = refs
    rows = q.shape[0]
    scale = 1.0 / math.sqrt(HS)
    allowed = kpos[...] <= qpos[...]
    allowed = jnp.concatenate([allowed] * group, axis=0)
    for g in range(kv_heads):
        k = jnp.concatenate([b[:, g * HS : (g + 1) * HS] for b in blocks], axis=0)
        lo = kv_heads * HS + g * HS
        v = jnp.concatenate([b[:, lo : lo + HS] for b in blocks], axis=0)
        heads = [g * group + j for j in range(group)]
        qs = jnp.concatenate([q[:, h * HS : (h + 1) * HS] for h in heads], axis=0)
        scores = (
            lax.dot_general(qs, k, (((1,), (1,)), ((), ())), preferred_element_type=jnp.float32)
            * scale
        )
        masked = jnp.where(allowed, scores, -1e30)
        best = jnp.max(masked, axis=-1, keepdims=True)
        weights = jnp.where(allowed, jnp.exp(masked - best), 0.0)
        total = jnp.sum(weights, axis=-1, keepdims=True)
        acc = jnp.dot(weights.astype(jnp.bfloat16), v, preferred_element_type=jnp.float32)
        attended = (acc / total).astype(jnp.bfloat16)
        for j, h in enumerate(heads):
            out[:, h * HS : (h + 1) * HS] = attended[j * rows : (j + 1) * rows]


def attend(q, qpos, kpos, blocks):
    rows, q_cols = q.shape
    kv_heads = blocks[0].shape[1] // (2 * HS)
    group = q_cols // HS // kv_heads

    def body(*refs):
        attend_kernel(*refs, kv_heads=kv_heads, group=group)

    keys = sum(b.shape[0] for b in blocks)
    return pl.pallas_call(
        body,
        out_shape=jax.ShapeDtypeStruct((rows, q_cols), jnp.bfloat16),
        compiler_params=pltpu.CompilerParams(vmem_limit_bytes=32 * 1024 * 1024),
        cost_estimate=pl.CostEstimate(
            flops=4 * rows * q_cols * keys,
            bytes_accessed=4 * rows * q_cols,
            transcendentals=rows * keys * q_cols // HS,
        ),
        name="attend",
    )(q, qpos, kpos, *blocks)


def out_part(dst, attended, w_out, split):
    rows, depth = attended.shape
    width = w_out.shape[2] // 4
    steps = width // NT
    half = rows // 2

    def body(dst_ref, a, w, *outs):
        part = jnp.dot(a[...], w[0], preferred_element_type=jnp.float32).astype(jnp.bfloat16)
        if split:
            outs[0][...] = part[:half]
            outs[1][...] = part[half:]
        else:
            outs[0][...] = part

    out_rows = [half, half] if split else [rows]
    return pl.pallas_call(
        body,
        grid_spec=pltpu.PrefetchScalarGridSpec(
            num_scalar_prefetch=1,
            grid=(steps,),
            in_specs=[
                pl.BlockSpec((rows, depth), lambda n, d: (0, 0)),
                pl.BlockSpec((1, depth, NT), lambda n, d: (0, 0, d[0] * steps + n)),
            ],
            out_specs=[pl.BlockSpec((r, NT), lambda n, d: (0, n)) for r in out_rows],
        ),
        out_shape=[jax.ShapeDtypeStruct((r, width), jnp.bfloat16) for r in out_rows],
        compiler_params=pltpu.CompilerParams(vmem_limit_bytes=16 * 1024 * 1024),
        cost_estimate=pl.CostEstimate(
            flops=2 * rows * depth * width, bytes_accessed=2 * depth * width, transcendentals=0
        ),
        name="out_part",
    )(dst, attended, w_out)


def add_all(x, parts):
    total = parts[0].astype(jnp.float32)
    for p in parts[1:]:
        total = total + p.astype(jnp.float32)
    return (x.astype(jnp.float32) + total).astype(jnp.bfloat16)


def per_device(tokens, norm_gain, wq, wk, wv, w_out):
    n_ctx = lax.axis_size("ctx")
    n_tp = lax.axis_size("tp")
    n_z = n_ctx // 4
    section = lax.axis_index("section")
    ctx = lax.axis_index("ctx")
    tp = lax.axis_index("tp")
    x_lo = ctx // (n_ctx // 2)
    z = (ctx // 2) % n_z
    core = ctx % 2
    half = tokens.shape[1]

    local = lax.iota(jnp.int32, half)

    def positions(z_of, core_of):
        base = (z_of * 2 + core_of) * half + local
        mine = x_lo * (n_ctx // 2) * half + base
        theirs = (1 - x_lo) * (n_ctx // 2) * half + base
        return jnp.concatenate([mine, theirs])

    qpos = positions(z, core)
    z_of = [(z - s) % n_z for s in range(n_z)]
    kpos = jnp.concatenate(
        [positions(zs, core) for zs in z_of] + [positions(zs, 1 - core) for zs in z_of]
    )
    pairs = lax.iota(jnp.int32, HS // 2).astype(jnp.float32)
    freqs = jnp.power(jnp.float32(500000.0), -2.0 * pairs / HS)
    angle = qpos.astype(jnp.float32)[:, None] * freqs[None, :]
    cosine = jnp.cos(angle)
    sine = jnp.sin(angle)
    rope = (
        jnp.concatenate([cosine, cosine], axis=1),
        jnp.concatenate([-sine, sine], axis=1),
    )
    qpos = qpos[:, None]
    kpos = kpos[None, :]
    src = [((tp - s) % n_tp).astype(jnp.int32)[None] for s in range(n_tp)]
    dst = [((tp + s) % n_tp).astype(jnp.int32)[None] for s in range(n_tp)]

    def project(slices, halves):
        carry = None
        for n, (s, xa, xb) in enumerate(slices):
            last = n == len(slices) - 1
            carry = qkv_part(
                src[s], xa, xb, halves, norm_gain, wq, wk, wv, carry, rope if last else None
            )
        return carry

    def mix(q, kv):
        mine = [kv] + [shift_z(kv, n_ctx, s) for s in range(1, n_z)]
        theirs = [other_core(b, n_ctx) for b in mine]
        return attend(q, qpos, kpos, mine + theirs)

    own = lax.dynamic_index_in_dim(tokens, x_lo, 0, keepdims=False)
    other = lax.dynamic_index_in_dim(tokens, 1 - x_lo, 0, keepdims=False)
    own_from = [own] + [shift_tp(own, n_tp, s) for s in range(1, n_tp)]
    other_from = [cross_tp(other, n_ctx, n_tp, s) for s in range(n_tp)]
    order = [0, 1, 3, 2]
    q, kv = project([(s, own_from[s], other_from[s]) for s in order], None)
    attended = mix(q, kv)
    parts = []
    for s in [2, 1, 3]:
        parts.append(shift_tp(out_part(dst[s], attended, w_out, False)[0], n_tp, s))
    parts.append(out_part(dst[0], attended, w_out, False)[0])
    x0 = jnp.concatenate([own, other_from[0]], axis=0)
    x1 = add_all(x0, parts)

    received = lax.ppermute(x1, "section", [(0, 1)])
    x_from = [received] + [shift_tp(received, n_tp, s) for s in range(1, n_tp)]
    q, kv = project([(s, x_from[s], x_from[s]) for s in order], 2)
    kept = jnp.where(section == 0, x1, received)
    kept_own = kept[:half]
    kept_cross = cross_tp(kept[half:], n_ctx, n_tp, 0)
    attended = mix(q, kv)
    own_parts, cross_parts = [], []
    for s in [2, 1, 3, 0]:
        pa, pb = out_part(dst[s], attended, w_out, True)
        own_parts.append(pa if s == 0 else shift_tp(pa, n_tp, s))
        cross_parts.append(cross_tp(pb, n_ctx, n_tp, s))
    out_own = jnp.where(section == 0, kept_own, add_all(kept_own, own_parts))
    out_cross = jnp.where(section == 0, kept_cross, add_all(kept_cross, cross_parts))
    first = jnp.where(x_lo == 0, out_own, out_cross)
    second = jnp.where(x_lo == 0, out_cross, out_own)
    return jnp.stack([first, second])[None]


def solution(mesh):
    return jax.shard_map(
        per_device,
        mesh=mesh,
        in_specs=(
            P(None, "ctx", "tp"),
            P("section", None),
            P("section", None, "tp"),
            P("section", None, "tp"),
            P("section", None, "tp"),
            P("section", "tp", None),
        ),
        out_specs=P("section", None, "ctx", "tp"),
        check_vma=False,
    )
```

time: 329 us -> 138 us (0.42)
  blocking collectives: 163 us -> 0 us
  starting transfers between devices: 9.45 us -> 61.7 us
  matrix products: 48.8 us -> 0 us
  waiting for transfers between devices: 61.3 us -> 25.7 us
  Pallas kernels: 0 us -> 28.3 us
  between operations: 13.4 us -> 0.51 us
  other arithmetic: 11 us -> 1.84 us
    all_gather x9 -> x0, blocking collectives: 163 us -> none  [the longest x3 68 us: attend_block(): lax.all_gather(keys, 'ctx', axis=0, tiled=True)]
    reduce_scatter x3 -> x0, waiting for transfers between devices: 57.4 us -> none  [per_device(): lax.psum_scatter(partial_value.astype(jnp.bfloat16), 'tp', scatter_dimens...]
    ppermute x2 -> x36, starting transfers between devices: 9.37 us -> 61.7 us  [the longest x8 17.4 us: other_core(): return lax.ppermute(block, 'ctx', [(c, c ^ 1) for c in range(n_ctx)])]
    dot_general x18 -> x0, matrix products: 48.8 us -> none  [the longest x3 18.4 us: attend_block(): jnp.dot(normed, w_query, preferred_element_type=jnp.float32)]
    pallas_call x0 -> x18, Pallas kernels: none -> 28.3 us  [the longest x8 11.2 us: qkv_part(): pl.pallas_call(body, grid_spec=pltpu.PrefetchScalarGridSpec(num_scalar_pr...]
    ppermute x2 -> x36, waiting for transfers between devices: 3.85 us -> 25.7 us  [the longest x12 12.8 us: shift_tp(): lax.ppermute(block, 'tp', [(i, (i + by) % n_tp) for i in range(n_tp)])]
    unnamed x22 -> x34, local copies, waits for them, and re-layouts: 0.05 us -> 17.3 us
    dot_general x2 -> x0, local copies, waits for them, and re-layouts: 15.4 us -> none  [the longest x1 11.3 us: attend_block(): jnp.dot(normed, w_query, preferred_element_type=jnp.float32)]
  transfers between devices with their start and end apart: 5 -> 36, of which waited for: 5 -> 12; matrix products, arithmetic and copies ran while one was open for 0% -> 1% of each run, Pallas kernels for 0% -> 15%
where the time goes in v1:
time: 138 us; the launch traced here: 136 us
  starting transfers between devices  61.7 us (45%)
  Pallas kernels  28.3 us (21%)
  waiting for transfers between devices  25.7 us (19%)
  local copies, waits for them, and re-layouts  18.5 us (13%)
  other arithmetic  1.84 us (1%)
    ppermute x8, starting transfers between devices, other_core(): return lax.ppermute(block, 'ctx', [(c, c ^ 1) for c in range(n_ctx)])  17.4 us
    unnamed x34, local copies, waits for them, and re-layouts  17.3 us
    ppermute x12, starting transfers between devices, shift_tp(): lax.ppermute(block, 'tp', [(i, (i + by) % n_tp) for i in range(n_tp)])  16.7 us
    ppermute x9, starting transfers between devices, cross_tp(): return lax.ppermute(block, CTX_AND_TP, route)  13.7 us
    ppermute x12, waiting for transfers between devices, shift_tp(): lax.ppermute(block, 'tp', [(i, (i + by) % n_tp) for i in range(n_tp)])  12.8 us
    pallas_call x8, Pallas kernels, qkv_part(): pl.pallas_call(body, grid_spec=pltpu.PrefetchScalarGridSpec(num_scalar_pr...  11.2 us
    pallas_call x8, Pallas kernels, out_part(): pl.pallas_call(body, grid_spec=pltpu.PrefetchScalarGridSpec(num_scalar_pr...  10.8 us
    ppermute x6, starting transfers between devices, shift_z(): return lax.ppermute(block, 'ctx', route)  9.5 us
  transfers between devices with their start and end apart: 36, of which 12 were waited for; matrix products, arithmetic and copies ran while one was open for 1% of the time, Pallas kernels for 15%

profile of v1, /device:TPU:1, one launch (start us, length us, event | category | flops | bytes accessed | tf_op | source)
XLA Modules:
  0.0 136.5 jit_solution(8096882990766703186)
XLA Ops:
  0.0 1.0 dynamic-slice_bitcast_fusion
  1.0 2.1 %collective-permute-start = (bf16[64,1024]{1,0:T(8,128)(2,1)S(1)}, bf16[64,1024]{1,0:T(8,128)(2,1)S(1)}, u32[]{:S(2)}, u32[]{:S(2)}) collective-permute-start(bf16[64,1024]{1,0:T(8,128)(2,1)S(1)} %get-tuple-element.56), channel_id=1, source_target_pairs={{0,32},{1,33},{2,34},{3,35},{4,36},{5,37},{6,38},{7,39},{8,40},{9,... | collective-permute-start | bytes 393224 | tf_op jit(solution)/shard_map/ppermute | solution.py:26
  3.1 1.3 collective-permute-start.6
  4.4 1.3 collective-permute-start.5
  5.7 1.4 %collective-permute-start.3 = (bf16[64,1024]{1,0:T(8,128)(2,1)S(1)}, bf16[64,1024]{1,0:T(8,128)(2,1)S(1)}, u32[]{:S(2)}, u32[]{:S(2)}) collective-permute-start(bf16[64,1024]{1,0:T(8,128)(2,1)S(1)} %get-tuple-element.57.refs_0_), channel_id=1, source_target_pairs={{0,3},{1,0},{2,1},{3,2},{4,7},{5,4},{6,5},{7,6},{8,11},{9,8},{10,9... | collective-permute-start | bytes 393224 | tf_op jit(solution)/shard_map/ppermute | solution.py:17
  7.1 1.2 collective-permute-start.4
  8.9 1.7 %collective-permute-start.1 = (bf16[64,1024]{1,0:T(8,128)(2,1)S(1)}, bf16[64,1024]{1,0:T(8,128)(2,1)S(1)}, u32[]{:S(2)}, u32[]{:S(2)}) collective-permute-start(bf16[64,1024]{1,0:T(8,128)(2,1)S(1)} %get-tuple-element.57.refs_0_), channel_id=1, source_target_pairs={{0,2},{1,3},{2,0},{3,1},{4,6},{5,7},{6,4},{7,5},{8,10},{9,11},{10,... | collective-permute-start | bytes 393224 | tf_op jit(solution)/shard_map/ppermute | solution.py:17
  10.6 1.1 collective-permute-done.5.refs_0_
  11.7 3.3 %collective-permute-start.2 = (bf16[64,1024]{1,0:T(8,128)(2,1)S(1)}, bf16[64,1024]{1,0:T(8,128)(2,1)S(1)}, u32[]{:S(2)}, u32[]{:S(2)}) collective-permute-start(bf16[64,1024]{1,0:T(8,128)(2,1)S(1)} %get-tuple-element.56), channel_id=1, source_target_pairs={{0,34},{1,35},{2,32},{3,33},{4,38},{5,39},{6,36},{7,37},{8,42},{9,... | collective-permute-start | bytes 393224 | tf_op jit(solution)/shard_map/ppermute | solution.py:26
  15.0 3.4 %copy-done = bf16[1,4096,1024]{2,1,0:T(8,128)(2,1)S(1)} copy-done((bf16[1,4096,1024]{2,1,0:T(8,128)(2,1)S(1)}, bf16[1,4096,1024]{2,1,0:T(8,128)(2,1)}, u32[]{:S(2)}) %copy-start) | copy-done | bytes 8388632
  18.4 1.6 %copy-done.4 = bf16[1,4096,256]{2,1,0:T(8,128)(2,1)S(1)} copy-done((bf16[1,4096,256]{2,1,0:T(8,128)(2,1)S(1)}, bf16[1,4096,256]{2,1,0:T(8,128)(2,1)}, u32[]{:S(2)}) %copy-start.4) | copy-done | bytes 2097176
  20.0 1.6 %copy-done.6 = bf16[1,4096,256]{2,1,0:T(8,128)(2,1)S(1)} copy-done((bf16[1,4096,256]{2,1,0:T(8,128)(2,1)S(1)}, bf16[1,4096,256]{2,1,0:T(8,128)(2,1)}, u32[]{:S(2)}) %copy-start.6) | copy-done | bytes 2097176
  21.6 0.7 copy-done.9
  22.3 1.3 qkv_part.6
  23.6 2.1 %copy-done.1 = bf16[1,4096,1024]{2,1,0:T(8,128)(2,1)S(1)} copy-done((bf16[1,4096,1024]{2,1,0:T(8,128)(2,1)S(1)}, bf16[1,4096,1024]{2,1,0:T(8,128)(2,1)}, u32[]{:S(2)}) %copy-start.1) | copy-done | bytes 8388632
  26.9 1.3 qkv_part.7
  28.2 1.3 qkv_part.8
  29.6 1.7 %qkv_last.2 = (bf16[128,1024]{1,0:T(8,128)(2,1)S(1)}, bf16[128,512]{1,0:T(8,128)(2,1)S(1)}) custom-call(s32[1]{0:T(128)} %bitcast.3.src_ref, bf16[64,1024]{1,0:T(8,128)(2,1)S(1)} %collective-permute-done.1.refs_0_, bf16[64,1024]{1,0:T(8,128)(2,1)S(1)} %collective-permute-done.2.refs_1_, bf16[1,4096]{1,0:T(2,128)(2,1)S(1)} %copy-done.9, ...), custom_call_target="tpu_custom_call" | custom-call | flops 402653184 | bytes 3145728 | tf_op jit(solution)/shard_map/qkv_last/pallas_call | solution.py:141
  31.2 1.7 %collective-permute-start.7 = (bf16[128,512]{1,0:T(8,128)(2,1)S(1)}, bf16[128,512]{1,0:T(8,128)(2,1)S(1)}, u32[]{:S(2)}, u32[]{:S(2)}) collective-permute-start(bf16[128,512]{1,0:T(8,128)(2,1)S(1)} %get-tuple-element.36.refs_3_), channel_id=1, source_target_pairs={{0,8},{4,12},{8,16},{12,20},{16,24},{20,28},{24,0},{28,4},{32,40},... | collective-permute-start | bytes 393224 | tf_op jit(solution)/shard_map/ppermute | solution.py:32
  32.9 3.3 %collective-permute-start.8 = (bf16[128,512]{1,0:T(8,128)(2,1)S(1)}, bf16[128,512]{1,0:T(8,128)(2,1)S(1)}, u32[]{:S(2)}, u32[]{:S(2)}) collective-permute-start(bf16[128,512]{1,0:T(8,128)(2,1)S(1)} %get-tuple-element.36.refs_3_), channel_id=1, source_target_pairs={{0,16},{4,20},{8,24},{12,28},{16,0},{20,4},{24,8},{28,12},{32,48},... | collective-permute-start | bytes 393224 | tf_op jit(solution)/shard_map/ppermute | solution.py:32
  36.2 0.7 collective-permute-start.9
  37.0 3.2 %collective-permute-start.10 = (bf16[128,512]{1,0:T(8,128)(2,1)S(1)}, bf16[128,512]{1,0:T(8,128)(2,1)S(1)}, u32[]{:S(2)}, u32[]{:S(2)}) collective-permute-start(bf16[128,512]{1,0:T(8,128)(2,1)S(1)} %get-tuple-element.36.refs_3_), channel_id=1, source_target_pairs={{0,4},{4,0},{8,12},{12,8},{16,20},{20,16},{24,28},{28,24},{32,36},... | collective-permute-start | bytes 393224 | tf_op jit(solution)/shard_map/ppermute | solution.py:36
  40.2 1.9 %collective-permute-start.11 = (bf16[128,512]{1,0:T(8,128)(2,1)S(1)}, bf16[128,512]{1,0:T(8,128)(2,1)}, u32[]{:S(2)}, u32[]{:S(2)}) collective-permute-start(bf16[128,512]{1,0:T(8,128)(2,1)S(1)} %collective-permute-done.7.refs_4_), channel_id=1, source_target_pairs={{0,4},{4,0},{8,12},{12,8},{16,20},{20,16},{24,28},{28,24},{32,36},... | collective-permute-start | bytes 393224 | tf_op jit(solution)/shard_map/ppermute | solution.py:36
  42.1 1.5 %collective-permute-start.12 = (bf16[128,512]{1,0:T(8,128)(2,1)S(1)}, bf16[128,512]{1,0:T(8,128)(2,1)}, u32[]{:S(2)}, u32[]{:S(2)}) collective-permute-start(bf16[128,512]{1,0:T(8,128)(2,1)S(1)} %collective-permute-done.8.refs_5_), channel_id=1, source_target_pairs={{0,4},{4,0},{8,12},{12,8},{16,20},{20,16},{24,28},{28,24},{32,36},... | collective-permute-start | bytes 393224 | tf_op jit(solution)/shard_map/ppermute | solution.py:36
  45.3 3.7 %attend.2.a = bf16[128,1024]{1,0:T(8,128)(2,1)S(1)} custom-call(bf16[128,1024]{1,0:T(8,128)(2,1)S(1)} %get-tuple-element.35.refs_0_, s32[128,1]{1,0:T(8,128)S(1)} %copy.7.refs_1_, s32[1,1024]{1,0:T(1,128)S(1)} %bitcast.26, bf16[128,512]{1,0:T(8,128)(2,1)S(1)} %get-tuple-element.36.refs_3_, bf16[128,512]{1,0:T(8,128)(2,1)S(1)} %collective-permute-done.7.refs_4_, ...), custom_call_target="tpu_custom_call" | custom-call | flops 536870912 | bytes 524288 | tf_op jit(solution)/shard_map/attend/pallas_call | solution.py:194
  49.0 3.4 %copy-done.2 = bf16[1,1024,4096]{2,1,0:T(8,128)(2,1)S(1)} copy-done((bf16[1,1024,4096]{2,1,0:T(8,128)(2,1)S(1)}, bf16[1,1024,4096]{2,1,0:T(8,128)(2,1)}, u32[]{:S(2)}) %copy-start.2) | copy-done | bytes 8388632
  52.4 1.3 out_part.8
  53.7 2.3 %collective-permute-start.14 = (bf16[128,1024]{1,0:T(8,128)(2,1)S(1)}, bf16[128,1024]{1,0:T(8,128)(2,1)S(1)}, u32[]{:S(2)}, u32[]{:S(2)}) collective-permute-start(bf16[128,1024]{1,0:T(8,128)(2,1)S(1)} %out_part.8), channel_id=1, source_target_pairs={{0,2},{1,3},{2,0},{3,1},{4,6},{5,7},{6,4},{7,5},{8,10},{9,11},{10,... | collective-permute-start | bytes 786440 | tf_op jit(solution)/shard_map/ppermute | solution.py:17
  56.0 1.3 out_part.9
  57.5 1.4 %out_part.10 = bf16[128,1024]{1,0:T(8,128)(2,1)S(1)} custom-call(s32[1]{0:T(128)} %bitcast.10.dst_ref, bf16[128,1024]{1,0:T(8,128)(2,1)S(1)} %attend.2.a, bf16[1,1024,4096]{2,1,0:T(8,128)(2,1)S(1)} %copy-done.2), custom_call_target="tpu_custom_call" | custom-call | flops 268435456 | bytes 2097152 | tf_op jit(solution)/shard_map/out_part/pallas_call | solution.py:222
  58.9 2.7 %collective-permute-start.16 = (bf16[128,1024]{1,0:T(8,128)(2,1)S(1)}, bf16[128,1024]{1,0:T(8,128)(2,1)S(1)}, u32[]{:S(2)}, u32[]{:S(2)}) collective-permute-start(bf16[128,1024]{1,0:T(8,128)(2,1)S(1)} %out_part.10), channel_id=1, source_target_pairs={{0,3},{1,0},{2,1},{3,2},{4,7},{5,4},{6,5},{7,6},{8,11},{9,8},{10,9... | collective-permute-start | bytes 786440 | tf_op jit(solution)/shard_map/ppermute | solution.py:17
  61.6 1.3 out_part.11
  62.9 6.2 %collective-permute-done.15 = bf16[128,1024]{1,0:T(8,128)(2,1)S(1)} collective-permute-done((bf16[128,1024]{1,0:T(8,128)(2,1)S(1)}, bf16[128,1024]{1,0:T(8,128)(2,1)S(1)}, u32[]{:S(2)}, u32[]{:S(2)}) %collective-permute-start.15) | collective-permute-done | bytes 262176 | tf_op jit(solution)/shard_map/ppermute | solution.py:17
  69.4 4.4 %collective-permute-start.17 = (bf16[128,1024]{1,0:T(8,128)(2,1)S(1)}, bf16[128,1024]{1,0:T(8,128)(2,1)S(1)}, u32[]{:S(2)}, u32[]{:S(2)}) collective-permute-start(bf16[128,1024]{1,0:T(8,128)(2,1)S(1)} %add_convert_fusion), channel_id=1, source_target_pairs={{0,64},{1,65},{2,66},{3,67},{4,68},{5,69},{6,70},{7,71},{8,72},{9,... | collective-permute-start | bytes 786440 | tf_op jit(solution)/shard_map/ppermute | solution.py:316
  73.7 5.1 %collective-permute-done.17.refs_0_.refs_1_ = bf16[128,1024]{1,0:T(8,128)(2,1)S(1)} collective-permute-done((bf16[128,1024]{1,0:T(8,128)(2,1)S(1)}, bf16[128,1024]{1,0:T(8,128)(2,1)S(1)}, u32[]{:S(2)}, u32[]{:S(2)}) %collective-permute-start.17) | collective-permute-done | bytes 262176 | tf_op jit(solution)/shard_map/ppermute | solution.py:316
  78.9 2.7 %collective-permute-start.19 = (bf16[128,1024]{1,0:T(8,128)(2,1)S(1)}, bf16[128,1024]{1,0:T(8,128)(2,1)S(1)}, u32[]{:S(2)}, u32[]{:S(2)}) collective-permute-start(bf16[128,1024]{1,0:T(8,128)(2,1)S(1)} %collective-permute-done.17.refs_0_.refs_1_), channel_id=1, source_target_pairs={{0,3},{1,0},{2,1},{3,2},{4,7},{5,4},{6,5},{7,6},{8,11},{9,8},{10,9... | collective-permute-start | bytes 786440 | tf_op jit(solution)/shard_map/ppermute | solution.py:17
  81.6 0.8 collective-permute-start.18
  82.4 1.3 qkv_part.9
  83.8 3.1 %collective-permute-done.20.refs_0_.refs_1_ = bf16[128,1024]{1,0:T(8,128)(2,1)S(1)} collective-permute-done((bf16[128,1024]{1,0:T(8,128)(2,1)S(1)}, bf16[128,1024]{1,0:T(8,128)(2,1)S(1)}, u32[]{:S(2)}, u32[]{:S(2)}) %collective-permute-start.20) | collective-permute-done | bytes 262176 | tf_op jit(solution)/shard_map/ppermute | solution.py:17
  86.9 1.3 qkv_part.10
  88.2 1.3 qkv_part.11
  89.6 2.3 %collective-permute-done.18.refs_0_.refs_1_ = bf16[128,1024]{1,0:T(8,128)(2,1)S(1)} collective-permute-done((bf16[128,1024]{1,0:T(8,128)(2,1)S(1)}, bf16[128,1024]{1,0:T(8,128)(2,1)S(1)}, u32[]{:S(2)}, u32[]{:S(2)}) %collective-permute-start.18) | collective-permute-done | bytes 262176 | tf_op jit(solution)/shard_map/ppermute | solution.py:17
  91.9 1.6 %qkv_last.3 = (bf16[128,1024]{1,0:T(8,128)(2,1)S(1)}, bf16[128,512]{1,0:T(8,128)(2,1)S(1)}) custom-call(s32[1]{0:T(128)} %bitcast.3.src_ref, bf16[128,1024]{1,0:T(8,128)(2,1)S(1)} %collective-permute-done.18.refs_0_.refs_1_, bf16[128,1024]{1,0:T(8,128)(2,1)S(1)} %collective-permute-done.18.refs_0_.refs_1_, bf16[1,4096]{1,0:T(2,128)(2,1)S(1)} %copy-done.10, ...), custom_call_target="tpu_custom_call" | custom-call | flops 402653184 | bytes 3145728 | tf_op jit(solution)/shard_map/qkv_last/pallas_call | solution.py:141
  93.5 0.7 collective-permute-start.21
  94.2 2.5 %collective-permute-start.22 = (bf16[128,512]{1,0:T(8,128)(2,1)S(1)}, bf16[128,512]{1,0:T(8,128)(2,1)S(1)}, u32[]{:S(2)}, u32[]{:S(2)}) collective-permute-start(bf16[128,512]{1,0:T(8,128)(2,1)S(1)} %get-tuple-element.44.refs_3_), channel_id=1, source_target_pairs={{0,16},{4,20},{8,24},{12,28},{16,0},{20,4},{24,8},{28,12},{32,48},... | collective-permute-start | bytes 393224 | tf_op jit(solution)/shard_map/ppermute | solution.py:32
  97.3 6.1 %collective-permute-start.24 = (bf16[128,512]{1,0:T(8,128)(2,1)S(1)}, bf16[128,512]{1,0:T(8,128)(2,1)S(1)}, u32[]{:S(2)}, u32[]{:S(2)}) collective-permute-start(bf16[128,512]{1,0:T(8,128)(2,1)S(1)} %get-tuple-element.44.refs_3_), channel_id=1, source_target_pairs={{0,4},{4,0},{8,12},{12,8},{16,20},{20,16},{24,28},{28,24},{32,36},... | collective-permute-start | bytes 393224 | tf_op jit(solution)/shard_map/ppermute | solution.py:36
  103.4 1.7 %collective-permute-start.25 = (bf16[128,512]{1,0:T(8,128)(2,1)S(1)}, bf16[128,512]{1,0:T(8,128)(2,1)S(1)}, u32[]{:S(2)}, u32[]{:S(2)}) collective-permute-start(bf16[128,512]{1,0:T(8,128)(2,1)S(1)} %collective-permute-done.21.refs_4_), channel_id=1, source_target_pairs={{0,4},{4,0},{8,12},{12,8},{16,20},{20,16},{24,28},{28,24},{32,36},... | collective-permute-start | bytes 393224 | tf_op jit(solution)/shard_map/ppermute | solution.py:36
  105.0 1.8 %collective-permute-start.26 = (bf16[128,512]{1,0:T(8,128)(2,1)S(1)}, bf16[128,512]{1,0:T(8,128)(2,1)S(1)}, u32[]{:S(2)}, u32[]{:S(2)}) collective-permute-start(bf16[128,512]{1,0:T(8,128)(2,1)S(1)} %collective-permute-done.22.refs_5_), channel_id=1, source_target_pairs={{0,4},{4,0},{8,12},{12,8},{16,20},{20,16},{24,28},{28,24},{32,36},... | collective-permute-start | bytes 393224 | tf_op jit(solution)/shard_map/ppermute | solution.py:36
  108.5 2.6 %attend.3.a = bf16[128,1024]{1,0:T(8,128)(2,1)S(1)} custom-call(bf16[128,1024]{1,0:T(8,128)(2,1)S(1)} %get-tuple-element.43.refs_0_, s32[128,1]{1,0:T(8,128)S(1)} %copy.7.refs_1_, s32[1,1024]{1,0:T(1,128)S(1)} %bitcast.27, bf16[128,512]{1,0:T(8,128)(2,1)S(1)} %get-tuple-element.44.refs_3_, bf16[128,512]{1,0:T(8,128)(2,1)S(1)} %collective-permute-done.21.refs_4_, ...), custom_call_target="tpu_custom_call" | custom-call | flops 536870912 | bytes 524288 | tf_op jit(solution)/shard_map/attend/pallas_call | solution.py:194
  111.1 3.4 %copy-done.3 = bf16[1,1024,4096]{2,1,0:T(8,128)(2,1)S(1)} copy-done((bf16[1,1024,4096]{2,1,0:T(8,128)(2,1)S(1)}, bf16[1,1024,4096]{2,1,0:T(8,128)(2,1)}, u32[]{:S(2)}) %copy-start.3) | copy-done | bytes 8388632
  114.5 1.3 out_part.12
  115.9 0.9 collective-permute-start.28
  116.8 1.3 out_part.13
  118.1 1.1 collective-permute-start.29
  119.3 1.3 out_part.14
  120.6 1.7 %collective-permute-start.30 = (bf16[64,1024]{1,0:T(8,128)(2,1)S(1)}, bf16[64,1024]{1,0:T(8,128)(2,1)S(1)}, u32[]{:S(2)}, u32[]{:S(2)}) collective-permute-start(bf16[64,1024]{1,0:T(8,128)(2,1)S(1)} %get-tuple-element.47), channel_id=1, source_target_pairs={{0,3},{1,0},{2,1},{3,2},{4,7},{5,4},{6,5},{7,6},{8,11},{9,8},{10,9... | collective-permute-start | bytes 393224 | tf_op jit(solution)/shard_map/ppermute | solution.py:17
  122.3 1.3 collective-permute-start.32
  123.6 1.3 out_part.15
  125.3 3.3 %collective-permute-start.34 = (bf16[64,1024]{1,0:T(8,128)(2,1)S(1)}, bf16[64,1024]{1,0:T(8,128)(2,1)S(1)}, u32[]{:S(2)}, u32[]{:S(2)}) collective-permute-start(bf16[64,1024]{1,0:T(8,128)(2,1)S(1)} %get-tuple-element.51), channel_id=1, source_target_pairs={{0,35},{1,32},{2,33},{3,34},{4,39},{5,36},{6,37},{7,38},{8,43},{9,... | collective-permute-start | bytes 393224 | tf_op jit(solution)/shard_map/ppermute | solution.py:26
  128.6 0.8 collective-permute-start.35
  129.4 2.3 %collective-permute-done.33 = bf16[64,1024]{1,0:T(8,128)(2,1)S(1)} collective-permute-done((bf16[64,1024]{1,0:T(8,128)(2,1)S(1)}, bf16[64,1024]{1,0:T(8,128)(2,1)S(1)}, u32[]{:S(2)}, u32[]{:S(2)}) %collective-permute-start.33) | collective-permute-done | bytes 131104 | tf_op jit(solution)/shard_map/ppermute | solution.py:26
  131.7 1.2 collective-permute-done.34
  132.9 2.6 %collective-permute-done.35 = bf16[64,1024]{1,0:T(8,128)(2,1)S(1)} collective-permute-done((bf16[64,1024]{1,0:T(8,128)(2,1)S(1)}, bf16[64,1024]{1,0:T(8,128)(2,1)S(1)}, u32[]{:S(2)}, u32[]{:S(2)}) %collective-permute-start.35) | collective-permute-done | bytes 131104 | tf_op jit(solution)/shard_map/ppermute | solution.py:26
  135.7 0.7 maximum_bitcast_fusion
  (86 shorter events, 6.7 us)
Async XLA Ops:
  1.0 7.9 %collective-permute-start = (bf16[64,1024]{1,0:T(8,128)(2,1)S(1)}, bf16[64,1024]{1,0:T(8,128)(2,1)S(1)}, u32[]{:S(2)}, u32[]{:S(2)}) collective-permute-start(bf16[64,1024]{1,0:T(8,128)(2,1)S(1)} %get-tuple-element.56), channel_id=1, source_target_pairs={{0,32},{1,33},{2,34},{3,35},{4,36},{5,37},{6,38},{7,39},{8,40},{9,... | collective-permute-start | bytes 393224 | tf_op jit(solution)/shard_map/ppermute | solution.py:26
  3.1 20.5 %collective-permute-start.6 = (bf16[64,1024]{1,0:T(8,128)(2,1)S(1)}, bf16[64,1024]{1,0:T(8,128)(2,1)S(1)}, u32[]{:S(2)}, u32[]{:S(2)}) collective-permute-start(bf16[64,1024]{1,0:T(8,128)(2,1)S(1)} %get-tuple-element.56), channel_id=1, source_target_pairs={{0,33},{1,34},{2,35},{3,32},{4,37},{5,38},{6,39},{7,36},{8,41},{9,... | collective-permute-start | bytes 393224 | tf_op jit(solution)/shard_map/ppermute | solution.py:26
  4.4 7.3 %collective-permute-start.5 = (bf16[64,1024]{1,0:T(8,128)(2,1)S(1)}, bf16[64,1024]{1,0:T(8,128)(2,1)S(1)}, u32[]{:S(2)}, u32[]{:S(2)}) collective-permute-start(bf16[64,1024]{1,0:T(8,128)(2,1)S(1)} %get-tuple-element.57.refs_0_), channel_id=1, source_target_pairs={{0,1},{1,2},{2,3},{3,0},{4,5},{5,6},{6,7},{7,4},{8,9},{9,10},{10,1... | collective-permute-start | bytes 393224 | tf_op jit(solution)/shard_map/ppermute | solution.py:17
  5.7 22.5 %collective-permute-start.3 = (bf16[64,1024]{1,0:T(8,128)(2,1)S(1)}, bf16[64,1024]{1,0:T(8,128)(2,1)S(1)}, u32[]{:S(2)}, u32[]{:S(2)}) collective-permute-start(bf16[64,1024]{1,0:T(8,128)(2,1)S(1)} %get-tuple-element.57.refs_0_), channel_id=1, source_target_pairs={{0,3},{1,0},{2,1},{3,2},{4,7},{5,4},{6,5},{7,6},{8,11},{9,8},{10,9... | collective-permute-start | bytes 393224 | tf_op jit(solution)/shard_map/ppermute | solution.py:17
  7.1 21.2 %collective-permute-start.4 = (bf16[64,1024]{1,0:T(8,128)(2,1)S(1)}, bf16[64,1024]{1,0:T(8,128)(2,1)S(1)}, u32[]{:S(2)}, u32[]{:S(2)}) collective-permute-start(bf16[64,1024]{1,0:T(8,128)(2,1)S(1)} %get-tuple-element.56), channel_id=1, source_target_pairs={{0,35},{1,32},{2,33},{3,34},{4,39},{5,36},{6,37},{7,38},{8,43},{9,... | collective-permute-start | bytes 393224 | tf_op jit(solution)/shard_map/ppermute | solution.py:26
  8.9 20.7 %collective-permute-start.1 = (bf16[64,1024]{1,0:T(8,128)(2,1)S(1)}, bf16[64,1024]{1,0:T(8,128)(2,1)S(1)}, u32[]{:S(2)}, u32[]{:S(2)}) collective-permute-start(bf16[64,1024]{1,0:T(8,128)(2,1)S(1)} %get-tuple-element.57.refs_0_), channel_id=1, source_target_pairs={{0,2},{1,3},{2,0},{3,1},{4,6},{5,7},{6,4},{7,5},{8,10},{9,11},{10,... | collective-permute-start | bytes 393224 | tf_op jit(solution)/shard_map/ppermute | solution.py:17
  11.7 17.9 %collective-permute-start.2 = (bf16[64,1024]{1,0:T(8,128)(2,1)S(1)}, bf16[64,1024]{1,0:T(8,128)(2,1)S(1)}, u32[]{:S(2)}, u32[]{:S(2)}) collective-permute-start(bf16[64,1024]{1,0:T(8,128)(2,1)S(1)} %get-tuple-element.56), channel_id=1, source_target_pairs={{0,34},{1,35},{2,32},{3,33},{4,38},{5,39},{6,36},{7,37},{8,42},{9,... | collective-permute-start | bytes 393224 | tf_op jit(solution)/shard_map/ppermute | solution.py:26
  15.0 3.4 %copy-start = (bf16[1,4096,1024]{2,1,0:T(8,128)(2,1)S(1)}, bf16[1,4096,1024]{2,1,0:T(8,128)(2,1)}, u32[]{:S(2)}) copy-start(bf16[1,4096,1024]{2,1,0:T(8,128)(2,1)} %refs_3_.15) | copy-start | bytes 25165828
  18.4 1.6 %copy-start.4 = (bf16[1,4096,256]{2,1,0:T(8,128)(2,1)S(1)}, bf16[1,4096,256]{2,1,0:T(8,128)(2,1)}, u32[]{:S(2)}) copy-start(bf16[1,4096,256]{2,1,0:T(8,128)(2,1)} %refs_4_.15) | copy-start | bytes 6291460
  20.0 1.6 %copy-start.6 = (bf16[1,4096,256]{2,1,0:T(8,128)(2,1)S(1)}, bf16[1,4096,256]{2,1,0:T(8,128)(2,1)}, u32[]{:S(2)}) copy-start(bf16[1,4096,256]{2,1,0:T(8,128)(2,1)} %refs_5_.15) | copy-start | bytes 6291460
  21.6 0.7 copy-start.9
  22.3 3.4 %copy-start.1 = (bf16[1,4096,1024]{2,1,0:T(8,128)(2,1)S(1)}, bf16[1,4096,1024]{2,1,0:T(8,128)(2,1)}, u32[]{:S(2)}) copy-start(bf16[1,4096,1024]{2,1,0:T(8,128)(2,1)} %refs_3_.15) | copy-start | bytes 25165828
  22.3 4.0 %copy-start.5 = (bf16[1,4096,256]{2,1,0:T(8,128)(2,1)S(1)}, bf16[1,4096,256]{2,1,0:T(8,128)(2,1)}, u32[]{:S(2)}) copy-start(bf16[1,4096,256]{2,1,0:T(8,128)(2,1)} %refs_4_.15) | copy-start | bytes 6291460
  22.3 4.6 %copy-start.7 = (bf16[1,4096,256]{2,1,0:T(8,128)(2,1)S(1)}, bf16[1,4096,256]{2,1,0:T(8,128)(2,1)}, u32[]{:S(2)}) copy-start(bf16[1,4096,256]{2,1,0:T(8,128)(2,1)} %refs_5_.15) | copy-start | bytes 6291460
  31.2 9.0 %collective-permute-start.7 = (bf16[128,512]{1,0:T(8,128)(2,1)S(1)}, bf16[128,512]{1,0:T(8,128)(2,1)S(1)}, u32[]{:S(2)}, u32[]{:S(2)}) collective-permute-start(bf16[128,512]{1,0:T(8,128)(2,1)S(1)} %get-tuple-element.36.refs_3_), channel_id=1, source_target_pairs={{0,8},{4,12},{8,16},{12,20},{16,24},{20,28},{24,0},{28,4},{32,40},... | collective-permute-start | bytes 393224 | tf_op jit(solution)/shard_map/ppermute | solution.py:32
  32.9 9.2 %collective-permute-start.8 = (bf16[128,512]{1,0:T(8,128)(2,1)S(1)}, bf16[128,512]{1,0:T(8,128)(2,1)S(1)}, u32[]{:S(2)}, u32[]{:S(2)}) collective-permute-start(bf16[128,512]{1,0:T(8,128)(2,1)S(1)} %get-tuple-element.36.refs_3_), channel_id=1, source_target_pairs={{0,16},{4,20},{8,24},{12,28},{16,0},{20,4},{24,8},{28,12},{32,48},... | collective-permute-start | bytes 393224 | tf_op jit(solution)/shard_map/ppermute | solution.py:32
  36.2 7.3 %collective-permute-start.9 = (bf16[128,512]{1,0:T(8,128)(2,1)S(1)}, bf16[128,512]{1,0:T(8,128)(2,1)S(1)}, u32[]{:S(2)}, u32[]{:S(2)}) collective-permute-start(bf16[128,512]{1,0:T(8,128)(2,1)S(1)} %get-tuple-element.36.refs_3_), channel_id=1, source_target_pairs={{0,24},{4,28},{8,0},{12,4},{16,8},{20,12},{24,16},{28,20},{32,56},... | collective-permute-start | bytes 393224 | tf_op jit(solution)/shard_map/ppermute | solution.py:32
  37.0 7.4 %collective-permute-start.10 = (bf16[128,512]{1,0:T(8,128)(2,1)S(1)}, bf16[128,512]{1,0:T(8,128)(2,1)S(1)}, u32[]{:S(2)}, u32[]{:S(2)}) collective-permute-start(bf16[128,512]{1,0:T(8,128)(2,1)S(1)} %get-tuple-element.36.refs_3_), channel_id=1, source_target_pairs={{0,4},{4,0},{8,12},{12,8},{16,20},{20,16},{24,28},{28,24},{32,36},... | collective-permute-start | bytes 393224 | tf_op jit(solution)/shard_map/ppermute | solution.py:36
  40.2 4.2 %collective-permute-start.11 = (bf16[128,512]{1,0:T(8,128)(2,1)S(1)}, bf16[128,512]{1,0:T(8,128)(2,1)}, u32[]{:S(2)}, u32[]{:S(2)}) collective-permute-start(bf16[128,512]{1,0:T(8,128)(2,1)S(1)} %collective-permute-done.7.refs_4_), channel_id=1, source_target_pairs={{0,4},{4,0},{8,12},{12,8},{16,20},{20,16},{24,28},{28,24},{32,36},... | collective-permute-start | bytes 393224 | tf_op jit(solution)/shard_map/ppermute | solution.py:36
  42.1 2.6 %collective-permute-start.12 = (bf16[128,512]{1,0:T(8,128)(2,1)S(1)}, bf16[128,512]{1,0:T(8,128)(2,1)}, u32[]{:S(2)}, u32[]{:S(2)}) collective-permute-start(bf16[128,512]{1,0:T(8,128)(2,1)S(1)} %collective-permute-done.8.refs_5_), channel_id=1, source_target_pairs={{0,4},{4,0},{8,12},{12,8},{16,20},{20,16},{24,28},{28,24},{32,36},... | collective-permute-start | bytes 393224 | tf_op jit(solution)/shard_map/ppermute | solution.py:36
  43.6 1.7 %collective-permute-start.13 = (bf16[128,512]{1,0:T(8,128)(2,1)S(1)}, bf16[128,512]{1,0:T(8,128)(2,1)}, u32[]{:S(2)}, u32[]{:S(2)}) collective-permute-start(bf16[128,512]{1,0:T(8,128)(2,1)S(1)} %collective-permute-done.9.refs_6_), channel_id=1, source_target_pairs={{0,4},{4,0},{8,12},{12,8},{16,20},{20,16},{24,28},{28,24},{32,36},... | collective-permute-start | bytes 393224 | tf_op jit(solution)/shard_map/ppermute | solution.py:36
  49.0 3.4 %copy-start.2 = (bf16[1,1024,4096]{2,1,0:T(8,128)(2,1)S(1)}, bf16[1,1024,4096]{2,1,0:T(8,128)(2,1)}, u32[]{:S(2)}) copy-start(bf16[1,1024,4096]{2,1,0:T(8,128)(2,1)} %w.15) | copy-start | bytes 25165828
  53.7 9.2 %collective-permute-start.14 = (bf16[128,1024]{1,0:T(8,128)(2,1)S(1)}, bf16[128,1024]{1,0:T(8,128)(2,1)S(1)}, u32[]{:S(2)}, u32[]{:S(2)}) collective-permute-start(bf16[128,1024]{1,0:T(8,128)(2,1)S(1)} %out_part.8), channel_id=1, source_target_pairs={{0,2},{1,3},{2,0},{3,1},{4,6},{5,7},{6,4},{7,5},{8,10},{9,11},{10,... | collective-permute-start | bytes 786440 | tf_op jit(solution)/shard_map/ppermute | solution.py:17
  56.0 5.6 %slice-start.2 = ((s8[8388608]{0:T(1024)(128)(4,1)}), s8[4194304]{0:T(1024)(128)(4,1)S(1)}, s32[]{:S(2)}) async-start(s8[8388608]{0:T(1024)(128)(4,1)} %bitcast.22), calls=%async_computation.2 | async-start | bytes 8388608
  57.3 4.2 %slice-start.3 = ((s8[8388608]{0:T(1024)(128)(4,1)}), s8[4194304]{0:T(1024)(128)(4,1)S(1)}, s32[]{:S(2)}) async-start(s8[8388608]{0:T(1024)(128)(4,1)} %bitcast.22), calls=%async_computation.3 | async-start | bytes 8388608
  57.4 11.8 %collective-permute-start.15 = (bf16[128,1024]{1,0:T(8,128)(2,1)S(1)}, bf16[128,1024]{1,0:T(8,128)(2,1)S(1)}, u32[]{:S(2)}, u32[]{:S(2)}) collective-permute-start(bf16[128,1024]{1,0:T(8,128)(2,1)S(1)} %out_part.9), channel_id=1, source_target_pairs={{0,1},{1,2},{2,3},{3,0},{4,5},{5,6},{6,7},{7,4},{8,9},{9,10},{10,1... | collective-permute-start | bytes 786440 | tf_op jit(solution)/shard_map/ppermute | solution.py:17
  57.4 25.0 %slice-start = ((s8[8388608]{0:T(1024)(128)(4,1)}), s8[4194304]{0:T(1024)(128)(4,1)S(1)}, s32[]{:S(2)}) async-start(s8[8388608]{0:T(1024)(128)(4,1)} %bitcast.20), calls=%async_computation | async-start | bytes 8388608
  57.5 25.0 %copy-start.8 = (bf16[1,4096,256]{2,1,0:T(8,128)(2,1)S(1)}, bf16[1,4096,256]{2,1,0:T(8,128)(2,1)}, u32[]{:S(2)}) copy-start(bf16[1,4096,256]{2,1,0:T(8,128)(2,1)} %refs_5_.15) | copy-start | bytes 6291460
  57.5 25.0 %copy-start.10 = (bf16[1,4096]{1,0:T(2,128)(2,1)S(1)}, bf16[1,4096]{1,0:T(2,128)(2,1)}, u32[]{:S(2)}) copy-start(bf16[1,4096]{1,0:T(2,128)(2,1)} %refs_2_.15) | copy-start | bytes 24580
  58.9 23.6 %slice-start.1 = ((s8[8388608]{0:T(1024)(128)(4,1)}), s8[4194304]{0:T(1024)(128)(4,1)S(1)}, s32[]{:S(2)}) async-start(s8[8388608]{0:T(1024)(128)(4,1)} %bitcast.20), calls=%async_computation.1 | async-start | bytes 8388608
  58.9 10.3 %collective-permute-start.16 = (bf16[128,1024]{1,0:T(8,128)(2,1)S(1)}, bf16[128,1024]{1,0:T(8,128)(2,1)S(1)}, u32[]{:S(2)}, u32[]{:S(2)}) collective-permute-start(bf16[128,1024]{1,0:T(8,128)(2,1)S(1)} %out_part.10), channel_id=1, source_target_pairs={{0,3},{1,0},{2,1},{3,2},{4,7},{5,4},{6,5},{7,6},{8,11},{9,8},{10,9... | collective-permute-start | bytes 786440 | tf_op jit(solution)/shard_map/ppermute | solution.py:17
  69.4 9.5 %collective-permute-start.17 = (bf16[128,1024]{1,0:T(8,128)(2,1)S(1)}, bf16[128,1024]{1,0:T(8,128)(2,1)S(1)}, u32[]{:S(2)}, u32[]{:S(2)}) collective-permute-start(bf16[128,1024]{1,0:T(8,128)(2,1)S(1)} %add_convert_fusion), channel_id=1, source_target_pairs={{0,64},{1,65},{2,66},{3,67},{4,68},{5,69},{6,70},{7,71},{8,72},{9,... | collective-permute-start | bytes 786440 | tf_op jit(solution)/shard_map/ppermute | solution.py:316
  78.9 8.0 %collective-permute-start.20 = (bf16[128,1024]{1,0:T(8,128)(2,1)S(1)}, bf16[128,1024]{1,0:T(8,128)(2,1)S(1)}, u32[]{:S(2)}, u32[]{:S(2)}) collective-permute-start(bf16[128,1024]{1,0:T(8,128)(2,1)S(1)} %collective-permute-done.17.refs_0_.refs_1_), channel_id=1, source_target_pairs={{0,1},{1,2},{2,3},{3,0},{4,5},{5,6},{6,7},{7,4},{8,9},{9,10},{10,1... | collective-permute-start | bytes 786440 | tf_op jit(solution)/shard_map/ppermute | solution.py:17
  78.9 9.3 %collective-permute-start.19 = (bf16[128,1024]{1,0:T(8,128)(2,1)S(1)}, bf16[128,1024]{1,0:T(8,128)(2,1)S(1)}, u32[]{:S(2)}, u32[]{:S(2)}) collective-permute-start(bf16[128,1024]{1,0:T(8,128)(2,1)S(1)} %collective-permute-done.17.refs_0_.refs_1_), channel_id=1, source_target_pairs={{0,3},{1,0},{2,1},{3,2},{4,7},{5,4},{6,5},{7,6},{8,11},{9,8},{10,9... | collective-permute-start | bytes 786440 | tf_op jit(solution)/shard_map/ppermute | solution.py:17
  81.6 10.3 %collective-permute-start.18 = (bf16[128,1024]{1,0:T(8,128)(2,1)S(1)}, bf16[128,1024]{1,0:T(8,128)(2,1)S(1)}, u32[]{:S(2)}, u32[]{:S(2)}) collective-permute-start(bf16[128,1024]{1,0:T(8,128)(2,1)S(1)} %collective-permute-done.17.refs_0_.refs_1_), channel_id=1, source_target_pairs={{0,2},{1,3},{2,0},{3,1},{4,6},{5,7},{6,4},{7,5},{8,10},{9,11},{10,... | collective-permute-start | bytes 786440 | tf_op jit(solution)/shard_map/ppermute | solution.py:17
  93.5 9.9 %collective-permute-start.21 = (bf16[128,512]{1,0:T(8,128)(2,1)S(1)}, bf16[128,512]{1,0:T(8,128)(2,1)S(1)}, u32[]{:S(2)}, u32[]{:S(2)}) collective-permute-start(bf16[128,512]{1,0:T(8,128)(2,1)S(1)} %get-tuple-element.44.refs_3_), channel_id=1, source_target_pairs={{0,8},{4,12},{8,16},{12,20},{16,24},{20,28},{24,0},{28,4},{32,40},... | collective-permute-start | bytes 393224 | tf_op jit(solution)/shard_map/ppermute | solution.py:32
  94.2 10.8 %collective-permute-start.22 = (bf16[128,512]{1,0:T(8,128)(2,1)S(1)}, bf16[128,512]{1,0:T(8,128)(2,1)S(1)}, u32[]{:S(2)}, u32[]{:S(2)}) collective-permute-start(bf16[128,512]{1,0:T(8,128)(2,1)S(1)} %get-tuple-element.44.refs_3_), channel_id=1, source_target_pairs={{0,16},{4,20},{8,24},{12,28},{16,0},{20,4},{24,8},{28,12},{32,48},... | collective-permute-start | bytes 393224 | tf_op jit(solution)/shard_map/ppermute | solution.py:32
  96.7 10.2 %collective-permute-start.23 = (bf16[128,512]{1,0:T(8,128)(2,1)S(1)}, bf16[128,512]{1,0:T(8,128)(2,1)S(1)}, u32[]{:S(2)}, u32[]{:S(2)}) collective-permute-start(bf16[128,512]{1,0:T(8,128)(2,1)S(1)} %get-tuple-element.44.refs_3_), channel_id=1, source_target_pairs={{0,24},{4,28},{8,0},{12,4},{16,8},{20,12},{24,16},{28,20},{32,56},... | collective-permute-start | bytes 393224 | tf_op jit(solution)/shard_map/ppermute | solution.py:32
  97.3 10.4 %collective-permute-start.24 = (bf16[128,512]{1,0:T(8,128)(2,1)S(1)}, bf16[128,512]{1,0:T(8,128)(2,1)S(1)}, u32[]{:S(2)}, u32[]{:S(2)}) collective-permute-start(bf16[128,512]{1,0:T(8,128)(2,1)S(1)} %get-tuple-element.44.refs_3_), channel_id=1, source_target_pairs={{0,4},{4,0},{8,12},{12,8},{16,20},{20,16},{24,28},{28,24},{32,36},... | collective-permute-start | bytes 393224 | tf_op jit(solution)/shard_map/ppermute | solution.py:36
  103.4 4.3 %collective-permute-start.25 = (bf16[128,512]{1,0:T(8,128)(2,1)S(1)}, bf16[128,512]{1,0:T(8,128)(2,1)S(1)}, u32[]{:S(2)}, u32[]{:S(2)}) collective-permute-start(bf16[128,512]{1,0:T(8,128)(2,1)S(1)} %collective-permute-done.21.refs_4_), channel_id=1, source_target_pairs={{0,4},{4,0},{8,12},{12,8},{16,20},{20,16},{24,28},{28,24},{32,36},... | collective-permute-start | bytes 393224 | tf_op jit(solution)/shard_map/ppermute | solution.py:36
  105.0 2.8 %collective-permute-start.26 = (bf16[128,512]{1,0:T(8,128)(2,1)S(1)}, bf16[128,512]{1,0:T(8,128)(2,1)S(1)}, u32[]{:S(2)}, u32[]{:S(2)}) collective-permute-start(bf16[128,512]{1,0:T(8,128)(2,1)S(1)} %collective-permute-done.22.refs_5_), channel_id=1, source_target_pairs={{0,4},{4,0},{8,12},{12,8},{16,20},{20,16},{24,28},{28,24},{32,36},... | collective-permute-start | bytes 393224 | tf_op jit(solution)/shard_map/ppermute | solution.py:36
  106.9 1.6 %collective-permute-start.27 = (bf16[128,512]{1,0:T(8,128)(2,1)S(1)}, bf16[128,512]{1,0:T(8,128)(2,1)S(1)}, u32[]{:S(2)}, u32[]{:S(2)}) collective-permute-start(bf16[128,512]{1,0:T(8,128)(2,1)S(1)} %collective-permute-done.23.refs_6_), channel_id=1, source_target_pairs={{0,4},{4,0},{8,12},{12,8},{16,20},{20,16},{24,28},{28,24},{32,36},... | collective-permute-start | bytes 393224 | tf_op jit(solution)/shard_map/ppermute | solution.py:36
  107.6 17.4 %collective-permute-start.31 = (bf16[64,1024]{1,0:T(8,128)(2,1)S(1)}, bf16[64,1024]{1,0:T(8,128)(2,1)S(1)}, u32[]{:S(2)}, u32[]{:S(2)}) collective-permute-start(bf16[64,1024]{1,0:T(8,128)(2,1)S(1)} %slice.9), channel_id=1, source_target_pairs={{0,32},{1,33},{2,34},{3,35},{4,36},{5,37},{6,38},{7,39},{8,40},{9,... | collective-permute-start | bytes 393224 | tf_op jit(solution)/shard_map/ppermute | solution.py:26
  111.1 3.4 %copy-start.3 = (bf16[1,1024,4096]{2,1,0:T(8,128)(2,1)S(1)}, bf16[1,1024,4096]{2,1,0:T(8,128)(2,1)}, u32[]{:S(2)}) copy-start(bf16[1,1024,4096]{2,1,0:T(8,128)(2,1)} %w.15) | copy-start | bytes 25165828
  115.8 7.7 %slice-start.4 = ((s8[8388608]{0:T(1024)(128)(4,1)}), s8[4194304]{0:T(1024)(128)(4,1)S(1)}, s32[]{:S(2)}) async-start(s8[8388608]{0:T(1024)(128)(4,1)} %bitcast.24), calls=%async_computation.4 | async-start | bytes 8388608
  115.9 9.5 %collective-permute-start.28 = (bf16[64,1024]{1,0:T(8,128)(2,1)S(1)}, bf16[64,1024]{1,0:T(8,128)(2,1)S(1)}, u32[]{:S(2)}, u32[]{:S(2)}) collective-permute-start(bf16[64,1024]{1,0:T(8,128)(2,1)S(1)} %get-tuple-element.45), channel_id=1, source_target_pairs={{0,2},{1,3},{2,0},{3,1},{4,6},{5,7},{6,4},{7,5},{8,10},{9,11},{10,... | collective-permute-start | bytes 393224 | tf_op jit(solution)/shard_map/ppermute | solution.py:17
  118.1 5.5 %slice-start.5 = ((s8[8388608]{0:T(1024)(128)(4,1)}), s8[4194304]{0:T(1024)(128)(4,1)S(1)}, s32[]{:S(2)}) async-start(s8[8388608]{0:T(1024)(128)(4,1)} %bitcast.24), calls=%async_computation.5 | async-start | bytes 8388608
  118.1 10.5 %collective-permute-start.29 = (bf16[64,1024]{1,0:T(8,128)(2,1)S(1)}, bf16[64,1024]{1,0:T(8,128)(2,1)S(1)}, u32[]{:S(2)}, u32[]{:S(2)}) collective-permute-start(bf16[64,1024]{1,0:T(8,128)(2,1)S(1)} %get-tuple-element.46), channel_id=1, source_target_pairs={{0,1},{1,2},{2,3},{3,0},{4,5},{5,6},{6,7},{7,4},{8,9},{9,10},{10,1... | collective-permute-start | bytes 393224 | tf_op jit(solution)/shard_map/ppermute | solution.py:17
  120.6 8.8 %collective-permute-start.30 = (bf16[64,1024]{1,0:T(8,128)(2,1)S(1)}, bf16[64,1024]{1,0:T(8,128)(2,1)S(1)}, u32[]{:S(2)}, u32[]{:S(2)}) collective-permute-start(bf16[64,1024]{1,0:T(8,128)(2,1)S(1)} %get-tuple-element.47), channel_id=1, source_target_pairs={{0,3},{1,0},{2,1},{3,2},{4,7},{5,4},{6,5},{7,6},{8,11},{9,8},{10,9... | collective-permute-start | bytes 393224 | tf_op jit(solution)/shard_map/ppermute | solution.py:17
  122.3 7.1 %collective-permute-start.32 = (bf16[64,1024]{1,0:T(8,128)(2,1)S(1)}, bf16[64,1024]{1,0:T(8,128)(2,1)S(1)}, u32[]{:S(2)}, u32[]{:S(2)}) collective-permute-start(bf16[64,1024]{1,0:T(8,128)(2,1)S(1)} %get-tuple-element.49), channel_id=1, source_target_pairs={{0,34},{1,35},{2,32},{3,33},{4,38},{5,39},{6,36},{7,37},{8,42},{9,... | collective-permute-start | bytes 393224 | tf_op jit(solution)/shard_map/ppermute | solution.py:26
  124.9 6.8 %collective-permute-start.33 = (bf16[64,1024]{1,0:T(8,128)(2,1)S(1)}, bf16[64,1024]{1,0:T(8,128)(2,1)S(1)}, u32[]{:S(2)}, u32[]{:S(2)}) collective-permute-start(bf16[64,1024]{1,0:T(8,128)(2,1)S(1)} %get-tuple-element.50), channel_id=1, source_target_pairs={{0,33},{1,34},{2,35},{3,32},{4,37},{5,38},{6,39},{7,36},{8,41},{9,... | collective-permute-start | bytes 393224 | tf_op jit(solution)/shard_map/ppermute | solution.py:26
  125.3 7.6 %collective-permute-start.34 = (bf16[64,1024]{1,0:T(8,128)(2,1)S(1)}, bf16[64,1024]{1,0:T(8,128)(2,1)S(1)}, u32[]{:S(2)}, u32[]{:S(2)}) collective-permute-start(bf16[64,1024]{1,0:T(8,128)(2,1)S(1)} %get-tuple-element.51), channel_id=1, source_target_pairs={{0,35},{1,32},{2,33},{3,34},{4,39},{5,36},{6,37},{7,38},{8,43},{9,... | collective-permute-start | bytes 393224 | tf_op jit(solution)/shard_map/ppermute | solution.py:26
  128.6 6.9 %collective-permute-start.35 = (bf16[64,1024]{1,0:T(8,128)(2,1)S(1)}, bf16[64,1024]{1,0:T(8,128)(2,1)S(1)}, u32[]{:S(2)}, u32[]{:S(2)}) collective-permute-start(bf16[64,1024]{1,0:T(8,128)(2,1)S(1)} %get-tuple-element.52), channel_id=1, source_target_pairs={{0,32},{1,33},{2,34},{3,35},{4,36},{5,37},{6,38},{7,39},{8,40},{9,... | collective-permute-start | bytes 393224 | tf_op jit(solution)/shard_map/ppermute | solution.py:26

commit v2 on v1

v2 whole, which is shorter than its diff:
```python
import itertools
import math
import jax
import jax.numpy as jnp
from jax import lax
from jax.experimental import pallas as pl
from jax.experimental.pallas import tpu as pltpu
from jax.sharding import PartitionSpec as P

HS = 128
EPS = 1e-05
CHUNKS = 2
VMEM = 56 * 1024 * 1024
AXES = ("section", "ctx", "tp")
FIRST, SECOND, BOTH = (0,), (1,), (0, 1)


def send(block, sections, by_tp=0, by_z=0, other_half=False, other_core=False, to=None):
    n_ctx = lax.axis_size("ctx")
    n_tp = lax.axis_size("tp")
    n_half = n_ctx // 2
    route = []
    for section, c, t in itertools.product(sections, range(n_ctx), range(n_tp)):
        there = (c % n_half + 2 * by_z) % n_half + c // n_half * n_half
        if other_half:
            there = (there + n_half) % n_ctx
        if other_core:
            there = there ^ 1
        end = section if to is None else to
        route.append(
            (
                (section * n_ctx + c) * n_tp + t,
                (end * n_ctx + there) * n_tp + (t + by_tp) % n_tp,
            )
        )
    return lax.ppermute(block, AXES, route)


def load_scaled(pieces, gain, offsets, scaled):
    total = None
    at = 0
    for n, rows_of in enumerate(pieces):
        x = jnp.concatenate([r[...] for r in rows_of], axis=0).astype(jnp.float32)
        width = x.shape[1]
        squares = jnp.sum(x * x, axis=-1, keepdims=True)
        total = squares if total is None else total + squares
        g = gain[:, pl.ds(pl.multiple_of(offsets(n), HS), width)]
        scaled[:, at : at + width] = (x * g).astype(jnp.bfloat16)
        at += width
    return total


def rotated(u, cos, sin):
    return u * cos + pltpu.roll(u, HS // 2, 1) * sin


def flat_pieces(pieces):
    return [r for _, rows_of in pieces for r in rows_of]


def regroup(refs, shapes):
    out, at = [], 0
    for n in shapes:
        out.append(refs[at : at + n])
        at += n
    return out, refs[at:]


def project_kv(pieces, gain, wk, wv, carry, rope, tile):
    counts = [len(r) for _, r in pieces]
    rows = sum(r.shape[0] for r in pieces[0][1])
    width = pieces[0][1][0].shape[1]
    kv_cols = wk.shape[2]
    per_piece = width // tile
    steps = per_piece * len(pieces)
    offs = jnp.stack([o for o, _ in pieces]).astype(jnp.int32)
    first, last = carry is None, rope is not None

    def body(off_ref, *refs):
        groups, refs = regroup(refs, counts)
        gain_ref, wk_ref, wv_ref = refs[:3]
        refs = refs[3:]
        if not first:
            acc_in, ss_in = refs[:2]
            refs = refs[2:]
        if last:
            cos, sin, out, r_out, acc, scaled = refs
        else:
            acc, r_out, scaled = refs
        i = pl.program_id(0)

        @pl.when(i == 0)
        def _():
            ss = load_scaled(groups, gain_ref, lambda n: off_ref[n], scaled)
            if not first:
                ss = ss + ss_in[...]
                acc[...] = acc_in[...]
            else:
                acc[...] = jnp.zeros_like(acc)
            r_out[...] = lax.rsqrt(ss / 4096.0 + EPS) if last else ss

        x = scaled[:, pl.ds(pl.multiple_of(i * tile, tile), tile)]
        acc[:, :kv_cols] += jnp.dot(x, wk_ref[0], preferred_element_type=jnp.float32)
        acc[:, kv_cols:] += jnp.dot(x, wv_ref[0], preferred_element_type=jnp.float32)

        if last:

            @pl.when(i == steps - 1)
            def _():
                r = r_out[...]
                for h in range(kv_cols // HS):
                    at = slice(h * HS, (h + 1) * HS)
                    out[:, at] = rotated(acc[:, at] * r, cos[...], sin[...]).astype(jnp.bfloat16)
                out[:, kv_cols:] = (acc[:, kv_cols:] * r).astype(jnp.bfloat16)

    def whole(shape):
        return pl.BlockSpec(shape, lambda i, o: (0,) * len(shape))

    w_spec = pl.BlockSpec(
        (1, tile, kv_cols), lambda i, o: (0, o[i // per_piece] // tile + i % per_piece, 0)
    )
    operands = flat_pieces(pieces) + [gain, wk, wv]
    in_specs = [whole(x.shape) for x in flat_pieces(pieces)] + [whole(gain.shape), w_spec, w_spec]
    if not first:
        operands += list(carry)
        in_specs += [whole(c.shape) for c in carry]
    scratch = [pltpu.VMEM((rows, width * len(pieces)), jnp.bfloat16)]
    if last:
        operands += list(rope)
        in_specs += [whole(c.shape) for c in rope]
        out_shape = [jax.ShapeDtypeStruct((rows, 2 * kv_cols), jnp.bfloat16)]
        scratch = [pltpu.VMEM((rows, 2 * kv_cols), jnp.float32)] + scratch
    else:
        out_shape = [jax.ShapeDtypeStruct((rows, 2 * kv_cols), jnp.float32)]
    out_shape.append(jax.ShapeDtypeStruct((rows, 1), jnp.float32))
    return pl.pallas_call(
        body,
        grid_spec=pltpu.PrefetchScalarGridSpec(
            num_scalar_prefetch=1,
            grid=(steps,),
            in_specs=in_specs,
            out_specs=[whole(o.shape) for o in out_shape],
            scratch_shapes=scratch,
        ),
        out_shape=out_shape,
        compiler_params=pltpu.CompilerParams(vmem_limit_bytes=VMEM),
        cost_estimate=pl.CostEstimate(
            flops=4 * rows * steps * tile * kv_cols,
            bytes_accessed=4 * steps * tile * kv_cols,
            transcendentals=0,
        ),
        name="project_kv",
    )(offs, *operands)


def project_q(pieces, gain, wq, r, rope, tile):
    counts = [len(p) for _, p in pieces]
    rows = sum(p.shape[0] for p in pieces[0][1])
    width = pieces[0][1][0].shape[1]
    cols = wq.shape[2]
    per_piece = width // tile
    steps = per_piece * len(pieces)
    offs = jnp.stack([o for o, _ in pieces]).astype(jnp.int32)

    def body(off_ref, *refs):
        groups, refs = regroup(refs, counts)
        gain_ref, w_ref, r_ref, cos, sin, out, acc, scaled = refs
        i = pl.program_id(0)

        @pl.when(i == 0)
        def _():
            load_scaled(groups, gain_ref, lambda n: off_ref[n], scaled)
            acc[...] = jnp.zeros_like(acc)

        x = scaled[:, pl.ds(pl.multiple_of(i * tile, tile), tile)]
        acc[...] += jnp.dot(x, w_ref[0], preferred_element_type=jnp.float32)

        @pl.when(i == steps - 1)
        def _():
            for h in range(cols // HS):
                at = slice(h * HS, (h + 1) * HS)
                out[:, at] = rotated(acc[:, at] * r_ref[...], cos[...], sin[...]).astype(
                    jnp.bfloat16
                )

    def whole(shape):
        return pl.BlockSpec(shape, lambda i, o: (0,) * len(shape))

    operands = flat_pieces(pieces) + [gain, wq, r, *rope]
    in_specs = [whole(x.shape) for x in operands]
    in_specs[len(flat_pieces(pieces)) + 1] = pl.BlockSpec(
        (1, tile, cols), lambda i, o: (0, o[i // per_piece] // tile + i % per_piece, 0)
    )
    return pl.pallas_call(
        body,
        grid_spec=pltpu.PrefetchScalarGridSpec(
            num_scalar_prefetch=1,
            grid=(steps,),
            in_specs=in_specs,
            out_specs=whole((rows, cols)),
            scratch_shapes=[
                pltpu.VMEM((rows, cols), jnp.float32),
                pltpu.VMEM((rows, width * len(pieces)), jnp.bfloat16),
            ],
        ),
        out_shape=jax.ShapeDtypeStruct((rows, cols), jnp.bfloat16),
        compiler_params=pltpu.CompilerParams(vmem_limit_bytes=VMEM),
        cost_estimate=pl.CostEstimate(
            flops=2 * rows * steps * tile * cols,
            bytes_accessed=2 * steps * tile * cols,
            transcendentals=0,
        ),
        name="project_q",
    )(offs, *operands)


def attend_kernel(q, qpos, kpos, *refs, kv_heads, group):
    *blocks, out = refs
    rows = q.shape[0]
    scale = 1.0 / math.sqrt(HS)
    allowed = kpos[...] <= qpos[...]
    allowed = jnp.concatenate([allowed] * group, axis=0)
    for g in range(kv_heads):
        k = jnp.concatenate([b[:, g * HS : (g + 1) * HS] for b in blocks], axis=0)
        lo = kv_heads * HS + g * HS
        v = jnp.concatenate([b[:, lo : lo + HS] for b in blocks], axis=0)
        heads = [g * group + j for j in range(group)]
        qs = jnp.concatenate([q[:, h * HS : (h + 1) * HS] for h in heads], axis=0)
        scores = (
            lax.dot_general(qs, k, (((1,), (1,)), ((), ())), preferred_element_type=jnp.float32)
            * scale
        )
        masked = jnp.where(allowed, scores, -1e30)
        best = jnp.max(masked, axis=-1, keepdims=True)
        weights = jnp.where(allowed, jnp.exp(masked - best), 0.0)
        total = jnp.sum(weights, axis=-1, keepdims=True)
        acc = jnp.dot(weights.astype(jnp.bfloat16), v, preferred_element_type=jnp.float32)
        attended = (acc / total).astype(jnp.bfloat16)
        for j, h in enumerate(heads):
            out[:, h * HS : (h + 1) * HS] = attended[j * rows : (j + 1) * rows]


def attend(q, qpos, kpos, blocks):
    rows, q_cols = q.shape
    kv_heads = blocks[0].shape[1] // (2 * HS)
    group = q_cols // HS // kv_heads

    def body(*refs):
        attend_kernel(*refs, kv_heads=kv_heads, group=group)

    keys = sum(b.shape[0] for b in blocks)
    return pl.pallas_call(
        body,
        out_shape=jax.ShapeDtypeStruct((rows, q_cols), jnp.bfloat16),
        compiler_params=pltpu.CompilerParams(vmem_limit_bytes=VMEM),
        cost_estimate=pl.CostEstimate(
            flops=4 * rows * q_cols * keys,
            bytes_accessed=4 * rows * q_cols,
            transcendentals=rows * keys * q_cols // HS,
        ),
        name="attend",
    )(q, qpos, kpos, *blocks)


def out_part(targets, attended, w_out, width, tile, split):
    rows, depth = attended.shape
    per_target = width // tile
    steps = per_target * len(targets)
    n_outs = 2 if split else 1
    half = rows // n_outs

    def body(col_ref, a, w, *outs):
        i = pl.program_id(0)
        part = jnp.dot(a[...], w[0], preferred_element_type=jnp.float32).astype(jnp.bfloat16)
        for n in range(len(targets)):

            @pl.when(i // per_target == n)
            def _():
                at = pl.ds(pl.multiple_of(i % per_target * tile, tile), tile)
                for m in range(n_outs):
                    outs[n * n_outs + m][:, at] = part[m * half : (m + 1) * half]

    cols = jnp.stack(targets).astype(jnp.int32)
    return pl.pallas_call(
        body,
        grid_spec=pltpu.PrefetchScalarGridSpec(
            num_scalar_prefetch=1,
            grid=(steps,),
            in_specs=[
                pl.BlockSpec((rows, depth), lambda i, c: (0, 0)),
                pl.BlockSpec(
                    (1, depth, tile),
                    lambda i, c: (0, 0, c[i // per_target] // tile + i % per_target),
                ),
            ],
            out_specs=[pl.BlockSpec((half, width), lambda i, c: (0, 0))] * n_outs * len(targets),
        ),
        out_shape=[jax.ShapeDtypeStruct((half, width), jnp.bfloat16)] * n_outs * len(targets),
        compiler_params=pltpu.CompilerParams(vmem_limit_bytes=VMEM),
        cost_estimate=pl.CostEstimate(
            flops=2 * rows * depth * width * len(targets),
            bytes_accessed=2 * depth * width * len(targets),
            transcendentals=0,
        ),
        name="out_part",
    )(cols, attended, w_out)


def add_all(x, parts):
    total = parts[0].astype(jnp.float32)
    for p in parts[1:]:
        total = total + p.astype(jnp.float32)
    return (x.astype(jnp.float32) + total).astype(jnp.bfloat16)


def per_device(tokens, norm_gain, wq, wk, wv, w_out):
    n_ctx = lax.axis_size("ctx")
    n_tp = lax.axis_size("tp")
    n_z = n_ctx // 4
    section = lax.axis_index("section")
    ctx = lax.axis_index("ctx")
    tp = lax.axis_index("tp")
    x_lo = ctx // (n_ctx // 2)
    z = (ctx // 2) % n_z
    core = ctx % 2
    half = tokens.shape[1]
    width = tokens.shape[2]
    chunk = width // CHUNKS
    gain = norm_gain.astype(jnp.float32)

    local = lax.iota(jnp.int32, half)

    def positions(z_of, core_of):
        base = (z_of * 2 + core_of) * half + local
        mine = x_lo * (n_ctx // 2) * half + base
        theirs = (1 - x_lo) * (n_ctx // 2) * half + base
        return jnp.concatenate([mine, theirs])

    qpos = positions(z, core)
    z_of = [(z - s) % n_z for s in range(n_z)]
    kpos = jnp.concatenate(
        [positions(zs, core) for zs in z_of] + [positions(zs, 1 - core) for zs in z_of]
    )
    pairs = lax.iota(jnp.int32, HS // 2).astype(jnp.float32)
    freqs = jnp.power(jnp.float32(500000.0), -2.0 * pairs / HS)
    angle = qpos.astype(jnp.float32)[:, None] * freqs[None, :]
    cosine = jnp.cos(angle)
    sine = jnp.sin(angle)
    rope = (
        jnp.concatenate([cosine, cosine], axis=1),
        jnp.concatenate([-sine, sine], axis=1),
    )
    qpos = qpos[:, None]
    kpos = kpos[None, :]
    src = [(tp - s) % n_tp * width for s in range(n_tp)]
    dst = [(tp + s) % n_tp * width for s in range(n_tp)]

    def mix(where, kv, make_q):
        mine = [kv] + [send(kv, where, by_z=s) for s in range(1, n_z)]
        q = make_q()
        theirs = [send(b, where, other_core=True) for b in mine]
        return attend(q, qpos, kpos, mine + theirs)

    own = lax.dynamic_index_in_dim(tokens, x_lo, 0, keepdims=False)
    other = lax.dynamic_index_in_dim(tokens, 1 - x_lo, 0, keepdims=False)
    own_from, other_from = [own], []
    for s in range(n_tp):
        if s:
            own_from.append(send(own, FIRST, by_tp=s))
        other_from.append(send(other, FIRST, by_tp=s, other_half=True))
    pieces = [(src[s], [own_from[s], other_from[s]]) for s in (0, 1, 3, 2)]
    carry = project_kv(pieces[:3], gain, wk, wv, None, None, 512)
    kv, r = project_kv(pieces[3:], gain, wk, wv, carry, rope, 512)
    attended = mix(FIRST, kv, lambda: project_q(pieces, gain, wq, r, rope, 512))

    x0 = jnp.concatenate([own, other_from[0]], axis=0)
    sums = []
    for c in range(CHUNKS):
        at = c * chunk
        parts = []
        (far,) = out_part([dst[2] + at], attended, w_out, chunk, 256, False)
        parts.append(send(far, FIRST, by_tp=2))
        near = out_part([dst[1] + at, dst[3] + at], attended, w_out, chunk, 256, False)
        parts.append(send(near[0], FIRST, by_tp=1))
        parts.append(send(near[1], FIRST, by_tp=3))
        parts.append(out_part([dst[0] + at], attended, w_out, chunk, 256, False)[0])
        sums.append(add_all(x0[:, at : at + chunk], parts))

    received = [send(x, FIRST, to=1) for x in sums]
    carry = None
    pieces = []
    for c in range(CHUNKS):
        got = [received[c]] + [send(received[c], SECOND, by_tp=s) for s in range(1, n_tp)]
        now = [(src[s] + c * chunk, [got[s]]) for s in (0, 1, 3, 2)]
        pieces += now
        carry = project_kv(now, gain, wk, wv, carry, rope if c == CHUNKS - 1 else None, chunk)
    kv, r = carry
    x1 = jnp.concatenate(
        [jnp.where(section == 0, a, b) for a, b in zip(sums, received)], axis=1
    )
    kept_own = x1[:half]
    kept_cross = x1[half:]
    kept_cross = send(kept_cross, BOTH, other_half=True)
    attended = mix(SECOND, kv, lambda: project_q(pieces, gain, wq, r, rope, chunk))
    own_parts, cross_parts = [], []
    for group in ((2,), (1, 3), (0,)):
        outs = out_part([dst[s] for s in group], attended, w_out, width, 256, True)
        for n, s in enumerate(group):
            cross_parts.append(send(outs[2 * n + 1], SECOND, by_tp=s, other_half=True))
            own_parts.append(outs[2 * n] if s == 0 else send(outs[2 * n], SECOND, by_tp=s))
    out_own = jnp.where(section == 0, kept_own, add_all(kept_own, own_parts))
    out_cross = jnp.where(section == 0, kept_cross, add_all(kept_cross, cross_parts))
    first = jnp.where(x_lo == 0, out_own, out_cross)
    second = jnp.where(x_lo == 0, out_cross, out_own)
    return jnp.stack([first, second])[None]


def solution(mesh):
    return jax.shard_map(
        per_device,
        mesh=mesh,
        in_specs=(
            P(None, "ctx", "tp"),
            P("section", None),
            P("section", None, "tp"),
            P("section", None, "tp"),
            P("section", None, "tp"),
            P("section", "tp", None),
        ),
        out_specs=P("section", None, "ctx", "tp"),
        check_vma=False,
    )
```

time: 138 us -> 249 us (1.80)
  the two profiles are of different devices: /device:TPU:1 before, /device:TPU:12 now
where the time goes in v2:
time: 249 us; the launch traced here: 247 us
  starting transfers between devices  86 us (35%)
  Pallas kernels  80.3 us (32%)
  waiting for transfers between devices  60.5 us (24%)
  other arithmetic  10 us (4%)
  local copies, waits for them, and re-layouts  9.05 us (4%)
    ppermute x43, starting transfers between devices, send(): return lax.ppermute(block, AXES, route)  86 us
    ppermute x43, waiting for transfers between devices, send(): return lax.ppermute(block, AXES, route)  60.5 us
    pallas_call x9, Pallas kernels, out_part(): pl.pallas_call(body, grid_spec=pltpu.PrefetchScalarGridSpec(num_scalar_pr...  33 us
    pallas_call x2, Pallas kernels, project_q(): pl.pallas_call(body, grid_spec=pltpu.PrefetchScalarGridSpec(num_scalar_pr...  19 us
    pallas_call x4, Pallas kernels, project_kv(): pl.pallas_call(body, grid_spec=pltpu.PrefetchScalarGridSpec(num_scalar_pr...  18.9 us
    pallas_call x2, Pallas kernels, attend(): pl.pallas_call(body, out_shape=jax.ShapeDtypeStruct((rows, q_cols), jnp.b...  9.38 us
    unnamed x72, local copies, waits for them, and re-layouts  5.98 us
  transfers between devices with their start and end apart: 43, of which 2 were waited for; matrix products, arithmetic and copies ran while one was open for 4% of the time, Pallas kernels for 26%

profile of v2, /device:TPU:12, one launch (start us, length us, event | category | flops | bytes accessed | tf_op | source)
XLA Modules:
  0.0 247.2 jit_solution(17488043475455977046)
XLA Ops:
  0.0 1.0 dynamic-slice_bitcast_fusion
  1.0 0.7 collective-permute-start
  1.7 0.7 collective-permute-start.2
  2.4 0.7 collective-permute-start.1
  3.0 0.7 collective-permute-start.3
  3.7 0.7 collective-permute-start.4
  5.0 0.7 pad_maximum_fusion.2.refs_7_.refs_11_.refs_9_
  5.7 0.7 pad_maximum_fusion.3.refs_8_.refs_12_.refs_10_
  6.5 1.3 convert_element_type.90.refs_6_.refs_2_.refs_8_.refs_4_
  8.5 0.7 collective-permute-start.6
  11.1 6.3 %project_kv.4 = (f32[128,512]{1,0:T(8,128)}, f32[128,1]{1,0:T(8,128)}) custom-call(s32[3]{0:T(128)} %pad_add_fusion.1.off_ref, bf16[64,1024]{1,0:T(8,128)(2,1)} %copy-done, bf16[64,1024]{1,0:T(8,128)(2,1)} %copy-done.2, bf16[64,1024]{1,0:T(8,128)(2,1)} %copy-done.7, bf16[64,1024]{1,0:T(8,128)(2,1)} %copy-done.6, bf16[64,1024]{1,0:T(8,128)(2,1)} %copy-done.8, ...), custom_call_target="tpu_custom_call" | custom-call | flops 402653184 | bytes 3145728 | tf_op jit(solution)/shard_map/project_kv/pallas_call | solution.py:136
  18.1 2.8 %project_kv.5 = (bf16[128,512]{1,0:T(8,128)(2,1)}, f32[128,1]{1,0:T(8,128)}) custom-call(s32[1]{0:T(128)} %bitcast.6.off_ref, bf16[64,1024]{1,0:T(8,128)(2,1)} %copy-done.10, bf16[64,1024]{1,0:T(8,128)(2,1)} %copy-done.11, f32[1,4096]{1,0:T(1,128)} %convert_element_type.90.refs_6_.refs_2_.refs_8_.refs_4_, bf16[1,4096,256]{2,1,0:T(8,128)(2,1)} %refs_5_.3, ...), custom_call_target="tpu_custom_call" | custom-call | flops 134217728 | bytes 1048576 | tf_op jit(solution)/shard_map/project_kv/pallas_call | solution.py:136
  21.6 0.7 collective-permute-start.8
  22.3 0.7 collective-permute-start.9
  24.3 0.7 collective-permute-start.11
  24.9 0.7 collective-permute-start.12
  25.6 0.7 collective-permute-start.13
  26.9 0.7 copy.7.refs_1_
  28.3 9.5 %project_q.2.refs_0_ = bf16[128,1024]{1,0:T(8,128)(2,1)} custom-call(s32[4]{0:T(128)} %pad_add_fusion.off_ref, bf16[64,1024]{1,0:T(8,128)(2,1)} %copy-done, bf16[64,1024]{1,0:T(8,128)(2,1)} %copy-done.2, bf16[64,1024]{1,0:T(8,128)(2,1)} %copy-done.7, bf16[64,1024]{1,0:T(8,128)(2,1)} %copy-done.6, bf16[64,1024]{1,0:T(8,128)(2,1)} %copy-done.8, ...), custom_call_target="tpu_custom_call" | custom-call | flops 1073741824 | bytes 8388608 | tf_op jit(solution)/shard_map/project_q/pallas_call | solution.py:194
  38.6 4.7 %attend.2.a = bf16[128,1024]{1,0:T(8,128)(2,1)} custom-call(bf16[128,1024]{1,0:T(8,128)(2,1)} %project_q.2.refs_0_, s32[128,1]{1,0:T(8,128)} %copy.7.refs_1_, s32[1,1024]{1,0:T(1,128)} %bitcast.27, bf16[128,512]{1,0:T(8,128)(2,1)} %get-tuple-element.28.refs_3_, bf16[128,512]{1,0:T(8,128)(2,1)} %copy-done.19, bf16[128,512]{1,0:T(8,128)(2,1)} %copy-done.20, ...), custom_call_target="tpu_custom_call" | custom-call | flops 536870912 | bytes 524288 | tf_op jit(solution)/shard_map/attend/pallas_call | solution.py:252
  43.3 4.4 %out_part.13 = (bf16[128,512]{1,0:T(8,128)(2,1)}, bf16[128,512]{1,0:T(8,128)(2,1)}) custom-call(s32[2]{0:T(128)} %pad_add_fusion.4.col_ref, bf16[128,1024]{1,0:T(8,128)(2,1)} %attend.2.a, bf16[1,1024,4096]{2,1,0:T(8,128)(2,1)} %w.17), custom_call_target="tpu_custom_call" | custom-call | flops 268435456 | bytes 2097152 | tf_op jit(solution)/shard_map/out_part/pallas_call | solution.py:284
  49.6 2.3 out_part.12
  52.6 4.4 %out_part.10 = (bf16[128,512]{1,0:T(8,128)(2,1)}, bf16[128,512]{1,0:T(8,128)(2,1)}) custom-call(s32[2]{0:T(128)} %pad_add_fusion.3.col_ref, bf16[128,1024]{1,0:T(8,128)(2,1)} %attend.2.a, bf16[1,1024,4096]{2,1,0:T(8,128)(2,1)} %w.17), custom_call_target="tpu_custom_call" | custom-call | flops 268435456 | bytes 2097152 | tf_op jit(solution)/shard_map/out_part/pallas_call | solution.py:284
  57.7 0.7 collective-permute-start.15
  58.4 2.3 out_part.9
  61.4 2.4 out_part.11
  63.8 2.3 out_part.14
  66.2 1.1 add_convert_fusion.2
  67.3 1.3 collective-permute-start.17
  68.6 1.3 collective-permute-start.21
  69.9 54.8 %collective-permute-done.17.refs_0_ = bf16[128,512]{1,0:T(8,128)(2,1)S(1)} collective-permute-done((bf16[128,512]{1,0:T(8,128)(2,1)S(1)}, bf16[128,512]{1,0:T(8,128)(2,1)S(1)}, u32[]{:S(2)}, u32[]{:S(2)}) %collective-permute-start.17) | collective-permute-done | bytes 131104 | tf_op jit(solution)/shard_map/ppermute | solution.py:36
  124.7 1.9 collective-permute-start.22
  126.6 0.7 stack.111.off_ref
  127.9 3.9 %collective-permute-start.23 = (bf16[128,512]{1,0:T(8,128)(2,1)S(1)}, bf16[128,512]{1,0:T(8,128)(2,1)S(1)}, u32[]{:S(2)}, u32[]{:S(2)}) collective-permute-start(bf16[128,512]{1,0:T(8,128)(2,1)S(1)} %collective-permute-done.17.refs_0_), channel_id=1, source_target_pairs={{64,67},{65,64},{66,65},{67,66},{68,71},{69,68},{70,69},{71,70},{7... | collective-permute-start | bytes 393224 | tf_op jit(solution)/shard_map/ppermute | solution.py:36
  131.8 3.3 %collective-permute-start.24 = (bf16[128,512]{1,0:T(8,128)(2,1)S(1)}, bf16[128,512]{1,0:T(8,128)(2,1)S(1)}, u32[]{:S(2)}, u32[]{:S(2)}) collective-permute-start(bf16[128,512]{1,0:T(8,128)(2,1)S(1)} %collective-permute-done.17.refs_0_), channel_id=1, source_target_pairs={{64,66},{65,67},{66,64},{67,65},{68,70},{69,71},{70,68},{71,69},{7... | collective-permute-start | bytes 393224 | tf_op jit(solution)/shard_map/ppermute | solution.py:36
  135.2 3.1 %collective-permute-start.25 = (bf16[128,512]{1,0:T(8,128)(2,1)S(1)}, bf16[128,512]{1,0:T(8,128)(2,1)S(1)}, u32[]{:S(2)}, u32[]{:S(2)}) collective-permute-start(bf16[128,512]{1,0:T(8,128)(2,1)S(1)} %collective-permute-done.21.refs_0_.refs_4_), channel_id=1, source_target_pairs={{64,65},{65,66},{66,67},{67,64},{68,69},{69,70},{70,71},{71,68},{7... | collective-permute-start | bytes 393224 | tf_op jit(solution)/shard_map/ppermute | solution.py:36
  138.3 2.8 %collective-permute-start.26 = (bf16[128,512]{1,0:T(8,128)(2,1)S(1)}, bf16[128,512]{1,0:T(8,128)(2,1)S(1)}, u32[]{:S(2)}, u32[]{:S(2)}) collective-permute-start(bf16[128,512]{1,0:T(8,128)(2,1)S(1)} %collective-permute-done.21.refs_0_.refs_4_), channel_id=1, source_target_pairs={{64,67},{65,64},{66,65},{67,66},{68,71},{69,68},{70,69},{71,70},{7... | collective-permute-start | bytes 393224 | tf_op jit(solution)/shard_map/ppermute | solution.py:36
  141.1 4.0 %collective-permute-start.27 = (bf16[128,512]{1,0:T(8,128)(2,1)S(1)}, bf16[128,512]{1,0:T(8,128)(2,1)S(1)}, u32[]{:S(2)}, u32[]{:S(2)}) collective-permute-start(bf16[128,512]{1,0:T(8,128)(2,1)S(1)} %collective-permute-done.21.refs_0_.refs_4_), channel_id=1, source_target_pairs={{64,66},{65,67},{66,64},{67,65},{68,70},{69,71},{70,68},{71,69},{7... | collective-permute-start | bytes 393224 | tf_op jit(solution)/shard_map/ppermute | solution.py:36
  146.4 4.7 %project_kv.6 = (f32[128,512]{1,0:T(8,128)}, f32[128,1]{1,0:T(8,128)}) custom-call(s32[4]{0:T(128)} %pad_add_fusion.off_ref, bf16[128,512]{1,0:T(8,128)(2,1)} %copy-done.4, bf16[128,512]{1,0:T(8,128)(2,1)} %copy-done.12, bf16[128,512]{1,0:T(8,128)(2,1)} %copy-done.13, bf16[128,512]{1,0:T(8,128)(2,1)} %copy-done.14, ...), custom_call_target="tpu_custom_call" | custom-call | flops 268435456 | bytes 2097152 | tf_op jit(solution)/shard_map/project_kv/pallas_call | solution.py:136
  151.9 5.0 %project_kv.7 = (bf16[128,512]{1,0:T(8,128)(2,1)}, f32[128,1]{1,0:T(8,128)}) custom-call(s32[4]{0:T(128)} %pad_add_fusion.5.off_ref, bf16[128,512]{1,0:T(8,128)(2,1)} %copy-done.5, bf16[128,512]{1,0:T(8,128)(2,1)} %copy-done.15, bf16[128,512]{1,0:T(8,128)(2,1)} %copy-done.16, bf16[128,512]{1,0:T(8,128)(2,1)} %copy-done.17, ...), custom_call_target="tpu_custom_call" | custom-call | flops 268435456 | bytes 2097152 | tf_op jit(solution)/shard_map/project_kv/pallas_call | solution.py:136
  157.0 2.9 %collective-permute-start.28 = (bf16[128,512]{1,0:T(8,128)(2,1)}, bf16[128,512]{1,0:T(8,128)(2,1)S(1)}, u32[]{:S(2)}, u32[]{:S(2)}) collective-permute-start(bf16[128,512]{1,0:T(8,128)(2,1)} %get-tuple-element.36.refs_3_), channel_id=1, source_target_pairs={{64,72},{65,73},{66,74},{67,75},{68,76},{69,77},{70,78},{71,79},{7... | collective-permute-start | bytes 393224 | tf_op jit(solution)/shard_map/ppermute | solution.py:36
  159.9 2.4 collective-permute-start.29
  162.3 4.1 %collective-permute-start.30 = (bf16[128,512]{1,0:T(8,128)(2,1)}, bf16[128,512]{1,0:T(8,128)(2,1)S(1)}, u32[]{:S(2)}, u32[]{:S(2)}) collective-permute-start(bf16[128,512]{1,0:T(8,128)(2,1)} %get-tuple-element.36.refs_3_), channel_id=1, source_target_pairs={{64,88},{65,89},{66,90},{67,91},{68,92},{69,93},{70,94},{71,95},{7... | collective-permute-start | bytes 393224 | tf_op jit(solution)/shard_map/ppermute | solution.py:36
  166.4 0.9 broadcast_select_fusion.1
  167.4 1.9 collective-permute-start.31
  169.3 2.4 collective-permute-start.32
  171.7 1.9 collective-permute-start.33
  173.7 2.4 collective-permute-start.34
  176.1 8.3 %collective-permute-start.38 = (bf16[64,1024]{1,0:T(8,128)(2,1)S(1)}, bf16[64,1024]{1,0:T(8,128)(2,1)S(1)}, u32[]{:S(2)}, u32[]{:S(2)}) collective-permute-start(bf16[64,1024]{1,0:T(8,128)(2,1)S(1)} %pad_maximum_fusion), channel_id=1, source_target_pairs={{0,32},{1,33},{2,34},{3,35},{4,36},{5,37},{6,38},{7,39},{8,40},{9,... | collective-permute-start | bytes 393224 | tf_op jit(solution)/shard_map/ppermute | solution.py:36
  184.4 9.5 %project_q.3.refs_0_ = bf16[128,1024]{1,0:T(8,128)(2,1)} custom-call(s32[8]{0:T(128)} %stack.111.off_ref, bf16[128,512]{1,0:T(8,128)(2,1)} %copy-done.4, bf16[128,512]{1,0:T(8,128)(2,1)} %copy-done.12, bf16[128,512]{1,0:T(8,128)(2,1)} %copy-done.13, bf16[128,512]{1,0:T(8,128)(2,1)} %copy-done.14, bf16[128,512]{1,0:T(8,128)(2,1)} %copy-done.5, ...), custom_call_target="tpu_custom_call" | custom-call | flops 1073741824 | bytes 8388608 | tf_op jit(solution)/shard_map/project_q/pallas_call | solution.py:194
  195.3 4.7 %attend.3.a = bf16[128,1024]{1,0:T(8,128)(2,1)} custom-call(bf16[128,1024]{1,0:T(8,128)(2,1)} %project_q.3.refs_0_, s32[128,1]{1,0:T(8,128)} %copy.7.refs_1_, s32[1,1024]{1,0:T(1,128)} %bitcast.28, bf16[128,512]{1,0:T(8,128)(2,1)} %get-tuple-element.36.refs_3_, bf16[128,512]{1,0:T(8,128)(2,1)} %copy-done.26, bf16[128,512]{1,0:T(8,128)(2,1)} %copy-done.27, ...), custom_call_target="tpu_custom_call" | custom-call | flops 536870912 | bytes 524288 | tf_op jit(solution)/shard_map/attend/pallas_call | solution.py:252
  200.0 7.3 %out_part.16 = (bf16[64,1024]{1,0:T(8,128)(2,1)}, bf16[64,1024]{1,0:T(8,128)(2,1)}, bf16[64,1024]{1,0:T(8,128)(2,1)}, bf16[64,1024]{1,0:T(8,128)(2,1)}) custom-call(s32[2]{0:T(128)} %pad_add_fusion.3.col_ref, bf16[128,1024]{1,0:T(8,128)(2,1)} %attend.3.a, bf16[1,1024,4096]{2,1,0:T(8,128)(2,1)} %w.17), custom_call_target="tpu_custom_call" | custom-call | flops 536870912 | bytes 4194304 | tf_op jit(solution)/shard_map/out_part/pallas_call | solution.py:284
  207.3 2.5 collective-permute-start.37
  209.7 3.5 %collective-permute-start.36 = (bf16[64,1024]{1,0:T(8,128)(2,1)}, bf16[64,1024]{1,0:T(8,128)(2,1)S(1)}, u32[]{:S(2)}, u32[]{:S(2)}) collective-permute-start(bf16[64,1024]{1,0:T(8,128)(2,1)} %get-tuple-element.38), channel_id=1, source_target_pairs={{64,65},{65,66},{66,67},{67,64},{68,69},{69,70},{70,71},{71,68},{7... | collective-permute-start | bytes 393224 | tf_op jit(solution)/shard_map/ppermute | solution.py:36
  213.3 3.8 %out_part.15 = (bf16[64,1024]{1,0:T(8,128)(2,1)}, bf16[64,1024]{1,0:T(8,128)(2,1)}) custom-call(s32[1]{0:T(128)} %bitcast.2.col_ref, bf16[128,1024]{1,0:T(8,128)(2,1)} %attend.3.a, bf16[1,1024,4096]{2,1,0:T(8,128)(2,1)} %w.17), custom_call_target="tpu_custom_call" | custom-call | flops 268435456 | bytes 2097152 | tf_op jit(solution)/shard_map/out_part/pallas_call | solution.py:284
  217.0 5.3 %collective-permute-start.35 = (bf16[64,1024]{1,0:T(8,128)(2,1)}, bf16[64,1024]{1,0:T(8,128)(2,1)S(1)}, u32[]{:S(2)}, u32[]{:S(2)}) collective-permute-start(bf16[64,1024]{1,0:T(8,128)(2,1)} %get-tuple-element.37), channel_id=1, source_target_pairs={{64,66},{65,67},{66,64},{67,65},{68,70},{69,71},{70,68},{71,69},{7... | collective-permute-start | bytes 393224 | tf_op jit(solution)/shard_map/ppermute | solution.py:36
  222.4 3.8 %out_part.17 = (bf16[64,1024]{1,0:T(8,128)(2,1)}, bf16[64,1024]{1,0:T(8,128)(2,1)}) custom-call(s32[1]{0:T(128)} %bitcast.3.col_ref, bf16[128,1024]{1,0:T(8,128)(2,1)} %attend.3.a, bf16[1,1024,4096]{2,1,0:T(8,128)(2,1)} %w.17), custom_call_target="tpu_custom_call" | custom-call | flops 268435456 | bytes 2097152 | tf_op jit(solution)/shard_map/out_part/pallas_call | solution.py:284
  226.1 3.1 %collective-permute-start.42 = (bf16[64,1024]{1,0:T(8,128)(2,1)}, bf16[64,1024]{1,0:T(8,128)(2,1)S(1)}, u32[]{:S(2)}, u32[]{:S(2)}) collective-permute-start(bf16[64,1024]{1,0:T(8,128)(2,1)} %get-tuple-element.44), channel_id=1, source_target_pairs={{64,96},{65,97},{66,98},{67,99},{68,100},{69,101},{70,102},{71,103... | collective-permute-start | bytes 393224 | tf_op jit(solution)/shard_map/ppermute | solution.py:36
  229.2 2.4 collective-permute-start.41
  231.7 4.3 %collective-permute-start.40 = (bf16[64,1024]{1,0:T(8,128)(2,1)S(1)}, bf16[64,1024]{1,0:T(8,128)(2,1)S(1)}, u32[]{:S(2)}, u32[]{:S(2)}) collective-permute-start(bf16[64,1024]{1,0:T(8,128)(2,1)S(1)} %copy-done.28), channel_id=1, source_target_pairs={{64,97},{65,98},{66,99},{67,96},{68,101},{69,102},{70,103},{71,100... | collective-permute-start | bytes 393224 | tf_op jit(solution)/shard_map/ppermute | solution.py:36
  236.0 3.6 %collective-permute-start.39 = (bf16[64,1024]{1,0:T(8,128)(2,1)S(1)}, bf16[64,1024]{1,0:T(8,128)(2,1)S(1)}, u32[]{:S(2)}, u32[]{:S(2)}) collective-permute-start(bf16[64,1024]{1,0:T(8,128)(2,1)S(1)} %copy-done.32), channel_id=1, source_target_pairs={{64,98},{65,99},{66,96},{67,97},{68,102},{69,103},{70,100},{71,101... | collective-permute-start | bytes 393224 | tf_op jit(solution)/shard_map/ppermute | solution.py:36
  239.7 5.6 %collective-permute-done.39 = bf16[64,1024]{1,0:T(8,128)(2,1)S(1)} collective-permute-done((bf16[64,1024]{1,0:T(8,128)(2,1)S(1)}, bf16[64,1024]{1,0:T(8,128)(2,1)S(1)}, u32[]{:S(2)}, u32[]{:S(2)}) %collective-permute-start.39) | collective-permute-done | bytes 131104 | tf_op jit(solution)/shard_map/ppermute | solution.py:36
  245.3 1.1 select_bitcast_fusion.1
  246.5 0.7 maximum_bitcast_fusion
  (142 shorter events, 15.4 us)
Async XLA Ops:
  1.0 8.8 %copy-start = (bf16[64,1024]{1,0:T(8,128)(2,1)}, bf16[64,1024]{1,0:T(8,128)(2,1)S(1)}, u32[]{:S(2)}) copy-start(bf16[64,1024]{1,0:T(8,128)(2,1)S(1)} %get-tuple-element.51.refs_0_) | copy-start | bytes 393220
  1.0 6.8 %collective-permute-start = (bf16[64,1024]{1,0:T(8,128)(2,1)S(1)}, bf16[64,1024]{1,0:T(8,128)(2,1)S(1)}, u32[]{:S(2)}, u32[]{:S(2)}) collective-permute-start(bf16[64,1024]{1,0:T(8,128)(2,1)S(1)} %get-tuple-element.50), channel_id=1, source_target_pairs={{0,32},{1,33},{2,34},{3,35},{4,36},{5,37},{6,38},{7,39},{8,40},{9,... | collective-permute-start | bytes 393224 | tf_op jit(solution)/shard_map/ppermute | solution.py:36
  1.7 8.1 %collective-permute-start.2 = (bf16[64,1024]{1,0:T(8,128)(2,1)S(1)}, bf16[64,1024]{1,0:T(8,128)(2,1)S(1)}, u32[]{:S(2)}, u32[]{:S(2)}) collective-permute-start(bf16[64,1024]{1,0:T(8,128)(2,1)S(1)} %get-tuple-element.50), channel_id=1, source_target_pairs={{0,33},{1,34},{2,35},{3,32},{4,37},{5,38},{6,39},{7,36},{8,41},{9,... | collective-permute-start | bytes 393224 | tf_op jit(solution)/shard_map/ppermute | solution.py:36
  2.4 6.2 %collective-permute-start.1 = (bf16[64,1024]{1,0:T(8,128)(2,1)S(1)}, bf16[64,1024]{1,0:T(8,128)(2,1)S(1)}, u32[]{:S(2)}, u32[]{:S(2)}) collective-permute-start(bf16[64,1024]{1,0:T(8,128)(2,1)S(1)} %get-tuple-element.51.refs_0_), channel_id=1, source_target_pairs={{0,1},{1,2},{2,3},{3,0},{4,5},{5,6},{6,7},{7,4},{8,9},{9,10},{10,1... | collective-permute-start | bytes 393224 | tf_op jit(solution)/shard_map/ppermute | solution.py:36
  3.0 6.8 %collective-permute-start.3 = (bf16[64,1024]{1,0:T(8,128)(2,1)S(1)}, bf16[64,1024]{1,0:T(8,128)(2,1)S(1)}, u32[]{:S(2)}, u32[]{:S(2)}) collective-permute-start(bf16[64,1024]{1,0:T(8,128)(2,1)S(1)} %get-tuple-element.51.refs_0_), channel_id=1, source_target_pairs={{0,3},{1,0},{2,1},{3,2},{4,7},{5,4},{6,5},{7,6},{8,11},{9,8},{10,9... | collective-permute-start | bytes 393224 | tf_op jit(solution)/shard_map/ppermute | solution.py:36
  3.7 6.1 %collective-permute-start.4 = (bf16[64,1024]{1,0:T(8,128)(2,1)S(1)}, bf16[64,1024]{1,0:T(8,128)(2,1)S(1)}, u32[]{:S(2)}, u32[]{:S(2)}) collective-permute-start(bf16[64,1024]{1,0:T(8,128)(2,1)S(1)} %get-tuple-element.50), channel_id=1, source_target_pairs={{0,35},{1,32},{2,33},{3,34},{4,39},{5,36},{6,37},{7,38},{8,43},{9,... | collective-permute-start | bytes 393224 | tf_op jit(solution)/shard_map/ppermute | solution.py:36
  7.8 2.0 copy-start.2
  7.8 9.6 %collective-permute-start.5 = (bf16[64,1024]{1,0:T(8,128)(2,1)S(1)}, bf16[64,1024]{1,0:T(8,128)(2,1)S(1)}, u32[]{:S(2)}, u32[]{:S(2)}) collective-permute-start(bf16[64,1024]{1,0:T(8,128)(2,1)S(1)} %get-tuple-element.51.refs_0_), channel_id=1, source_target_pairs={{0,2},{1,3},{2,0},{3,1},{4,6},{5,7},{6,4},{7,5},{8,10},{9,11},{10,... | collective-permute-start | bytes 393224 | tf_op jit(solution)/shard_map/ppermute | solution.py:36
  8.5 1.3 copy-start.7
  8.5 8.9 %collective-permute-start.6 = (bf16[64,1024]{1,0:T(8,128)(2,1)S(1)}, bf16[64,1024]{1,0:T(8,128)(2,1)S(1)}, u32[]{:S(2)}, u32[]{:S(2)}) collective-permute-start(bf16[64,1024]{1,0:T(8,128)(2,1)S(1)} %get-tuple-element.50), channel_id=1, source_target_pairs={{0,34},{1,35},{2,32},{3,33},{4,38},{5,39},{6,36},{7,37},{8,42},{9,... | collective-permute-start | bytes 393224 | tf_op jit(solution)/shard_map/ppermute | solution.py:36
  20.9 3.3 %collective-permute-start.7 = (bf16[128,512]{1,0:T(8,128)(2,1)}, bf16[128,512]{1,0:T(8,128)(2,1)S(1)}, u32[]{:S(2)}, u32[]{:S(2)}) collective-permute-start(bf16[128,512]{1,0:T(8,128)(2,1)} %get-tuple-element.28.refs_3_), channel_id=1, source_target_pairs={{0,8},{1,9},{2,10},{3,11},{4,12},{5,13},{6,14},{7,15},{8,16},{9,17... | collective-permute-start | bytes 393224 | tf_op jit(solution)/shard_map/ppermute | solution.py:36
  21.6 3.3 %collective-permute-start.8 = (bf16[128,512]{1,0:T(8,128)(2,1)}, bf16[128,512]{1,0:T(8,128)(2,1)S(1)}, u32[]{:S(2)}, u32[]{:S(2)}) collective-permute-start(bf16[128,512]{1,0:T(8,128)(2,1)} %get-tuple-element.28.refs_3_), channel_id=1, source_target_pairs={{0,16},{1,17},{2,18},{3,19},{4,20},{5,21},{6,22},{7,23},{8,24},{9,... | collective-permute-start | bytes 393224 | tf_op jit(solution)/shard_map/ppermute | solution.py:36
  22.3 3.3 %collective-permute-start.9 = (bf16[128,512]{1,0:T(8,128)(2,1)}, bf16[128,512]{1,0:T(8,128)(2,1)S(1)}, u32[]{:S(2)}, u32[]{:S(2)}) collective-permute-start(bf16[128,512]{1,0:T(8,128)(2,1)} %get-tuple-element.28.refs_3_), channel_id=1, source_target_pairs={{0,24},{1,25},{2,26},{3,27},{4,28},{5,29},{6,30},{7,31},{8,0},{9,1... | collective-permute-start | bytes 393224 | tf_op jit(solution)/shard_map/ppermute | solution.py:36
  23.6 14.3 %collective-permute-start.10 = (bf16[128,512]{1,0:T(8,128)(2,1)}, bf16[128,512]{1,0:T(8,128)(2,1)S(1)}, u32[]{:S(2)}, u32[]{:S(2)}) collective-permute-start(bf16[128,512]{1,0:T(8,128)(2,1)} %get-tuple-element.28.refs_3_), channel_id=1, source_target_pairs={{0,4},{1,5},{2,6},{3,7},{4,0},{5,1},{6,2},{7,3},{8,12},{9,13},{10,... | collective-permute-start | bytes 393224 | tf_op jit(solution)/shard_map/ppermute | solution.py:36
  24.2 13.7 %copy-start.19 = (bf16[128,512]{1,0:T(8,128)(2,1)}, bf16[128,512]{1,0:T(8,128)(2,1)S(1)}, u32[]{:S(2)}) copy-start(bf16[128,512]{1,0:T(8,128)(2,1)S(1)} %collective-permute-done.7.refs_4_) | copy-start | bytes 393220
  24.3 13.6 %collective-permute-start.11 = (bf16[128,512]{1,0:T(8,128)(2,1)S(1)}, bf16[128,512]{1,0:T(8,128)(2,1)S(1)}, u32[]{:S(2)}, u32[]{:S(2)}) collective-permute-start(bf16[128,512]{1,0:T(8,128)(2,1)S(1)} %collective-permute-done.7.refs_4_), channel_id=1, source_target_pairs={{0,4},{1,5},{2,6},{3,7},{4,0},{5,1},{6,2},{7,3},{8,12},{9,13},{10,... | collective-permute-start | bytes 393224 | tf_op jit(solution)/shard_map/ppermute | solution.py:36
  24.9 13.0 %copy-start.20 = (bf16[128,512]{1,0:T(8,128)(2,1)}, bf16[128,512]{1,0:T(8,128)(2,1)S(1)}, u32[]{:S(2)}) copy-start(bf16[128,512]{1,0:T(8,128)(2,1)S(1)} %collective-permute-done.8.refs_5_) | copy-start | bytes 393220
  24.9 12.9 %collective-permute-start.12 = (bf16[128,512]{1,0:T(8,128)(2,1)S(1)}, bf16[128,512]{1,0:T(8,128)(2,1)S(1)}, u32[]{:S(2)}, u32[]{:S(2)}) collective-permute-start(bf16[128,512]{1,0:T(8,128)(2,1)S(1)} %collective-permute-done.8.refs_5_), channel_id=1, source_target_pairs={{0,4},{1,5},{2,6},{3,7},{4,0},{5,1},{6,2},{7,3},{8,12},{9,13},{10,... | collective-permute-start | bytes 393224 | tf_op jit(solution)/shard_map/ppermute | solution.py:36
  25.6 12.3 %copy-start.21 = (bf16[128,512]{1,0:T(8,128)(2,1)}, bf16[128,512]{1,0:T(8,128)(2,1)S(1)}, u32[]{:S(2)}) copy-start(bf16[128,512]{1,0:T(8,128)(2,1)S(1)} %collective-permute-done.9.refs_6_) | copy-start | bytes 393220
  25.6 12.2 %collective-permute-start.13 = (bf16[128,512]{1,0:T(8,128)(2,1)S(1)}, bf16[128,512]{1,0:T(8,128)(2,1)S(1)}, u32[]{:S(2)}, u32[]{:S(2)}) collective-permute-start(bf16[128,512]{1,0:T(8,128)(2,1)S(1)} %collective-permute-done.9.refs_6_), channel_id=1, source_target_pairs={{0,4},{1,5},{2,6},{3,7},{4,0},{5,1},{6,2},{7,3},{8,12},{9,13},{10,... | collective-permute-start | bytes 393224 | tf_op jit(solution)/shard_map/ppermute | solution.py:36
  37.9 0.7 copy-start.24
  37.9 0.7 copy-start.25
  47.7 13.0 %collective-permute-start.20 = (bf16[128,512]{1,0:T(8,128)(2,1)}, bf16[128,512]{1,0:T(8,128)(2,1)S(1)}, u32[]{:S(2)}, u32[]{:S(2)}) collective-permute-start(bf16[128,512]{1,0:T(8,128)(2,1)} %get-tuple-element.32), channel_id=1, source_target_pairs={{0,3},{1,0},{2,1},{3,2},{4,7},{5,4},{6,5},{7,6},{8,11},{9,8},{10,9... | collective-permute-start | bytes 393224 | tf_op jit(solution)/shard_map/ppermute | solution.py:36
  49.0 17.2 %collective-permute-start.19 = (bf16[128,512]{1,0:T(8,128)(2,1)}, bf16[128,512]{1,0:T(8,128)(2,1)S(1)}, u32[]{:S(2)}, u32[]{:S(2)}) collective-permute-start(bf16[128,512]{1,0:T(8,128)(2,1)} %get-tuple-element.31), channel_id=1, source_target_pairs={{0,1},{1,2},{2,3},{3,0},{4,5},{5,6},{6,7},{7,4},{8,9},{9,10},{10,1... | collective-permute-start | bytes 393224 | tf_op jit(solution)/shard_map/ppermute | solution.py:36
  52.0 14.2 %collective-permute-start.18 = (bf16[128,512]{1,0:T(8,128)(2,1)}, bf16[128,512]{1,0:T(8,128)(2,1)S(1)}, u32[]{:S(2)}, u32[]{:S(2)}) collective-permute-start(bf16[128,512]{1,0:T(8,128)(2,1)} %out_part.12), channel_id=1, source_target_pairs={{0,2},{1,3},{2,0},{3,1},{4,6},{5,7},{6,4},{7,5},{8,10},{9,11},{10,... | collective-permute-start | bytes 393224 | tf_op jit(solution)/shard_map/ppermute | solution.py:36
  57.0 9.1 %collective-permute-start.16 = (bf16[128,512]{1,0:T(8,128)(2,1)}, bf16[128,512]{1,0:T(8,128)(2,1)S(1)}, u32[]{:S(2)}, u32[]{:S(2)}) collective-permute-start(bf16[128,512]{1,0:T(8,128)(2,1)} %get-tuple-element.30), channel_id=1, source_target_pairs={{0,3},{1,0},{2,1},{3,2},{4,7},{5,4},{6,5},{7,6},{8,11},{9,8},{10,9... | collective-permute-start | bytes 393224 | tf_op jit(solution)/shard_map/ppermute | solution.py:36
  57.7 8.4 %collective-permute-start.15 = (bf16[128,512]{1,0:T(8,128)(2,1)}, bf16[128,512]{1,0:T(8,128)(2,1)S(1)}, u32[]{:S(2)}, u32[]{:S(2)}) collective-permute-start(bf16[128,512]{1,0:T(8,128)(2,1)} %get-tuple-element.29), channel_id=1, source_target_pairs={{0,1},{1,2},{2,3},{3,0},{4,5},{5,6},{6,7},{7,4},{8,9},{9,10},{10,1... | collective-permute-start | bytes 393224 | tf_op jit(solution)/shard_map/ppermute | solution.py:36
  60.7 5.4 %collective-permute-start.14 = (bf16[128,512]{1,0:T(8,128)(2,1)}, bf16[128,512]{1,0:T(8,128)(2,1)S(1)}, u32[]{:S(2)}, u32[]{:S(2)}) collective-permute-start(bf16[128,512]{1,0:T(8,128)(2,1)} %out_part.9), channel_id=1, source_target_pairs={{0,2},{1,3},{2,0},{3,1},{4,6},{5,7},{6,4},{7,5},{8,10},{9,11},{10,... | collective-permute-start | bytes 393224 | tf_op jit(solution)/shard_map/ppermute | solution.py:36
  61.4 4.8 %copy-start.1 = (bf16[64,1024]{1,0:T(8,128)(2,1)S(1)}, bf16[64,1024]{1,0:T(8,128)(2,1)}, u32[]{:S(2)}) copy-start(bf16[64,1024]{1,0:T(8,128)(2,1)} %copy-done) | copy-start | bytes 393220
  61.4 4.8 %copy-start.3 = (bf16[64,1024]{1,0:T(8,128)(2,1)S(1)}, bf16[64,1024]{1,0:T(8,128)(2,1)}, u32[]{:S(2)}) copy-start(bf16[64,1024]{1,0:T(8,128)(2,1)} %copy-done.2) | copy-start | bytes 393220
  63.8 2.4 copy-start.18
  67.3 57.4 %collective-permute-start.17 = (bf16[128,512]{1,0:T(8,128)(2,1)S(1)}, bf16[128,512]{1,0:T(8,128)(2,1)S(1)}, u32[]{:S(2)}, u32[]{:S(2)}) collective-permute-start(bf16[128,512]{1,0:T(8,128)(2,1)S(1)} %get-tuple-element.49), channel_id=1, source_target_pairs={{0,64},{1,65},{2,66},{3,67},{4,68},{5,69},{6,70},{7,71},{8,72},{9,... | collective-permute-start | bytes 393224 | tf_op jit(solution)/shard_map/ppermute | solution.py:36
  68.6 66.6 %collective-permute-start.21 = (bf16[128,512]{1,0:T(8,128)(2,1)S(1)}, bf16[128,512]{1,0:T(8,128)(2,1)S(1)}, u32[]{:S(2)}, u32[]{:S(2)}) collective-permute-start(bf16[128,512]{1,0:T(8,128)(2,1)S(1)} %get-tuple-element.48), channel_id=1, source_target_pairs={{0,64},{1,65},{2,66},{3,67},{4,68},{5,69},{6,70},{7,71},{8,72},{9,... | collective-permute-start | bytes 393224 | tf_op jit(solution)/shard_map/ppermute | solution.py:36
  124.7 20.5 %copy-start.4 = (bf16[128,512]{1,0:T(8,128)(2,1)}, bf16[128,512]{1,0:T(8,128)(2,1)S(1)}, u32[]{:S(2)}) copy-start(bf16[128,512]{1,0:T(8,128)(2,1)S(1)} %collective-permute-done.17.refs_0_) | copy-start | bytes 393220
  124.7 16.3 %collective-permute-start.22 = (bf16[128,512]{1,0:T(8,128)(2,1)S(1)}, bf16[128,512]{1,0:T(8,128)(2,1)S(1)}, u32[]{:S(2)}, u32[]{:S(2)}) collective-permute-start(bf16[128,512]{1,0:T(8,128)(2,1)S(1)} %collective-permute-done.17.refs_0_), channel_id=1, source_target_pairs={{64,65},{65,66},{66,67},{67,64},{68,69},{69,70},{70,71},{71,68},{7... | collective-permute-start | bytes 393224 | tf_op jit(solution)/shard_map/ppermute | solution.py:36
  127.9 17.2 %collective-permute-start.23 = (bf16[128,512]{1,0:T(8,128)(2,1)S(1)}, bf16[128,512]{1,0:T(8,128)(2,1)S(1)}, u32[]{:S(2)}, u32[]{:S(2)}) collective-permute-start(bf16[128,512]{1,0:T(8,128)(2,1)S(1)} %collective-permute-done.17.refs_0_), channel_id=1, source_target_pairs={{64,67},{65,64},{66,65},{67,66},{68,71},{69,68},{70,69},{71,70},{7... | collective-permute-start | bytes 393224 | tf_op jit(solution)/shard_map/ppermute | solution.py:36
  131.8 13.3 %collective-permute-start.24 = (bf16[128,512]{1,0:T(8,128)(2,1)S(1)}, bf16[128,512]{1,0:T(8,128)(2,1)S(1)}, u32[]{:S(2)}, u32[]{:S(2)}) collective-permute-start(bf16[128,512]{1,0:T(8,128)(2,1)S(1)} %collective-permute-done.17.refs_0_), channel_id=1, source_target_pairs={{64,66},{65,67},{66,64},{67,65},{68,70},{69,71},{70,68},{71,69},{7... | collective-permute-start | bytes 393224 | tf_op jit(solution)/shard_map/ppermute | solution.py:36
  135.2 16.1 %copy-start.5 = (bf16[128,512]{1,0:T(8,128)(2,1)}, bf16[128,512]{1,0:T(8,128)(2,1)S(1)}, u32[]{:S(2)}) copy-start(bf16[128,512]{1,0:T(8,128)(2,1)S(1)} %collective-permute-done.21.refs_0_.refs_4_) | copy-start | bytes 393220
  135.2 16.0 %collective-permute-start.25 = (bf16[128,512]{1,0:T(8,128)(2,1)S(1)}, bf16[128,512]{1,0:T(8,128)(2,1)S(1)}, u32[]{:S(2)}, u32[]{:S(2)}) collective-permute-start(bf16[128,512]{1,0:T(8,128)(2,1)S(1)} %collective-permute-done.21.refs_0_.refs_4_), channel_id=1, source_target_pairs={{64,65},{65,66},{66,67},{67,64},{68,69},{69,70},{70,71},{71,68},{7... | collective-permute-start | bytes 393224 | tf_op jit(solution)/shard_map/ppermute | solution.py:36
  138.3 12.9 %collective-permute-start.26 = (bf16[128,512]{1,0:T(8,128)(2,1)S(1)}, bf16[128,512]{1,0:T(8,128)(2,1)S(1)}, u32[]{:S(2)}, u32[]{:S(2)}) collective-permute-start(bf16[128,512]{1,0:T(8,128)(2,1)S(1)} %collective-permute-done.21.refs_0_.refs_4_), channel_id=1, source_target_pairs={{64,67},{65,64},{66,65},{67,66},{68,71},{69,68},{70,69},{71,70},{7... | collective-permute-start | bytes 393224 | tf_op jit(solution)/shard_map/ppermute | solution.py:36
  141.1 4.1 %copy-start.12 = (bf16[128,512]{1,0:T(8,128)(2,1)}, bf16[128,512]{1,0:T(8,128)(2,1)S(1)}, u32[]{:S(2)}) copy-start(bf16[128,512]{1,0:T(8,128)(2,1)S(1)} %collective-permute-done.22.refs_1_) | copy-start | bytes 393220
  141.1 10.1 %collective-permute-start.27 = (bf16[128,512]{1,0:T(8,128)(2,1)S(1)}, bf16[128,512]{1,0:T(8,128)(2,1)S(1)}, u32[]{:S(2)}, u32[]{:S(2)}) collective-permute-start(bf16[128,512]{1,0:T(8,128)(2,1)S(1)} %collective-permute-done.21.refs_0_.refs_4_), channel_id=1, source_target_pairs={{64,66},{65,67},{66,64},{67,65},{68,70},{69,71},{70,68},{71,69},{7... | collective-permute-start | bytes 393224 | tf_op jit(solution)/shard_map/ppermute | solution.py:36
  151.2 0.7 copy-start.17
  157.0 12.3 %collective-permute-start.28 = (bf16[128,512]{1,0:T(8,128)(2,1)}, bf16[128,512]{1,0:T(8,128)(2,1)S(1)}, u32[]{:S(2)}, u32[]{:S(2)}) collective-permute-start(bf16[128,512]{1,0:T(8,128)(2,1)} %get-tuple-element.36.refs_3_), channel_id=1, source_target_pairs={{64,72},{65,73},{66,74},{67,75},{68,76},{69,77},{70,78},{71,79},{7... | collective-permute-start | bytes 393224 | tf_op jit(solution)/shard_map/ppermute | solution.py:36
  159.9 11.8 %collective-permute-start.29 = (bf16[128,512]{1,0:T(8,128)(2,1)}, bf16[128,512]{1,0:T(8,128)(2,1)S(1)}, u32[]{:S(2)}, u32[]{:S(2)}) collective-permute-start(bf16[128,512]{1,0:T(8,128)(2,1)} %get-tuple-element.36.refs_3_), channel_id=1, source_target_pairs={{64,80},{65,81},{66,82},{67,83},{68,84},{69,85},{70,86},{71,87},{7... | collective-permute-start | bytes 393224 | tf_op jit(solution)/shard_map/ppermute | solution.py:36
  162.3 11.4 %collective-permute-start.30 = (bf16[128,512]{1,0:T(8,128)(2,1)}, bf16[128,512]{1,0:T(8,128)(2,1)S(1)}, u32[]{:S(2)}, u32[]{:S(2)}) collective-permute-start(bf16[128,512]{1,0:T(8,128)(2,1)} %get-tuple-element.36.refs_3_), channel_id=1, source_target_pairs={{64,88},{65,89},{66,90},{67,91},{68,92},{69,93},{70,94},{71,95},{7... | collective-permute-start | bytes 393224 | tf_op jit(solution)/shard_map/ppermute | solution.py:36
  167.4 26.6 %collective-permute-start.31 = (bf16[128,512]{1,0:T(8,128)(2,1)}, bf16[128,512]{1,0:T(8,128)(2,1)S(1)}, u32[]{:S(2)}, u32[]{:S(2)}) collective-permute-start(bf16[128,512]{1,0:T(8,128)(2,1)} %get-tuple-element.36.refs_3_), channel_id=1, source_target_pairs={{64,68},{65,69},{66,70},{67,71},{68,64},{69,65},{70,66},{71,67},{7... | collective-permute-start | bytes 393224 | tf_op jit(solution)/shard_map/ppermute | solution.py:36
  169.3 24.7 %copy-start.26 = (bf16[128,512]{1,0:T(8,128)(2,1)}, bf16[128,512]{1,0:T(8,128)(2,1)S(1)}, u32[]{:S(2)}) copy-start(bf16[128,512]{1,0:T(8,128)(2,1)S(1)} %collective-permute-done.28.refs_4_) | copy-start | bytes 393220
  169.3 24.6 %collective-permute-start.32 = (bf16[128,512]{1,0:T(8,128)(2,1)S(1)}, bf16[128,512]{1,0:T(8,128)(2,1)S(1)}, u32[]{:S(2)}, u32[]{:S(2)}) collective-permute-start(bf16[128,512]{1,0:T(8,128)(2,1)S(1)} %collective-permute-done.28.refs_4_), channel_id=1, source_target_pairs={{64,68},{65,69},{66,70},{67,71},{68,64},{69,65},{70,66},{71,67},{7... | collective-permute-start | bytes 393224 | tf_op jit(solution)/shard_map/ppermute | solution.py:36
  171.7 22.3 %copy-start.27 = (bf16[128,512]{1,0:T(8,128)(2,1)}, bf16[128,512]{1,0:T(8,128)(2,1)S(1)}, u32[]{:S(2)}) copy-start(bf16[128,512]{1,0:T(8,128)(2,1)S(1)} %collective-permute-done.29.refs_5_) | copy-start | bytes 393220
  171.7 22.2 %collective-permute-start.33 = (bf16[128,512]{1,0:T(8,128)(2,1)S(1)}, bf16[128,512]{1,0:T(8,128)(2,1)S(1)}, u32[]{:S(2)}, u32[]{:S(2)}) collective-permute-start(bf16[128,512]{1,0:T(8,128)(2,1)S(1)} %collective-permute-done.29.refs_5_), channel_id=1, source_target_pairs={{64,68},{65,69},{66,70},{67,71},{68,64},{69,65},{70,66},{71,67},{7... | collective-permute-start | bytes 393224 | tf_op jit(solution)/shard_map/ppermute | solution.py:36
  173.7 20.3 %copy-start.29 = (bf16[128,512]{1,0:T(8,128)(2,1)}, bf16[128,512]{1,0:T(8,128)(2,1)S(1)}, u32[]{:S(2)}) copy-start(bf16[128,512]{1,0:T(8,128)(2,1)S(1)} %collective-permute-done.30.refs_6_) | copy-start | bytes 393220
  173.7 20.3 %collective-permute-start.34 = (bf16[128,512]{1,0:T(8,128)(2,1)S(1)}, bf16[128,512]{1,0:T(8,128)(2,1)S(1)}, u32[]{:S(2)}, u32[]{:S(2)}) collective-permute-start(bf16[128,512]{1,0:T(8,128)(2,1)S(1)} %collective-permute-done.30.refs_6_), channel_id=1, source_target_pairs={{64,68},{65,69},{66,70},{67,71},{68,64},{69,65},{70,66},{71,67},{7... | collective-permute-start | bytes 393224 | tf_op jit(solution)/shard_map/ppermute | solution.py:36
  176.1 53.1 %collective-permute-start.38 = (bf16[64,1024]{1,0:T(8,128)(2,1)S(1)}, bf16[64,1024]{1,0:T(8,128)(2,1)S(1)}, u32[]{:S(2)}, u32[]{:S(2)}) collective-permute-start(bf16[64,1024]{1,0:T(8,128)(2,1)S(1)} %pad_maximum_fusion), channel_id=1, source_target_pairs={{0,32},{1,33},{2,34},{3,35},{4,36},{5,37},{6,38},{7,39},{8,40},{9,... | collective-permute-start | bytes 393224 | tf_op jit(solution)/shard_map/ppermute | solution.py:36
  207.3 24.4 %collective-permute-start.37 = (bf16[64,1024]{1,0:T(8,128)(2,1)}, bf16[64,1024]{1,0:T(8,128)(2,1)S(1)}, u32[]{:S(2)}, u32[]{:S(2)}) collective-permute-start(bf16[64,1024]{1,0:T(8,128)(2,1)} %get-tuple-element.39), channel_id=1, source_target_pairs={{64,67},{65,64},{66,65},{67,66},{68,71},{69,68},{70,69},{71,70},{7... | collective-permute-start | bytes 393224 | tf_op jit(solution)/shard_map/ppermute | solution.py:36
  209.7 19.5 %copy-start.30 = (bf16[64,1024]{1,0:T(8,128)(2,1)S(1)}, bf16[64,1024]{1,0:T(8,128)(2,1)}, u32[]{:S(2)}) copy-start(bf16[64,1024]{1,0:T(8,128)(2,1)} %get-tuple-element.43) | copy-start | bytes 393220
  209.7 21.9 %copy-start.28 = (bf16[64,1024]{1,0:T(8,128)(2,1)S(1)}, bf16[64,1024]{1,0:T(8,128)(2,1)}, u32[]{:S(2)}) copy-start(bf16[64,1024]{1,0:T(8,128)(2,1)} %get-tuple-element.42) | copy-start | bytes 393220
  209.7 26.3 %collective-permute-start.36 = (bf16[64,1024]{1,0:T(8,128)(2,1)}, bf16[64,1024]{1,0:T(8,128)(2,1)S(1)}, u32[]{:S(2)}, u32[]{:S(2)}) collective-permute-start(bf16[64,1024]{1,0:T(8,128)(2,1)} %get-tuple-element.38), channel_id=1, source_target_pairs={{64,65},{65,66},{66,67},{67,64},{68,69},{69,70},{70,71},{71,68},{7... | collective-permute-start | bytes 393224 | tf_op jit(solution)/shard_map/ppermute | solution.py:36
  217.0 19.0 %copy-start.32 = (bf16[64,1024]{1,0:T(8,128)(2,1)S(1)}, bf16[64,1024]{1,0:T(8,128)(2,1)}, u32[]{:S(2)}) copy-start(bf16[64,1024]{1,0:T(8,128)(2,1)} %get-tuple-element.41) | copy-start | bytes 393220
  217.0 22.6 %collective-permute-start.35 = (bf16[64,1024]{1,0:T(8,128)(2,1)}, bf16[64,1024]{1,0:T(8,128)(2,1)S(1)}, u32[]{:S(2)}, u32[]{:S(2)}) collective-permute-start(bf16[64,1024]{1,0:T(8,128)(2,1)} %get-tuple-element.37), channel_id=1, source_target_pairs={{64,66},{65,67},{66,64},{67,65},{68,70},{69,71},{70,68},{71,69},{7... | collective-permute-start | bytes 393224 | tf_op jit(solution)/shard_map/ppermute | solution.py:36
  226.1 13.5 %collective-permute-start.42 = (bf16[64,1024]{1,0:T(8,128)(2,1)}, bf16[64,1024]{1,0:T(8,128)(2,1)S(1)}, u32[]{:S(2)}, u32[]{:S(2)}) collective-permute-start(bf16[64,1024]{1,0:T(8,128)(2,1)} %get-tuple-element.44), channel_id=1, source_target_pairs={{64,96},{65,97},{66,98},{67,99},{68,100},{69,101},{70,102},{71,103... | collective-permute-start | bytes 393224 | tf_op jit(solution)/shard_map/ppermute | solution.py:36
  229.2 10.4 %collective-permute-start.41 = (bf16[64,1024]{1,0:T(8,128)(2,1)S(1)}, bf16[64,1024]{1,0:T(8,128)(2,1)S(1)}, u32[]{:S(2)}, u32[]{:S(2)}) collective-permute-start(bf16[64,1024]{1,0:T(8,128)(2,1)S(1)} %copy-done.30), channel_id=1, source_target_pairs={{64,99},{65,96},{66,97},{67,98},{68,103},{69,100},{70,101},{71,102... | collective-permute-start | bytes 393224 | tf_op jit(solution)/shard_map/ppermute | solution.py:36
  231.7 8.0 %collective-permute-start.40 = (bf16[64,1024]{1,0:T(8,128)(2,1)S(1)}, bf16[64,1024]{1,0:T(8,128)(2,1)S(1)}, u32[]{:S(2)}, u32[]{:S(2)}) collective-permute-start(bf16[64,1024]{1,0:T(8,128)(2,1)S(1)} %copy-done.28), channel_id=1, source_target_pairs={{64,97},{65,98},{66,99},{67,96},{68,101},{69,102},{70,103},{71,100... | collective-permute-start | bytes 393224 | tf_op jit(solution)/shard_map/ppermute | solution.py:36
  236.0 9.3 %collective-permute-start.39 = (bf16[64,1024]{1,0:T(8,128)(2,1)S(1)}, bf16[64,1024]{1,0:T(8,128)(2,1)S(1)}, u32[]{:S(2)}, u32[]{:S(2)}) collective-permute-start(bf16[64,1024]{1,0:T(8,128)(2,1)S(1)} %copy-done.32), channel_id=1, source_target_pairs={{64,98},{65,99},{66,96},{67,97},{68,102},{69,103},{70,100},{71,101... | collective-permute-start | bytes 393224 | tf_op jit(solution)/shard_map/ppermute | solution.py:36
  (15 other events, 9.9 us)

commit v3 on v0

v3 whole, which is shorter than its diff:
```python
import itertools
import math
import jax
import jax.numpy as jnp
from jax import lax
from jax.experimental import pallas as pl
from jax.experimental.pallas import tpu as pltpu
from jax.sharding import PartitionSpec as P

HS = 128
EPS = 1e-05
CHUNKS = 2
SMALL = 12 * 1024 * 1024
LARGE = 28 * 1024 * 1024
SHIFTS = (2, 1, 3, 0)
AXES = ("section", "ctx", "tp")


def send(block, by_tp=0, by_z=0, other_half=False, other_core=False, next_layer=False):
    n_section = lax.axis_size("section")
    n_ctx = lax.axis_size("ctx")
    n_tp = lax.axis_size("tp")
    n_half = n_ctx // 2
    route = []
    for e, c, t in itertools.product(range(n_section), range(n_ctx), range(n_tp)):
        there = (c % n_half + 2 * by_z) % n_half + c // n_half * n_half
        if other_half or next_layer:
            there = (there + n_half) % n_ctx
        if other_core:
            there = there ^ 1
        end = (e + next_layer) % n_section
        route.append(
            ((e * n_ctx + c) * n_tp + t, (end * n_ctx + there) * n_tp + (t + by_tp) % n_tp)
        )
    return lax.ppermute(block, AXES, route)


def in_vmem(kernel, operands, out_shape, name, in_hbm=(), scratch=(), limit=None, flops=0):
    n_bytes = sum(x.size * x.dtype.itemsize for x in (*operands, *in_hbm))
    specs = [pl.BlockSpec(memory_space=pltpu.VMEM)] * len(operands)
    specs += [pl.BlockSpec(memory_space=pl.ANY)] * len(in_hbm)
    return pl.pallas_call(
        kernel,
        in_specs=specs,
        out_specs=[pl.BlockSpec(memory_space=pltpu.VMEM)] * len(out_shape),
        out_shape=[jax.ShapeDtypeStruct(shape, dtype) for shape, dtype in out_shape],
        scratch_shapes=list(scratch),
        compiler_params=pltpu.CompilerParams(vmem_limit_bytes=limit or SMALL),
        cost_estimate=pl.CostEstimate(flops=flops, bytes_accessed=n_bytes, transcendentals=0),
        name=name,
    )(*operands, *[pltpu.with_memory_space_constraint(w, pltpu.HBM) for w in in_hbm])


def from_slice(shift, at, width):
    n_tp = lax.axis_size("tp")
    tp = lax.axis_index("tp")
    return pl.multiple_of(lax.rem(tp + (n_tp - shift) % n_tp, n_tp) * width + at, HS)


def scaled_piece(rows_of, gain, start):
    x = jnp.concatenate([r[...] for r in rows_of], axis=0).astype(jnp.float32)
    g = gain[:, pl.ds(start, x.shape[1])]
    return (x * g).astype(jnp.bfloat16), jnp.sum(x * x, axis=-1, keepdims=True)


def rotated(u, cos, sin):
    return u * cos + pltpu.roll(u, HS // 2, 1) * sin


def flat_pieces(pieces):
    return [r for _, _, rows_of in pieces for r in rows_of]


def regroup(refs, pieces):
    out, at = [], 0
    for _, _, rows_of in pieces:
        out.append(refs[at : at + len(rows_of)])
        at += len(rows_of)
    return out, refs[at:]


def project_kv(pieces, slice_width, gain, weights, carry, rope, following):
    rows = sum(x.shape[0] for x in pieces[0][2])
    width = pieces[0][2][0].shape[1]
    kv_cols = weights[0].shape[-1]
    n = len(pieces)
    first, last = carry is None, rope is not None
    n_next = len(following)

    def body(*refs):
        groups, refs = regroup(refs, pieces)
        gain_ref = refs[0]
        refs = refs[1:]
        if not first:
            acc_in, ss_in = refs[:2]
            refs = refs[2:]
        if last:
            cos, sin = refs[:2]
            refs = refs[2:]
        w_refs = refs[:2]
        refs = refs[2:]
        copies = []
        if n_next:
            outs, next_refs, (held_k, held_v, sems) = refs[:2], refs[2:4], refs[4:]
            for j, (shift, at, *_) in enumerate(list(pieces) + list(following)):
                there = pl.ds(from_slice(shift, at, slice_width), width)
                to = pl.ds((j if j < n else j - n) * width, width)
                for m in range(2):
                    hold = (held_k, held_v)[m] if j < n else next_refs[m]
                    copies.append(
                        pltpu.make_async_copy(
                            w_refs[m].at[0, there, :], hold.at[to, :], sems.at[j, m]
                        )
                    )
            for c in copies:
                c.start()
            w_refs = (held_k, held_v)
        else:
            outs = refs
        ss = k = v = None
        if not first:
            ss, k, v = ss_in[...], acc_in[:, :kv_cols], acc_in[:, kv_cols:]
        for j, ((shift, at, _), rows_of) in enumerate(zip(pieces, groups)):
            start = from_slice(shift, at, slice_width)
            x, squares = scaled_piece(rows_of, gain_ref, start)
            here = slice(j * width, (j + 1) * width)
            if copies:
                copies[2 * j].wait()
            pk = jnp.dot(x, w_refs[0][here, :], preferred_element_type=jnp.float32)
            if copies:
                copies[2 * j + 1].wait()
            pv = jnp.dot(x, w_refs[1][here, :], preferred_element_type=jnp.float32)
            ss = squares if ss is None else ss + squares
            k = pk if k is None else k + pk
            v = pv if v is None else v + pv
        if last:
            out, r_out = outs
            r = lax.rsqrt(ss / 4096.0 + EPS)
            r_out[...] = r
            for h in range(kv_cols // HS):
                at = slice(h * HS, (h + 1) * HS)
                out[:, at] = rotated(k[:, at] * r, cos[...], sin[...]).astype(jnp.bfloat16)
            out[:, kv_cols:] = (v * r).astype(jnp.bfloat16)
        else:
            acc, ss_out = outs
            acc[:, :kv_cols] = k
            acc[:, kv_cols:] = v
            ss_out[...] = ss
        for c in copies[2 * n :]:
            c.wait()

    operands = flat_pieces(pieces) + [gain]
    operands += [] if first else list(carry)
    operands += list(rope) if last else []
    kind = jnp.bfloat16 if last else jnp.float32
    out_shape = [((rows, 2 * kv_cols), kind), ((rows, 1), jnp.float32)]
    scratch = []
    if n_next:
        out_shape += [((n_next * width, kv_cols), jnp.bfloat16)] * 2
        scratch = [pltpu.VMEM((n * width, kv_cols), jnp.bfloat16)] * 2
        scratch.append(pltpu.SemaphoreType.DMA((n + n_next, 2)))
    else:
        operands += list(weights)
    got = in_vmem(
        body,
        operands,
        out_shape,
        "project_kv",
        in_hbm=weights if n_next else (),
        scratch=scratch,
        flops=4 * rows * n * width * kv_cols,
    )
    return got[:2], got[2:]


def project_q(pieces, slice_width, gain, wq, r, rope):
    rows = sum(x.shape[0] for x in pieces[0][2])
    width = pieces[0][2][0].shape[1]
    cols = wq.shape[2]
    n = len(pieces)

    def body(*refs):
        groups, refs = regroup(refs, pieces)
        gain_ref, r_ref, cos, sin, w_ref, out, held, sems = refs
        starts = [from_slice(shift, at, slice_width) for shift, at, _ in pieces]
        copies = [
            pltpu.make_async_copy(w_ref.at[0, pl.ds(start, width), :], held.at[j], sems.at[j])
            for j, start in enumerate(starts)
        ]
        for c in copies:
            c.start()
        acc = None
        for j, rows_of in enumerate(groups):
            x, _ = scaled_piece(rows_of, gain_ref, starts[j])
            copies[j].wait()
            part = jnp.dot(x, held[j], preferred_element_type=jnp.float32)
            acc = part if acc is None else acc + part
        for h in range(cols // HS):
            at = slice(h * HS, (h + 1) * HS)
            out[:, at] = rotated(acc[:, at] * r_ref[...], cos[...], sin[...]).astype(
                jnp.bfloat16
            )

    return in_vmem(
        body,
        flat_pieces(pieces) + [gain, r, *rope],
        [((rows, cols), jnp.bfloat16)],
        "project_q",
        in_hbm=[wq],
        scratch=[
            pltpu.VMEM((n, width, cols), jnp.bfloat16),
            pltpu.SemaphoreType.DMA((n,)),
        ],
        limit=LARGE,
        flops=2 * rows * wq.size,
    )[0]


def attend_and_project(q, qpos, kpos, blocks, w_out, chunks, split):
    rows, q_cols = q.shape
    kv_heads = blocks[0].shape[1] // (2 * HS)
    group = q_cols // HS // kv_heads
    scale = 1.0 / math.sqrt(HS)
    n_blocks = len(blocks)
    keys = sum(b.shape[0] for b in blocks)
    _, depth, out_cols = w_out.shape
    slice_width = out_cols // len(SHIFTS)
    width = slice_width // chunks
    parts = [(c, s) for c in range(chunks) for s in SHIFTS]
    n_cut = 2 if split else 1
    half = rows // n_cut

    def body(q, qpos, kpos, *refs):
        block_refs, refs = refs[:n_blocks], refs[n_blocks:]
        w_ref, refs = refs[0], refs[1:]
        outs, (attended, held, sems) = refs[:-3], refs[-3:]
        copies = []
        for j, (c, s) in enumerate(parts):
            there = pl.ds(from_slice(-s, c * width, slice_width), width)
            copies.append(pltpu.make_async_copy(w_ref.at[0, :, there], held.at[j], sems.at[j]))
        for c in copies:
            c.start()
        allowed = kpos[...] <= qpos[...]
        allowed = jnp.concatenate([allowed] * group, axis=0)
        for g in range(kv_heads):
            k = jnp.concatenate([b[:, g * HS : (g + 1) * HS] for b in block_refs], axis=0)
            lo = kv_heads * HS + g * HS
            v = jnp.concatenate([b[:, lo : lo + HS] for b in block_refs], axis=0)
            heads = [g * group + j for j in range(group)]
            qs = jnp.concatenate([q[:, h * HS : (h + 1) * HS] for h in heads], axis=0)
            scores = lax.dot_general(
                qs, k, (((1,), (1,)), ((), ())), preferred_element_type=jnp.float32
            )
            masked = jnp.where(allowed, scores * scale, -1e30)
            best = jnp.max(masked, axis=-1, keepdims=True)
            weights = jnp.where(allowed, jnp.exp(masked - best), 0.0)
            total = jnp.sum(weights, axis=-1, keepdims=True)
            acc = jnp.dot(weights.astype(jnp.bfloat16), v, preferred_element_type=jnp.float32)
            normal = (acc / total).astype(jnp.bfloat16)
            for j, h in enumerate(heads):
                attended[:, h * HS : (h + 1) * HS] = normal[j * rows : (j + 1) * rows]
        for j in range(len(parts)):
            copies[j].wait()
            part = jnp.dot(attended[...], held[j], preferred_element_type=jnp.float32).astype(
                jnp.bfloat16
            )
            for m in range(n_cut):
                outs[j * n_cut + m][...] = part[m * half : (m + 1) * half]

    got = in_vmem(
        body,
        [q, qpos, kpos, *blocks],
        [((half, width), jnp.bfloat16)] * len(parts) * n_cut,
        "attend_and_project",
        in_hbm=[w_out],
        scratch=[
            pltpu.VMEM((rows, q_cols), jnp.bfloat16),
            pltpu.VMEM((len(parts), depth, width), jnp.bfloat16),
            pltpu.SemaphoreType.DMA((len(parts),)),
        ],
        limit=LARGE,
        flops=4 * rows * q_cols * keys + 2 * rows * w_out.size,
    )
    return [got[j * n_cut : (j + 1) * n_cut] for j in range(len(parts))]


def add_all(x, parts):
    total = parts[0].astype(jnp.float32)
    for p in parts[1:]:
        total = total + p.astype(jnp.float32)
    return (x.astype(jnp.float32) + total).astype(jnp.bfloat16)


def per_device(tokens, norm_gain, wq, wk, wv, w_out):
    n_ctx = lax.axis_size("ctx")
    n_tp = lax.axis_size("tp")
    n_z = n_ctx // 4
    section = lax.axis_index("section")
    ctx = lax.axis_index("ctx")
    x_lo = ctx // (n_ctx // 2)
    z = (ctx // 2) % n_z
    core = ctx % 2
    half = tokens.shape[1]
    width = tokens.shape[2]
    chunk = width // CHUNKS
    gain = norm_gain.astype(jnp.float32)

    local = lax.iota(jnp.int32, half)

    def positions(z_of, core_of):
        base = (z_of * 2 + core_of) * half + local
        mine = x_lo * (n_ctx // 2) * half + base
        theirs = (1 - x_lo) * (n_ctx // 2) * half + base
        return jnp.concatenate([mine, theirs])

    z_of = [(z - s) % n_z for s in range(n_z)]
    qpos = positions(z, core)
    kpos = jnp.concatenate(
        [positions(zs, core) for zs in z_of] + [positions(zs, 1 - core) for zs in z_of]
    )

    def tables(qpos):
        pairs = lax.iota(jnp.int32, HS // 2).astype(jnp.float32)
        freqs = jnp.power(jnp.float32(500000.0), -2.0 * pairs / HS)
        angle = qpos.astype(jnp.float32)[:, None] * freqs[None, :]
        cosine = jnp.cos(angle)
        sine = jnp.sin(angle)
        return (
            jnp.concatenate([cosine, cosine], axis=1),
            jnp.concatenate([-sine, sine], axis=1),
        )

    def swapped(rows):
        return jnp.concatenate([rows[half : 2 * half], rows[:half]], axis=0)

    rope = tables(qpos)

    def mix(kv, make_q, qpos, kpos, chunks, split):
        mine = [kv] + [send(kv, by_z=s) for s in (2, 1, 3)]
        q = make_q()
        theirs = [send(b, other_core=True) for b in mine]
        mine = [mine[0], mine[2], mine[1], mine[3]]
        theirs = [theirs[0], theirs[2], theirs[1], theirs[3]]
        return attend_and_project(
            q, qpos[:, None], kpos[None, :], mine + theirs, w_out, chunks, split
        )

    own = lax.dynamic_index_in_dim(tokens, x_lo, 0, keepdims=False)
    other = lax.dynamic_index_in_dim(tokens, 1 - x_lo, 0, keepdims=False)
    own_from, other_from = [own], []
    for s in range(n_tp):
        if s:
            own_from.append(send(own, by_tp=s))
        other_from.append(send(other, by_tp=s, other_half=True))
    pieces = [(s, 0, [own_from[s], other_from[s]]) for s in (0, 1, 3, 2)]
    carry, held = project_kv(pieces[:3], width, gain, (wk, wv), None, None, pieces[3:])
    (kv, r), _ = project_kv(pieces[3:], width, gain, held, carry, rope, ())
    got = mix(
        kv, lambda: project_q(pieces, width, gain, wq, r, rope), qpos, kpos, CHUNKS, False
    )
    x0 = jnp.concatenate([own, other_from[0]], axis=0)
    sums = []
    for c in range(CHUNKS):
        at = c * chunk
        parts = []
        for s, (block,) in zip(SHIFTS, got[c * n_tp : (c + 1) * n_tp]):
            parts.append(send(block, by_tp=s) if s else block)
        sums.append(add_all(x0[:, at : at + chunk], parts))

    received = [send(x, next_layer=True) for x in sums]
    qpos = swapped(qpos)
    kpos = swapped(kpos.reshape(-1, 2 * half).T).T.reshape(-1)
    rope = tuple(swapped(t) for t in rope)
    carry, held = None, (wk, wv)
    pieces = []
    for c in range(CHUNKS):
        got = [received[c]] + [send(received[c], by_tp=s) for s in (2, 1, 3)]
        pieces.append([(s, c * chunk, [g]) for s, g in zip((0, 2, 1, 3), got)])
    for c in range(CHUNKS):
        last = c == CHUNKS - 1
        following = () if last else pieces[c + 1]
        carry, held = project_kv(
            pieces[c], width, gain, held, carry, rope if last else None, following
        )
    kv, r = carry
    x1 = jnp.concatenate(sums, axis=1)
    came = jnp.concatenate(received, axis=1)
    kept_own = jnp.where(section == 0, x1[:half], came[half:])
    kept_cross = send(jnp.where(section == 0, x1[half:], came[:half]), other_half=True)
    every = [p for group in pieces for p in group]
    got = mix(kv, lambda: project_q(every, width, gain, wq, r, rope), qpos, kpos, 1, True)
    own_parts, cross_parts = [], []
    for s, (theirs, mine) in zip(SHIFTS, got):
        cross_parts.append(send(theirs, by_tp=s, other_half=True))
        own_parts.append(send(mine, by_tp=s) if s else mine)
    out_own = jnp.where(section == 0, kept_own, add_all(kept_own, own_parts))
    out_cross = jnp.where(section == 0, kept_cross, add_all(kept_cross, cross_parts))
    own_first = x_lo == section
    first = jnp.where(own_first, out_own, out_cross)
    second = jnp.where(own_first, out_cross, out_own)
    return jnp.stack([first, second])[None]


def solution(mesh):
    return jax.shard_map(
        per_device,
        mesh=mesh,
        in_specs=(
            P(None, "ctx", "tp"),
            P("section", None),
            P("section", None, "tp"),
            P("section", None, "tp"),
            P("section", None, "tp"),
            P("section", "tp", None),
        ),
        out_specs=P("section", None, "ctx", "tp"),
        check_vma=False,
    )
```

time: 329 us -> 122 us (0.37)
  blocking collectives: 163 us -> 0 us
  starting transfers between devices: 9.45 us -> 62.2 us
  matrix products: 48.8 us -> 0 us
  waiting for transfers between devices: 61.3 us -> 27.2 us
  Pallas kernels: 0 us -> 25.9 us
  local copies, waits for them, and re-layouts: 20.2 us -> 1.38 us
  between operations: 13.4 us -> 0.38 us
  other arithmetic: 11 us -> 2.79 us
    all_gather x9 -> x0, blocking collectives: 163 us -> none  [the longest x3 68 us: attend_block(): lax.all_gather(keys, 'ctx', axis=0, tiled=True)]
    reduce_scatter x3 -> x0, waiting for transfers between devices: 57.4 us -> none  [per_device(): lax.psum_scatter(partial_value.astype(jnp.bfloat16), 'tp', scatter_dimens...]
    ppermute x2 -> x43, starting transfers between devices: 9.37 us -> 62.2 us  [send(): return lax.ppermute(block, AXES, route)]
    dot_general x18 -> x0, matrix products: 48.8 us -> none  [the longest x3 18.4 us: attend_block(): jnp.dot(normed, w_query, preferred_element_type=jnp.float32)]
    pallas_call x0 -> x8, Pallas kernels: none -> 25.9 us  [in_vmem(): pl.pallas_call(kernel, in_specs=specs, out_specs=[pl.BlockSpec(memory_spa...]
    ppermute x2 -> x43, waiting for transfers between devices: 3.85 us -> 27.2 us  [send(): return lax.ppermute(block, AXES, route)]
    dot_general x2 -> x0, local copies, waits for them, and re-layouts: 15.4 us -> none  [the longest x1 11.3 us: attend_block(): jnp.dot(normed, w_query, preferred_element_type=jnp.float32)]
  transfers between devices with their start and end apart: 5 -> 43, of which waited for: 5 -> 14; matrix products, arithmetic and copies ran while one was open for 0% -> 2% of each run, Pallas kernels for 0% -> 16%
where the time goes in v3:
time: 122 us; the launch traced here: 120 us
  starting transfers between devices  62.2 us (51%)
  waiting for transfers between devices  27.2 us (22%)
  Pallas kernels  25.9 us (21%)
  other arithmetic  2.79 us (2%)
  local copies, waits for them, and re-layouts  1.38 us (1%)
    ppermute x43, starting transfers between devices, send(): return lax.ppermute(block, AXES, route)  62.2 us
    ppermute x43, waiting for transfers between devices, send(): return lax.ppermute(block, AXES, route)  27.2 us
    pallas_call x8, Pallas kernels, in_vmem(): pl.pallas_call(kernel, in_specs=specs, out_specs=[pl.BlockSpec(memory_spa...  25.9 us
  transfers between devices with their start and end apart: 43, of which 14 were waited for; matrix products, arithmetic and copies ran while one was open for 2% of the time, Pallas kernels for 16%

profile of v3, /device:TPU:1, one launch (start us, length us, event | category | flops | bytes accessed | tf_op | source)
XLA Modules:
  0.0 119.9 jit_solution(6396530750082364057)
XLA Ops:
  0.0 1.0 dynamic-slice_bitcast_fusion
  1.0 2.1 %collective-permute-start = (bf16[64,1024]{1,0:T(8,128)(2,1)S(1)}, bf16[64,1024]{1,0:T(8,128)(2,1)S(1)}, u32[]{:S(2)}, u32[]{:S(2)}) collective-permute-start(bf16[64,1024]{1,0:T(8,128)(2,1)S(1)} %get-tuple-element.66), channel_id=1, source_target_pairs={{0,32},{1,33},{2,34},{3,35},{4,36},{5,37},{6,38},{7,39},{8,40},{9,... | collective-permute-start | bytes 393224 | tf_op jit(solution)/shard_map/ppermute | solution.py:35
  3.1 1.3 %collective-permute-start.2 = (bf16[64,1024]{1,0:T(8,128)(2,1)S(1)}, bf16[64,1024]{1,0:T(8,128)(2,1)S(1)}, u32[]{:S(2)}, u32[]{:S(2)}) collective-permute-start(bf16[64,1024]{1,0:T(8,128)(2,1)S(1)} %get-tuple-element.66), channel_id=1, source_target_pairs={{0,33},{1,34},{2,35},{3,32},{4,37},{5,38},{6,39},{7,36},{8,41},{9,... | collective-permute-start | bytes 393224 | tf_op jit(solution)/shard_map/ppermute | solution.py:35
  4.4 1.3 %collective-permute-start.1 = (bf16[64,1024]{1,0:T(8,128)(2,1)S(1)}, bf16[64,1024]{1,0:T(8,128)(2,1)S(1)}, u32[]{:S(2)}, u32[]{:S(2)}) collective-permute-start(bf16[64,1024]{1,0:T(8,128)(2,1)S(1)} %get-tuple-element.67.refs_0_), channel_id=1, source_target_pairs={{0,1},{1,2},{2,3},{3,0},{4,5},{5,6},{6,7},{7,4},{8,9},{9,10},{10,1... | collective-permute-start | bytes 393224 | tf_op jit(solution)/shard_map/ppermute | solution.py:35
  5.7 1.4 %collective-permute-start.3 = (bf16[64,1024]{1,0:T(8,128)(2,1)S(1)}, bf16[64,1024]{1,0:T(8,128)(2,1)S(1)}, u32[]{:S(2)}, u32[]{:S(2)}) collective-permute-start(bf16[64,1024]{1,0:T(8,128)(2,1)S(1)} %get-tuple-element.67.refs_0_), channel_id=1, source_target_pairs={{0,3},{1,0},{2,1},{3,2},{4,7},{5,4},{6,5},{7,6},{8,11},{9,8},{10,9... | collective-permute-start | bytes 393224 | tf_op jit(solution)/shard_map/ppermute | solution.py:35
  7.1 1.2 collective-permute-start.4
  8.3 0.3 fusion.9
  8.9 0.7 convert_element_type.90.refs_6_.refs_2_.refs_8_.refs_4_
  9.7 1.7 %collective-permute-start.5 = (bf16[64,1024]{1,0:T(8,128)(2,1)S(1)}, bf16[64,1024]{1,0:T(8,128)(2,1)S(1)}, u32[]{:S(2)}, u32[]{:S(2)}) collective-permute-start(bf16[64,1024]{1,0:T(8,128)(2,1)S(1)} %get-tuple-element.67.refs_0_), channel_id=1, source_target_pairs={{0,2},{1,3},{2,0},{3,1},{4,6},{5,7},{6,4},{7,5},{8,10},{9,11},{10,... | collective-permute-start | bytes 393224 | tf_op jit(solution)/shard_map/ppermute | solution.py:35
  11.4 0.3 collective-permute-done.1.refs_2_
  11.7 3.3 %collective-permute-start.6 = (bf16[64,1024]{1,0:T(8,128)(2,1)S(1)}, bf16[64,1024]{1,0:T(8,128)(2,1)S(1)}, u32[]{:S(2)}, u32[]{:S(2)}) collective-permute-start(bf16[64,1024]{1,0:T(8,128)(2,1)S(1)} %get-tuple-element.66), channel_id=1, source_target_pairs={{0,34},{1,35},{2,32},{3,33},{4,38},{5,39},{6,36},{7,37},{8,42},{9,... | collective-permute-start | bytes 393224 | tf_op jit(solution)/shard_map/ppermute | solution.py:35
  15.0 2.6 %project_kv.4 = (f32[128,512]{1,0:T(8,128)S(1)}, f32[128,1]{1,0:T(8,128)S(1)}, bf16[1024,256]{1,0:T(8,128)(2,1)S(1)}, bf16[1024,256]{1,0:T(8,128)(2,1)S(1)}) custom-call(bf16[64,1024]{1,0:T(8,128)(2,1)S(1)} %get-tuple-element.67.refs_0_, bf16[64,1024]{1,0:T(8,128)(2,1)S(1)} %collective-permute-done.refs_1_, ...), custom_call_target="tpu_custom_call" | custom-call | flops 402653184 | bytes 4997120 | tf_op jit(solution)/shard_map/project_kv/pallas_call | solution.py:42
  17.6 0.4 collective-permute-done.6.refs_1_.refs_7_
  18.0 0.4 project_kv.5
  18.4 1.7 %collective-permute-start.7 = (bf16[128,512]{1,0:T(8,128)(2,1)S(1)}, bf16[128,512]{1,0:T(8,128)(2,1)S(1)}, u32[]{:S(2)}, u32[]{:S(2)}) collective-permute-start(bf16[128,512]{1,0:T(8,128)(2,1)S(1)} %get-tuple-element.38.refs_0_), channel_id=1, source_target_pairs={{0,8},{1,9},{2,10},{3,11},{4,12},{5,13},{6,14},{7,15},{8,16},{9,17... | collective-permute-start | bytes 393224 | tf_op jit(solution)/shard_map/ppermute | solution.py:35
  20.1 3.3 %collective-permute-start.8 = (bf16[128,512]{1,0:T(8,128)(2,1)S(1)}, bf16[128,512]{1,0:T(8,128)(2,1)S(1)}, u32[]{:S(2)}, u32[]{:S(2)}) collective-permute-start(bf16[128,512]{1,0:T(8,128)(2,1)S(1)} %get-tuple-element.38.refs_0_), channel_id=1, source_target_pairs={{0,16},{1,17},{2,18},{3,19},{4,20},{5,21},{6,22},{7,23},{8,24},{9,... | collective-permute-start | bytes 393224 | tf_op jit(solution)/shard_map/ppermute | solution.py:35
  23.4 0.7 collective-permute-start.9
  24.1 4.5 %collective-permute-start.10 = (bf16[128,512]{1,0:T(8,128)(2,1)S(1)}, bf16[128,512]{1,0:T(8,128)(2,1)S(1)}, u32[]{:S(2)}, u32[]{:S(2)}) collective-permute-start(bf16[128,512]{1,0:T(8,128)(2,1)S(1)} %get-tuple-element.38.refs_0_), channel_id=1, source_target_pairs={{0,4},{1,5},{2,6},{3,7},{4,0},{5,1},{6,2},{7,3},{8,12},{9,13},{10,... | collective-permute-start | bytes 393224 | tf_op jit(solution)/shard_map/ppermute | solution.py:35
  28.7 0.6 collective-permute-start.11
  29.3 2.7 %collective-permute-start.12 = (bf16[128,512]{1,0:T(8,128)(2,1)S(1)}, bf16[128,512]{1,0:T(8,128)(2,1)S(1)}, u32[]{:S(2)}, u32[]{:S(2)}) collective-permute-start(bf16[128,512]{1,0:T(8,128)(2,1)S(1)} %collective-permute-done.8.refs_2_), channel_id=1, source_target_pairs={{0,4},{1,5},{2,6},{3,7},{4,0},{5,1},{6,2},{7,3},{8,12},{9,13},{10,... | collective-permute-start | bytes 393224 | tf_op jit(solution)/shard_map/ppermute | solution.py:35
  32.0 0.6 collective-permute-start.13
  32.8 4.1 %project_q.2.q = bf16[128,1024]{1,0:T(8,128)(2,1)S(1)} custom-call(bf16[64,1024]{1,0:T(8,128)(2,1)S(1)} %get-tuple-element.67.refs_0_, bf16[64,1024]{1,0:T(8,128)(2,1)S(1)} %collective-permute-done.refs_1_, bf16[64,1024]{1,0:T(8,128)(2,1)S(1)} %collective-permute-done.1.refs_2_, bf16[64,1024]{1,0:T(8,128)(2,1)S(1)} %collective-permute-done.2.refs_3_, ...), custom_call_target="tpu_custom_call" | custom-call | flops 1073741824 | bytes 9585152 | tf_op jit(solution)/shard_map/project_q/pallas_call | solution.py:42
  36.9 6.1 %attend_and_project.2 = (bf16[128,512]{1,0:T(8,128)(2,1)S(1)}, bf16[128,512]{1,0:T(8,128)(2,1)S(1)}, bf16[128,512]{1,0:T(8,128)(2,1)S(1)}, bf16[128,512]{1,0:T(8...) custom-call(bf16[128,1024]{1,0:T(8,128)(2,1)S(1)} %project_q.2.q, ...), custom_call_target="tpu_custom_call" | custom-call | flops 1610612736 | bytes 9703936 | tf_op jit(solution)/shard_map/attend_and_project/pallas_call | solution.py:42
  43.0 1.7 %collective-permute-start.19 = (bf16[128,512]{1,0:T(8,128)(2,1)S(1)}, bf16[128,512]{1,0:T(8,128)(2,1)S(1)}, u32[]{:S(2)}, u32[]{:S(2)}) collective-permute-start(bf16[128,512]{1,0:T(8,128)(2,1)S(1)} %get-tuple-element.45), channel_id=1, source_target_pairs={{0,3},{1,0},{2,1},{3,2},{4,7},{5,4},{6,5},{7,6},{8,11},{9,8},{10,9... | collective-permute-start | bytes 393224 | tf_op jit(solution)/shard_map/ppermute | solution.py:35
  44.7 1.4 %collective-permute-start.17 = (bf16[128,512]{1,0:T(8,128)(2,1)S(1)}, bf16[128,512]{1,0:T(8,128)(2,1)S(1)}, u32[]{:S(2)}, u32[]{:S(2)}) collective-permute-start(bf16[128,512]{1,0:T(8,128)(2,1)S(1)} %get-tuple-element.43), channel_id=1, source_target_pairs={{0,2},{1,3},{2,0},{3,1},{4,6},{5,7},{6,4},{7,5},{8,10},{9,11},{10,... | collective-permute-start | bytes 393224 | tf_op jit(solution)/shard_map/ppermute | solution.py:35
  46.1 1.7 %collective-permute-start.16 = (bf16[128,512]{1,0:T(8,128)(2,1)S(1)}, bf16[128,512]{1,0:T(8,128)(2,1)S(1)}, u32[]{:S(2)}, u32[]{:S(2)}) collective-permute-start(bf16[128,512]{1,0:T(8,128)(2,1)S(1)} %get-tuple-element.41), channel_id=1, source_target_pairs={{0,3},{1,0},{2,1},{3,2},{4,7},{5,4},{6,5},{7,6},{8,11},{9,8},{10,9... | collective-permute-start | bytes 393224 | tf_op jit(solution)/shard_map/ppermute | solution.py:35
  48.0 0.4 collective-permute-done.19
  48.4 1.4 %collective-permute-start.14 = (bf16[128,512]{1,0:T(8,128)(2,1)S(1)}, bf16[128,512]{1,0:T(8,128)(2,1)S(1)}, u32[]{:S(2)}, u32[]{:S(2)}) collective-permute-start(bf16[128,512]{1,0:T(8,128)(2,1)S(1)} %get-tuple-element.39), channel_id=1, source_target_pairs={{0,2},{1,3},{2,0},{3,1},{4,6},{5,7},{6,4},{7,5},{8,10},{9,11},{10,... | collective-permute-start | bytes 393224 | tf_op jit(solution)/shard_map/ppermute | solution.py:35
  49.8 3.5 %collective-permute-done.18 = bf16[128,512]{1,0:T(8,128)(2,1)S(1)} collective-permute-done((bf16[128,512]{1,0:T(8,128)(2,1)S(1)}, bf16[128,512]{1,0:T(8,128)(2,1)S(1)}, u32[]{:S(2)}, u32[]{:S(2)}) %collective-permute-start.18) | collective-permute-done | bytes 131104 | tf_op jit(solution)/shard_map/ppermute | solution.py:35
  53.3 0.8 collective-permute-done.16
  54.1 5.0 %collective-permute-done.15 = bf16[128,512]{1,0:T(8,128)(2,1)S(1)} collective-permute-done((bf16[128,512]{1,0:T(8,128)(2,1)S(1)}, bf16[128,512]{1,0:T(8,128)(2,1)S(1)}, u32[]{:S(2)}, u32[]{:S(2)}) %collective-permute-start.15) | collective-permute-done | bytes 131104 | tf_op jit(solution)/shard_map/ppermute | solution.py:35
  59.2 0.2 add_convert_fusion.2
  59.3 3.2 %collective-permute-start.20 = (bf16[128,512]{1,0:T(8,128)(2,1)S(1)}, bf16[128,512]{1,0:T(8,128)(2,1)S(1)}, u32[]{:S(2)}, u32[]{:S(2)}) collective-permute-start(bf16[128,512]{1,0:T(8,128)(2,1)S(1)} %get-tuple-element.65), channel_id=1, source_target_pairs={{0,96},{1,97},{2,98},{3,99},{4,100},{5,101},{6,102},{7,103},{8,104... | collective-permute-start | bytes 393224 | tf_op jit(solution)/shard_map/ppermute | solution.py:35
  62.8 2.1 %collective-permute-done.20.refs_0_ = bf16[128,512]{1,0:T(8,128)(2,1)S(1)} collective-permute-done((bf16[128,512]{1,0:T(8,128)(2,1)S(1)}, bf16[128,512]{1,0:T(8,128)(2,1)S(1)}, u32[]{:S(2)}, u32[]{:S(2)}) %collective-permute-start.20) | collective-permute-done | bytes 131104 | tf_op jit(solution)/shard_map/ppermute | solution.py:35
  64.9 0.2 collective-permute-start.22
  65.2 2.7 %collective-permute-start.24 = (bf16[128,512]{1,0:T(8,128)(2,1)S(1)}, bf16[128,512]{1,0:T(8,128)(2,1)S(1)}, u32[]{:S(2)}, u32[]{:S(2)}) collective-permute-start(bf16[128,512]{1,0:T(8,128)(2,1)S(1)} %collective-permute-done.20.refs_0_), channel_id=1, source_target_pairs={{0,3},{1,0},{2,1},{3,2},{4,7},{5,4},{6,5},{7,6},{8,11},{9,8},{10,9... | collective-permute-start | bytes 393224 | tf_op jit(solution)/shard_map/ppermute | solution.py:35
  68.0 1.6 %collective-permute-start.25 = (bf16[128,512]{1,0:T(8,128)(2,1)S(1)}, bf16[128,512]{1,0:T(8,128)(2,1)S(1)}, u32[]{:S(2)}, u32[]{:S(2)}) collective-permute-start(bf16[128,512]{1,0:T(8,128)(2,1)S(1)} %collective-permute-done.21.refs_0_.refs_4_), channel_id=1, source_target_pairs={{0,2},{1,3},{2,0},{3,1},{4,6},{5,7},{6,4},{7,5},{8,10},{9,11},{10,... | collective-permute-start | bytes 393224 | tf_op jit(solution)/shard_map/ppermute | solution.py:35
  69.6 0.8 collective-permute-done.22.refs_1_
  70.4 1.9 %collective-permute-start.27 = (bf16[128,512]{1,0:T(8,128)(2,1)S(1)}, bf16[128,512]{1,0:T(8,128)(2,1)S(1)}, u32[]{:S(2)}, u32[]{:S(2)}) collective-permute-start(bf16[128,512]{1,0:T(8,128)(2,1)S(1)} %collective-permute-done.21.refs_0_.refs_4_), channel_id=1, source_target_pairs={{0,3},{1,0},{2,1},{3,2},{4,7},{5,4},{6,5},{7,6},{8,11},{9,8},{10,9... | collective-permute-start | bytes 393224 | tf_op jit(solution)/shard_map/ppermute | solution.py:35
  72.3 0.4 collective-permute-done.24.refs_3_
  72.7 2.3 %project_kv.6 = (f32[128,512]{1,0:T(8,128)S(1)}, f32[128,1]{1,0:T(8,128)S(1)}, bf16[2048,256]{1,0:T(8,128)(2,1)S(1)}, bf16[2048,256]{1,0:T(8,128)(2,1)S(1)}) custom-call(bf16[128,512]{1,0:T(8,128)(2,1)S(1)} %collective-permute-done.20.refs_0_, bf16[128,512]{1,0:T(8,128)(2,1)S(1)} %collective-permute-done.22.refs_1_, ...), custom_call_target="tpu_custom_call" | custom-call | flops 268435456 | bytes 4734976 | tf_op jit(solution)/shard_map/project_kv/pallas_call | solution.py:42
  75.0 2.8 %collective-permute-done.26.refs_2_.refs_6_ = bf16[128,512]{1,0:T(8,128)(2,1)S(1)} collective-permute-done((bf16[128,512]{1,0:T(8,128)(2,1)S(1)}, bf16[128,512]{1,0:T(8,128)(2,1)S(1)}, u32[]{:S(2)}, u32[]{:S(2)}) %collective-permute-start.26) | collective-permute-done | bytes 131104 | tf_op jit(solution)/shard_map/ppermute | solution.py:35
  77.8 0.6 project_kv.7
  78.4 2.9 %collective-permute-start.28 = (bf16[128,512]{1,0:T(8,128)(2,1)S(1)}, bf16[128,512]{1,0:T(8,128)(2,1)S(1)}, u32[]{:S(2)}, u32[]{:S(2)}) collective-permute-start(bf16[128,512]{1,0:T(8,128)(2,1)S(1)} %get-tuple-element.52.refs_0_), channel_id=1, source_target_pairs={{0,8},{1,9},{2,10},{3,11},{4,12},{5,13},{6,14},{7,15},{8,16},{9,17... | collective-permute-start | bytes 393224 | tf_op jit(solution)/shard_map/ppermute | solution.py:35
  81.3 1.5 %collective-permute-start.29 = (bf16[128,512]{1,0:T(8,128)(2,1)S(1)}, bf16[128,512]{1,0:T(8,128)(2,1)S(1)}, u32[]{:S(2)}, u32[]{:S(2)}) collective-permute-start(bf16[128,512]{1,0:T(8,128)(2,1)S(1)} %get-tuple-element.52.refs_0_), channel_id=1, source_target_pairs={{0,16},{1,17},{2,18},{3,19},{4,20},{5,21},{6,22},{7,23},{8,24},{9,... | collective-permute-start | bytes 393224 | tf_op jit(solution)/shard_map/ppermute | solution.py:35
  82.7 1.6 %collective-permute-start.30 = (bf16[128,512]{1,0:T(8,128)(2,1)S(1)}, bf16[128,512]{1,0:T(8,128)(2,1)S(1)}, u32[]{:S(2)}, u32[]{:S(2)}) collective-permute-start(bf16[128,512]{1,0:T(8,128)(2,1)S(1)} %get-tuple-element.52.refs_0_), channel_id=1, source_target_pairs={{0,24},{1,25},{2,26},{3,27},{4,28},{5,29},{6,30},{7,31},{8,0},{9,1... | collective-permute-start | bytes 393224 | tf_op jit(solution)/shard_map/ppermute | solution.py:35
  84.4 3.0 %collective-permute-start.31 = (bf16[128,512]{1,0:T(8,128)(2,1)S(1)}, bf16[128,512]{1,0:T(8,128)(2,1)S(1)}, u32[]{:S(2)}, u32[]{:S(2)}) collective-permute-start(bf16[128,512]{1,0:T(8,128)(2,1)S(1)} %get-tuple-element.52.refs_0_), channel_id=1, source_target_pairs={{0,4},{1,5},{2,6},{3,7},{4,0},{5,1},{6,2},{7,3},{8,12},{9,13},{10,... | collective-permute-start | bytes 393224 | tf_op jit(solution)/shard_map/ppermute | solution.py:35
  87.4 1.3 %collective-permute-start.32 = (bf16[128,512]{1,0:T(8,128)(2,1)S(1)}, bf16[128,512]{1,0:T(8,128)(2,1)S(1)}, u32[]{:S(2)}, u32[]{:S(2)}) collective-permute-start(bf16[128,512]{1,0:T(8,128)(2,1)S(1)} %collective-permute-done.28.refs_1_), channel_id=1, source_target_pairs={{0,4},{1,5},{2,6},{3,7},{4,0},{5,1},{6,2},{7,3},{8,12},{9,13},{10,... | collective-permute-start | bytes 393224 | tf_op jit(solution)/shard_map/ppermute | solution.py:35
  88.7 1.4 %collective-permute-start.33 = (bf16[128,512]{1,0:T(8,128)(2,1)S(1)}, bf16[128,512]{1,0:T(8,128)(2,1)S(1)}, u32[]{:S(2)}, u32[]{:S(2)}) collective-permute-start(bf16[128,512]{1,0:T(8,128)(2,1)S(1)} %collective-permute-done.29.refs_2_), channel_id=1, source_target_pairs={{0,4},{1,5},{2,6},{3,7},{4,0},{5,1},{6,2},{7,3},{8,12},{9,13},{10,... | collective-permute-start | bytes 393224 | tf_op jit(solution)/shard_map/ppermute | solution.py:35
  90.1 0.6 collective-permute-start.34
  90.7 0.5 collective-permute-start.38
  91.2 3.9 %project_q.3.q = bf16[128,1024]{1,0:T(8,128)(2,1)S(1)} custom-call(bf16[128,512]{1,0:T(8,128)(2,1)S(1)} %collective-permute-done.20.refs_0_, bf16[128,512]{1,0:T(8,128)(2,1)S(1)} %collective-permute-done.22.refs_1_, bf16[128,512]{1,0:T(8,128)(2,1)S(1)} %collective-permute-done.23.refs_2_, bf16[128,512]{1,0:T(8,128)(2,1)S(1)} %collective-permute-done.24.refs_3_, ...), custom_call_target="tpu_custom_call" | custom-call | flops 1073741824 | bytes 9585152 | tf_op jit(solution)/shard_map/project_q/pallas_call | solution.py:42
  95.2 6.1 %attend_and_project.3 = (bf16[64,1024]{1,0:T(8,128)(2,1)S(1)}, bf16[64,1024]{1,0:T(8,128)(2,1)S(1)}, bf16[64,1024]{1,0:T(8,128)(2,1)S(1)}, bf16[64,1024]{1,0:T(8...) custom-call(bf16[128,1024]{1,0:T(8,128)(2,1)S(1)} %project_q.3.q, ...), custom_call_target="tpu_custom_call" | custom-call | flops 1610612736 | bytes 9703936 | tf_op jit(solution)/shard_map/attend_and_project/pallas_call | solution.py:42
  101.2 2.2 %collective-permute-start.37 = (bf16[64,1024]{1,0:T(8,128)(2,1)S(1)}, bf16[64,1024]{1,0:T(8,128)(2,1)S(1)}, u32[]{:S(2)}, u32[]{:S(2)}) collective-permute-start(bf16[64,1024]{1,0:T(8,128)(2,1)S(1)} %get-tuple-element.55), channel_id=1, source_target_pairs={{0,3},{1,0},{2,1},{3,2},{4,7},{5,4},{6,5},{7,6},{8,11},{9,8},{10,9... | collective-permute-start | bytes 393224 | tf_op jit(solution)/shard_map/ppermute | solution.py:35
  103.4 1.3 %collective-permute-start.35 = (bf16[64,1024]{1,0:T(8,128)(2,1)S(1)}, bf16[64,1024]{1,0:T(8,128)(2,1)S(1)}, u32[]{:S(2)}, u32[]{:S(2)}) collective-permute-start(bf16[64,1024]{1,0:T(8,128)(2,1)S(1)} %get-tuple-element.53), channel_id=1, source_target_pairs={{0,2},{1,3},{2,0},{3,1},{4,6},{5,7},{6,4},{7,5},{8,10},{9,11},{10,... | collective-permute-start | bytes 393224 | tf_op jit(solution)/shard_map/ppermute | solution.py:35
  104.7 1.1 collective-permute-start.42
  105.8 1.5 %collective-permute-start.41 = (bf16[64,1024]{1,0:T(8,128)(2,1)S(1)}, bf16[64,1024]{1,0:T(8,128)(2,1)S(1)}, u32[]{:S(2)}, u32[]{:S(2)}) collective-permute-start(bf16[64,1024]{1,0:T(8,128)(2,1)S(1)} %get-tuple-element.59), channel_id=1, source_target_pairs={{0,35},{1,32},{2,33},{3,34},{4,39},{5,36},{6,37},{7,38},{8,43},{9,... | collective-permute-start | bytes 393224 | tf_op jit(solution)/shard_map/ppermute | solution.py:35
  107.3 0.9 collective-permute-start.40
  108.2 3.9 %collective-permute-done.36 = bf16[64,1024]{1,0:T(8,128)(2,1)S(1)} collective-permute-done((bf16[64,1024]{1,0:T(8,128)(2,1)S(1)}, bf16[64,1024]{1,0:T(8,128)(2,1)S(1)}, u32[]{:S(2)}, u32[]{:S(2)}) %collective-permute-start.36) | collective-permute-done | bytes 131104 | tf_op jit(solution)/shard_map/ppermute | solution.py:35
  112.1 1.0 collective-permute-done.41
  113.1 2.5 %collective-permute-done.40 = bf16[64,1024]{1,0:T(8,128)(2,1)S(1)} collective-permute-done((bf16[64,1024]{1,0:T(8,128)(2,1)S(1)}, bf16[64,1024]{1,0:T(8,128)(2,1)S(1)}, u32[]{:S(2)}, u32[]{:S(2)}) %collective-permute-start.40) | collective-permute-done | bytes 131104 | tf_op jit(solution)/shard_map/ppermute | solution.py:35
  115.6 3.3 %collective-permute-done.39 = bf16[64,1024]{1,0:T(8,128)(2,1)S(1)} collective-permute-done((bf16[64,1024]{1,0:T(8,128)(2,1)S(1)}, bf16[64,1024]{1,0:T(8,128)(2,1)S(1)}, u32[]{:S(2)}, u32[]{:S(2)}) %collective-permute-start.39) | collective-permute-done | bytes 131104 | tf_op jit(solution)/shard_map/ppermute | solution.py:35
  118.9 0.2 select_bitcast_fusion.1
  119.2 0.7 maximum_bitcast_fusion
  (62 shorter events, 1.4 us)
Async XLA Ops:
  1.0 8.7 %collective-permute-start = (bf16[64,1024]{1,0:T(8,128)(2,1)S(1)}, bf16[64,1024]{1,0:T(8,128)(2,1)S(1)}, u32[]{:S(2)}, u32[]{:S(2)}) collective-permute-start(bf16[64,1024]{1,0:T(8,128)(2,1)S(1)} %get-tuple-element.66), channel_id=1, source_target_pairs={{0,32},{1,33},{2,34},{3,35},{4,36},{5,37},{6,38},{7,39},{8,40},{9,... | collective-permute-start | bytes 393224 | tf_op jit(solution)/shard_map/ppermute | solution.py:35
  3.1 11.9 %collective-permute-start.2 = (bf16[64,1024]{1,0:T(8,128)(2,1)S(1)}, bf16[64,1024]{1,0:T(8,128)(2,1)S(1)}, u32[]{:S(2)}, u32[]{:S(2)}) collective-permute-start(bf16[64,1024]{1,0:T(8,128)(2,1)S(1)} %get-tuple-element.66), channel_id=1, source_target_pairs={{0,33},{1,34},{2,35},{3,32},{4,37},{5,38},{6,39},{7,36},{8,41},{9,... | collective-permute-start | bytes 393224 | tf_op jit(solution)/shard_map/ppermute | solution.py:35
  4.4 7.3 %collective-permute-start.1 = (bf16[64,1024]{1,0:T(8,128)(2,1)S(1)}, bf16[64,1024]{1,0:T(8,128)(2,1)S(1)}, u32[]{:S(2)}, u32[]{:S(2)}) collective-permute-start(bf16[64,1024]{1,0:T(8,128)(2,1)S(1)} %get-tuple-element.67.refs_0_), channel_id=1, source_target_pairs={{0,1},{1,2},{2,3},{3,0},{4,5},{5,6},{6,7},{7,4},{8,9},{9,10},{10,1... | collective-permute-start | bytes 393224 | tf_op jit(solution)/shard_map/ppermute | solution.py:35
  5.7 9.3 %collective-permute-start.3 = (bf16[64,1024]{1,0:T(8,128)(2,1)S(1)}, bf16[64,1024]{1,0:T(8,128)(2,1)S(1)}, u32[]{:S(2)}, u32[]{:S(2)}) collective-permute-start(bf16[64,1024]{1,0:T(8,128)(2,1)S(1)} %get-tuple-element.67.refs_0_), channel_id=1, source_target_pairs={{0,3},{1,0},{2,1},{3,2},{4,7},{5,4},{6,5},{7,6},{8,11},{9,8},{10,9... | collective-permute-start | bytes 393224 | tf_op jit(solution)/shard_map/ppermute | solution.py:35
  7.1 8.0 %collective-permute-start.4 = (bf16[64,1024]{1,0:T(8,128)(2,1)S(1)}, bf16[64,1024]{1,0:T(8,128)(2,1)S(1)}, u32[]{:S(2)}, u32[]{:S(2)}) collective-permute-start(bf16[64,1024]{1,0:T(8,128)(2,1)S(1)} %get-tuple-element.66), channel_id=1, source_target_pairs={{0,35},{1,32},{2,33},{3,34},{4,39},{5,36},{6,37},{7,38},{8,43},{9,... | collective-permute-start | bytes 393224 | tf_op jit(solution)/shard_map/ppermute | solution.py:35
  9.7 7.9 %collective-permute-start.5 = (bf16[64,1024]{1,0:T(8,128)(2,1)S(1)}, bf16[64,1024]{1,0:T(8,128)(2,1)S(1)}, u32[]{:S(2)}, u32[]{:S(2)}) collective-permute-start(bf16[64,1024]{1,0:T(8,128)(2,1)S(1)} %get-tuple-element.67.refs_0_), channel_id=1, source_target_pairs={{0,2},{1,3},{2,0},{3,1},{4,6},{5,7},{6,4},{7,5},{8,10},{9,11},{10,... | collective-permute-start | bytes 393224 | tf_op jit(solution)/shard_map/ppermute | solution.py:35
  11.7 6.3 %collective-permute-start.6 = (bf16[64,1024]{1,0:T(8,128)(2,1)S(1)}, bf16[64,1024]{1,0:T(8,128)(2,1)S(1)}, u32[]{:S(2)}, u32[]{:S(2)}) collective-permute-start(bf16[64,1024]{1,0:T(8,128)(2,1)S(1)} %get-tuple-element.66), channel_id=1, source_target_pairs={{0,34},{1,35},{2,32},{3,33},{4,38},{5,39},{6,36},{7,37},{8,42},{9,... | collective-permute-start | bytes 393224 | tf_op jit(solution)/shard_map/ppermute | solution.py:35
  18.4 10.3 %collective-permute-start.7 = (bf16[128,512]{1,0:T(8,128)(2,1)S(1)}, bf16[128,512]{1,0:T(8,128)(2,1)S(1)}, u32[]{:S(2)}, u32[]{:S(2)}) collective-permute-start(bf16[128,512]{1,0:T(8,128)(2,1)S(1)} %get-tuple-element.38.refs_0_), channel_id=1, source_target_pairs={{0,8},{1,9},{2,10},{3,11},{4,12},{5,13},{6,14},{7,15},{8,16},{9,17... | collective-permute-start | bytes 393224 | tf_op jit(solution)/shard_map/ppermute | solution.py:35
  20.1 9.2 %collective-permute-start.8 = (bf16[128,512]{1,0:T(8,128)(2,1)S(1)}, bf16[128,512]{1,0:T(8,128)(2,1)S(1)}, u32[]{:S(2)}, u32[]{:S(2)}) collective-permute-start(bf16[128,512]{1,0:T(8,128)(2,1)S(1)} %get-tuple-element.38.refs_0_), channel_id=1, source_target_pairs={{0,16},{1,17},{2,18},{3,19},{4,20},{5,21},{6,22},{7,23},{8,24},{9,... | collective-permute-start | bytes 393224 | tf_op jit(solution)/shard_map/ppermute | solution.py:35
  23.4 8.6 %collective-permute-start.9 = (bf16[128,512]{1,0:T(8,128)(2,1)S(1)}, bf16[128,512]{1,0:T(8,128)(2,1)S(1)}, u32[]{:S(2)}, u32[]{:S(2)}) collective-permute-start(bf16[128,512]{1,0:T(8,128)(2,1)S(1)} %get-tuple-element.38.refs_0_), channel_id=1, source_target_pairs={{0,24},{1,25},{2,26},{3,27},{4,28},{5,29},{6,30},{7,31},{8,0},{9,1... | collective-permute-start | bytes 393224 | tf_op jit(solution)/shard_map/ppermute | solution.py:35
  24.1 12.7 %collective-permute-start.10 = (bf16[128,512]{1,0:T(8,128)(2,1)S(1)}, bf16[128,512]{1,0:T(8,128)(2,1)S(1)}, u32[]{:S(2)}, u32[]{:S(2)}) collective-permute-start(bf16[128,512]{1,0:T(8,128)(2,1)S(1)} %get-tuple-element.38.refs_0_), channel_id=1, source_target_pairs={{0,4},{1,5},{2,6},{3,7},{4,0},{5,1},{6,2},{7,3},{8,12},{9,13},{10,... | collective-permute-start | bytes 393224 | tf_op jit(solution)/shard_map/ppermute | solution.py:35
  28.7 8.2 %collective-permute-start.11 = (bf16[128,512]{1,0:T(8,128)(2,1)S(1)}, bf16[128,512]{1,0:T(8,128)(2,1)S(1)}, u32[]{:S(2)}, u32[]{:S(2)}) collective-permute-start(bf16[128,512]{1,0:T(8,128)(2,1)S(1)} %collective-permute-done.7.refs_1_), channel_id=1, source_target_pairs={{0,4},{1,5},{2,6},{3,7},{4,0},{5,1},{6,2},{7,3},{8,12},{9,13},{10,... | collective-permute-start | bytes 393224 | tf_op jit(solution)/shard_map/ppermute | solution.py:35
  29.3 7.6 %collective-permute-start.12 = (bf16[128,512]{1,0:T(8,128)(2,1)S(1)}, bf16[128,512]{1,0:T(8,128)(2,1)S(1)}, u32[]{:S(2)}, u32[]{:S(2)}) collective-permute-start(bf16[128,512]{1,0:T(8,128)(2,1)S(1)} %collective-permute-done.8.refs_2_), channel_id=1, source_target_pairs={{0,4},{1,5},{2,6},{3,7},{4,0},{5,1},{6,2},{7,3},{8,12},{9,13},{10,... | collective-permute-start | bytes 393224 | tf_op jit(solution)/shard_map/ppermute | solution.py:35
  32.0 4.9 %collective-permute-start.13 = (bf16[128,512]{1,0:T(8,128)(2,1)S(1)}, bf16[128,512]{1,0:T(8,128)(2,1)S(1)}, u32[]{:S(2)}, u32[]{:S(2)}) collective-permute-start(bf16[128,512]{1,0:T(8,128)(2,1)S(1)} %collective-permute-done.9.refs_3_), channel_id=1, source_target_pairs={{0,4},{1,5},{2,6},{3,7},{4,0},{5,1},{6,2},{7,3},{8,12},{9,13},{10,... | collective-permute-start | bytes 393224 | tf_op jit(solution)/shard_map/ppermute | solution.py:35
  43.0 5.4 %collective-permute-start.19 = (bf16[128,512]{1,0:T(8,128)(2,1)S(1)}, bf16[128,512]{1,0:T(8,128)(2,1)S(1)}, u32[]{:S(2)}, u32[]{:S(2)}) collective-permute-start(bf16[128,512]{1,0:T(8,128)(2,1)S(1)} %get-tuple-element.45), channel_id=1, source_target_pairs={{0,3},{1,0},{2,1},{3,2},{4,7},{5,4},{6,5},{7,6},{8,11},{9,8},{10,9... | collective-permute-start | bytes 393224 | tf_op jit(solution)/shard_map/ppermute | solution.py:35
  44.7 8.6 %collective-permute-start.18 = (bf16[128,512]{1,0:T(8,128)(2,1)S(1)}, bf16[128,512]{1,0:T(8,128)(2,1)S(1)}, u32[]{:S(2)}, u32[]{:S(2)}) collective-permute-start(bf16[128,512]{1,0:T(8,128)(2,1)S(1)} %get-tuple-element.44), channel_id=1, source_target_pairs={{0,1},{1,2},{2,3},{3,0},{4,5},{5,6},{6,7},{7,4},{8,9},{9,10},{10,1... | collective-permute-start | bytes 393224 | tf_op jit(solution)/shard_map/ppermute | solution.py:35
  44.7 8.6 %collective-permute-start.17 = (bf16[128,512]{1,0:T(8,128)(2,1)S(1)}, bf16[128,512]{1,0:T(8,128)(2,1)S(1)}, u32[]{:S(2)}, u32[]{:S(2)}) collective-permute-start(bf16[128,512]{1,0:T(8,128)(2,1)S(1)} %get-tuple-element.43), channel_id=1, source_target_pairs={{0,2},{1,3},{2,0},{3,1},{4,6},{5,7},{6,4},{7,5},{8,10},{9,11},{10,... | collective-permute-start | bytes 393224 | tf_op jit(solution)/shard_map/ppermute | solution.py:35
  46.1 8.0 %collective-permute-start.16 = (bf16[128,512]{1,0:T(8,128)(2,1)S(1)}, bf16[128,512]{1,0:T(8,128)(2,1)S(1)}, u32[]{:S(2)}, u32[]{:S(2)}) collective-permute-start(bf16[128,512]{1,0:T(8,128)(2,1)S(1)} %get-tuple-element.41), channel_id=1, source_target_pairs={{0,3},{1,0},{2,1},{3,2},{4,7},{5,4},{6,5},{7,6},{8,11},{9,8},{10,9... | collective-permute-start | bytes 393224 | tf_op jit(solution)/shard_map/ppermute | solution.py:35
  47.8 11.3 %collective-permute-start.15 = (bf16[128,512]{1,0:T(8,128)(2,1)S(1)}, bf16[128,512]{1,0:T(8,128)(2,1)S(1)}, u32[]{:S(2)}, u32[]{:S(2)}) collective-permute-start(bf16[128,512]{1,0:T(8,128)(2,1)S(1)} %get-tuple-element.40), channel_id=1, source_target_pairs={{0,1},{1,2},{2,3},{3,0},{4,5},{5,6},{6,7},{7,4},{8,9},{9,10},{10,1... | collective-permute-start | bytes 393224 | tf_op jit(solution)/shard_map/ppermute | solution.py:35
  48.4 10.8 %collective-permute-start.14 = (bf16[128,512]{1,0:T(8,128)(2,1)S(1)}, bf16[128,512]{1,0:T(8,128)(2,1)S(1)}, u32[]{:S(2)}, u32[]{:S(2)}) collective-permute-start(bf16[128,512]{1,0:T(8,128)(2,1)S(1)} %get-tuple-element.39), channel_id=1, source_target_pairs={{0,2},{1,3},{2,0},{3,1},{4,6},{5,7},{6,4},{7,5},{8,10},{9,11},{10,... | collective-permute-start | bytes 393224 | tf_op jit(solution)/shard_map/ppermute | solution.py:35
  59.3 5.6 %collective-permute-start.20 = (bf16[128,512]{1,0:T(8,128)(2,1)S(1)}, bf16[128,512]{1,0:T(8,128)(2,1)S(1)}, u32[]{:S(2)}, u32[]{:S(2)}) collective-permute-start(bf16[128,512]{1,0:T(8,128)(2,1)S(1)} %get-tuple-element.65), channel_id=1, source_target_pairs={{0,96},{1,97},{2,98},{3,99},{4,100},{5,101},{6,102},{7,103},{8,104... | collective-permute-start | bytes 393224 | tf_op jit(solution)/shard_map/ppermute | solution.py:35
  62.8 5.2 %collective-permute-start.21 = (bf16[128,512]{1,0:T(8,128)(2,1)S(1)}, bf16[128,512]{1,0:T(8,128)(2,1)S(1)}, u32[]{:S(2)}, u32[]{:S(2)}) collective-permute-start(bf16[128,512]{1,0:T(8,128)(2,1)S(1)} %get-tuple-element.64), channel_id=1, source_target_pairs={{0,96},{1,97},{2,98},{3,99},{4,100},{5,101},{6,102},{7,103},{8,104... | collective-permute-start | bytes 393224 | tf_op jit(solution)/shard_map/ppermute | solution.py:35
  64.9 5.4 %collective-permute-start.22 = (bf16[128,512]{1,0:T(8,128)(2,1)S(1)}, bf16[128,512]{1,0:T(8,128)(2,1)S(1)}, u32[]{:S(2)}, u32[]{:S(2)}) collective-permute-start(bf16[128,512]{1,0:T(8,128)(2,1)S(1)} %collective-permute-done.20.refs_0_), channel_id=1, source_target_pairs={{0,2},{1,3},{2,0},{3,1},{4,6},{5,7},{6,4},{7,5},{8,10},{9,11},{10,... | collective-permute-start | bytes 393224 | tf_op jit(solution)/shard_map/ppermute | solution.py:35
  65.1 7.2 %collective-permute-start.23 = (bf16[128,512]{1,0:T(8,128)(2,1)S(1)}, bf16[128,512]{1,0:T(8,128)(2,1)S(1)}, u32[]{:S(2)}, u32[]{:S(2)}) collective-permute-start(bf16[128,512]{1,0:T(8,128)(2,1)S(1)} %collective-permute-done.20.refs_0_), channel_id=1, source_target_pairs={{0,1},{1,2},{2,3},{3,0},{4,5},{5,6},{6,7},{7,4},{8,9},{9,10},{10,1... | collective-permute-start | bytes 393224 | tf_op jit(solution)/shard_map/ppermute | solution.py:35
  65.2 7.5 %collective-permute-start.24 = (bf16[128,512]{1,0:T(8,128)(2,1)S(1)}, bf16[128,512]{1,0:T(8,128)(2,1)S(1)}, u32[]{:S(2)}, u32[]{:S(2)}) collective-permute-start(bf16[128,512]{1,0:T(8,128)(2,1)S(1)} %collective-permute-done.20.refs_0_), channel_id=1, source_target_pairs={{0,3},{1,0},{2,1},{3,2},{4,7},{5,4},{6,5},{7,6},{8,11},{9,8},{10,9... | collective-permute-start | bytes 393224 | tf_op jit(solution)/shard_map/ppermute | solution.py:35
  68.0 7.1 %collective-permute-start.25 = (bf16[128,512]{1,0:T(8,128)(2,1)S(1)}, bf16[128,512]{1,0:T(8,128)(2,1)S(1)}, u32[]{:S(2)}, u32[]{:S(2)}) collective-permute-start(bf16[128,512]{1,0:T(8,128)(2,1)S(1)} %collective-permute-done.21.refs_0_.refs_4_), channel_id=1, source_target_pairs={{0,2},{1,3},{2,0},{3,1},{4,6},{5,7},{6,4},{7,5},{8,10},{9,11},{10,... | collective-permute-start | bytes 393224 | tf_op jit(solution)/shard_map/ppermute | solution.py:35
  69.6 8.2 %collective-permute-start.26 = (bf16[128,512]{1,0:T(8,128)(2,1)S(1)}, bf16[128,512]{1,0:T(8,128)(2,1)S(1)}, u32[]{:S(2)}, u32[]{:S(2)}) collective-permute-start(bf16[128,512]{1,0:T(8,128)(2,1)S(1)} %collective-permute-done.21.refs_0_.refs_4_), channel_id=1, source_target_pairs={{0,1},{1,2},{2,3},{3,0},{4,5},{5,6},{6,7},{7,4},{8,9},{9,10},{10,1... | collective-permute-start | bytes 393224 | tf_op jit(solution)/shard_map/ppermute | solution.py:35
  70.4 7.4 %collective-permute-start.27 = (bf16[128,512]{1,0:T(8,128)(2,1)S(1)}, bf16[128,512]{1,0:T(8,128)(2,1)S(1)}, u32[]{:S(2)}, u32[]{:S(2)}) collective-permute-start(bf16[128,512]{1,0:T(8,128)(2,1)S(1)} %collective-permute-done.21.refs_0_.refs_4_), channel_id=1, source_target_pairs={{0,3},{1,0},{2,1},{3,2},{4,7},{5,4},{6,5},{7,6},{8,11},{9,8},{10,9... | collective-permute-start | bytes 393224 | tf_op jit(solution)/shard_map/ppermute | solution.py:35
  78.4 9.0 %collective-permute-start.28 = (bf16[128,512]{1,0:T(8,128)(2,1)S(1)}, bf16[128,512]{1,0:T(8,128)(2,1)S(1)}, u32[]{:S(2)}, u32[]{:S(2)}) collective-permute-start(bf16[128,512]{1,0:T(8,128)(2,1)S(1)} %get-tuple-element.52.refs_0_), channel_id=1, source_target_pairs={{0,8},{1,9},{2,10},{3,11},{4,12},{5,13},{6,14},{7,15},{8,16},{9,17... | collective-permute-start | bytes 393224 | tf_op jit(solution)/shard_map/ppermute | solution.py:35
  81.3 7.4 %collective-permute-start.29 = (bf16[128,512]{1,0:T(8,128)(2,1)S(1)}, bf16[128,512]{1,0:T(8,128)(2,1)S(1)}, u32[]{:S(2)}, u32[]{:S(2)}) collective-permute-start(bf16[128,512]{1,0:T(8,128)(2,1)S(1)} %get-tuple-element.52.refs_0_), channel_id=1, source_target_pairs={{0,16},{1,17},{2,18},{3,19},{4,20},{5,21},{6,22},{7,23},{8,24},{9,... | collective-permute-start | bytes 393224 | tf_op jit(solution)/shard_map/ppermute | solution.py:35
  82.7 7.4 %collective-permute-start.30 = (bf16[128,512]{1,0:T(8,128)(2,1)S(1)}, bf16[128,512]{1,0:T(8,128)(2,1)S(1)}, u32[]{:S(2)}, u32[]{:S(2)}) collective-permute-start(bf16[128,512]{1,0:T(8,128)(2,1)S(1)} %get-tuple-element.52.refs_0_), channel_id=1, source_target_pairs={{0,24},{1,25},{2,26},{3,27},{4,28},{5,29},{6,30},{7,31},{8,0},{9,1... | collective-permute-start | bytes 393224 | tf_op jit(solution)/shard_map/ppermute | solution.py:35
  84.4 10.7 %collective-permute-start.31 = (bf16[128,512]{1,0:T(8,128)(2,1)S(1)}, bf16[128,512]{1,0:T(8,128)(2,1)S(1)}, u32[]{:S(2)}, u32[]{:S(2)}) collective-permute-start(bf16[128,512]{1,0:T(8,128)(2,1)S(1)} %get-tuple-element.52.refs_0_), channel_id=1, source_target_pairs={{0,4},{1,5},{2,6},{3,7},{4,0},{5,1},{6,2},{7,3},{8,12},{9,13},{10,... | collective-permute-start | bytes 393224 | tf_op jit(solution)/shard_map/ppermute | solution.py:35
  87.4 7.8 %collective-permute-start.32 = (bf16[128,512]{1,0:T(8,128)(2,1)S(1)}, bf16[128,512]{1,0:T(8,128)(2,1)S(1)}, u32[]{:S(2)}, u32[]{:S(2)}) collective-permute-start(bf16[128,512]{1,0:T(8,128)(2,1)S(1)} %collective-permute-done.28.refs_1_), channel_id=1, source_target_pairs={{0,4},{1,5},{2,6},{3,7},{4,0},{5,1},{6,2},{7,3},{8,12},{9,13},{10,... | collective-permute-start | bytes 393224 | tf_op jit(solution)/shard_map/ppermute | solution.py:35
  88.7 6.5 %collective-permute-start.33 = (bf16[128,512]{1,0:T(8,128)(2,1)S(1)}, bf16[128,512]{1,0:T(8,128)(2,1)S(1)}, u32[]{:S(2)}, u32[]{:S(2)}) collective-permute-start(bf16[128,512]{1,0:T(8,128)(2,1)S(1)} %collective-permute-done.29.refs_2_), channel_id=1, source_target_pairs={{0,4},{1,5},{2,6},{3,7},{4,0},{5,1},{6,2},{7,3},{8,12},{9,13},{10,... | collective-permute-start | bytes 393224 | tf_op jit(solution)/shard_map/ppermute | solution.py:35
  90.1 5.0 %collective-permute-start.34 = (bf16[128,512]{1,0:T(8,128)(2,1)S(1)}, bf16[128,512]{1,0:T(8,128)(2,1)S(1)}, u32[]{:S(2)}, u32[]{:S(2)}) collective-permute-start(bf16[128,512]{1,0:T(8,128)(2,1)S(1)} %collective-permute-done.30.refs_3_), channel_id=1, source_target_pairs={{0,4},{1,5},{2,6},{3,7},{4,0},{5,1},{6,2},{7,3},{8,12},{9,13},{10,... | collective-permute-start | bytes 393224 | tf_op jit(solution)/shard_map/ppermute | solution.py:35
  90.7 15.1 %collective-permute-start.38 = (bf16[64,1024]{1,0:T(8,128)(2,1)S(1)}, bf16[64,1024]{1,0:T(8,128)(2,1)S(1)}, u32[]{:S(2)}, u32[]{:S(2)}) collective-permute-start(bf16[64,1024]{1,0:T(8,128)(2,1)S(1)} %slice_select_fusion), channel_id=1, source_target_pairs={{0,32},{1,33},{2,34},{3,35},{4,36},{5,37},{6,38},{7,39},{8,40},{9,... | collective-permute-start | bytes 393224 | tf_op jit(solution)/shard_map/ppermute | solution.py:35
  101.2 6.0 %collective-permute-start.37 = (bf16[64,1024]{1,0:T(8,128)(2,1)S(1)}, bf16[64,1024]{1,0:T(8,128)(2,1)S(1)}, u32[]{:S(2)}, u32[]{:S(2)}) collective-permute-start(bf16[64,1024]{1,0:T(8,128)(2,1)S(1)} %get-tuple-element.55), channel_id=1, source_target_pairs={{0,3},{1,0},{2,1},{3,2},{4,7},{5,4},{6,5},{7,6},{8,11},{9,8},{10,9... | collective-permute-start | bytes 393224 | tf_op jit(solution)/shard_map/ppermute | solution.py:35
  103.4 8.7 %collective-permute-start.36 = (bf16[64,1024]{1,0:T(8,128)(2,1)S(1)}, bf16[64,1024]{1,0:T(8,128)(2,1)S(1)}, u32[]{:S(2)}, u32[]{:S(2)}) collective-permute-start(bf16[64,1024]{1,0:T(8,128)(2,1)S(1)} %get-tuple-element.54), channel_id=1, source_target_pairs={{0,1},{1,2},{2,3},{3,0},{4,5},{5,6},{6,7},{7,4},{8,9},{9,10},{10,1... | collective-permute-start | bytes 393224 | tf_op jit(solution)/shard_map/ppermute | solution.py:35
  103.4 8.7 %collective-permute-start.35 = (bf16[64,1024]{1,0:T(8,128)(2,1)S(1)}, bf16[64,1024]{1,0:T(8,128)(2,1)S(1)}, u32[]{:S(2)}, u32[]{:S(2)}) collective-permute-start(bf16[64,1024]{1,0:T(8,128)(2,1)S(1)} %get-tuple-element.53), channel_id=1, source_target_pairs={{0,2},{1,3},{2,0},{3,1},{4,6},{5,7},{6,4},{7,5},{8,10},{9,11},{10,... | collective-permute-start | bytes 393224 | tf_op jit(solution)/shard_map/ppermute | solution.py:35
  104.7 7.4 %collective-permute-start.42 = (bf16[64,1024]{1,0:T(8,128)(2,1)S(1)}, bf16[64,1024]{1,0:T(8,128)(2,1)S(1)}, u32[]{:S(2)}, u32[]{:S(2)}) collective-permute-start(bf16[64,1024]{1,0:T(8,128)(2,1)S(1)} %get-tuple-element.60), channel_id=1, source_target_pairs={{0,32},{1,33},{2,34},{3,35},{4,36},{5,37},{6,38},{7,39},{8,40},{9,... | collective-permute-start | bytes 393224 | tf_op jit(solution)/shard_map/ppermute | solution.py:35
  105.8 7.2 %collective-permute-start.41 = (bf16[64,1024]{1,0:T(8,128)(2,1)S(1)}, bf16[64,1024]{1,0:T(8,128)(2,1)S(1)}, u32[]{:S(2)}, u32[]{:S(2)}) collective-permute-start(bf16[64,1024]{1,0:T(8,128)(2,1)S(1)} %get-tuple-element.59), channel_id=1, source_target_pairs={{0,35},{1,32},{2,33},{3,34},{4,39},{5,36},{6,37},{7,38},{8,43},{9,... | collective-permute-start | bytes 393224 | tf_op jit(solution)/shard_map/ppermute | solution.py:35
  107.3 8.3 %collective-permute-start.40 = (bf16[64,1024]{1,0:T(8,128)(2,1)S(1)}, bf16[64,1024]{1,0:T(8,128)(2,1)S(1)}, u32[]{:S(2)}, u32[]{:S(2)}) collective-permute-start(bf16[64,1024]{1,0:T(8,128)(2,1)S(1)} %get-tuple-element.58), channel_id=1, source_target_pairs={{0,33},{1,34},{2,35},{3,32},{4,37},{5,38},{6,39},{7,36},{8,41},{9,... | collective-permute-start | bytes 393224 | tf_op jit(solution)/shard_map/ppermute | solution.py:35
  112.1 6.8 %collective-permute-start.39 = (bf16[64,1024]{1,0:T(8,128)(2,1)S(1)}, bf16[64,1024]{1,0:T(8,128)(2,1)S(1)}, u32[]{:S(2)}, u32[]{:S(2)}) collective-permute-start(bf16[64,1024]{1,0:T(8,128)(2,1)S(1)} %get-tuple-element.57), channel_id=1, source_target_pairs={{0,34},{1,35},{2,32},{3,33},{4,38},{5,39},{6,36},{7,37},{8,42},{9,... | collective-permute-start | bytes 393224 | tf_op jit(solution)/shard_map/ppermute | solution.py:35

commit v4 on v3

--- a/solution.py
+++ b/solution.py
@@ -79,6 +79,28 @@
     return out, refs[at:]
 
 
+def bring(after, *weights):
+    def body(after_ref, *refs):
+        n = len(weights)
+        sems = refs[-1]
+        copies = [
+            pltpu.make_async_copy(refs[i].at[0], refs[n + i], sems.at[i]) for i in range(n)
+        ]
+        for c in copies:
+            c.start()
+        for c in copies:
+            c.wait()
+
+    return in_vmem(
+        body,
+        [after],
+        [(w.shape[1:], w.dtype) for w in weights],
+        "bring",
+        in_hbm=weights,
+        scratch=[pltpu.SemaphoreType.DMA((len(weights),))],
+    )
+
+
 def project_kv(pieces, slice_width, gain, weights, carry, rope, following):
     rows = sum(x.shape[0] for x in pieces[0][2])
     width = pieces[0][2][0].shape[1]
@@ -86,6 +108,7 @@
     n = len(pieces)
     first, last = carry is None, rope is not None
     n_next = len(following)
+    whole = not n_next and weights[0].shape[0] > n * width
 
     def body(*refs):
         groups, refs = regroup(refs, pieces)
@@ -123,7 +146,7 @@
         for j, ((shift, at, _), rows_of) in enumerate(zip(pieces, groups)):
             start = from_slice(shift, at, slice_width)
             x, squares = scaled_piece(rows_of, gain_ref, start)
-            here = slice(j * width, (j + 1) * width)
+            here = pl.ds(start, width) if whole else slice(j * width, (j + 1) * width)
             if copies:
                 copies[2 * j].wait()
             pk = jnp.dot(x, w_refs[0][here, :], preferred_element_type=jnp.float32)
@@ -195,11 +218,10 @@
             copies[j].wait()
             part = jnp.dot(x, held[j], preferred_element_type=jnp.float32)
             acc = part if acc is None else acc + part
+        r = r_ref[...] * (math.log2(math.e) / math.sqrt(HS))
         for h in range(cols // HS):
             at = slice(h * HS, (h + 1) * HS)
-            out[:, at] = rotated(acc[:, at] * r_ref[...], cos[...], sin[...]).astype(
-                jnp.bfloat16
-            )
+            out[:, at] = rotated(acc[:, at] * r, cos[...], sin[...]).astype(jnp.bfloat16)
 
     return in_vmem(
         body,
@@ -216,79 +238,143 @@
     )[0]
 
 
-def attend_and_project(q, qpos, kpos, blocks, w_out, chunks, split):
+def attend_and_project(q, qpos, kpos, blocks, w_out, width, split, now, later):
     rows, q_cols = q.shape
     kv_heads = blocks[0].shape[1] // (2 * HS)
     group = q_cols // HS // kv_heads
-    scale = 1.0 / math.sqrt(HS)
     n_blocks = len(blocks)
     keys = sum(b.shape[0] for b in blocks)
     _, depth, out_cols = w_out.shape
-    slice_width = out_cols // len(SHIFTS)
-    width = slice_width // chunks
-    parts = [(c, s) for c in range(chunks) for s in SHIFTS]
+    slice_width = out_cols // lax.axis_size("tp")
     n_cut = 2 if split else 1
     half = rows // n_cut
+    n_now, n_later = len(now), len(later)
 
     def body(q, qpos, kpos, *refs):
         block_refs, refs = refs[:n_blocks], refs[n_blocks:]
         w_ref, refs = refs[0], refs[1:]
-        outs, (attended, held, sems) = refs[:-3], refs[-3:]
+        outs, refs = refs[: n_now * n_cut], refs[n_now * n_cut :]
+        attended, later_ref, held, sems = refs
         copies = []
-        for j, (c, s) in enumerate(parts):
-            there = pl.ds(from_slice(-s, c * width, slice_width), width)
-            copies.append(pltpu.make_async_copy(w_ref.at[0, :, there], held.at[j], sems.at[j]))
+        for j, (at, s) in enumerate(list(now) + list(later)):
+            there = pl.ds(from_slice(-s, at, slice_width), width)
+            to = held.at[j] if j < n_now else later_ref.at[j - n_now]
+            copies.append(pltpu.make_async_copy(w_ref.at[0, :, there], to, sems.at[j]))
         for c in copies:
             c.start()
-        allowed = kpos[...] <= qpos[...]
-        allowed = jnp.concatenate([allowed] * group, axis=0)
+        bias = jnp.where(kpos[...] <= qpos[...], 0.0, -1e30)
+        ones = jnp.ones((keys, HS), jnp.bfloat16)
         for g in range(kv_heads):
             k = jnp.concatenate([b[:, g * HS : (g + 1) * HS] for b in block_refs], axis=0)
             lo = kv_heads * HS + g * HS
             v = jnp.concatenate([b[:, lo : lo + HS] for b in block_refs], axis=0)
+            v = jnp.concatenate([v, ones], axis=1)
             heads = [g * group + j for j in range(group)]
             qs = jnp.concatenate([q[:, h * HS : (h + 1) * HS] for h in heads], axis=0)
             scores = lax.dot_general(
                 qs, k, (((1,), (1,)), ((), ())), preferred_element_type=jnp.float32
             )
-            masked = jnp.where(allowed, scores * scale, -1e30)
-            best = jnp.max(masked, axis=-1, keepdims=True)
-            weights = jnp.where(allowed, jnp.exp(masked - best), 0.0)
-            total = jnp.sum(weights, axis=-1, keepdims=True)
-            acc = jnp.dot(weights.astype(jnp.bfloat16), v, preferred_element_type=jnp.float32)
-            normal = (acc / total).astype(jnp.bfloat16)
+            scores = scores.reshape(group, rows, keys) + bias[None]
+            best = jnp.max(scores, axis=-1, keepdims=True)
+            weights = jnp.exp2(scores - best).astype(jnp.bfloat16).reshape(group * rows, keys)
+            acc = jnp.dot(weights, v, preferred_element_type=jnp.float32)
+            normal = (acc[:, :HS] / acc[:, HS:]).astype(jnp.bfloat16)
             for j, h in enumerate(heads):
                 attended[:, h * HS : (h + 1) * HS] = normal[j * rows : (j + 1) * rows]
-        for j in range(len(parts)):
+        for j in range(n_now):
             copies[j].wait()
             part = jnp.dot(attended[...], held[j], preferred_element_type=jnp.float32).astype(
                 jnp.bfloat16
             )
             for m in range(n_cut):
                 outs[j * n_cut + m][...] = part[m * half : (m + 1) * half]
+        for c in copies[n_now:]:
+            c.wait()
 
     got = in_vmem(
         body,
         [q, qpos, kpos, *blocks],
-        [((half, width), jnp.bfloat16)] * len(parts) * n_cut,
+        [((half, width), jnp.bfloat16)] * n_now * n_cut
+        + [((rows, q_cols), jnp.bfloat16), ((n_later, depth, width), jnp.bfloat16)],
         "attend_and_project",
         in_hbm=[w_out],
         scratch=[
-            pltpu.VMEM((rows, q_cols), jnp.bfloat16),
-            pltpu.VMEM((len(parts), depth, width), jnp.bfloat16),
-            pltpu.SemaphoreType.DMA((len(parts),)),
+            pltpu.VMEM((n_now, depth, width), jnp.bfloat16),
+            pltpu.SemaphoreType.DMA((n_now + n_later,)),
         ],
         limit=LARGE,
         flops=4 * rows * q_cols * keys + 2 * rows * w_out.size,
     )
-    return [got[j * n_cut : (j + 1) * n_cut] for j in range(len(parts))]
-
-
-def add_all(x, parts):
-    total = parts[0].astype(jnp.float32)
+    parts = [got[j * n_cut : (j + 1) * n_cut] for j in range(n_now)]
+    return parts, got[-2], got[-1]
+
+
+def project_out(attended, weights, split):
+    rows, depth = attended.shape
+    n, _, width = weights.shape
+    n_cut = 2 if split else 1
+    half = rows // n_cut
+
+    def body(a, w, *outs):
+        for j in range(n):
+            part = jnp.dot(a[...], w[j], preferred_element_type=jnp.float32).astype(
+                jnp.bfloat16
+            )
+            for m in range(n_cut):
+                outs[j * n_cut + m][...] = part[m * half : (m + 1) * half]
+
+    got = in_vmem(
+        body,
+        [attended, weights],
+        [((half, width), jnp.bfloat16)] * n * n_cut,
+        "project_out",
+        flops=2 * rows * depth * width * n,
+    )
+    return [got[j * n_cut : (j + 1) * n_cut] for j in range(n)]
+
+
+def total_of(parts):
+    total = parts[0][...].astype(jnp.float32)
     for p in parts[1:]:
-        total = total + p.astype(jnp.float32)
-    return (x.astype(jnp.float32) + total).astype(jnp.bfloat16)
+        total = total + p[...].astype(jnp.float32)
+    return total
+
+
+def add_parts(x_rows, at, parts):
+    rows, width = parts[0].shape
+    n = len(x_rows)
+
+    def body(*refs):
+        x = jnp.concatenate([r[:, at : at + width] for r in refs[:n]], axis=0)
+        out = refs[-1]
+        out[...] = (x.astype(jnp.float32) + total_of(refs[n:-1])).astype(jnp.bfloat16)
+
+    return in_vmem(body, [*x_rows, *parts], [((rows, width), jnp.bfloat16)], "add_parts")[0]
+
+
+def finish(kept_own, own_parts, kept_cross, cross_parts):
+    half, width = kept_own.shape
+    n_own, n_cross = len(own_parts), len(cross_parts)
+    n_half = lax.axis_size("ctx") // 2
+
+    def body(*refs):
+        ko, kc, refs = refs[0], refs[1], refs[2:]
+        out = refs[-1]
+        section = lax.axis_index("section")
+        x_lo = lax.axis_index("ctx") // n_half
+        first = section == 0
+        own = ko[...].astype(jnp.float32) + jnp.where(first, 0.0, total_of(refs[:n_own]))
+        cross = kc[...].astype(jnp.float32) + jnp.where(first, 0.0, total_of(refs[n_own:-1]))
+        own_first = x_lo == section
+        out[0, 0] = jnp.where(own_first, own, cross).astype(jnp.bfloat16)
+        out[0, 1] = jnp.where(own_first, cross, own).astype(jnp.bfloat16)
+
+    return in_vmem(
+        body,
+        [kept_own, kept_cross, *own_parts, *cross_parts],
+        [((1, 2, half, width), jnp.bfloat16)],
+        "finish",
+    )[0]
 
 
 def per_device(tokens, norm_gain, wq, wk, wv, w_out):
@@ -335,70 +421,82 @@
 
     rope = tables(qpos)
 
-    def mix(kv, make_q, qpos, kpos, chunks, split):
-        mine = [kv] + [send(kv, by_z=s) for s in (2, 1, 3)]
-        q = make_q()
-        theirs = [send(b, other_core=True) for b in mine]
-        mine = [mine[0], mine[2], mine[1], mine[3]]
-        theirs = [theirs[0], theirs[2], theirs[1], theirs[3]]
+    def mix(kv, make_q, qpos, kpos, width, split, now, later):
+        theirs = [send(kv, other_core=True)]
+        mine = [send(kv, by_z=s) for s in (2, 1, 3)]
+        q, *mine = lax.optimization_barrier((make_q(), *mine))
+        theirs += [send(mine[n], other_core=True) for n in (1, 0, 2)]
+        mine = [kv, mine[1], mine[0], mine[2]]
         return attend_and_project(
-            q, qpos[:, None], kpos[None, :], mine + theirs, w_out, chunks, split
+            q, qpos[:, None], kpos[None, :], mine + theirs, w_out, width, split, now, later
         )
 
     own = lax.dynamic_index_in_dim(tokens, x_lo, 0, keepdims=False)
     other = lax.dynamic_index_in_dim(tokens, 1 - x_lo, 0, keepdims=False)
-    own_from, other_from = [own], []
-    for s in range(n_tp):
+    own_from, other_from = {0: own}, {}
+    for s in (2, 1, 3, 0):
         if s:
-            own_from.append(send(own, by_tp=s))
-        other_from.append(send(other, by_tp=s, other_half=True))
+            own_from[s] = send(own, by_tp=s)
+        other_from[s] = send(other, by_tp=s, other_half=True)
     pieces = [(s, 0, [own_from[s], other_from[s]]) for s in (0, 1, 3, 2)]
     carry, held = project_kv(pieces[:3], width, gain, (wk, wv), None, None, pieces[3:])
     (kv, r), _ = project_kv(pieces[3:], width, gain, held, carry, rope, ())
-    got = mix(
-        kv, lambda: project_q(pieces, width, gain, wq, r, rope), qpos, kpos, CHUNKS, False
-    )
-    x0 = jnp.concatenate([own, other_from[0]], axis=0)
+    chunked = [[(c * chunk, s) for s in SHIFTS] for c in range(CHUNKS)]
+    got, attended, held = mix(
+        kv,
+        lambda: project_q(pieces, width, gain, wq, r, rope),
+        qpos,
+        kpos,
+        chunk,
+        False,
+        chunked[0],
+        sum(chunked[1:], []),
+    )
+    got += project_out(attended, held, False)
     sums = []
     for c in range(CHUNKS):
-        at = c * chunk
         parts = []
         for s, (block,) in zip(SHIFTS, got[c * n_tp : (c + 1) * n_tp]):
             parts.append(send(block, by_tp=s) if s else block)
-        sums.append(add_all(x0[:, at : at + chunk], parts))
+        sums.append(add_parts([own, other_from[0]], c * chunk, parts))
 
     received = [send(x, next_layer=True) for x in sums]
     qpos = swapped(qpos)
     kpos = swapped(kpos.reshape(-1, 2 * half).T).T.reshape(-1)
     rope = tuple(swapped(t) for t in rope)
-    carry, held = None, (wk, wv)
+    near = bring(sums[-1][:8, :HS], wk, wv)
+    carry = None
     pieces = []
     for c in range(CHUNKS):
-        got = [received[c]] + [send(received[c], by_tp=s) for s in (2, 1, 3)]
-        pieces.append([(s, c * chunk, [g]) for s, g in zip((0, 2, 1, 3), got)])
+        came = {0: received[c]}
+        for s in (2, 1, 3):
+            came[s] = send(received[c], by_tp=s)
+        pieces.append([(s, c * chunk, [came[s]]) for s in (0, 1, 3, 2)])
     for c in range(CHUNKS):
         last = c == CHUNKS - 1
-        following = () if last else pieces[c + 1]
-        carry, held = project_kv(
-            pieces[c], width, gain, held, carry, rope if last else None, following
-        )
+        carry, _ = project_kv(pieces[c], width, gain, near, carry, rope if last else None, ())
     kv, r = carry
     x1 = jnp.concatenate(sums, axis=1)
     came = jnp.concatenate(received, axis=1)
     kept_own = jnp.where(section == 0, x1[:half], came[half:])
     kept_cross = send(jnp.where(section == 0, x1[half:], came[:half]), other_half=True)
     every = [p for group in pieces for p in group]
-    got = mix(kv, lambda: project_q(every, width, gain, wq, r, rope), qpos, kpos, 1, True)
+    got, attended, held = mix(
+        kv,
+        lambda: project_q(every, width, gain, wq, r, rope),
+        qpos,
+        kpos,
+        width,
+        True,
+        [(0, 2)],
+        [(0, s) for s in (1, 3, 0)],
+    )
+    got += project_out(attended, held, True)
     own_parts, cross_parts = [], []
     for s, (theirs, mine) in zip(SHIFTS, got):
         cross_parts.append(send(theirs, by_tp=s, other_half=True))
         own_parts.append(send(mine, by_tp=s) if s else mine)
-    out_own = jnp.where(section == 0, kept_own, add_all(kept_own, own_parts))
-    out_cross = jnp.where(section == 0, kept_cross, add_all(kept_cross, cross_parts))
-    own_first = x_lo == section
-    first = jnp.where(own_first, out_own, out_cross)
-    second = jnp.where(own_first, out_cross, out_own)
-    return jnp.stack([first, second])[None]
+    return finish(kept_own, own_parts, kept_cross, cross_parts)
 
 
 def solution(mesh):

time: 122 us -> 113 us (0.926)
  starting transfers between devices: 62.2 us -> 58.1 us
  waiting for transfers between devices: 27.2 us -> 23.4 us
    ppermute x43, starting transfers between devices: 62.2 us -> 58.1 us  [send(): return lax.ppermute(block, AXES, route)]
    ppermute x43, waiting for transfers between devices: 27.2 us -> 23.4 us  [send(): return lax.ppermute(block, AXES, route)]
    pallas_call x8 -> x14, Pallas kernels: 25.9 us -> 26.8 us  [in_vmem(): pl.pallas_call(kernel, in_specs=specs, out_specs=[pl.BlockSpec(memory_spa...]
  transfers between devices with their start and end apart: 43 -> 43, of which waited for: 14 -> 20; matrix products, arithmetic and copies ran while one was open for 2% -> 2% of each run, Pallas kernels for 16% -> 18%
where the time goes in v4:
time: 113 us; the launch traced here: 112 us
  starting transfers between devices  58.1 us (51%)
  Pallas kernels  26.8 us (24%)
  waiting for transfers between devices  23.4 us (21%)
  other arithmetic  1.68 us (1%)
  local copies, waits for them, and re-layouts  1.38 us (1%)
    ppermute x43, starting transfers between devices, send(): return lax.ppermute(block, AXES, route)  58.1 us
    pallas_call x14, Pallas kernels, in_vmem(): pl.pallas_call(kernel, in_specs=specs, out_specs=[pl.BlockSpec(memory_spa...  26.8 us
    ppermute x43, waiting for transfers between devices, send(): return lax.ppermute(block, AXES, route)  23.4 us
  transfers between devices with their start and end apart: 43, of which 20 were waited for; matrix products, arithmetic and copies ran while one was open for 2% of the time, Pallas kernels for 18%

profile of v4, /device:TPU:1, one launch (start us, length us, event | category | flops | bytes accessed | tf_op | source)
XLA Modules:
  0.0 111.8 jit_solution(11606989328045525814)
XLA Ops:
  0.0 1.0 dynamic-slice_bitcast_fusion
  1.0 4.6 %collective-permute-start.4 = (bf16[64,1024]{1,0:T(8,128)(2,1)S(1)}, bf16[64,1024]{1,0:T(8,128)(2,1)S(1)}, u32[]{:S(2)}, u32[]{:S(2)}) collective-permute-start(bf16[64,1024]{1,0:T(8,128)(2,1)S(1)} %get-tuple-element.87), channel_id=1, source_target_pairs={{0,35},{1,32},{2,33},{3,34},{4,39},{5,36},{6,37},{7,38},{8,43},{9,... | collective-permute-start | bytes 393224 | tf_op jit(solution)/shard_map/ppermute | solution.py:35
  5.6 0.3 collective-permute-start
  5.8 3.6 %collective-permute-start.3 = (bf16[64,1024]{1,0:T(8,128)(2,1)S(1)}, bf16[64,1024]{1,0:T(8,128)(2,1)S(1)}, u32[]{:S(2)}, u32[]{:S(2)}) collective-permute-start(bf16[64,1024]{1,0:T(8,128)(2,1)S(1)} %get-tuple-element.88.refs_0_), channel_id=1, source_target_pairs={{0,3},{1,0},{2,1},{3,2},{4,7},{5,4},{6,5},{7,6},{8,11},{9,8},{10,9... | collective-permute-start | bytes 393224 | tf_op jit(solution)/shard_map/ppermute | solution.py:35
  9.6 0.3 fusion.6
  10.2 0.7 convert_element_type.17.refs_6_.refs_2_.refs_8_.refs_4_
  10.9 1.2 %collective-permute-start.6 = (bf16[64,1024]{1,0:T(8,128)(2,1)S(1)}, bf16[64,1024]{1,0:T(8,128)(2,1)S(1)}, u32[]{:S(2)}, u32[]{:S(2)}) collective-permute-start(bf16[64,1024]{1,0:T(8,128)(2,1)S(1)} %get-tuple-element.87), channel_id=1, source_target_pairs={{0,34},{1,35},{2,32},{3,33},{4,38},{5,39},{6,36},{7,37},{8,42},{9,... | collective-permute-start | bytes 393224 | tf_op jit(solution)/shard_map/ppermute | solution.py:35
  12.1 1.8 %collective-permute-start.5 = (bf16[64,1024]{1,0:T(8,128)(2,1)S(1)}, bf16[64,1024]{1,0:T(8,128)(2,1)S(1)}, u32[]{:S(2)}, u32[]{:S(2)}) collective-permute-start(bf16[64,1024]{1,0:T(8,128)(2,1)S(1)} %get-tuple-element.88.refs_0_), channel_id=1, source_target_pairs={{0,2},{1,3},{2,0},{3,1},{4,6},{5,7},{6,4},{7,5},{8,10},{9,11},{10,... | collective-permute-start | bytes 393224 | tf_op jit(solution)/shard_map/ppermute | solution.py:35
  14.0 0.4 collective-permute-done.refs_1_
  14.3 0.8 collective-permute-done.1.refs_2_
  15.1 2.6 %project_kv.4 = (f32[128,512]{1,0:T(8,128)S(1)}, f32[128,1]{1,0:T(8,128)S(1)}, bf16[1024,256]{1,0:T(8,128)(2,1)S(1)}, bf16[1024,256]{1,0:T(8,128)(2,1)S(1)}) custom-call(bf16[64,1024]{1,0:T(8,128)(2,1)S(1)} %get-tuple-element.88.refs_0_, bf16[64,1024]{1,0:T(8,128)(2,1)S(1)} %collective-permute-done.refs_1_, ...), custom_call_target="tpu_custom_call" | custom-call | flops 402653184 | bytes 4997120 | tf_op jit(solution)/shard_map/project_kv/pallas_call | solution.py:42
  17.7 3.1 %collective-permute-done.5.refs_0_.refs_6_ = bf16[64,1024]{1,0:T(8,128)(2,1)S(1)} collective-permute-done((bf16[64,1024]{1,0:T(8,128)(2,1)S(1)}, bf16[64,1024]{1,0:T(8,128)(2,1)S(1)}, u32[]{:S(2)}, u32[]{:S(2)}) %collective-permute-start.5) | collective-permute-done | bytes 131104 | tf_op jit(solution)/shard_map/ppermute | solution.py:35
  20.8 0.4 project_kv.5
  21.2 3.8 %collective-permute-start.9 = (bf16[128,512]{1,0:T(8,128)(2,1)S(1)}, bf16[128,512]{1,0:T(8,128)(2,1)S(1)}, u32[]{:S(2)}, u32[]{:S(2)}) collective-permute-start(bf16[128,512]{1,0:T(8,128)(2,1)S(1)} %get-tuple-element.50.refs_0_), channel_id=1, source_target_pairs={{0,24},{1,25},{2,26},{3,27},{4,28},{5,29},{6,30},{7,31},{8,0},{9,1... | collective-permute-start | bytes 393224 | tf_op jit(solution)/shard_map/ppermute | solution.py:35
  25.0 1.3 %collective-permute-start.7 = (bf16[128,512]{1,0:T(8,128)(2,1)S(1)}, bf16[128,512]{1,0:T(8,128)(2,1)S(1)}, u32[]{:S(2)}, u32[]{:S(2)}) collective-permute-start(bf16[128,512]{1,0:T(8,128)(2,1)S(1)} %get-tuple-element.50.refs_0_), channel_id=1, source_target_pairs={{0,16},{1,17},{2,18},{3,19},{4,20},{5,21},{6,22},{7,23},{8,24},{9,... | collective-permute-start | bytes 393224 | tf_op jit(solution)/shard_map/ppermute | solution.py:35
  26.5 5.6 %collective-permute-start.10 = (bf16[128,512]{1,0:T(8,128)(2,1)S(1)}, bf16[128,512]{1,0:T(8,128)(2,1)S(1)}, u32[]{:S(2)}, u32[]{:S(2)}) collective-permute-start(bf16[128,512]{1,0:T(8,128)(2,1)S(1)} %get-tuple-element.50.refs_0_), channel_id=1, source_target_pairs={{0,4},{1,5},{2,6},{3,7},{4,0},{5,1},{6,2},{7,3},{8,12},{9,13},{10,... | collective-permute-start | bytes 393224 | tf_op jit(solution)/shard_map/ppermute | solution.py:35
  32.2 4.1 %project_q.2.q = bf16[128,1024]{1,0:T(8,128)(2,1)S(1)} custom-call(bf16[64,1024]{1,0:T(8,128)(2,1)S(1)} %get-tuple-element.88.refs_0_, bf16[64,1024]{1,0:T(8,128)(2,1)S(1)} %collective-permute-done.refs_1_, bf16[64,1024]{1,0:T(8,128)(2,1)S(1)} %collective-permute-done.1.refs_2_, bf16[64,1024]{1,0:T(8,128)(2,1)S(1)} %collective-permute-done.2.refs_3_, ...), custom_call_target="tpu_custom_call" | custom-call | flops 1073741824 | bytes 9585152 | tf_op jit(solution)/shard_map/project_q/pallas_call | solution.py:42
  36.3 1.4 %collective-permute-start.11 = (bf16[128,512]{1,0:T(8,128)(2,1)S(1)}, bf16[128,512]{1,0:T(8,128)(2,1)S(1)}, u32[]{:S(2)}, u32[]{:S(2)}) collective-permute-start(bf16[128,512]{1,0:T(8,128)(2,1)S(1)} %collective-permute-done.8.refs_1_), channel_id=1, source_target_pairs={{0,4},{1,5},{2,6},{3,7},{4,0},{5,1},{6,2},{7,3},{8,12},{9,13},{10,... | collective-permute-start | bytes 393224 | tf_op jit(solution)/shard_map/ppermute | solution.py:35
  37.7 0.5 collective-permute-start.13
  38.3 0.4 collective-permute-done.11.refs_5_
  38.7 0.4 collective-permute-done.12.refs_6_
  39.0 0.2 collective-permute-done.13.refs_7_
  39.2 4.9 %attend_and_project.2 = (bf16[128,512]{1,0:T(8,128)(2,1)S(1)}, bf16[128,512]{1,0:T(8,128)(2,1)S(1)}, bf16[128,512]{1,0:T(8,128)(2,1)S(1)}, bf16[128,512]{1,0:T(8...) custom-call(bf16[128,1024]{1,0:T(8,128)(2,1)S(1)} %project_q.2.q, ...), custom_call_target="tpu_custom_call" | custom-call | flops 1610612736 | bytes 9703936 | tf_op jit(solution)/shard_map/attend_and_project/pallas_call | solution.py:42
  44.3 2.7 %collective-permute-start.16 = (bf16[128,512]{1,0:T(8,128)(2,1)S(1)}, bf16[128,512]{1,0:T(8,128)(2,1)S(1)}, u32[]{:S(2)}, u32[]{:S(2)}) collective-permute-start(bf16[128,512]{1,0:T(8,128)(2,1)S(1)} %get-tuple-element.57), channel_id=1, source_target_pairs={{0,3},{1,0},{2,1},{3,2},{4,7},{5,4},{6,5},{7,6},{8,11},{9,8},{10,9... | collective-permute-start | bytes 393224 | tf_op jit(solution)/shard_map/ppermute | solution.py:35
  47.0 0.7 project_out.2
  47.7 1.8 %collective-permute-start.17 = (bf16[128,512]{1,0:T(8,128)(2,1)S(1)}, bf16[128,512]{1,0:T(8,128)(2,1)S(1)}, u32[]{:S(2)}, u32[]{:S(2)}) collective-permute-start(bf16[128,512]{1,0:T(8,128)(2,1)S(1)} %get-tuple-element.61), channel_id=1, source_target_pairs={{0,2},{1,3},{2,0},{3,1},{4,6},{5,7},{6,4},{7,5},{8,10},{9,11},{10,... | collective-permute-start | bytes 393224 | tf_op jit(solution)/shard_map/ppermute | solution.py:35
  49.5 1.0 collective-permute-done.14.refs_2_
  50.5 1.7 %collective-permute-start.19 = (bf16[128,512]{1,0:T(8,128)(2,1)S(1)}, bf16[128,512]{1,0:T(8,128)(2,1)S(1)}, u32[]{:S(2)}, u32[]{:S(2)}) collective-permute-start(bf16[128,512]{1,0:T(8,128)(2,1)S(1)} %get-tuple-element.63), channel_id=1, source_target_pairs={{0,3},{1,0},{2,1},{3,2},{4,7},{5,4},{6,5},{7,6},{8,11},{9,8},{10,9... | collective-permute-start | bytes 393224 | tf_op jit(solution)/shard_map/ppermute | solution.py:35
  52.2 1.5 %collective-permute-done.15.refs_3_ = bf16[128,512]{1,0:T(8,128)(2,1)S(1)} collective-permute-done((bf16[128,512]{1,0:T(8,128)(2,1)S(1)}, bf16[128,512]{1,0:T(8,128)(2,1)S(1)}, u32[]{:S(2)}, u32[]{:S(2)}) %collective-permute-start.15) | collective-permute-done | bytes 131104 | tf_op jit(solution)/shard_map/ppermute | solution.py:35
  53.8 1.9 %collective-permute-start.20 = (bf16[128,512]{1,0:T(8,128)(2,1)S(1)}, bf16[128,512]{1,0:T(8,128)(2,1)S(1)}, u32[]{:S(2)}, u32[]{:S(2)}) collective-permute-start(bf16[128,512]{1,0:T(8,128)(2,1)S(1)} %add_parts.2), channel_id=1, source_target_pairs={{0,96},{1,97},{2,98},{3,99},{4,100},{5,101},{6,102},{7,103},{8,104... | collective-permute-start | bytes 393224 | tf_op jit(solution)/shard_map/ppermute | solution.py:35
  55.8 0.4 collective-permute-done.17.refs_2_
  56.1 2.8 %collective-permute-done.18.refs_3_ = bf16[128,512]{1,0:T(8,128)(2,1)S(1)} collective-permute-done((bf16[128,512]{1,0:T(8,128)(2,1)S(1)}, bf16[128,512]{1,0:T(8,128)(2,1)S(1)}, u32[]{:S(2)}, u32[]{:S(2)}) %collective-permute-start.18) | collective-permute-done | bytes 131104 | tf_op jit(solution)/shard_map/ppermute | solution.py:35
  59.1 1.9 %collective-permute-start.21 = (bf16[128,512]{1,0:T(8,128)(2,1)S(1)}, bf16[128,512]{1,0:T(8,128)(2,1)S(1)}, u32[]{:S(2)}, u32[]{:S(2)}) collective-permute-start(bf16[128,512]{1,0:T(8,128)(2,1)S(1)} %add_parts.3), channel_id=1, source_target_pairs={{0,96},{1,97},{2,98},{3,99},{4,100},{5,101},{6,102},{7,103},{8,104... | collective-permute-start | bytes 393224 | tf_op jit(solution)/shard_map/ppermute | solution.py:35
  61.0 0.4 collective-permute-start.25
  61.4 0.4 collective-permute-start.24
  61.8 1.1 collective-permute-start.23
  63.1 2.2 %bring.1 = (bf16[4096,256]{1,0:T(8,128)(2,1)S(1)}, bf16[4096,256]{1,0:T(8,128)(2,1)S(1)}) custom-call(bf16[8,128]{1,0:T(8,128)(2,1)S(1)} %slice.48.after_ref, bf16[1,4096,256]{2,1,0:T(8,128)(2,1)} %refs_0_.1, bf16[1,4096,256]{2,1,0:T(8,128)(2,1)} %refs_1_.1), custom_call_target="tpu_custom_call" | custom-call | bytes 4196352 | tf_op jit(solution)/shard_map/bring/pallas_call | solution.py:42
  65.3 2.6 %collective-permute-start.28 = (bf16[128,512]{1,0:T(8,128)(2,1)S(1)}, bf16[128,512]{1,0:T(8,128)(2,1)S(1)}, u32[]{:S(2)}, u32[]{:S(2)}) collective-permute-start(bf16[128,512]{1,0:T(8,128)(2,1)S(1)} %collective-permute-done.21.refs_0_.refs_4_), channel_id=1, source_target_pairs={{0,2},{1,3},{2,0},{3,1},{4,6},{5,7},{6,4},{7,5},{8,10},{9,11},{10,... | collective-permute-start | bytes 393224 | tf_op jit(solution)/shard_map/ppermute | solution.py:35
  68.0 0.7 collective-permute-start.27
  68.6 0.8 collective-permute-start.26
  69.6 0.4 project_kv.6
  70.0 2.5 %collective-permute-done.28.refs_3_.refs_7_ = bf16[128,512]{1,0:T(8,128)(2,1)S(1)} collective-permute-done((bf16[128,512]{1,0:T(8,128)(2,1)S(1)}, bf16[128,512]{1,0:T(8,128)(2,1)S(1)}, u32[]{:S(2)}, u32[]{:S(2)}) %collective-permute-start.28) | collective-permute-done | bytes 131104 | tf_op jit(solution)/shard_map/ppermute | solution.py:35
  72.5 2.4 %collective-permute-done.26.refs_1_.refs_5_ = bf16[128,512]{1,0:T(8,128)(2,1)S(1)} collective-permute-done((bf16[128,512]{1,0:T(8,128)(2,1)S(1)}, bf16[128,512]{1,0:T(8,128)(2,1)S(1)}, u32[]{:S(2)}, u32[]{:S(2)}) %collective-permute-start.26) | collective-permute-done | bytes 131104 | tf_op jit(solution)/shard_map/ppermute | solution.py:35
  74.9 0.5 project_kv.7
  75.4 1.9 %collective-permute-start.31 = (bf16[128,512]{1,0:T(8,128)(2,1)S(1)}, bf16[128,512]{1,0:T(8,128)(2,1)S(1)}, u32[]{:S(2)}, u32[]{:S(2)}) collective-permute-start(bf16[128,512]{1,0:T(8,128)(2,1)S(1)} %get-tuple-element.70.refs_0_), channel_id=1, source_target_pairs={{0,24},{1,25},{2,26},{3,27},{4,28},{5,29},{6,30},{7,31},{8,0},{9,1... | collective-permute-start | bytes 393224 | tf_op jit(solution)/shard_map/ppermute | solution.py:35
  77.3 1.3 %collective-permute-start.29 = (bf16[128,512]{1,0:T(8,128)(2,1)S(1)}, bf16[128,512]{1,0:T(8,128)(2,1)S(1)}, u32[]{:S(2)}, u32[]{:S(2)}) collective-permute-start(bf16[128,512]{1,0:T(8,128)(2,1)S(1)} %get-tuple-element.70.refs_0_), channel_id=1, source_target_pairs={{0,16},{1,17},{2,18},{3,19},{4,20},{5,21},{6,22},{7,23},{8,24},{9,... | collective-permute-start | bytes 393224 | tf_op jit(solution)/shard_map/ppermute | solution.py:35
  78.6 3.4 %collective-permute-start.32 = (bf16[128,512]{1,0:T(8,128)(2,1)S(1)}, bf16[128,512]{1,0:T(8,128)(2,1)S(1)}, u32[]{:S(2)}, u32[]{:S(2)}) collective-permute-start(bf16[128,512]{1,0:T(8,128)(2,1)S(1)} %get-tuple-element.70.refs_0_), channel_id=1, source_target_pairs={{0,4},{1,5},{2,6},{3,7},{4,0},{5,1},{6,2},{7,3},{8,12},{9,13},{10,... | collective-permute-start | bytes 393224 | tf_op jit(solution)/shard_map/ppermute | solution.py:35
  82.0 3.9 %project_q.3.q = bf16[128,1024]{1,0:T(8,128)(2,1)S(1)} custom-call(bf16[128,512]{1,0:T(8,128)(2,1)S(1)} %collective-permute-done.20.refs_0_, bf16[128,512]{1,0:T(8,128)(2,1)S(1)} %collective-permute-done.23.refs_1_, bf16[128,512]{1,0:T(8,128)(2,1)S(1)} %collective-permute-done.24.refs_2_, bf16[128,512]{1,0:T(8,128)(2,1)S(1)} %collective-permute-done.25.refs_3_, ...), custom_call_target="tpu_custom_call" | custom-call | flops 1073741824 | bytes 9585152 | tf_op jit(solution)/shard_map/project_q/pallas_call | solution.py:42
  86.0 2.0 %collective-permute-start.33 = (bf16[128,512]{1,0:T(8,128)(2,1)S(1)}, bf16[128,512]{1,0:T(8,128)(2,1)S(1)}, u32[]{:S(2)}, u32[]{:S(2)}) collective-permute-start(bf16[128,512]{1,0:T(8,128)(2,1)S(1)} %collective-permute-done.30.refs_1_), channel_id=1, source_target_pairs={{0,4},{1,5},{2,6},{3,7},{4,0},{5,1},{6,2},{7,3},{8,12},{9,13},{10,... | collective-permute-start | bytes 393224 | tf_op jit(solution)/shard_map/ppermute | solution.py:35
  88.0 0.5 collective-permute-start.35
  88.7 0.3 collective-permute-done.33.refs_5_
  89.0 0.4 collective-permute-done.34.refs_6_
  89.5 5.0 %attend_and_project.3 = (bf16[64,1024]{1,0:T(8,128)(2,1)S(1)}, bf16[64,1024]{1,0:T(8,128)(2,1)S(1)}, bf16[128,1024]{1,0:T(8,128)(2,1)S(1)}, bf16[3,1024,1024]{2,1,0:T(8,128)(2,1)S(1)}) custom-call(bf16[128,1024]{1,0:T(8,128)(2,1)S(1)} %project_q.3.q, s32[128,1]{1,0:T(8,128)S(1)} %copy.8.qpos, s32[1,1024]{1,0:T(1,128)S(1)} %bitcast.17, ...), custom_call_target="tpu_custom_call" | custom-call | flops 1610612736 | bytes 9703936 | tf_op jit(solution)/shard_map/attend_and_project/pallas_call | solution.py:42
  94.5 0.9 collective-permute-start.36
  95.4 2.7 %collective-permute-start.39 = (bf16[64,1024]{1,0:T(8,128)(2,1)S(1)}, bf16[64,1024]{1,0:T(8,128)(2,1)S(1)}, u32[]{:S(2)}, u32[]{:S(2)}) collective-permute-start(bf16[64,1024]{1,0:T(8,128)(2,1)S(1)} %get-tuple-element.81), channel_id=1, source_target_pairs={{0,34},{1,35},{2,32},{3,33},{4,38},{5,39},{6,36},{7,37},{8,42},{9,... | collective-permute-start | bytes 393224 | tf_op jit(solution)/shard_map/ppermute | solution.py:35
  98.1 1.0 project_out.3
  99.2 2.7 %collective-permute-start.38 = (bf16[64,1024]{1,0:T(8,128)(2,1)S(1)}, bf16[64,1024]{1,0:T(8,128)(2,1)S(1)}, u32[]{:S(2)}, u32[]{:S(2)}) collective-permute-start(bf16[64,1024]{1,0:T(8,128)(2,1)S(1)} %get-tuple-element.79), channel_id=1, source_target_pairs={{0,3},{1,0},{2,1},{3,2},{4,7},{5,4},{6,5},{7,6},{8,11},{9,8},{10,9... | collective-permute-start | bytes 393224 | tf_op jit(solution)/shard_map/ppermute | solution.py:35
  101.9 2.0 %collective-permute-done.36.refs_2_ = bf16[64,1024]{1,0:T(8,128)(2,1)S(1)} collective-permute-done((bf16[64,1024]{1,0:T(8,128)(2,1)S(1)}, bf16[64,1024]{1,0:T(8,128)(2,1)S(1)}, u32[]{:S(2)}, u32[]{:S(2)}) %collective-permute-start.36) | collective-permute-done | bytes 131104 | tf_op jit(solution)/shard_map/ppermute | solution.py:35
  103.9 1.6 %collective-permute-start.41 = (bf16[64,1024]{1,0:T(8,128)(2,1)S(1)}, bf16[64,1024]{1,0:T(8,128)(2,1)S(1)}, u32[]{:S(2)}, u32[]{:S(2)}) collective-permute-start(bf16[64,1024]{1,0:T(8,128)(2,1)S(1)} %get-tuple-element.83), channel_id=1, source_target_pairs={{0,35},{1,32},{2,33},{3,34},{4,39},{5,36},{6,37},{7,38},{8,43},{9,... | collective-permute-start | bytes 393224 | tf_op jit(solution)/shard_map/ppermute | solution.py:35
  105.5 0.9 collective-permute-start.42
  106.3 2.3 %collective-permute-done.37.refs_3_ = bf16[64,1024]{1,0:T(8,128)(2,1)S(1)} collective-permute-done((bf16[64,1024]{1,0:T(8,128)(2,1)S(1)}, bf16[64,1024]{1,0:T(8,128)(2,1)S(1)}, u32[]{:S(2)}, u32[]{:S(2)}) %collective-permute-start.37) | collective-permute-done | bytes 131104 | tf_op jit(solution)/shard_map/ppermute | solution.py:35
  108.6 0.3 collective-permute-done.41.refs_8_
  108.9 2.0 %collective-permute-done.42.refs_9_ = bf16[64,1024]{1,0:T(8,128)(2,1)S(1)} collective-permute-done((bf16[64,1024]{1,0:T(8,128)(2,1)S(1)}, bf16[64,1024]{1,0:T(8,128)(2,1)S(1)}, u32[]{:S(2)}, u32[]{:S(2)}) %collective-permute-start.42) | collective-permute-done | bytes 131104 | tf_op jit(solution)/shard_map/ppermute | solution.py:35
  110.9 0.9 finish.1
  (65 shorter events, 1.9 us)
Async XLA Ops:
  1.0 9.9 %collective-permute-start.4 = (bf16[64,1024]{1,0:T(8,128)(2,1)S(1)}, bf16[64,1024]{1,0:T(8,128)(2,1)S(1)}, u32[]{:S(2)}, u32[]{:S(2)}) collective-permute-start(bf16[64,1024]{1,0:T(8,128)(2,1)S(1)} %get-tuple-element.87), channel_id=1, source_target_pairs={{0,35},{1,32},{2,33},{3,34},{4,39},{5,36},{6,37},{7,38},{8,43},{9,... | collective-permute-start | bytes 393224 | tf_op jit(solution)/shard_map/ppermute | solution.py:35
  5.5 6.6 %collective-permute-start.2 = (bf16[64,1024]{1,0:T(8,128)(2,1)S(1)}, bf16[64,1024]{1,0:T(8,128)(2,1)S(1)}, u32[]{:S(2)}, u32[]{:S(2)}) collective-permute-start(bf16[64,1024]{1,0:T(8,128)(2,1)S(1)} %get-tuple-element.87), channel_id=1, source_target_pairs={{0,33},{1,34},{2,35},{3,32},{4,37},{5,38},{6,39},{7,36},{8,41},{9,... | collective-permute-start | bytes 393224 | tf_op jit(solution)/shard_map/ppermute | solution.py:35
  5.6 8.8 %collective-permute-start = (bf16[64,1024]{1,0:T(8,128)(2,1)S(1)}, bf16[64,1024]{1,0:T(8,128)(2,1)S(1)}, u32[]{:S(2)}, u32[]{:S(2)}) collective-permute-start(bf16[64,1024]{1,0:T(8,128)(2,1)S(1)} %get-tuple-element.87), channel_id=1, source_target_pairs={{0,32},{1,33},{2,34},{3,35},{4,36},{5,37},{6,38},{7,39},{8,40},{9,... | collective-permute-start | bytes 393224 | tf_op jit(solution)/shard_map/ppermute | solution.py:35
  5.8 8.5 %collective-permute-start.3 = (bf16[64,1024]{1,0:T(8,128)(2,1)S(1)}, bf16[64,1024]{1,0:T(8,128)(2,1)S(1)}, u32[]{:S(2)}, u32[]{:S(2)}) collective-permute-start(bf16[64,1024]{1,0:T(8,128)(2,1)S(1)} %get-tuple-element.88.refs_0_), channel_id=1, source_target_pairs={{0,3},{1,0},{2,1},{3,2},{4,7},{5,4},{6,5},{7,6},{8,11},{9,8},{10,9... | collective-permute-start | bytes 393224 | tf_op jit(solution)/shard_map/ppermute | solution.py:35
  9.4 5.7 %collective-permute-start.1 = (bf16[64,1024]{1,0:T(8,128)(2,1)S(1)}, bf16[64,1024]{1,0:T(8,128)(2,1)S(1)}, u32[]{:S(2)}, u32[]{:S(2)}) collective-permute-start(bf16[64,1024]{1,0:T(8,128)(2,1)S(1)} %get-tuple-element.88.refs_0_), channel_id=1, source_target_pairs={{0,1},{1,2},{2,3},{3,0},{4,5},{5,6},{6,7},{7,4},{8,9},{9,10},{10,1... | collective-permute-start | bytes 393224 | tf_op jit(solution)/shard_map/ppermute | solution.py:35
  10.9 6.7 %collective-permute-start.6 = (bf16[64,1024]{1,0:T(8,128)(2,1)S(1)}, bf16[64,1024]{1,0:T(8,128)(2,1)S(1)}, u32[]{:S(2)}, u32[]{:S(2)}) collective-permute-start(bf16[64,1024]{1,0:T(8,128)(2,1)S(1)} %get-tuple-element.87), channel_id=1, source_target_pairs={{0,34},{1,35},{2,32},{3,33},{4,38},{5,39},{6,36},{7,37},{8,42},{9,... | collective-permute-start | bytes 393224 | tf_op jit(solution)/shard_map/ppermute | solution.py:35
  12.1 8.7 %collective-permute-start.5 = (bf16[64,1024]{1,0:T(8,128)(2,1)S(1)}, bf16[64,1024]{1,0:T(8,128)(2,1)S(1)}, u32[]{:S(2)}, u32[]{:S(2)}) collective-permute-start(bf16[64,1024]{1,0:T(8,128)(2,1)S(1)} %get-tuple-element.88.refs_0_), channel_id=1, source_target_pairs={{0,2},{1,3},{2,0},{3,1},{4,6},{5,7},{6,4},{7,5},{8,10},{9,11},{10,... | collective-permute-start | bytes 393224 | tf_op jit(solution)/shard_map/ppermute | solution.py:35
  21.2 15.0 %collective-permute-start.9 = (bf16[128,512]{1,0:T(8,128)(2,1)S(1)}, bf16[128,512]{1,0:T(8,128)(2,1)S(1)}, u32[]{:S(2)}, u32[]{:S(2)}) collective-permute-start(bf16[128,512]{1,0:T(8,128)(2,1)S(1)} %get-tuple-element.50.refs_0_), channel_id=1, source_target_pairs={{0,24},{1,25},{2,26},{3,27},{4,28},{5,29},{6,30},{7,31},{8,0},{9,1... | collective-permute-start | bytes 393224 | tf_op jit(solution)/shard_map/ppermute | solution.py:35
  25.0 11.2 %collective-permute-start.8 = (bf16[128,512]{1,0:T(8,128)(2,1)S(1)}, bf16[128,512]{1,0:T(8,128)(2,1)S(1)}, u32[]{:S(2)}, u32[]{:S(2)}) collective-permute-start(bf16[128,512]{1,0:T(8,128)(2,1)S(1)} %get-tuple-element.50.refs_0_), channel_id=1, source_target_pairs={{0,8},{1,9},{2,10},{3,11},{4,12},{5,13},{6,14},{7,15},{8,16},{9,17... | collective-permute-start | bytes 393224 | tf_op jit(solution)/shard_map/ppermute | solution.py:35
  25.0 11.2 %collective-permute-start.7 = (bf16[128,512]{1,0:T(8,128)(2,1)S(1)}, bf16[128,512]{1,0:T(8,128)(2,1)S(1)}, u32[]{:S(2)}, u32[]{:S(2)}) collective-permute-start(bf16[128,512]{1,0:T(8,128)(2,1)S(1)} %get-tuple-element.50.refs_0_), channel_id=1, source_target_pairs={{0,16},{1,17},{2,18},{3,19},{4,20},{5,21},{6,22},{7,23},{8,24},{9,... | collective-permute-start | bytes 393224 | tf_op jit(solution)/shard_map/ppermute | solution.py:35
  26.5 11.7 %collective-permute-start.10 = (bf16[128,512]{1,0:T(8,128)(2,1)S(1)}, bf16[128,512]{1,0:T(8,128)(2,1)S(1)}, u32[]{:S(2)}, u32[]{:S(2)}) collective-permute-start(bf16[128,512]{1,0:T(8,128)(2,1)S(1)} %get-tuple-element.50.refs_0_), channel_id=1, source_target_pairs={{0,4},{1,5},{2,6},{3,7},{4,0},{5,1},{6,2},{7,3},{8,12},{9,13},{10,... | collective-permute-start | bytes 393224 | tf_op jit(solution)/shard_map/ppermute | solution.py:35
  36.3 2.4 %collective-permute-start.11 = (bf16[128,512]{1,0:T(8,128)(2,1)S(1)}, bf16[128,512]{1,0:T(8,128)(2,1)S(1)}, u32[]{:S(2)}, u32[]{:S(2)}) collective-permute-start(bf16[128,512]{1,0:T(8,128)(2,1)S(1)} %collective-permute-done.8.refs_1_), channel_id=1, source_target_pairs={{0,4},{1,5},{2,6},{3,7},{4,0},{5,1},{6,2},{7,3},{8,12},{9,13},{10,... | collective-permute-start | bytes 393224 | tf_op jit(solution)/shard_map/ppermute | solution.py:35
  37.7 1.3 %collective-permute-start.12 = (bf16[128,512]{1,0:T(8,128)(2,1)S(1)}, bf16[128,512]{1,0:T(8,128)(2,1)S(1)}, u32[]{:S(2)}, u32[]{:S(2)}) collective-permute-start(bf16[128,512]{1,0:T(8,128)(2,1)S(1)} %collective-permute-done.7.refs_2_), channel_id=1, source_target_pairs={{0,4},{1,5},{2,6},{3,7},{4,0},{5,1},{6,2},{7,3},{8,12},{9,13},{10,... | collective-permute-start | bytes 393224 | tf_op jit(solution)/shard_map/ppermute | solution.py:35
  37.7 1.5 %collective-permute-start.13 = (bf16[128,512]{1,0:T(8,128)(2,1)S(1)}, bf16[128,512]{1,0:T(8,128)(2,1)S(1)}, u32[]{:S(2)}, u32[]{:S(2)}) collective-permute-start(bf16[128,512]{1,0:T(8,128)(2,1)S(1)} %collective-permute-done.9.refs_3_), channel_id=1, source_target_pairs={{0,4},{1,5},{2,6},{3,7},{4,0},{5,1},{6,2},{7,3},{8,12},{9,13},{10,... | collective-permute-start | bytes 393224 | tf_op jit(solution)/shard_map/ppermute | solution.py:35
  44.1 6.4 %collective-permute-start.14 = (bf16[128,512]{1,0:T(8,128)(2,1)S(1)}, bf16[128,512]{1,0:T(8,128)(2,1)S(1)}, u32[]{:S(2)}, u32[]{:S(2)}) collective-permute-start(bf16[128,512]{1,0:T(8,128)(2,1)S(1)} %get-tuple-element.55), channel_id=1, source_target_pairs={{0,2},{1,3},{2,0},{3,1},{4,6},{5,7},{6,4},{7,5},{8,10},{9,11},{10,... | collective-permute-start | bytes 393224 | tf_op jit(solution)/shard_map/ppermute | solution.py:35
  44.2 9.5 %collective-permute-start.15 = (bf16[128,512]{1,0:T(8,128)(2,1)S(1)}, bf16[128,512]{1,0:T(8,128)(2,1)S(1)}, u32[]{:S(2)}, u32[]{:S(2)}) collective-permute-start(bf16[128,512]{1,0:T(8,128)(2,1)S(1)} %get-tuple-element.56), channel_id=1, source_target_pairs={{0,1},{1,2},{2,3},{3,0},{4,5},{5,6},{6,7},{7,4},{8,9},{9,10},{10,1... | collective-permute-start | bytes 393224 | tf_op jit(solution)/shard_map/ppermute | solution.py:35
  44.3 9.4 %collective-permute-start.16 = (bf16[128,512]{1,0:T(8,128)(2,1)S(1)}, bf16[128,512]{1,0:T(8,128)(2,1)S(1)}, u32[]{:S(2)}, u32[]{:S(2)}) collective-permute-start(bf16[128,512]{1,0:T(8,128)(2,1)S(1)} %get-tuple-element.57), channel_id=1, source_target_pairs={{0,3},{1,0},{2,1},{3,2},{4,7},{5,4},{6,5},{7,6},{8,11},{9,8},{10,9... | collective-permute-start | bytes 393224 | tf_op jit(solution)/shard_map/ppermute | solution.py:35
  47.7 8.4 %collective-permute-start.17 = (bf16[128,512]{1,0:T(8,128)(2,1)S(1)}, bf16[128,512]{1,0:T(8,128)(2,1)S(1)}, u32[]{:S(2)}, u32[]{:S(2)}) collective-permute-start(bf16[128,512]{1,0:T(8,128)(2,1)S(1)} %get-tuple-element.61), channel_id=1, source_target_pairs={{0,2},{1,3},{2,0},{3,1},{4,6},{5,7},{6,4},{7,5},{8,10},{9,11},{10,... | collective-permute-start | bytes 393224 | tf_op jit(solution)/shard_map/ppermute | solution.py:35
  49.5 9.5 %collective-permute-start.18 = (bf16[128,512]{1,0:T(8,128)(2,1)S(1)}, bf16[128,512]{1,0:T(8,128)(2,1)S(1)}, u32[]{:S(2)}, u32[]{:S(2)}) collective-permute-start(bf16[128,512]{1,0:T(8,128)(2,1)S(1)} %get-tuple-element.62), channel_id=1, source_target_pairs={{0,1},{1,2},{2,3},{3,0},{4,5},{5,6},{6,7},{7,4},{8,9},{9,10},{10,1... | collective-permute-start | bytes 393224 | tf_op jit(solution)/shard_map/ppermute | solution.py:35
  50.5 8.5 %collective-permute-start.19 = (bf16[128,512]{1,0:T(8,128)(2,1)S(1)}, bf16[128,512]{1,0:T(8,128)(2,1)S(1)}, u32[]{:S(2)}, u32[]{:S(2)}) collective-permute-start(bf16[128,512]{1,0:T(8,128)(2,1)S(1)} %get-tuple-element.63), channel_id=1, source_target_pairs={{0,3},{1,0},{2,1},{3,2},{4,7},{5,4},{6,5},{7,6},{8,11},{9,8},{10,9... | collective-permute-start | bytes 393224 | tf_op jit(solution)/shard_map/ppermute | solution.py:35
  53.8 7.2 %collective-permute-start.20 = (bf16[128,512]{1,0:T(8,128)(2,1)S(1)}, bf16[128,512]{1,0:T(8,128)(2,1)S(1)}, u32[]{:S(2)}, u32[]{:S(2)}) collective-permute-start(bf16[128,512]{1,0:T(8,128)(2,1)S(1)} %add_parts.2), channel_id=1, source_target_pairs={{0,96},{1,97},{2,98},{3,99},{4,100},{5,101},{6,102},{7,103},{8,104... | collective-permute-start | bytes 393224 | tf_op jit(solution)/shard_map/ppermute | solution.py:35
  59.1 6.2 %collective-permute-start.21 = (bf16[128,512]{1,0:T(8,128)(2,1)S(1)}, bf16[128,512]{1,0:T(8,128)(2,1)S(1)}, u32[]{:S(2)}, u32[]{:S(2)}) collective-permute-start(bf16[128,512]{1,0:T(8,128)(2,1)S(1)} %add_parts.3), channel_id=1, source_target_pairs={{0,96},{1,97},{2,98},{3,99},{4,100},{5,101},{6,102},{7,103},{8,104... | collective-permute-start | bytes 393224 | tf_op jit(solution)/shard_map/ppermute | solution.py:35
  61.0 7.7 %collective-permute-start.25 = (bf16[128,512]{1,0:T(8,128)(2,1)S(1)}, bf16[128,512]{1,0:T(8,128)(2,1)S(1)}, u32[]{:S(2)}, u32[]{:S(2)}) collective-permute-start(bf16[128,512]{1,0:T(8,128)(2,1)S(1)} %collective-permute-done.20.refs_0_), channel_id=1, source_target_pairs={{0,2},{1,3},{2,0},{3,1},{4,6},{5,7},{6,4},{7,5},{8,10},{9,11},{10,... | collective-permute-start | bytes 393224 | tf_op jit(solution)/shard_map/ppermute | solution.py:35
  61.4 8.0 %collective-permute-start.24 = (bf16[128,512]{1,0:T(8,128)(2,1)S(1)}, bf16[128,512]{1,0:T(8,128)(2,1)S(1)}, u32[]{:S(2)}, u32[]{:S(2)}) collective-permute-start(bf16[128,512]{1,0:T(8,128)(2,1)S(1)} %collective-permute-done.20.refs_0_), channel_id=1, source_target_pairs={{0,3},{1,0},{2,1},{3,2},{4,7},{5,4},{6,5},{7,6},{8,11},{9,8},{10,9... | collective-permute-start | bytes 393224 | tf_op jit(solution)/shard_map/ppermute | solution.py:35
  61.8 7.8 %collective-permute-start.23 = (bf16[128,512]{1,0:T(8,128)(2,1)S(1)}, bf16[128,512]{1,0:T(8,128)(2,1)S(1)}, u32[]{:S(2)}, u32[]{:S(2)}) collective-permute-start(bf16[128,512]{1,0:T(8,128)(2,1)S(1)} %collective-permute-done.20.refs_0_), channel_id=1, source_target_pairs={{0,1},{1,2},{2,3},{3,0},{4,5},{5,6},{6,7},{7,4},{8,9},{9,10},{10,1... | collective-permute-start | bytes 393224 | tf_op jit(solution)/shard_map/ppermute | solution.py:35
  65.3 7.2 %collective-permute-start.28 = (bf16[128,512]{1,0:T(8,128)(2,1)S(1)}, bf16[128,512]{1,0:T(8,128)(2,1)S(1)}, u32[]{:S(2)}, u32[]{:S(2)}) collective-permute-start(bf16[128,512]{1,0:T(8,128)(2,1)S(1)} %collective-permute-done.21.refs_0_.refs_4_), channel_id=1, source_target_pairs={{0,2},{1,3},{2,0},{3,1},{4,6},{5,7},{6,4},{7,5},{8,10},{9,11},{10,... | collective-permute-start | bytes 393224 | tf_op jit(solution)/shard_map/ppermute | solution.py:35
  68.0 4.6 %collective-permute-start.27 = (bf16[128,512]{1,0:T(8,128)(2,1)S(1)}, bf16[128,512]{1,0:T(8,128)(2,1)S(1)}, u32[]{:S(2)}, u32[]{:S(2)}) collective-permute-start(bf16[128,512]{1,0:T(8,128)(2,1)S(1)} %collective-permute-done.21.refs_0_.refs_4_), channel_id=1, source_target_pairs={{0,3},{1,0},{2,1},{3,2},{4,7},{5,4},{6,5},{7,6},{8,11},{9,8},{10,9... | collective-permute-start | bytes 393224 | tf_op jit(solution)/shard_map/ppermute | solution.py:35
  68.6 6.2 %collective-permute-start.26 = (bf16[128,512]{1,0:T(8,128)(2,1)S(1)}, bf16[128,512]{1,0:T(8,128)(2,1)S(1)}, u32[]{:S(2)}, u32[]{:S(2)}) collective-permute-start(bf16[128,512]{1,0:T(8,128)(2,1)S(1)} %collective-permute-done.21.refs_0_.refs_4_), channel_id=1, source_target_pairs={{0,1},{1,2},{2,3},{3,0},{4,5},{5,6},{6,7},{7,4},{8,9},{9,10},{10,1... | collective-permute-start | bytes 393224 | tf_op jit(solution)/shard_map/ppermute | solution.py:35
  75.4 10.5 %collective-permute-start.31 = (bf16[128,512]{1,0:T(8,128)(2,1)S(1)}, bf16[128,512]{1,0:T(8,128)(2,1)S(1)}, u32[]{:S(2)}, u32[]{:S(2)}) collective-permute-start(bf16[128,512]{1,0:T(8,128)(2,1)S(1)} %get-tuple-element.70.refs_0_), channel_id=1, source_target_pairs={{0,24},{1,25},{2,26},{3,27},{4,28},{5,29},{6,30},{7,31},{8,0},{9,1... | collective-permute-start | bytes 393224 | tf_op jit(solution)/shard_map/ppermute | solution.py:35
  77.3 8.6 %collective-permute-start.30 = (bf16[128,512]{1,0:T(8,128)(2,1)S(1)}, bf16[128,512]{1,0:T(8,128)(2,1)S(1)}, u32[]{:S(2)}, u32[]{:S(2)}) collective-permute-start(bf16[128,512]{1,0:T(8,128)(2,1)S(1)} %get-tuple-element.70.refs_0_), channel_id=1, source_target_pairs={{0,8},{1,9},{2,10},{3,11},{4,12},{5,13},{6,14},{7,15},{8,16},{9,17... | collective-permute-start | bytes 393224 | tf_op jit(solution)/shard_map/ppermute | solution.py:35
  77.3 8.7 %collective-permute-start.29 = (bf16[128,512]{1,0:T(8,128)(2,1)S(1)}, bf16[128,512]{1,0:T(8,128)(2,1)S(1)}, u32[]{:S(2)}, u32[]{:S(2)}) collective-permute-start(bf16[128,512]{1,0:T(8,128)(2,1)S(1)} %get-tuple-element.70.refs_0_), channel_id=1, source_target_pairs={{0,16},{1,17},{2,18},{3,19},{4,20},{5,21},{6,22},{7,23},{8,24},{9,... | collective-permute-start | bytes 393224 | tf_op jit(solution)/shard_map/ppermute | solution.py:35
  78.6 10.1 %collective-permute-start.32 = (bf16[128,512]{1,0:T(8,128)(2,1)S(1)}, bf16[128,512]{1,0:T(8,128)(2,1)S(1)}, u32[]{:S(2)}, u32[]{:S(2)}) collective-permute-start(bf16[128,512]{1,0:T(8,128)(2,1)S(1)} %get-tuple-element.70.refs_0_), channel_id=1, source_target_pairs={{0,4},{1,5},{2,6},{3,7},{4,0},{5,1},{6,2},{7,3},{8,12},{9,13},{10,... | collective-permute-start | bytes 393224 | tf_op jit(solution)/shard_map/ppermute | solution.py:35
  86.0 3.0 %collective-permute-start.33 = (bf16[128,512]{1,0:T(8,128)(2,1)S(1)}, bf16[128,512]{1,0:T(8,128)(2,1)S(1)}, u32[]{:S(2)}, u32[]{:S(2)}) collective-permute-start(bf16[128,512]{1,0:T(8,128)(2,1)S(1)} %collective-permute-done.30.refs_1_), channel_id=1, source_target_pairs={{0,4},{1,5},{2,6},{3,7},{4,0},{5,1},{6,2},{7,3},{8,12},{9,13},{10,... | collective-permute-start | bytes 393224 | tf_op jit(solution)/shard_map/ppermute | solution.py:35
  88.0 1.3 %collective-permute-start.34 = (bf16[128,512]{1,0:T(8,128)(2,1)S(1)}, bf16[128,512]{1,0:T(8,128)(2,1)S(1)}, u32[]{:S(2)}, u32[]{:S(2)}) collective-permute-start(bf16[128,512]{1,0:T(8,128)(2,1)S(1)} %collective-permute-done.29.refs_2_), channel_id=1, source_target_pairs={{0,4},{1,5},{2,6},{3,7},{4,0},{5,1},{6,2},{7,3},{8,12},{9,13},{10,... | collective-permute-start | bytes 393224 | tf_op jit(solution)/shard_map/ppermute | solution.py:35
  88.0 1.5 %collective-permute-start.35 = (bf16[128,512]{1,0:T(8,128)(2,1)S(1)}, bf16[128,512]{1,0:T(8,128)(2,1)S(1)}, u32[]{:S(2)}, u32[]{:S(2)}) collective-permute-start(bf16[128,512]{1,0:T(8,128)(2,1)S(1)} %collective-permute-done.31.refs_3_), channel_id=1, source_target_pairs={{0,4},{1,5},{2,6},{3,7},{4,0},{5,1},{6,2},{7,3},{8,12},{9,13},{10,... | collective-permute-start | bytes 393224 | tf_op jit(solution)/shard_map/ppermute | solution.py:35
  88.5 13.3 %collective-permute-start.22 = (bf16[64,1024]{1,0:T(8,128)(2,1)S(1)}, bf16[64,1024]{1,0:T(8,128)(2,1)S(1)}, u32[]{:S(2)}, u32[]{:S(2)}) collective-permute-start(bf16[64,1024]{1,0:T(8,128)(2,1)S(1)} %get-tuple-element.85), channel_id=1, source_target_pairs={{0,32},{1,33},{2,34},{3,35},{4,36},{5,37},{6,38},{7,39},{8,40},{9,... | collective-permute-start | bytes 393224 | tf_op jit(solution)/shard_map/ppermute | solution.py:35
  94.5 9.4 %collective-permute-start.36 = (bf16[64,1024]{1,0:T(8,128)(2,1)S(1)}, bf16[64,1024]{1,0:T(8,128)(2,1)S(1)}, u32[]{:S(2)}, u32[]{:S(2)}) collective-permute-start(bf16[64,1024]{1,0:T(8,128)(2,1)S(1)} %get-tuple-element.75), channel_id=1, source_target_pairs={{0,2},{1,3},{2,0},{3,1},{4,6},{5,7},{6,4},{7,5},{8,10},{9,11},{10,... | collective-permute-start | bytes 393224 | tf_op jit(solution)/shard_map/ppermute | solution.py:35
  95.4 10.0 %collective-permute-start.39 = (bf16[64,1024]{1,0:T(8,128)(2,1)S(1)}, bf16[64,1024]{1,0:T(8,128)(2,1)S(1)}, u32[]{:S(2)}, u32[]{:S(2)}) collective-permute-start(bf16[64,1024]{1,0:T(8,128)(2,1)S(1)} %get-tuple-element.81), channel_id=1, source_target_pairs={{0,34},{1,35},{2,32},{3,33},{4,38},{5,39},{6,36},{7,37},{8,42},{9,... | collective-permute-start | bytes 393224 | tf_op jit(solution)/shard_map/ppermute | solution.py:35
  99.1 9.5 %collective-permute-start.37 = (bf16[64,1024]{1,0:T(8,128)(2,1)S(1)}, bf16[64,1024]{1,0:T(8,128)(2,1)S(1)}, u32[]{:S(2)}, u32[]{:S(2)}) collective-permute-start(bf16[64,1024]{1,0:T(8,128)(2,1)S(1)} %get-tuple-element.78), channel_id=1, source_target_pairs={{0,1},{1,2},{2,3},{3,0},{4,5},{5,6},{6,7},{7,4},{8,9},{9,10},{10,1... | collective-permute-start | bytes 393224 | tf_op jit(solution)/shard_map/ppermute | solution.py:35
  99.2 9.4 %collective-permute-start.38 = (bf16[64,1024]{1,0:T(8,128)(2,1)S(1)}, bf16[64,1024]{1,0:T(8,128)(2,1)S(1)}, u32[]{:S(2)}, u32[]{:S(2)}) collective-permute-start(bf16[64,1024]{1,0:T(8,128)(2,1)S(1)} %get-tuple-element.79), channel_id=1, source_target_pairs={{0,3},{1,0},{2,1},{3,2},{4,7},{5,4},{6,5},{7,6},{8,11},{9,8},{10,9... | collective-permute-start | bytes 393224 | tf_op jit(solution)/shard_map/ppermute | solution.py:35
  101.9 6.7 %collective-permute-start.40 = (bf16[64,1024]{1,0:T(8,128)(2,1)S(1)}, bf16[64,1024]{1,0:T(8,128)(2,1)S(1)}, u32[]{:S(2)}, u32[]{:S(2)}) collective-permute-start(bf16[64,1024]{1,0:T(8,128)(2,1)S(1)} %get-tuple-element.82), channel_id=1, source_target_pairs={{0,33},{1,34},{2,35},{3,32},{4,37},{5,38},{6,39},{7,36},{8,41},{9,... | collective-permute-start | bytes 393224 | tf_op jit(solution)/shard_map/ppermute | solution.py:35
  103.9 5.0 %collective-permute-start.41 = (bf16[64,1024]{1,0:T(8,128)(2,1)S(1)}, bf16[64,1024]{1,0:T(8,128)(2,1)S(1)}, u32[]{:S(2)}, u32[]{:S(2)}) collective-permute-start(bf16[64,1024]{1,0:T(8,128)(2,1)S(1)} %get-tuple-element.83), channel_id=1, source_target_pairs={{0,35},{1,32},{2,33},{3,34},{4,39},{5,36},{6,37},{7,38},{8,43},{9,... | collective-permute-start | bytes 393224 | tf_op jit(solution)/shard_map/ppermute | solution.py:35
  105.5 5.5 %collective-permute-start.42 = (bf16[64,1024]{1,0:T(8,128)(2,1)S(1)}, bf16[64,1024]{1,0:T(8,128)(2,1)S(1)}, u32[]{:S(2)}, u32[]{:S(2)}) collective-permute-start(bf16[64,1024]{1,0:T(8,128)(2,1)S(1)} %get-tuple-element.84), channel_id=1, source_target_pairs={{0,32},{1,33},{2,34},{3,35},{4,36},{5,37},{6,38},{7,39},{8,40},{9,... | collective-permute-start | bytes 393224 | tf_op jit(solution)/shard_map/ppermute | solution.py:35

commit v5 on v3

v5 whole, which is shorter than its diff:
```python
import itertools
import math
import jax
import jax.numpy as jnp
from jax import lax
from jax.experimental import pallas as pl
from jax.experimental.pallas import tpu as pltpu
from jax.sharding import PartitionSpec as P

HS = 128
EPS = 1e-05
CHUNKS = 2
SMALL = 10 * 1024 * 1024
SHIFTS = (2, 1, 3, 0)
ORDER = (0, 1, 3, 2)
Z_ORDER = (2, 1, 3)
FLOPS_PER_US = 1_150_000_000
BESIDE_X0 = 3
BESIDE_FIRST, BESIDE_KV, BESIDE_Q, BESIDE_MIX = 5, 2, 4, 4
DIAG = False
AXES = ("section", "ctx", "tp")


def send(block, by_tp=0, by_z=0, other_half=False, other_core=False, next_layer=False):
    n_section = lax.axis_size("section")
    n_ctx = lax.axis_size("ctx")
    n_tp = lax.axis_size("tp")
    n_half = n_ctx // 2
    route = []
    for e, c, t in itertools.product(range(n_section), range(n_ctx), range(n_tp)):
        there = (c % n_half + 2 * by_z) % n_half + c // n_half * n_half
        if other_half or next_layer:
            there = (there + n_half) % n_ctx
        if other_core:
            there = there ^ 1
        end = (e + next_layer) % n_section
        route.append(
            ((e * n_ctx + c) * n_tp + t, (end * n_ctx + there) * n_tp + (t + by_tp) % n_tp)
        )
    return lax.ppermute(block, AXES, route)


def in_vmem(kernel, operands, out_shape, name, in_hbm=(), scratch=(), flops=0, beside=0):
    n_bytes = sum(x.size * x.dtype.itemsize for x in (*operands, *in_hbm))
    specs = [pl.BlockSpec(memory_space=pltpu.VMEM)] * len(operands)
    specs += [pl.BlockSpec(memory_space=pl.ANY)] * len(in_hbm)
    return pl.pallas_call(
        kernel,
        in_specs=specs,
        out_specs=[pl.BlockSpec(memory_space=pltpu.VMEM)] * len(out_shape),
        out_shape=[jax.ShapeDtypeStruct(shape, dtype) for shape, dtype in out_shape],
        scratch_shapes=list(scratch),
        compiler_params=pltpu.CompilerParams(vmem_limit_bytes=SMALL),
        cost_estimate=pl.CostEstimate(flops=flops + beside * FLOPS_PER_US, bytes_accessed=n_bytes, transcendentals=0),
        name=name,
    )(*operands, *[pltpu.with_memory_space_constraint(w, pltpu.HBM) for w in in_hbm])


def from_slice(shift, at, width):
    n_tp = lax.axis_size("tp")
    tp = lax.axis_index("tp")
    return pl.multiple_of(lax.rem(tp + (n_tp - shift) % n_tp, n_tp) * width + at, HS)


def scaled_piece(rows_of, gain, start):
    x = jnp.concatenate([r[...] for r in rows_of], axis=0).astype(jnp.float32)
    g = gain[:, pl.ds(start, x.shape[1])]
    return (x * g).astype(jnp.bfloat16), jnp.sum(x * x, axis=-1, keepdims=True)


def rotated(u, cos, sin):
    return u * cos + pltpu.roll(u, HS // 2, 1) * sin


def flat_pieces(pieces):
    return [r for _, _, rows_of in pieces for r in rows_of]


def regroup(refs, pieces):
    out, at = [], 0
    for _, _, rows_of in pieces:
        out.append(refs[at : at + len(rows_of)])
        at += len(rows_of)
    return out, refs[at:]


def rows_of_segments(tokens):
    _, half, width = tokens.shape
    n_half = lax.axis_size("ctx") // 2

    def body(tokens_ref, own, other, sems):
        x_lo = lax.axis_index("ctx") // n_half
        copies = [
            pltpu.make_async_copy(tokens_ref.at[x_lo], own, sems.at[0]),
            pltpu.make_async_copy(tokens_ref.at[1 - x_lo], other, sems.at[1]),
        ]
        for c in copies:
            c.start()
        for c in copies:
            c.wait()

    return in_vmem(
        body,
        [],
        [((half, width), tokens.dtype)] * 2,
        "rows_of_segments",
        in_hbm=[tokens],
        scratch=[pltpu.SemaphoreType.DMA((2,))],
        beside=BESIDE_FIRST,
    )


def stacked(upper, lower):
    rows, width = upper.shape

    def body(a, b, out):
        out[:rows] = a[...]
        out[rows:] = b[...]

    return in_vmem(
        body, [upper, lower], [((2 * rows, width), upper.dtype)], "stacked", beside=BESIDE_X0
    )[0]


def project_kv(pieces, slice_width, gain, wk, wv, carry, rope):
    rows = sum(x.shape[0] for x in pieces[0][2])
    width = pieces[0][2][0].shape[1]
    kv_cols = wk.shape[2]
    n = len(pieces)
    first, last = carry is None, rope is not None

    def body(*refs):
        groups, refs = regroup(refs, pieces)
        gain_ref, wk_ref, wv_ref = refs[:3]
        refs = refs[3:]
        ss = k = v = None
        if not first:
            acc_in, ss_in = refs[:2]
            refs = refs[2:]
            ss, k, v = ss_in[...], acc_in[:, :kv_cols], acc_in[:, kv_cols:]
        for (shift, at, _), rows_of in zip(pieces, groups):
            start = from_slice(shift, at, slice_width)
            x, squares = scaled_piece(rows_of, gain_ref, start)
            here = pl.ds(start, width)
            pk = jnp.dot(x, wk_ref[0, here, :], preferred_element_type=jnp.float32)
            pv = jnp.dot(x, wv_ref[0, here, :], preferred_element_type=jnp.float32)
            ss = squares if ss is None else ss + squares
            k = pk if k is None else k + pk
            v = pv if v is None else v + pv
        if last:
            cos, sin, out, r_out = refs
            r = lax.rsqrt(ss / 4096.0 + EPS)
            r_out[...] = r
            for h in range(kv_cols // HS):
                at = slice(h * HS, (h + 1) * HS)
                out[:, at] = rotated(k[:, at] * r, cos[...], sin[...]).astype(jnp.bfloat16)
            out[:, kv_cols:] = (v * r).astype(jnp.bfloat16)
        else:
            acc, ss_out = refs
            acc[:, :kv_cols] = k
            acc[:, kv_cols:] = v
            ss_out[...] = ss

    operands = flat_pieces(pieces) + [gain, wk, wv]
    operands += [] if first else list(carry)
    operands += list(rope) if last else []
    kind = jnp.bfloat16 if last else jnp.float32
    return in_vmem(
        body,
        operands,
        [((rows, 2 * kv_cols), kind), ((rows, 1), jnp.float32)],
        "project_kv",
        flops=4 * rows * n * width * kv_cols,
        beside=BESIDE_KV,
    )


def project_q(pieces, slice_width, gain, wq, r, rope):
    rows = sum(x.shape[0] for x in pieces[0][2])
    width = pieces[0][2][0].shape[1]
    cols = wq.shape[2]

    def body(*refs):
        groups, refs = regroup(refs, pieces)
        gain_ref, w_ref, r_ref, cos, sin, out = refs
        acc = None
        for (shift, at, _), rows_of in zip(pieces, groups):
            start = from_slice(shift, at, slice_width)
            x, _ = scaled_piece(rows_of, gain_ref, start)
            part = jnp.dot(
                x, w_ref[0, pl.ds(start, width), :], preferred_element_type=jnp.float32
            )
            acc = part if acc is None else acc + part
        r = r_ref[...] * (math.log2(math.e) / math.sqrt(HS))
        for h in range(cols // HS):
            at = slice(h * HS, (h + 1) * HS)
            out[:, at] = rotated(acc[:, at] * r, cos[...], sin[...]).astype(jnp.bfloat16)

    return in_vmem(
        body,
        flat_pieces(pieces) + [gain, wq, r, *rope],
        [((rows, cols), jnp.bfloat16)],
        "project_q",
        flops=2 * rows * wq.size,
        beside=BESIDE_Q,
    )[0]


def attend_and_project(q, qpos, kpos, blocks, w_out, width, layer, parts):
    rows, q_cols = q.shape
    kv_heads = blocks[0].shape[1] // (2 * HS)
    group = q_cols // HS // kv_heads
    n_blocks = len(blocks)
    half = rows // 2
    keys = half * n_blocks
    n_half = lax.axis_size("ctx") // 2
    slice_width = w_out.shape[2] // lax.axis_size("tp")

    def body(q, qpos, kpos, *refs):
        block_refs, refs = refs[:n_blocks], refs[n_blocks:]
        w_ref, *outs, attended = refs
        x_lo = lax.axis_index("ctx") // n_half
        early = x_lo if layer == 0 else 1 - x_lo
        low = pl.ds(pl.multiple_of(early * half, half), half)
        high = pl.ds(pl.multiple_of((1 - early) * half, half), half)
        bias = jnp.where(kpos[...] <= qpos[...], 0.0, -1e30)
        ones = jnp.ones((keys, HS), jnp.bfloat16)

        def keys_of(rows_of, g):
            return jnp.concatenate(
                [b[rows_of, g * HS : (g + 1) * HS] for b in block_refs], axis=0
            )

        def values_of(rows_of, g):
            return jnp.concatenate([keys_of(rows_of, kv_heads + g), ones], axis=1)

        def score(qs, k):
            return lax.dot_general(
                qs, k, (((1,), (1,)), ((), ())), preferred_element_type=jnp.float32
            ).reshape(group, half, keys)

        def weigh(scores, best, v):
            weights = jnp.exp2(scores - best).astype(jnp.bfloat16)
            return jnp.dot(
                weights.reshape(group * half, keys), v, preferred_element_type=jnp.float32
            )

        for g in range(kv_heads):
            heads = [g * group + j for j in range(group)]
            k_low, k_high = keys_of(low, g), keys_of(high, g)
            v_low, v_high = values_of(low, g), values_of(high, g)
            q_low, q_high = (
                jnp.concatenate([q[r, h * HS : (h + 1) * HS] for h in heads], axis=0)
                for r in (low, high)
            )
            same = score(q_low, k_low) + bias[None]
            best = jnp.max(same, axis=-1, keepdims=True)
            acc_low = weigh(same, best, v_low)
            before = score(q_high, k_low)
            same = score(q_high, k_high) + bias[None]
            best = jnp.maximum(
                jnp.max(before, axis=-1, keepdims=True), jnp.max(same, axis=-1, keepdims=True)
            )
            acc_high = weigh(before, best, v_low) + weigh(same, best, v_high)
            for r, acc in ((low, acc_low), (high, acc_high)):
                normal = (acc[:, :HS] / acc[:, HS:]).astype(jnp.bfloat16)
                for j, h in enumerate(heads):
                    attended[r, h * HS : (h + 1) * HS] = normal[j * half : (j + 1) * half]
        project_parts(attended, w_ref, slice_width, width, parts, outs)

    got = in_vmem(
        body,
        [q, qpos, kpos, *blocks, w_out],
        [((n, width), jnp.bfloat16) for *_, n in parts] + [((rows, q_cols), jnp.bfloat16)],
        "attend_and_project",
        flops=6 * rows * q_cols * keys + 2 * rows * w_out.size,
        beside=BESIDE_MIX,
    )
    return got[:-1], got[-1]


def project_parts(attended, w_ref, slice_width, width, parts, outs):
    done = {}
    for (at, shift, row, n), out in zip(parts, outs):
        if (at, shift) not in done:
            there = pl.ds(from_slice(-shift, at, slice_width), width)
            done[at, shift] = jnp.dot(
                attended[...], w_ref[0, :, there], preferred_element_type=jnp.float32
            ).astype(jnp.bfloat16)
        out[...] = done[at, shift][row : row + n]


def project_out(attended, w_out, width, parts):
    slice_width = w_out.shape[2] // lax.axis_size("tp")

    def body(a, w, *outs):
        project_parts(a, w, slice_width, width, parts, outs)

    return in_vmem(
        body,
        [attended, w_out],
        [((n, width), jnp.bfloat16) for *_, n in parts],
        "project_out",
        flops=2 * sum(n for *_, n in parts) * attended.shape[1] * width,
    )


def total_of(parts):
    total = parts[0][...].astype(jnp.float32)
    for p in parts[1:]:
        total = total + p[...].astype(jnp.float32)
    return total


def add_parts(x, at, parts):
    rows, width = parts[0].shape

    def body(x_ref, *refs):
        *refs, out = refs
        x = x_ref[:, at : at + width].astype(jnp.float32)
        out[...] = (x + total_of(refs)).astype(jnp.bfloat16)

    return in_vmem(body, [x, *parts], [((rows, width), jnp.bfloat16)], "add_parts")[0]


def last_cross(kept, x, parts):
    n = len(parts)

    def body(kept_ref, x_ref, *refs):
        section = lax.axis_index("section")
        total = x_ref[...].astype(jnp.float32) + total_of(refs[:n])
        refs[n][...] = jnp.where(section == 0, kept_ref[...], total.astype(jnp.bfloat16))

    return in_vmem(body, [kept, x, *parts], [(x.shape, jnp.bfloat16)], "last_cross")[0]


def finish(kept, x, parts, cross):
    half, width = x.shape
    n = len(parts)
    n_half = lax.axis_size("ctx") // 2

    def body(kept_ref, x_ref, *refs):
        section = lax.axis_index("section")
        x_lo = lax.axis_index("ctx") // n_half
        total = x_ref[...].astype(jnp.float32) + total_of(refs[:n])
        own = jnp.where(section == 0, kept_ref[...], total.astype(jnp.bfloat16))
        cross_ref, out = refs[n:]
        own_first = x_lo == section
        out[0, 0] = jnp.where(own_first, own, cross_ref[...])
        out[0, 1] = jnp.where(own_first, cross_ref[...], own)

    return in_vmem(
        body, [kept, x, *parts, cross], [((1, 2, half, width), jnp.bfloat16)], "finish"
    )[0]


def per_device(tokens, norm_gain, wq, wk, wv, w_out):
    n_ctx = lax.axis_size("ctx")
    n_tp = lax.axis_size("tp")
    n_z = n_ctx // 4
    ctx = lax.axis_index("ctx")
    x_lo = ctx // (n_ctx // 2)
    z = (ctx // 2) % n_z
    core = ctx % 2
    half = tokens.shape[1]
    width = tokens.shape[2]
    chunk = width // CHUNKS

    local = lax.iota(jnp.int32, half)

    def positions(z_of, core_of):
        base = (z_of * 2 + core_of) * half + local
        mine = x_lo * (n_ctx // 2) * half + base
        theirs = (1 - x_lo) * (n_ctx // 2) * half + base
        return jnp.concatenate([mine, theirs])

    z_of = [(z - s) % n_z for s in (0, *Z_ORDER)]
    positions_of = positions(z, core)
    qpos = ((z * 2 + core) * half + local)[:, None]
    kpos = jnp.concatenate(
        [(zs * 2 + c) * half + local for c in (core, 1 - core) for zs in z_of]
    )[None, :]

    def tables(qpos):
        pairs = lax.iota(jnp.int32, HS // 2).astype(jnp.float32)
        freqs = jnp.power(jnp.float32(500000.0), -2.0 * pairs / HS)
        angle = qpos.astype(jnp.float32)[:, None] * freqs[None, :]
        cosine = jnp.cos(angle)
        sine = jnp.sin(angle)
        return (
            jnp.concatenate([cosine, cosine], axis=1),
            jnp.concatenate([-sine, sine], axis=1),
        )

    def swapped(rows):
        return jnp.concatenate([rows[half : 2 * half], rows[:half]], axis=0)


    def mix(kv, make_q, w_out, width, layer, parts):
        theirs = [send(kv, other_core=True)]
        sent = {s: send(kv, by_z=s) for s in (3, 1, 2)}
        q, early = lax.optimization_barrier((make_q(), sent[Z_ORDER[-1]]))
        sent[Z_ORDER[-1]] = early
        mine = [sent[s] for s in Z_ORDER]
        theirs += [send(block, other_core=True) for block in mine]
        blocks = [kv, *mine, *theirs]
        return attend_and_project(q, qpos, kpos, blocks, w_out, width, layer, parts)

    own, other = rows_of_segments(tokens)
    own_from = {s: send(own, by_tp=s) for s in (3, 1, 2)}
    other = send(other, other_half=True)
    positions_of, gain, qpos, kpos, other = lax.optimization_barrier(
        (positions_of, norm_gain, qpos, kpos, other)
    )
    gain = gain.astype(jnp.float32)
    rope = tables(positions_of)
    other_from = {s: send(other, by_tp=s) for s in (3, 1, 2)}
    own_from[0], other_from[0] = own, other
    x0 = stacked(own, other)
    pieces = [(s, 0, [x0] if s == 0 else [own_from[s], other_from[s]]) for s in (0, 2, 1, 3)]
    carry = project_kv(pieces[:2], width, gain, wk, wv, None, None)
    kv, r = project_kv(pieces[2:], width, gain, wk, wv, carry, rope)
    chunked = [[(c * chunk, s, 0, 2 * half) for s in SHIFTS] for c in range(CHUNKS)]
    got, attended = mix(
        kv,
        lambda: project_q(pieces, width, gain, wq, r, rope),
        w_out,
        chunk,
        0,
        chunked[0],
    )
    got += project_out(attended, w_out, chunk, sum(chunked[1:], []))
    sums = []
    for c in range(CHUNKS):
        parts = []
        for s, block in zip(SHIFTS, got[c * n_tp : (c + 1) * n_tp]):
            parts.append(send(block, by_tp=s) if s else block)
        sums.append(add_parts(x0, c * chunk, parts))

    rope = tuple(swapped(t) for t in rope)
    carry = None
    every = []
    came = []
    for c in range(CHUNKS):
        last = c == CHUNKS - 1
        came.append(send(sums[c], next_layer=True))
        x_from = {0: came[c]}
        if DIAG:
            x_from[2] = send(sums[c], next_layer=True, by_tp=2)
        for s in (1, 3) if DIAG else (3, 1, 2):
            x_from[s] = send(came[c], by_tp=s)
        pieces = [(s, c * chunk, [x_from[s]]) for s in ORDER]
        every += pieces
        carry = project_kv(pieces, width, gain, wk, wv, carry, rope if last else None)
    kv, r = carry
    kept = jnp.concatenate(sums, axis=1)
    x1 = jnp.concatenate(came, axis=1)
    got, attended = mix(
        kv,
        lambda: project_q(every, width, gain, wq, r, rope),
        w_out,
        width,
        1,
        [(0, s, row, half) for row in (0, half) for s in SHIFTS],
    )
    rest = got[n_tp:]
    parts = [send(block, by_tp=s) if s else block for s, block in zip(SHIFTS, got)]
    cross = send(last_cross(kept[half:], x1[:half], parts), other_half=True)
    parts = [send(block, by_tp=s) if s else block for s, block in zip(SHIFTS, rest)]
    return finish(kept[:half], x1[half:], parts, cross)


def solution(mesh):
    return jax.shard_map(
        per_device,
        mesh=mesh,
        in_specs=(
            P(None, "ctx", "tp"),
            P("section", None),
            P("section", None, "tp"),
            P("section", None, "tp"),
            P("section", None, "tp"),
            P("section", "tp", None),
        ),
        out_specs=P("section", None, "ctx", "tp"),
        check_vma=False,
    )
```

time: 122 us -> 106 us (0.87); the launches traced: 120 us -> 106 us
  waiting for transfers between devices: 27.2 us -> 42.9 us
  starting transfers between devices: 62.2 us -> 48.6 us
  Pallas kernels: 25.9 us -> 13.4 us
  other arithmetic: 2.79 us -> 0.81 us
  local copies, waits for them, and re-layouts: 1.38 us -> 0.16 us
    ppermute x43 -> x42, waiting for transfers between devices: 27.2 us -> 42.9 us  [send(): return lax.ppermute(block, AXES, route)]
    ppermute x43 -> x42, starting transfers between devices: 62.2 us -> 48.6 us  [send(): return lax.ppermute(block, AXES, route)]
    pallas_call x8 -> x15, Pallas kernels: 25.9 us -> 13.4 us  [in_vmem(): pl.pallas_call(kernel, in_specs=specs, out_specs=[pl.BlockSpec(memory_spa...]
  transfers between devices with their start and end apart: 43 -> 42, of which waited for: 14 -> 23; matrix products, arithmetic and copies ran while one was open for 2% -> 1% of each run, Pallas kernels for 16% -> 4%
where the time goes in v5:
time: 106 us
  starting transfers between devices  48.6 us (46%)
  waiting for transfers between devices  42.9 us (40%)
  Pallas kernels  13.4 us (13%)
    ppermute x42, starting transfers between devices, send(): return lax.ppermute(block, AXES, route)  48.6 us
    ppermute x42, waiting for transfers between devices, send(): return lax.ppermute(block, AXES, route)  42.9 us
    pallas_call x15, Pallas kernels, in_vmem(): pl.pallas_call(kernel, in_specs=specs, out_specs=[pl.BlockSpec(memory_spa...  13.4 us
  transfers between devices with their start and end apart: 42, of which 23 were waited for; matrix products, arithmetic and copies ran while one was open for 1% of the time, Pallas kernels for 4%

profile of v5, /device:TPU:1, one launch (start us, length us, event | category | flops | bytes accessed | tf_op | source)
XLA Modules:
  0.0 106.2 jit_solution(2081230794910354831)
XLA Ops:
  0.0 1.0 rows_of_segments.1
  1.0 3.6 %collective-permute-start.5 = (bf16[64,1024]{1,0:T(8,128)(2,1)S(1)}, bf16[64,1024]{1,0:T(8,128)(2,1)S(1)}, u32[]{:S(2)}, u32[]{:S(2)}) collective-permute-start(bf16[64,1024]{1,0:T(8,128)(2,1)S(1)} %get-tuple-element.41.a), channel_id=1, source_target_pairs={{0,3},{1,0},{2,1},{3,2},{4,7},{5,4},{6,5},{7,6},{8,11},{9,8},{10,9... | collective-permute-start | bytes 393224 | tf_op jit(solution)/shard_map/ppermute | solution.py:40
  4.7 1.6 %collective-permute-start.1 = (bf16[64,1024]{1,0:T(8,128)(2,1)S(1)}, bf16[64,1024]{1,0:T(8,128)(2,1)S(1)}, u32[]{:S(2)}, u32[]{:S(2)}) collective-permute-start(bf16[64,1024]{1,0:T(8,128)(2,1)S(1)} %get-tuple-element.41.a), channel_id=1, source_target_pairs={{0,2},{1,3},{2,0},{3,1},{4,6},{5,7},{6,4},{7,5},{8,10},{9,11},{10,... | collective-permute-start | bytes 393224 | tf_op jit(solution)/shard_map/ppermute | solution.py:40
  6.3 1.2 %collective-permute-start = (bf16[64,1024]{1,0:T(8,128)(2,1)S(1)}, bf16[64,1024]{1,0:T(8,128)(2,1)S(1)}, u32[]{:S(2)}, u32[]{:S(2)}) collective-permute-start(bf16[64,1024]{1,0:T(8,128)(2,1)S(1)} %get-tuple-element.42), channel_id=1, source_target_pairs={{0,32},{1,33},{2,34},{3,35},{4,36},{5,37},{6,38},{7,39},{8,40},{9,... | collective-permute-start | bytes 393224 | tf_op jit(solution)/shard_map/ppermute | solution.py:40
  7.7 2.7 %collective-permute-done.b = bf16[64,1024]{1,0:T(8,128)(2,1)S(1)} collective-permute-done((bf16[64,1024]{1,0:T(8,128)(2,1)S(1)}, bf16[64,1024]{1,0:T(8,128)(2,1)S(1)}, u32[]{:S(2)}, u32[]{:S(2)}) %collective-permute-start) | collective-permute-done | bytes 131104 | tf_op jit(solution)/shard_map/ppermute | solution.py:40
  10.4 1.0 collective-permute-start.6
  11.4 2.4 %collective-permute-start.2 = (bf16[64,1024]{1,0:T(8,128)(2,1)S(1)}, bf16[64,1024]{1,0:T(8,128)(2,1)S(1)}, u32[]{:S(2)}, u32[]{:S(2)}) collective-permute-start(bf16[64,1024]{1,0:T(8,128)(2,1)S(1)} %collective-permute-done.b), channel_id=1, source_target_pairs={{0,2},{1,3},{2,0},{3,1},{4,6},{5,7},{6,4},{7,5},{8,10},{9,11},{10,... | collective-permute-start | bytes 393224 | tf_op jit(solution)/shard_map/ppermute | solution.py:40
  14.5 2.3 %collective-permute-done.2.refs_2_ = bf16[64,1024]{1,0:T(8,128)(2,1)S(1)} collective-permute-done((bf16[64,1024]{1,0:T(8,128)(2,1)S(1)}, bf16[64,1024]{1,0:T(8,128)(2,1)S(1)}, u32[]{:S(2)}, u32[]{:S(2)}) %collective-permute-start.2) | collective-permute-done | bytes 131104 | tf_op jit(solution)/shard_map/ppermute | solution.py:40
  16.8 0.5 project_kv.4
  17.3 3.6 %collective-permute-done.4.refs_1_.refs_4_ = bf16[64,1024]{1,0:T(8,128)(2,1)S(1)} collective-permute-done((bf16[64,1024]{1,0:T(8,128)(2,1)S(1)}, bf16[64,1024]{1,0:T(8,128)(2,1)S(1)}, u32[]{:S(2)}, u32[]{:S(2)}) %collective-permute-start.4) | collective-permute-done | bytes 131104 | tf_op jit(solution)/shard_map/ppermute | solution.py:40
  20.9 0.6 project_kv.5
  21.5 2.8 %collective-permute-start.10 = (bf16[128,512]{1,0:T(8,128)(2,1)S(1)}, bf16[128,512]{1,0:T(8,128)(2,1)S(1)}, u32[]{:S(2)}, u32[]{:S(2)}) collective-permute-start(bf16[128,512]{1,0:T(8,128)(2,1)S(1)} %get-tuple-element.49.refs_0_), channel_id=1, source_target_pairs={{0,4},{1,5},{2,6},{3,7},{4,0},{5,1},{6,2},{7,3},{8,12},{9,13},{10,... | collective-permute-start | bytes 393224 | tf_op jit(solution)/shard_map/ppermute | solution.py:40
  24.3 1.6 %collective-permute-start.9 = (bf16[128,512]{1,0:T(8,128)(2,1)S(1)}, bf16[128,512]{1,0:T(8,128)(2,1)S(1)}, u32[]{:S(2)}, u32[]{:S(2)}) collective-permute-start(bf16[128,512]{1,0:T(8,128)(2,1)S(1)} %get-tuple-element.49.refs_0_), channel_id=1, source_target_pairs={{0,8},{1,9},{2,10},{3,11},{4,12},{5,13},{6,14},{7,15},{8,16},{9,17... | collective-permute-start | bytes 393224 | tf_op jit(solution)/shard_map/ppermute | solution.py:40
  25.9 3.3 %collective-permute-start.8 = (bf16[128,512]{1,0:T(8,128)(2,1)S(1)}, bf16[128,512]{1,0:T(8,128)(2,1)S(1)}, u32[]{:S(2)}, u32[]{:S(2)}) collective-permute-start(bf16[128,512]{1,0:T(8,128)(2,1)S(1)} %get-tuple-element.49.refs_0_), channel_id=1, source_target_pairs={{0,16},{1,17},{2,18},{3,19},{4,20},{5,21},{6,22},{7,23},{8,24},{9,... | collective-permute-start | bytes 393224 | tf_op jit(solution)/shard_map/ppermute | solution.py:40
  29.2 0.7 collective-permute-start.7
  30.0 1.4 %project_q.2.q = bf16[128,1024]{1,0:T(8,128)(2,1)S(1)} custom-call(bf16[128,1024]{1,0:T(8,128)(2,1)S(1)} %stacked.1.refs_0_.x_ref, bf16[64,1024]{1,0:T(8,128)(2,1)S(1)} %collective-permute-done.1.refs_1_, bf16[64,1024]{1,0:T(8,128)(2,1)S(1)} %collective-permute-done.2.refs_2_, bf16[64,1024]{1,0:T(8,128)(2,1)S(1)} %collective-permute-done.3.refs_0_.refs_3_, ...), custom_call_target="tpu_custom_call" | custom-call | flops 5673741824 | bytes 9585152 | tf_op jit(solution)/shard_map/project_q/pallas_call | solution.py:47
  31.4 3.5 %collective-permute-done.7.refs_3_ = bf16[128,512]{1,0:T(8,128)(2,1)S(1)} collective-permute-done((bf16[128,512]{1,0:T(8,128)(2,1)S(1)}, bf16[128,512]{1,0:T(8,128)(2,1)S(1)}, u32[]{:S(2)}, u32[]{:S(2)}) %collective-permute-start.7) | collective-permute-done | bytes 131104 | tf_op jit(solution)/shard_map/ppermute | solution.py:40
  34.9 1.0 collective-permute-start.12
  35.9 0.6 collective-permute-start.11
  36.5 0.4 collective-permute-done.12.refs_6_
  36.9 0.6 collective-permute-done.11.refs_5_
  37.8 2.5 %attend_and_project.2 = (bf16[128,512]{1,0:T(8,128)(2,1)S(1)}, bf16[128,512]{1,0:T(8,128)(2,1)S(1)}, bf16[128,512]{1,0:T(8,128)(2,1)S(1)}, bf16[128,512]{1,0:T(8,128)(2,1)S(1)}, bf16[128,1024]{1,0:T(8,128)(2,1)S(1)}) custom-call(bf16[128,1024]{1,0:T(8,128)(2,1)S(1)} %project_q.2.q, s32[64,1]{1,0:T(8,128)S(1)} %iota_add_fusion.qpos, s32[1,512]{1,0:T(1,128)S(1)} %bitcast.3, ...), custom_call_target="tpu_custom_call" | custom-call | flops 6076395008 | bytes 9701632 | tf_op jit(solution)/shard_map/attend_and_project/pallas_call | solution.py:47
  40.3 0.6 collective-permute-start.14
  40.9 2.7 %collective-permute-start.16 = (bf16[128,512]{1,0:T(8,128)(2,1)S(1)}, bf16[128,512]{1,0:T(8,128)(2,1)S(1)}, u32[]{:S(2)}, u32[]{:S(2)}) collective-permute-start(bf16[128,512]{1,0:T(8,128)(2,1)S(1)} %get-tuple-element.56), channel_id=1, source_target_pairs={{0,3},{1,0},{2,1},{3,2},{4,7},{5,4},{6,5},{7,6},{8,11},{9,8},{10,9... | collective-permute-start | bytes 393224 | tf_op jit(solution)/shard_map/ppermute | solution.py:40
  43.7 0.8 project_out.1
  44.5 1.3 %collective-permute-start.17 = (bf16[128,512]{1,0:T(8,128)(2,1)S(1)}, bf16[128,512]{1,0:T(8,128)(2,1)S(1)}, u32[]{:S(2)}, u32[]{:S(2)}) collective-permute-start(bf16[128,512]{1,0:T(8,128)(2,1)S(1)} %get-tuple-element.59), channel_id=1, source_target_pairs={{0,2},{1,3},{2,0},{3,1},{4,6},{5,7},{6,4},{7,5},{8,10},{9,11},{10,... | collective-permute-start | bytes 393224 | tf_op jit(solution)/shard_map/ppermute | solution.py:40
  45.8 1.1 %collective-permute-done.14.refs_0_ = bf16[128,512]{1,0:T(8,128)(2,1)S(1)} collective-permute-done((bf16[128,512]{1,0:T(8,128)(2,1)S(1)}, bf16[128,512]{1,0:T(8,128)(2,1)S(1)}, u32[]{:S(2)}, u32[]{:S(2)}) %collective-permute-start.14) | collective-permute-done | bytes 131104 | tf_op jit(solution)/shard_map/ppermute | solution.py:40
  46.9 1.6 %collective-permute-start.19 = (bf16[128,512]{1,0:T(8,128)(2,1)S(1)}, bf16[128,512]{1,0:T(8,128)(2,1)S(1)}, u32[]{:S(2)}, u32[]{:S(2)}) collective-permute-start(bf16[128,512]{1,0:T(8,128)(2,1)S(1)} %get-tuple-element.61), channel_id=1, source_target_pairs={{0,3},{1,0},{2,1},{3,2},{4,7},{5,4},{6,5},{7,6},{8,11},{9,8},{10,9... | collective-permute-start | bytes 393224 | tf_op jit(solution)/shard_map/ppermute | solution.py:40
  48.4 2.1 %collective-permute-done.15.refs_1_ = bf16[128,512]{1,0:T(8,128)(2,1)S(1)} collective-permute-done((bf16[128,512]{1,0:T(8,128)(2,1)S(1)}, bf16[128,512]{1,0:T(8,128)(2,1)S(1)}, u32[]{:S(2)}, u32[]{:S(2)}) %collective-permute-start.15) | collective-permute-done | bytes 131104 | tf_op jit(solution)/shard_map/ppermute | solution.py:40
  50.7 2.6 %collective-permute-start.20 = (bf16[128,512]{1,0:T(8,128)(2,1)S(1)}, bf16[128,512]{1,0:T(8,128)(2,1)S(1)}, u32[]{:S(2)}, u32[]{:S(2)}) collective-permute-start(bf16[128,512]{1,0:T(8,128)(2,1)S(1)} %add_parts.2), channel_id=1, source_target_pairs={{0,96},{1,97},{2,98},{3,99},{4,100},{5,101},{6,102},{7,103},{8,104... | collective-permute-start | bytes 393224 | tf_op jit(solution)/shard_map/ppermute | solution.py:40
  53.4 2.3 %collective-permute-done.18.refs_1_ = bf16[128,512]{1,0:T(8,128)(2,1)S(1)} collective-permute-done((bf16[128,512]{1,0:T(8,128)(2,1)S(1)}, bf16[128,512]{1,0:T(8,128)(2,1)S(1)}, u32[]{:S(2)}, u32[]{:S(2)}) %collective-permute-start.18) | collective-permute-done | bytes 131104 | tf_op jit(solution)/shard_map/ppermute | solution.py:40
  55.7 2.6 %collective-permute-start.21 = (bf16[128,512]{1,0:T(8,128)(2,1)S(1)}, bf16[128,512]{1,0:T(8,128)(2,1)S(1)}, u32[]{:S(2)}, u32[]{:S(2)}) collective-permute-start(bf16[128,512]{1,0:T(8,128)(2,1)S(1)} %add_parts.3), channel_id=1, source_target_pairs={{0,96},{1,97},{2,98},{3,99},{4,100},{5,101},{6,102},{7,103},{8,104... | collective-permute-start | bytes 393224 | tf_op jit(solution)/shard_map/ppermute | solution.py:40
  58.3 0.6 collective-permute-start.24
  58.9 1.2 %collective-permute-start.23 = (bf16[128,512]{1,0:T(8,128)(2,1)S(1)}, bf16[128,512]{1,0:T(8,128)(2,1)S(1)}, u32[]{:S(2)}, u32[]{:S(2)}) collective-permute-start(bf16[128,512]{1,0:T(8,128)(2,1)S(1)} %collective-permute-done.20.refs_0_), channel_id=1, source_target_pairs={{0,3},{1,0},{2,1},{3,2},{4,7},{5,4},{6,5},{7,6},{8,11},{9,8},{10,9... | collective-permute-start | bytes 393224 | tf_op jit(solution)/shard_map/ppermute | solution.py:40
  60.4 1.1 %collective-permute-done.21.refs_0_.refs_4_ = bf16[128,512]{1,0:T(8,128)(2,1)S(1)} collective-permute-done((bf16[128,512]{1,0:T(8,128)(2,1)S(1)}, bf16[128,512]{1,0:T(8,128)(2,1)S(1)}, u32[]{:S(2)}, u32[]{:S(2)}) %collective-permute-start.21) | collective-permute-done | bytes 131104 | tf_op jit(solution)/shard_map/ppermute | solution.py:40
  61.5 1.4 %collective-permute-start.27 = (bf16[128,512]{1,0:T(8,128)(2,1)S(1)}, bf16[128,512]{1,0:T(8,128)(2,1)S(1)}, u32[]{:S(2)}, u32[]{:S(2)}) collective-permute-start(bf16[128,512]{1,0:T(8,128)(2,1)S(1)} %collective-permute-done.21.refs_0_.refs_4_), channel_id=1, source_target_pairs={{0,2},{1,3},{2,0},{3,1},{4,6},{5,7},{6,4},{7,5},{8,10},{9,11},{10,... | collective-permute-start | bytes 393224 | tf_op jit(solution)/shard_map/ppermute | solution.py:40
  62.8 0.6 collective-permute-start.26
  63.4 0.5 collective-permute-done.24.refs_3_
  63.9 0.4 collective-permute-start.25
  64.3 3.2 %collective-permute-done.22.refs_1_ = bf16[128,512]{1,0:T(8,128)(2,1)S(1)} collective-permute-done((bf16[128,512]{1,0:T(8,128)(2,1)S(1)}, bf16[128,512]{1,0:T(8,128)(2,1)S(1)}, u32[]{:S(2)}, u32[]{:S(2)}) %collective-permute-start.22) | collective-permute-done | bytes 131104 | tf_op jit(solution)/shard_map/ppermute | solution.py:40
  67.5 0.5 project_kv.6
  68.0 1.6 %collective-permute-done.27.refs_3_.refs_7_ = bf16[128,512]{1,0:T(8,128)(2,1)S(1)} collective-permute-done((bf16[128,512]{1,0:T(8,128)(2,1)S(1)}, bf16[128,512]{1,0:T(8,128)(2,1)S(1)}, u32[]{:S(2)}, u32[]{:S(2)}) %collective-permute-start.27) | collective-permute-done | bytes 131104 | tf_op jit(solution)/shard_map/ppermute | solution.py:40
  69.6 0.7 collective-permute-done.26.refs_2_.refs_6_
  70.3 2.4 %collective-permute-done.25.refs_1_.refs_5_ = bf16[128,512]{1,0:T(8,128)(2,1)S(1)} collective-permute-done((bf16[128,512]{1,0:T(8,128)(2,1)S(1)}, bf16[128,512]{1,0:T(8,128)(2,1)S(1)}, u32[]{:S(2)}, u32[]{:S(2)}) %collective-permute-start.25) | collective-permute-done | bytes 131104 | tf_op jit(solution)/shard_map/ppermute | solution.py:40
  72.7 0.6 project_kv.7
  73.3 1.5 %collective-permute-start.31 = (bf16[128,512]{1,0:T(8,128)(2,1)S(1)}, bf16[128,512]{1,0:T(8,128)(2,1)S(1)}, u32[]{:S(2)}, u32[]{:S(2)}) collective-permute-start(bf16[128,512]{1,0:T(8,128)(2,1)S(1)} %get-tuple-element.66.refs_0_), channel_id=1, source_target_pairs={{0,4},{1,5},{2,6},{3,7},{4,0},{5,1},{6,2},{7,3},{8,12},{9,13},{10,... | collective-permute-start | bytes 393224 | tf_op jit(solution)/shard_map/ppermute | solution.py:40
  74.8 1.1 collective-permute-start.30
  75.8 2.1 %collective-permute-start.29 = (bf16[128,512]{1,0:T(8,128)(2,1)S(1)}, bf16[128,512]{1,0:T(8,128)(2,1)S(1)}, u32[]{:S(2)}, u32[]{:S(2)}) collective-permute-start(bf16[128,512]{1,0:T(8,128)(2,1)S(1)} %get-tuple-element.66.refs_0_), channel_id=1, source_target_pairs={{0,16},{1,17},{2,18},{3,19},{4,20},{5,21},{6,22},{7,23},{8,24},{9,... | collective-permute-start | bytes 393224 | tf_op jit(solution)/shard_map/ppermute | solution.py:40
  77.9 1.1 %collective-permute-start.28 = (bf16[128,512]{1,0:T(8,128)(2,1)S(1)}, bf16[128,512]{1,0:T(8,128)(2,1)S(1)}, u32[]{:S(2)}, u32[]{:S(2)}) collective-permute-start(bf16[128,512]{1,0:T(8,128)(2,1)S(1)} %get-tuple-element.66.refs_0_), channel_id=1, source_target_pairs={{0,24},{1,25},{2,26},{3,27},{4,28},{5,29},{6,30},{7,31},{8,0},{9,1... | collective-permute-start | bytes 393224 | tf_op jit(solution)/shard_map/ppermute | solution.py:40
  79.0 1.4 %project_q.3.q = bf16[128,1024]{1,0:T(8,128)(2,1)S(1)} custom-call(bf16[128,512]{1,0:T(8,128)(2,1)S(1)} %collective-permute-done.20.refs_0_, bf16[128,512]{1,0:T(8,128)(2,1)S(1)} %collective-permute-done.22.refs_1_, bf16[128,512]{1,0:T(8,128)(2,1)S(1)} %collective-permute-done.23.refs_2_, bf16[128,512]{1,0:T(8,128)(2,1)S(1)} %collective-permute-done.24.refs_3_, ...), custom_call_target="tpu_custom_call" | custom-call | flops 5673741824 | bytes 9585152 | tf_op jit(solution)/shard_map/project_q/pallas_call | solution.py:47
  80.4 3.7 %collective-permute-done.28.refs_3_ = bf16[128,512]{1,0:T(8,128)(2,1)S(1)} collective-permute-done((bf16[128,512]{1,0:T(8,128)(2,1)S(1)}, bf16[128,512]{1,0:T(8,128)(2,1)S(1)}, u32[]{:S(2)}, u32[]{:S(2)}) %collective-permute-start.28) | collective-permute-done | bytes 131104 | tf_op jit(solution)/shard_map/ppermute | solution.py:40
  84.1 1.2 %collective-permute-start.34 = (bf16[128,512]{1,0:T(8,128)(2,1)S(1)}, bf16[128,512]{1,0:T(8,128)(2,1)S(1)}, u32[]{:S(2)}, u32[]{:S(2)}) collective-permute-start(bf16[128,512]{1,0:T(8,128)(2,1)S(1)} %collective-permute-done.28.refs_3_), channel_id=1, source_target_pairs={{0,4},{1,5},{2,6},{3,7},{4,0},{5,1},{6,2},{7,3},{8,12},{9,13},{10,... | collective-permute-start | bytes 393224 | tf_op jit(solution)/shard_map/ppermute | solution.py:40
  85.3 0.5 collective-permute-start.32
  85.9 0.8 collective-permute-done.33.refs_6_
  86.8 3.2 %attend_and_project.3 = (bf16[64,1024]{1,0:T(8,128)(2,1)S(1)}, bf16[64,1024]{1,0:T(8,128)(2,1)S(1)}, bf16[64,1024]{1,0:T(8,128)(2,1)S(1)}, bf16[64,1024]{1,0:T(8...) custom-call(bf16[128,1024]{1,0:T(8,128)(2,1)S(1)} %project_q.3.q, ...), custom_call_target="tpu_custom_call" | custom-call | flops 6076395008 | bytes 9701632 | tf_op jit(solution)/shard_map/attend_and_project/pallas_call | solution.py:47
  90.0 0.6 collective-permute-start.38
  90.9 2.4 %collective-permute-start.40 = (bf16[64,1024]{1,0:T(8,128)(2,1)S(1)}, bf16[64,1024]{1,0:T(8,128)(2,1)S(1)}, u32[]{:S(2)}, u32[]{:S(2)}) collective-permute-start(bf16[64,1024]{1,0:T(8,128)(2,1)S(1)} %get-tuple-element.75), channel_id=1, source_target_pairs={{0,3},{1,0},{2,1},{3,2},{4,7},{5,4},{6,5},{7,6},{8,11},{9,8},{10,9... | collective-permute-start | bytes 393224 | tf_op jit(solution)/shard_map/ppermute | solution.py:40
  93.3 1.3 %collective-permute-start.35 = (bf16[64,1024]{1,0:T(8,128)(2,1)S(1)}, bf16[64,1024]{1,0:T(8,128)(2,1)S(1)}, u32[]{:S(2)}, u32[]{:S(2)}) collective-permute-start(bf16[64,1024]{1,0:T(8,128)(2,1)S(1)} %get-tuple-element.69), channel_id=1, source_target_pairs={{0,2},{1,3},{2,0},{3,1},{4,6},{5,7},{6,4},{7,5},{8,10},{9,11},{10,... | collective-permute-start | bytes 393224 | tf_op jit(solution)/shard_map/ppermute | solution.py:40
  94.6 1.8 %collective-permute-done.38.refs_0_ = bf16[64,1024]{1,0:T(8,128)(2,1)S(1)} collective-permute-done((bf16[64,1024]{1,0:T(8,128)(2,1)S(1)}, bf16[64,1024]{1,0:T(8,128)(2,1)S(1)}, u32[]{:S(2)}, u32[]{:S(2)}) %collective-permute-start.38) | collective-permute-done | bytes 131104 | tf_op jit(solution)/shard_map/ppermute | solution.py:40
  96.3 0.9 collective-permute-start.37
  97.3 3.1 %collective-permute-done.39.refs_1_ = bf16[64,1024]{1,0:T(8,128)(2,1)S(1)} collective-permute-done((bf16[64,1024]{1,0:T(8,128)(2,1)S(1)}, bf16[64,1024]{1,0:T(8,128)(2,1)S(1)}, u32[]{:S(2)}, u32[]{:S(2)}) %collective-permute-start.39) | collective-permute-done | bytes 131104 | tf_op jit(solution)/shard_map/ppermute | solution.py:40
  100.6 1.4 %collective-permute-done.35.refs_0_ = bf16[64,1024]{1,0:T(8,128)(2,1)S(1)} collective-permute-done((bf16[64,1024]{1,0:T(8,128)(2,1)S(1)}, bf16[64,1024]{1,0:T(8,128)(2,1)S(1)}, u32[]{:S(2)}, u32[]{:S(2)}) %collective-permute-start.35) | collective-permute-done | bytes 131104 | tf_op jit(solution)/shard_map/ppermute | solution.py:40
  102.0 3.4 %collective-permute-done.36.refs_1_ = bf16[64,1024]{1,0:T(8,128)(2,1)S(1)} collective-permute-done((bf16[64,1024]{1,0:T(8,128)(2,1)S(1)}, bf16[64,1024]{1,0:T(8,128)(2,1)S(1)}, u32[]{:S(2)}, u32[]{:S(2)}) %collective-permute-start.36) | collective-permute-done | bytes 131104 | tf_op jit(solution)/shard_map/ppermute | solution.py:40
  105.4 0.8 finish.1
  (73 shorter events, 2.6 us)
Async XLA Ops:
  1.0 13.3 %copy-start.2 = (bf16[1,4096]{1,0:T(2,128)(2,1)S(1)}, bf16[1,4096]{1,0:T(2,128)(2,1)}, u32[]{:S(2)}) copy-start(bf16[1,4096]{1,0:T(2,128)(2,1)} %param.7) | copy-start | bytes 24580
  1.0 15.8 %copy-start = (bf16[1,4096,256]{2,1,0:T(8,128)(2,1)S(1)}, bf16[1,4096,256]{2,1,0:T(8,128)(2,1)}, u32[]{:S(2)}) copy-start(bf16[1,4096,256]{2,1,0:T(8,128)(2,1)} %refs_5_.7) | copy-start | bytes 6291460
  1.0 16.3 %collective-permute-start.5 = (bf16[64,1024]{1,0:T(8,128)(2,1)S(1)}, bf16[64,1024]{1,0:T(8,128)(2,1)S(1)}, u32[]{:S(2)}, u32[]{:S(2)}) collective-permute-start(bf16[64,1024]{1,0:T(8,128)(2,1)S(1)} %get-tuple-element.41.a), channel_id=1, source_target_pairs={{0,3},{1,0},{2,1},{3,2},{4,7},{5,4},{6,5},{7,6},{8,11},{9,8},{10,9... | collective-permute-start | bytes 393224 | tf_op jit(solution)/shard_map/ppermute | solution.py:40
  4.6 12.6 %collective-permute-start.3 = (bf16[64,1024]{1,0:T(8,128)(2,1)S(1)}, bf16[64,1024]{1,0:T(8,128)(2,1)S(1)}, u32[]{:S(2)}, u32[]{:S(2)}) collective-permute-start(bf16[64,1024]{1,0:T(8,128)(2,1)S(1)} %get-tuple-element.41.a), channel_id=1, source_target_pairs={{0,1},{1,2},{2,3},{3,0},{4,5},{5,6},{6,7},{7,4},{8,9},{9,10},{10,1... | collective-permute-start | bytes 393224 | tf_op jit(solution)/shard_map/ppermute | solution.py:40
  4.7 9.7 %collective-permute-start.1 = (bf16[64,1024]{1,0:T(8,128)(2,1)S(1)}, bf16[64,1024]{1,0:T(8,128)(2,1)S(1)}, u32[]{:S(2)}, u32[]{:S(2)}) collective-permute-start(bf16[64,1024]{1,0:T(8,128)(2,1)S(1)} %get-tuple-element.41.a), channel_id=1, source_target_pairs={{0,2},{1,3},{2,0},{3,1},{4,6},{5,7},{6,4},{7,5},{8,10},{9,11},{10,... | collective-permute-start | bytes 393224 | tf_op jit(solution)/shard_map/ppermute | solution.py:40
  6.3 4.1 %collective-permute-start = (bf16[64,1024]{1,0:T(8,128)(2,1)S(1)}, bf16[64,1024]{1,0:T(8,128)(2,1)S(1)}, u32[]{:S(2)}, u32[]{:S(2)}) collective-permute-start(bf16[64,1024]{1,0:T(8,128)(2,1)S(1)} %get-tuple-element.42), channel_id=1, source_target_pairs={{0,32},{1,33},{2,34},{3,35},{4,36},{5,37},{6,38},{7,39},{8,40},{9,... | collective-permute-start | bytes 393224 | tf_op jit(solution)/shard_map/ppermute | solution.py:40
  7.7 9.0 %copy-start.1 = (bf16[1,4096,256]{2,1,0:T(8,128)(2,1)S(1)}, bf16[1,4096,256]{2,1,0:T(8,128)(2,1)}, u32[]{:S(2)}) copy-start(bf16[1,4096,256]{2,1,0:T(8,128)(2,1)} %refs_6_.5) | copy-start | bytes 6291460
  10.4 6.9 %collective-permute-start.6 = (bf16[64,1024]{1,0:T(8,128)(2,1)S(1)}, bf16[64,1024]{1,0:T(8,128)(2,1)S(1)}, u32[]{:S(2)}, u32[]{:S(2)}) collective-permute-start(bf16[64,1024]{1,0:T(8,128)(2,1)S(1)} %collective-permute-done.b), channel_id=1, source_target_pairs={{0,3},{1,0},{2,1},{3,2},{4,7},{5,4},{6,5},{7,6},{8,11},{9,8},{10,9... | collective-permute-start | bytes 393224 | tf_op jit(solution)/shard_map/ppermute | solution.py:40
  11.4 5.3 %collective-permute-start.2 = (bf16[64,1024]{1,0:T(8,128)(2,1)S(1)}, bf16[64,1024]{1,0:T(8,128)(2,1)S(1)}, u32[]{:S(2)}, u32[]{:S(2)}) collective-permute-start(bf16[64,1024]{1,0:T(8,128)(2,1)S(1)} %collective-permute-done.b), channel_id=1, source_target_pairs={{0,2},{1,3},{2,0},{3,1},{4,6},{5,7},{6,4},{7,5},{8,10},{9,11},{10,... | collective-permute-start | bytes 393224 | tf_op jit(solution)/shard_map/ppermute | solution.py:40
  14.3 15.7 %slice-start.2 = ((s8[8388608]{0:T(1024)(128)(4,1)}), s8[4194304]{0:T(1024)(128)(4,1)S(1)}, s32[]{:S(2)}) async-start(s8[8388608]{0:T(1024)(128)(4,1)} %bitcast.5), calls=%async_computation.2 | async-start | bytes 8388608
  14.4 15.6 %slice-start.3 = ((s8[8388608]{0:T(1024)(128)(4,1)}), s8[4194304]{0:T(1024)(128)(4,1)S(1)}, s32[]{:S(2)}) async-start(s8[8388608]{0:T(1024)(128)(4,1)} %bitcast.5), calls=%async_computation.3 | async-start | bytes 8388608
  14.4 6.5 %collective-permute-start.4 = (bf16[64,1024]{1,0:T(8,128)(2,1)S(1)}, bf16[64,1024]{1,0:T(8,128)(2,1)S(1)}, u32[]{:S(2)}, u32[]{:S(2)}) collective-permute-start(bf16[64,1024]{1,0:T(8,128)(2,1)S(1)} %collective-permute-done.b), channel_id=1, source_target_pairs={{0,1},{1,2},{2,3},{3,0},{4,5},{5,6},{6,7},{7,4},{8,9},{9,10},{10,1... | collective-permute-start | bytes 393224 | tf_op jit(solution)/shard_map/ppermute | solution.py:40
  20.9 16.9 %slice-start = ((s8[8388608]{0:T(1024)(128)(4,1)}), s8[4194304]{0:T(1024)(128)(4,1)S(1)}, s32[]{:S(2)}) async-start(s8[8388608]{0:T(1024)(128)(4,1)} %bitcast.1), calls=%async_computation | async-start | bytes 8388608
  21.5 15.0 %collective-permute-start.10 = (bf16[128,512]{1,0:T(8,128)(2,1)S(1)}, bf16[128,512]{1,0:T(8,128)(2,1)S(1)}, u32[]{:S(2)}, u32[]{:S(2)}) collective-permute-start(bf16[128,512]{1,0:T(8,128)(2,1)S(1)} %get-tuple-element.49.refs_0_), channel_id=1, source_target_pairs={{0,4},{1,5},{2,6},{3,7},{4,0},{5,1},{6,2},{7,3},{8,12},{9,13},{10,... | collective-permute-start | bytes 393224 | tf_op jit(solution)/shard_map/ppermute | solution.py:40
  24.3 10.6 %collective-permute-start.9 = (bf16[128,512]{1,0:T(8,128)(2,1)S(1)}, bf16[128,512]{1,0:T(8,128)(2,1)S(1)}, u32[]{:S(2)}, u32[]{:S(2)}) collective-permute-start(bf16[128,512]{1,0:T(8,128)(2,1)S(1)} %get-tuple-element.49.refs_0_), channel_id=1, source_target_pairs={{0,8},{1,9},{2,10},{3,11},{4,12},{5,13},{6,14},{7,15},{8,16},{9,17... | collective-permute-start | bytes 393224 | tf_op jit(solution)/shard_map/ppermute | solution.py:40
  25.9 9.9 %collective-permute-start.8 = (bf16[128,512]{1,0:T(8,128)(2,1)S(1)}, bf16[128,512]{1,0:T(8,128)(2,1)S(1)}, u32[]{:S(2)}, u32[]{:S(2)}) collective-permute-start(bf16[128,512]{1,0:T(8,128)(2,1)S(1)} %get-tuple-element.49.refs_0_), channel_id=1, source_target_pairs={{0,16},{1,17},{2,18},{3,19},{4,20},{5,21},{6,22},{7,23},{8,24},{9,... | collective-permute-start | bytes 393224 | tf_op jit(solution)/shard_map/ppermute | solution.py:40
  29.2 5.7 %collective-permute-start.7 = (bf16[128,512]{1,0:T(8,128)(2,1)S(1)}, bf16[128,512]{1,0:T(8,128)(2,1)S(1)}, u32[]{:S(2)}, u32[]{:S(2)}) collective-permute-start(bf16[128,512]{1,0:T(8,128)(2,1)S(1)} %get-tuple-element.49.refs_0_), channel_id=1, source_target_pairs={{0,24},{1,25},{2,26},{3,27},{4,28},{5,29},{6,30},{7,31},{8,0},{9,1... | collective-permute-start | bytes 393224 | tf_op jit(solution)/shard_map/ppermute | solution.py:40
  30.0 7.9 %slice-start.1 = ((s8[8388608]{0:T(1024)(128)(4,1)}), s8[4194304]{0:T(1024)(128)(4,1)S(1)}, s32[]{:S(2)}) async-start(s8[8388608]{0:T(1024)(128)(4,1)} %bitcast.1), calls=%async_computation.1 | async-start | bytes 8388608
  34.9 2.0 %collective-permute-start.12 = (bf16[128,512]{1,0:T(8,128)(2,1)S(1)}, bf16[128,512]{1,0:T(8,128)(2,1)S(1)}, u32[]{:S(2)}, u32[]{:S(2)}) collective-permute-start(bf16[128,512]{1,0:T(8,128)(2,1)S(1)} %collective-permute-done.9.refs_2_), channel_id=1, source_target_pairs={{0,4},{1,5},{2,6},{3,7},{4,0},{5,1},{6,2},{7,3},{8,12},{9,13},{10,... | collective-permute-start | bytes 393224 | tf_op jit(solution)/shard_map/ppermute | solution.py:40
  35.9 1.6 %collective-permute-start.11 = (bf16[128,512]{1,0:T(8,128)(2,1)S(1)}, bf16[128,512]{1,0:T(8,128)(2,1)S(1)}, u32[]{:S(2)}, u32[]{:S(2)}) collective-permute-start(bf16[128,512]{1,0:T(8,128)(2,1)S(1)} %collective-permute-done.8.refs_1_), channel_id=1, source_target_pairs={{0,4},{1,5},{2,6},{3,7},{4,0},{5,1},{6,2},{7,3},{8,12},{9,13},{10,... | collective-permute-start | bytes 393224 | tf_op jit(solution)/shard_map/ppermute | solution.py:40
  36.5 1.3 %collective-permute-start.13 = (bf16[128,512]{1,0:T(8,128)(2,1)S(1)}, bf16[128,512]{1,0:T(8,128)(2,1)S(1)}, u32[]{:S(2)}, u32[]{:S(2)}) collective-permute-start(bf16[128,512]{1,0:T(8,128)(2,1)S(1)} %collective-permute-done.7.refs_3_), channel_id=1, source_target_pairs={{0,4},{1,5},{2,6},{3,7},{4,0},{5,1},{6,2},{7,3},{8,12},{9,13},{10,... | collective-permute-start | bytes 393224 | tf_op jit(solution)/shard_map/ppermute | solution.py:40
  40.3 6.5 %collective-permute-start.14 = (bf16[128,512]{1,0:T(8,128)(2,1)S(1)}, bf16[128,512]{1,0:T(8,128)(2,1)S(1)}, u32[]{:S(2)}, u32[]{:S(2)}) collective-permute-start(bf16[128,512]{1,0:T(8,128)(2,1)S(1)} %get-tuple-element.54), channel_id=1, source_target_pairs={{0,2},{1,3},{2,0},{3,1},{4,6},{5,7},{6,4},{7,5},{8,10},{9,11},{10,... | collective-permute-start | bytes 393224 | tf_op jit(solution)/shard_map/ppermute | solution.py:40
  40.9 9.7 %collective-permute-start.15 = (bf16[128,512]{1,0:T(8,128)(2,1)S(1)}, bf16[128,512]{1,0:T(8,128)(2,1)S(1)}, u32[]{:S(2)}, u32[]{:S(2)}) collective-permute-start(bf16[128,512]{1,0:T(8,128)(2,1)S(1)} %get-tuple-element.55), channel_id=1, source_target_pairs={{0,1},{1,2},{2,3},{3,0},{4,5},{5,6},{6,7},{7,4},{8,9},{9,10},{10,1... | collective-permute-start | bytes 393224 | tf_op jit(solution)/shard_map/ppermute | solution.py:40
  40.9 9.7 %collective-permute-start.16 = (bf16[128,512]{1,0:T(8,128)(2,1)S(1)}, bf16[128,512]{1,0:T(8,128)(2,1)S(1)}, u32[]{:S(2)}, u32[]{:S(2)}) collective-permute-start(bf16[128,512]{1,0:T(8,128)(2,1)S(1)} %get-tuple-element.56), channel_id=1, source_target_pairs={{0,3},{1,0},{2,1},{3,2},{4,7},{5,4},{6,5},{7,6},{8,11},{9,8},{10,9... | collective-permute-start | bytes 393224 | tf_op jit(solution)/shard_map/ppermute | solution.py:40
  44.5 8.9 %collective-permute-start.17 = (bf16[128,512]{1,0:T(8,128)(2,1)S(1)}, bf16[128,512]{1,0:T(8,128)(2,1)S(1)}, u32[]{:S(2)}, u32[]{:S(2)}) collective-permute-start(bf16[128,512]{1,0:T(8,128)(2,1)S(1)} %get-tuple-element.59), channel_id=1, source_target_pairs={{0,2},{1,3},{2,0},{3,1},{4,6},{5,7},{6,4},{7,5},{8,10},{9,11},{10,... | collective-permute-start | bytes 393224 | tf_op jit(solution)/shard_map/ppermute | solution.py:40
  45.8 9.9 %collective-permute-start.18 = (bf16[128,512]{1,0:T(8,128)(2,1)S(1)}, bf16[128,512]{1,0:T(8,128)(2,1)S(1)}, u32[]{:S(2)}, u32[]{:S(2)}) collective-permute-start(bf16[128,512]{1,0:T(8,128)(2,1)S(1)} %get-tuple-element.60), channel_id=1, source_target_pairs={{0,1},{1,2},{2,3},{3,0},{4,5},{5,6},{6,7},{7,4},{8,9},{9,10},{10,1... | collective-permute-start | bytes 393224 | tf_op jit(solution)/shard_map/ppermute | solution.py:40
  46.9 8.8 %collective-permute-start.19 = (bf16[128,512]{1,0:T(8,128)(2,1)S(1)}, bf16[128,512]{1,0:T(8,128)(2,1)S(1)}, u32[]{:S(2)}, u32[]{:S(2)}) collective-permute-start(bf16[128,512]{1,0:T(8,128)(2,1)S(1)} %get-tuple-element.61), channel_id=1, source_target_pairs={{0,3},{1,0},{2,1},{3,2},{4,7},{5,4},{6,5},{7,6},{8,11},{9,8},{10,9... | collective-permute-start | bytes 393224 | tf_op jit(solution)/shard_map/ppermute | solution.py:40
  50.7 7.6 %collective-permute-start.20 = (bf16[128,512]{1,0:T(8,128)(2,1)S(1)}, bf16[128,512]{1,0:T(8,128)(2,1)S(1)}, u32[]{:S(2)}, u32[]{:S(2)}) collective-permute-start(bf16[128,512]{1,0:T(8,128)(2,1)S(1)} %add_parts.2), channel_id=1, source_target_pairs={{0,96},{1,97},{2,98},{3,99},{4,100},{5,101},{6,102},{7,103},{8,104... | collective-permute-start | bytes 393224 | tf_op jit(solution)/shard_map/ppermute | solution.py:40
  55.7 5.7 %collective-permute-start.21 = (bf16[128,512]{1,0:T(8,128)(2,1)S(1)}, bf16[128,512]{1,0:T(8,128)(2,1)S(1)}, u32[]{:S(2)}, u32[]{:S(2)}) collective-permute-start(bf16[128,512]{1,0:T(8,128)(2,1)S(1)} %add_parts.3), channel_id=1, source_target_pairs={{0,96},{1,97},{2,98},{3,99},{4,100},{5,101},{6,102},{7,103},{8,104... | collective-permute-start | bytes 393224 | tf_op jit(solution)/shard_map/ppermute | solution.py:40
  58.3 5.6 %collective-permute-start.24 = (bf16[128,512]{1,0:T(8,128)(2,1)S(1)}, bf16[128,512]{1,0:T(8,128)(2,1)S(1)}, u32[]{:S(2)}, u32[]{:S(2)}) collective-permute-start(bf16[128,512]{1,0:T(8,128)(2,1)S(1)} %collective-permute-done.20.refs_0_), channel_id=1, source_target_pairs={{0,2},{1,3},{2,0},{3,1},{4,6},{5,7},{6,4},{7,5},{8,10},{9,11},{10,... | collective-permute-start | bytes 393224 | tf_op jit(solution)/shard_map/ppermute | solution.py:40
  58.9 5.4 %collective-permute-start.23 = (bf16[128,512]{1,0:T(8,128)(2,1)S(1)}, bf16[128,512]{1,0:T(8,128)(2,1)S(1)}, u32[]{:S(2)}, u32[]{:S(2)}) collective-permute-start(bf16[128,512]{1,0:T(8,128)(2,1)S(1)} %collective-permute-done.20.refs_0_), channel_id=1, source_target_pairs={{0,3},{1,0},{2,1},{3,2},{4,7},{5,4},{6,5},{7,6},{8,11},{9,8},{10,9... | collective-permute-start | bytes 393224 | tf_op jit(solution)/shard_map/ppermute | solution.py:40
  60.0 7.5 %collective-permute-start.22 = (bf16[128,512]{1,0:T(8,128)(2,1)S(1)}, bf16[128,512]{1,0:T(8,128)(2,1)S(1)}, u32[]{:S(2)}, u32[]{:S(2)}) collective-permute-start(bf16[128,512]{1,0:T(8,128)(2,1)S(1)} %collective-permute-done.20.refs_0_), channel_id=1, source_target_pairs={{0,1},{1,2},{2,3},{3,0},{4,5},{5,6},{6,7},{7,4},{8,9},{9,10},{10,1... | collective-permute-start | bytes 393224 | tf_op jit(solution)/shard_map/ppermute | solution.py:40
  61.5 8.1 %collective-permute-start.27 = (bf16[128,512]{1,0:T(8,128)(2,1)S(1)}, bf16[128,512]{1,0:T(8,128)(2,1)S(1)}, u32[]{:S(2)}, u32[]{:S(2)}) collective-permute-start(bf16[128,512]{1,0:T(8,128)(2,1)S(1)} %collective-permute-done.21.refs_0_.refs_4_), channel_id=1, source_target_pairs={{0,2},{1,3},{2,0},{3,1},{4,6},{5,7},{6,4},{7,5},{8,10},{9,11},{10,... | collective-permute-start | bytes 393224 | tf_op jit(solution)/shard_map/ppermute | solution.py:40
  62.8 7.5 %collective-permute-start.26 = (bf16[128,512]{1,0:T(8,128)(2,1)S(1)}, bf16[128,512]{1,0:T(8,128)(2,1)S(1)}, u32[]{:S(2)}, u32[]{:S(2)}) collective-permute-start(bf16[128,512]{1,0:T(8,128)(2,1)S(1)} %collective-permute-done.21.refs_0_.refs_4_), channel_id=1, source_target_pairs={{0,3},{1,0},{2,1},{3,2},{4,7},{5,4},{6,5},{7,6},{8,11},{9,8},{10,9... | collective-permute-start | bytes 393224 | tf_op jit(solution)/shard_map/ppermute | solution.py:40
  63.9 8.8 %collective-permute-start.25 = (bf16[128,512]{1,0:T(8,128)(2,1)S(1)}, bf16[128,512]{1,0:T(8,128)(2,1)S(1)}, u32[]{:S(2)}, u32[]{:S(2)}) collective-permute-start(bf16[128,512]{1,0:T(8,128)(2,1)S(1)} %collective-permute-done.21.refs_0_.refs_4_), channel_id=1, source_target_pairs={{0,1},{1,2},{2,3},{3,0},{4,5},{5,6},{6,7},{7,4},{8,9},{9,10},{10,1... | collective-permute-start | bytes 393224 | tf_op jit(solution)/shard_map/ppermute | solution.py:40
  73.3 12.5 %collective-permute-start.31 = (bf16[128,512]{1,0:T(8,128)(2,1)S(1)}, bf16[128,512]{1,0:T(8,128)(2,1)S(1)}, u32[]{:S(2)}, u32[]{:S(2)}) collective-permute-start(bf16[128,512]{1,0:T(8,128)(2,1)S(1)} %get-tuple-element.66.refs_0_), channel_id=1, source_target_pairs={{0,4},{1,5},{2,6},{3,7},{4,0},{5,1},{6,2},{7,3},{8,12},{9,13},{10,... | collective-permute-start | bytes 393224 | tf_op jit(solution)/shard_map/ppermute | solution.py:40
  74.8 10.5 %collective-permute-start.30 = (bf16[128,512]{1,0:T(8,128)(2,1)S(1)}, bf16[128,512]{1,0:T(8,128)(2,1)S(1)}, u32[]{:S(2)}, u32[]{:S(2)}) collective-permute-start(bf16[128,512]{1,0:T(8,128)(2,1)S(1)} %get-tuple-element.66.refs_0_), channel_id=1, source_target_pairs={{0,8},{1,9},{2,10},{3,11},{4,12},{5,13},{6,14},{7,15},{8,16},{9,17... | collective-permute-start | bytes 393224 | tf_op jit(solution)/shard_map/ppermute | solution.py:40
  75.8 9.5 %collective-permute-start.29 = (bf16[128,512]{1,0:T(8,128)(2,1)S(1)}, bf16[128,512]{1,0:T(8,128)(2,1)S(1)}, u32[]{:S(2)}, u32[]{:S(2)}) collective-permute-start(bf16[128,512]{1,0:T(8,128)(2,1)S(1)} %get-tuple-element.66.refs_0_), channel_id=1, source_target_pairs={{0,16},{1,17},{2,18},{3,19},{4,20},{5,21},{6,22},{7,23},{8,24},{9,... | collective-permute-start | bytes 393224 | tf_op jit(solution)/shard_map/ppermute | solution.py:40
  77.9 6.2 %collective-permute-start.28 = (bf16[128,512]{1,0:T(8,128)(2,1)S(1)}, bf16[128,512]{1,0:T(8,128)(2,1)S(1)}, u32[]{:S(2)}, u32[]{:S(2)}) collective-permute-start(bf16[128,512]{1,0:T(8,128)(2,1)S(1)} %get-tuple-element.66.refs_0_), channel_id=1, source_target_pairs={{0,24},{1,25},{2,26},{3,27},{4,28},{5,29},{6,30},{7,31},{8,0},{9,1... | collective-permute-start | bytes 393224 | tf_op jit(solution)/shard_map/ppermute | solution.py:40
  84.1 2.7 %collective-permute-start.34 = (bf16[128,512]{1,0:T(8,128)(2,1)S(1)}, bf16[128,512]{1,0:T(8,128)(2,1)S(1)}, u32[]{:S(2)}, u32[]{:S(2)}) collective-permute-start(bf16[128,512]{1,0:T(8,128)(2,1)S(1)} %collective-permute-done.28.refs_3_), channel_id=1, source_target_pairs={{0,4},{1,5},{2,6},{3,7},{4,0},{5,1},{6,2},{7,3},{8,12},{9,13},{10,... | collective-permute-start | bytes 393224 | tf_op jit(solution)/shard_map/ppermute | solution.py:40
  85.3 1.3 %collective-permute-start.33 = (bf16[128,512]{1,0:T(8,128)(2,1)S(1)}, bf16[128,512]{1,0:T(8,128)(2,1)S(1)}, u32[]{:S(2)}, u32[]{:S(2)}) collective-permute-start(bf16[128,512]{1,0:T(8,128)(2,1)S(1)} %collective-permute-done.30.refs_2_), channel_id=1, source_target_pairs={{0,4},{1,5},{2,6},{3,7},{4,0},{5,1},{6,2},{7,3},{8,12},{9,13},{10,... | collective-permute-start | bytes 393224 | tf_op jit(solution)/shard_map/ppermute | solution.py:40
  85.3 1.5 %collective-permute-start.32 = (bf16[128,512]{1,0:T(8,128)(2,1)S(1)}, bf16[128,512]{1,0:T(8,128)(2,1)S(1)}, u32[]{:S(2)}, u32[]{:S(2)}) collective-permute-start(bf16[128,512]{1,0:T(8,128)(2,1)S(1)} %collective-permute-done.29.refs_1_), channel_id=1, source_target_pairs={{0,4},{1,5},{2,6},{3,7},{4,0},{5,1},{6,2},{7,3},{8,12},{9,13},{10,... | collective-permute-start | bytes 393224 | tf_op jit(solution)/shard_map/ppermute | solution.py:40
  90.0 6.3 %collective-permute-start.38 = (bf16[64,1024]{1,0:T(8,128)(2,1)S(1)}, bf16[64,1024]{1,0:T(8,128)(2,1)S(1)}, u32[]{:S(2)}, u32[]{:S(2)}) collective-permute-start(bf16[64,1024]{1,0:T(8,128)(2,1)S(1)} %get-tuple-element.73), channel_id=1, source_target_pairs={{0,2},{1,3},{2,0},{3,1},{4,6},{5,7},{6,4},{7,5},{8,10},{9,11},{10,... | collective-permute-start | bytes 393224 | tf_op jit(solution)/shard_map/ppermute | solution.py:40
  90.6 9.8 %collective-permute-start.39 = (bf16[64,1024]{1,0:T(8,128)(2,1)S(1)}, bf16[64,1024]{1,0:T(8,128)(2,1)S(1)}, u32[]{:S(2)}, u32[]{:S(2)}) collective-permute-start(bf16[64,1024]{1,0:T(8,128)(2,1)S(1)} %get-tuple-element.74), channel_id=1, source_target_pairs={{0,1},{1,2},{2,3},{3,0},{4,5},{5,6},{6,7},{7,4},{8,9},{9,10},{10,1... | collective-permute-start | bytes 393224 | tf_op jit(solution)/shard_map/ppermute | solution.py:40
  90.9 9.5 %collective-permute-start.40 = (bf16[64,1024]{1,0:T(8,128)(2,1)S(1)}, bf16[64,1024]{1,0:T(8,128)(2,1)S(1)}, u32[]{:S(2)}, u32[]{:S(2)}) collective-permute-start(bf16[64,1024]{1,0:T(8,128)(2,1)S(1)} %get-tuple-element.75), channel_id=1, source_target_pairs={{0,3},{1,0},{2,1},{3,2},{4,7},{5,4},{6,5},{7,6},{8,11},{9,8},{10,9... | collective-permute-start | bytes 393224 | tf_op jit(solution)/shard_map/ppermute | solution.py:40
  93.3 8.7 %collective-permute-start.35 = (bf16[64,1024]{1,0:T(8,128)(2,1)S(1)}, bf16[64,1024]{1,0:T(8,128)(2,1)S(1)}, u32[]{:S(2)}, u32[]{:S(2)}) collective-permute-start(bf16[64,1024]{1,0:T(8,128)(2,1)S(1)} %get-tuple-element.69), channel_id=1, source_target_pairs={{0,2},{1,3},{2,0},{3,1},{4,6},{5,7},{6,4},{7,5},{8,10},{9,11},{10,... | collective-permute-start | bytes 393224 | tf_op jit(solution)/shard_map/ppermute | solution.py:40
  94.6 10.8 %collective-permute-start.36 = (bf16[64,1024]{1,0:T(8,128)(2,1)S(1)}, bf16[64,1024]{1,0:T(8,128)(2,1)S(1)}, u32[]{:S(2)}, u32[]{:S(2)}) collective-permute-start(bf16[64,1024]{1,0:T(8,128)(2,1)S(1)} %get-tuple-element.70), channel_id=1, source_target_pairs={{0,1},{1,2},{2,3},{3,0},{4,5},{5,6},{6,7},{7,4},{8,9},{9,10},{10,1... | collective-permute-start | bytes 393224 | tf_op jit(solution)/shard_map/ppermute | solution.py:40
  96.3 9.1 %collective-permute-start.37 = (bf16[64,1024]{1,0:T(8,128)(2,1)S(1)}, bf16[64,1024]{1,0:T(8,128)(2,1)S(1)}, u32[]{:S(2)}, u32[]{:S(2)}) collective-permute-start(bf16[64,1024]{1,0:T(8,128)(2,1)S(1)} %get-tuple-element.71), channel_id=1, source_target_pairs={{0,3},{1,0},{2,1},{3,2},{4,7},{5,4},{6,5},{7,6},{8,11},{9,8},{10,9... | collective-permute-start | bytes 393224 | tf_op jit(solution)/shard_map/ppermute | solution.py:40
  100.5 4.9 %collective-permute-start.41 = (bf16[64,1024]{1,0:T(8,128)(2,1)S(1)}, bf16[64,1024]{1,0:T(8,128)(2,1)S(1)}, u32[]{:S(2)}, u32[]{:S(2)}) collective-permute-start(bf16[64,1024]{1,0:T(8,128)(2,1)S(1)} %last_cross.1), channel_id=1, source_target_pairs={{0,32},{1,33},{2,34},{3,35},{4,36},{5,37},{6,38},{7,39},{8,40},{9,... | collective-permute-start | bytes 393224 | tf_op jit(solution)/shard_map/ppermute | solution.py:40

commit v6 on v5

--- a/solution.py
+++ b/solution.py
@@ -13,9 +13,9 @@
 SMALL = 10 * 1024 * 1024
 SHIFTS = (2, 1, 3, 0)
 ORDER = (0, 1, 3, 2)
-Z_ORDER = (2, 1, 3)
+Z_ORDER = (3, 2, 1)
 FLOPS_PER_US = 1_150_000_000
-BESIDE_X0 = 3
+BESIDE_GAIN = 3
 BESIDE_FIRST, BESIDE_KV, BESIDE_Q, BESIDE_MIX = 5, 2, 4, 4
 DIAG = False
 AXES = ("section", "ctx", "tp")
@@ -73,14 +73,18 @@
 
 
 def flat_pieces(pieces):
-    return [r for _, _, rows_of in pieces for r in rows_of]
+    most = max(len(rows_of) for _, _, rows_of in pieces)
+    return [rows_of[n] for n in range(most) for _, _, rows_of in pieces if n < len(rows_of)]
 
 
 def regroup(refs, pieces):
-    out, at = [], 0
-    for _, _, rows_of in pieces:
-        out.append(refs[at : at + len(rows_of)])
-        at += len(rows_of)
+    out = [[] for _ in pieces]
+    at = 0
+    for n in range(max(len(rows_of) for _, _, rows_of in pieces)):
+        for j, (_, _, rows_of) in enumerate(pieces):
+            if n < len(rows_of):
+                out[j].append(refs[at])
+                at += 1
     return out, refs[at:]
 
 
@@ -118,7 +122,16 @@
         out[rows:] = b[...]
 
     return in_vmem(
-        body, [upper, lower], [((2 * rows, width), upper.dtype)], "stacked", beside=BESIDE_X0
+        body, [upper, lower], [((2 * rows, width), upper.dtype)], "stacked"
+    )[0]
+
+
+def widened(gain):
+    def body(g, out):
+        out[...] = g[...].astype(jnp.float32)
+
+    return in_vmem(
+        body, [gain], [(gain.shape, jnp.float32)], "widened", beside=BESIDE_GAIN
     )[0]
 
 
@@ -315,42 +328,40 @@
 def add_parts(x, at, parts):
     rows, width = parts[0].shape
 
-    def body(x_ref, *refs):
-        *refs, out = refs
+    def body(*refs):
+        *refs, x_ref, out = refs
         x = x_ref[:, at : at + width].astype(jnp.float32)
         out[...] = (x + total_of(refs)).astype(jnp.bfloat16)
 
-    return in_vmem(body, [x, *parts], [((rows, width), jnp.bfloat16)], "add_parts")[0]
+    return in_vmem(body, [*parts, x], [((rows, width), jnp.bfloat16)], "add_parts")[0]
 
 
 def last_cross(kept, x, parts):
-    n = len(parts)
-
-    def body(kept_ref, x_ref, *refs):
+    def body(*refs):
+        *refs, kept_ref, x_ref, out = refs
         section = lax.axis_index("section")
-        total = x_ref[...].astype(jnp.float32) + total_of(refs[:n])
-        refs[n][...] = jnp.where(section == 0, kept_ref[...], total.astype(jnp.bfloat16))
-
-    return in_vmem(body, [kept, x, *parts], [(x.shape, jnp.bfloat16)], "last_cross")[0]
+        total = x_ref[...].astype(jnp.float32) + total_of(refs)
+        out[...] = jnp.where(section == 0, kept_ref[...], total.astype(jnp.bfloat16))
+
+    return in_vmem(body, [*parts, kept, x], [(x.shape, jnp.bfloat16)], "last_cross")[0]
 
 
 def finish(kept, x, parts, cross):
     half, width = x.shape
-    n = len(parts)
     n_half = lax.axis_size("ctx") // 2
 
-    def body(kept_ref, x_ref, *refs):
+    def body(*refs):
+        *refs, cross_ref, kept_ref, x_ref, out = refs
         section = lax.axis_index("section")
         x_lo = lax.axis_index("ctx") // n_half
-        total = x_ref[...].astype(jnp.float32) + total_of(refs[:n])
+        total = x_ref[...].astype(jnp.float32) + total_of(refs)
         own = jnp.where(section == 0, kept_ref[...], total.astype(jnp.bfloat16))
-        cross_ref, out = refs[n:]
         own_first = x_lo == section
         out[0, 0] = jnp.where(own_first, own, cross_ref[...])
         out[0, 1] = jnp.where(own_first, cross_ref[...], own)
 
     return in_vmem(
-        body, [kept, x, *parts, cross], [((1, 2, half, width), jnp.bfloat16)], "finish"
+        body, [*parts, cross, kept, x], [((1, 2, half, width), jnp.bfloat16)], "finish"
     )[0]
 
 
@@ -397,12 +408,12 @@
 
 
     def mix(kv, make_q, w_out, width, layer, parts):
-        theirs = [send(kv, other_core=True)]
-        sent = {s: send(kv, by_z=s) for s in (3, 1, 2)}
-        q, early = lax.optimization_barrier((make_q(), sent[Z_ORDER[-1]]))
-        sent[Z_ORDER[-1]] = early
+        theirs = send(kv, other_core=True)
+        sent = {s: send(kv, by_z=s) for s in Z_ORDER}
+        first = Z_ORDER[0]
+        q, theirs, sent[first] = lax.optimization_barrier((make_q(), theirs, sent[first]))
         mine = [sent[s] for s in Z_ORDER]
-        theirs += [send(block, other_core=True) for block in mine]
+        theirs = [theirs] + [send(block, other_core=True) for block in mine]
         blocks = [kv, *mine, *theirs]
         return attend_and_project(q, qpos, kpos, blocks, w_out, width, layer, parts)
 
@@ -412,12 +423,11 @@
     positions_of, gain, qpos, kpos, other = lax.optimization_barrier(
         (positions_of, norm_gain, qpos, kpos, other)
     )
-    gain = gain.astype(jnp.float32)
+    gain = widened(gain)
     rope = tables(positions_of)
     other_from = {s: send(other, by_tp=s) for s in (3, 1, 2)}
     own_from[0], other_from[0] = own, other
-    x0 = stacked(own, other)
-    pieces = [(s, 0, [x0] if s == 0 else [own_from[s], other_from[s]]) for s in (0, 2, 1, 3)]
+    pieces = [(s, 0, [own_from[s], other_from[s]]) for s in (1, 3, 0, 2)]
     carry = project_kv(pieces[:2], width, gain, wk, wv, None, None)
     kv, r = project_kv(pieces[2:], width, gain, wk, wv, carry, rope)
     chunked = [[(c * chunk, s, 0, 2 * half) for s in SHIFTS] for c in range(CHUNKS)]
@@ -430,6 +440,7 @@
         chunked[0],
     )
     got += project_out(attended, w_out, chunk, sum(chunked[1:], []))
+    x0 = stacked(own, other)
     sums = []
     for c in range(CHUNKS):
         parts = []

time: 106 us -> 103 us (0.972)
  waiting for transfers between devices: 42.9 us -> 31.1 us
  starting transfers between devices: 48.6 us -> 57.1 us
    ppermute x42, waiting for transfers between devices: 42.9 us -> 31.1 us  [send(): return lax.ppermute(block, AXES, route)]
    ppermute x42, starting transfers between devices: 48.6 us -> 57.1 us  [send(): return lax.ppermute(block, AXES, route)]
    pallas_call x15 -> x16, Pallas kernels: 13.4 us -> 13.4 us  [in_vmem(): pl.pallas_call(kernel, in_specs=specs, out_specs=[pl.BlockSpec(memory_spa...]
  transfers between devices with their start and end apart: 42 -> 42, of which waited for: 23 -> 23; matrix products, arithmetic and copies ran while one was open for 1% -> 1% of each run, Pallas kernels for 4% -> 5%
where the time goes in v6:
time: 103 us
  starting transfers between devices  57.1 us (55%)
  waiting for transfers between devices  31.1 us (30%)
  Pallas kernels  13.4 us (13%)
    ppermute x42, starting transfers between devices, send(): return lax.ppermute(block, AXES, route)  57.1 us
    ppermute x42, waiting for transfers between devices, send(): return lax.ppermute(block, AXES, route)  31.1 us
    pallas_call x16, Pallas kernels, in_vmem(): pl.pallas_call(kernel, in_specs=specs, out_specs=[pl.BlockSpec(memory_spa...  13.4 us
  transfers between devices with their start and end apart: 42, of which 23 were waited for; matrix products, arithmetic and copies ran while one was open for 1% of the time, Pallas kernels for 5%

profile of v6, /device:TPU:1, one launch (start us, length us, event | category | flops | bytes accessed | tf_op | source)
XLA Modules:
  0.0 102.9 jit_solution(15077757985115222600)
XLA Ops:
  0.0 1.0 rows_of_segments.1
  1.0 3.8 %collective-permute-start.2 = (bf16[64,1024]{1,0:T(8,128)(2,1)S(1)}, bf16[64,1024]{1,0:T(8,128)(2,1)S(1)}, u32[]{:S(2)}, u32[]{:S(2)}) collective-permute-start(bf16[64,1024]{1,0:T(8,128)(2,1)S(1)} %get-tuple-element.43.refs_0_.refs_2_.a), channel_id=1, source_target_pairs={{0,2},{1,3},{2,0},{3,1},{4,6},{5,7},{6,4},{7,5},{8,10},{9,11},{10,... | collective-permute-start | bytes 393224 | tf_op jit(solution)/shard_map/ppermute | solution.py:40
  4.8 0.8 collective-permute-start.1
  5.6 0.7 collective-permute-start
  6.3 1.2 %collective-permute-start.3 = (bf16[64,1024]{1,0:T(8,128)(2,1)S(1)}, bf16[64,1024]{1,0:T(8,128)(2,1)S(1)}, u32[]{:S(2)}, u32[]{:S(2)}) collective-permute-start(bf16[64,1024]{1,0:T(8,128)(2,1)S(1)} %get-tuple-element.44), channel_id=1, source_target_pairs={{0,32},{1,33},{2,34},{3,35},{4,36},{5,37},{6,38},{7,39},{8,40},{9,... | collective-permute-start | bytes 393224 | tf_op jit(solution)/shard_map/ppermute | solution.py:40
  7.8 2.4 %collective-permute-done.3.refs_2_.refs_6_.b = bf16[64,1024]{1,0:T(8,128)(2,1)S(1)} collective-permute-done((bf16[64,1024]{1,0:T(8,128)(2,1)S(1)}, bf16[64,1024]{1,0:T(8,128)(2,1)S(1)}, u32[]{:S(2)}, u32[]{:S(2)}) %collective-permute-start.3) | collective-permute-done | bytes 131104 | tf_op jit(solution)/shard_map/ppermute | solution.py:40
  10.1 2.3 %collective-permute-start.5 = (bf16[64,1024]{1,0:T(8,128)(2,1)S(1)}, bf16[64,1024]{1,0:T(8,128)(2,1)S(1)}, u32[]{:S(2)}, u32[]{:S(2)}) collective-permute-start(bf16[64,1024]{1,0:T(8,128)(2,1)S(1)} %collective-permute-done.3.refs_2_.refs_6_.b), channel_id=1, source_target_pairs={{0,3},{1,0},{2,1},{3,2},{4,7},{5,4},{6,5},{7,6},{8,11},{9,8},{10,9... | collective-permute-start | bytes 393224 | tf_op jit(solution)/shard_map/ppermute | solution.py:40
  12.4 0.3 fusion.5
  13.0 1.3 %collective-permute-start.6 = (bf16[64,1024]{1,0:T(8,128)(2,1)S(1)}, bf16[64,1024]{1,0:T(8,128)(2,1)S(1)}, u32[]{:S(2)}, u32[]{:S(2)}) collective-permute-start(bf16[64,1024]{1,0:T(8,128)(2,1)S(1)} %collective-permute-done.3.refs_2_.refs_6_.b), channel_id=1, source_target_pairs={{0,2},{1,3},{2,0},{3,1},{4,6},{5,7},{6,4},{7,5},{8,10},{9,11},{10,... | collective-permute-start | bytes 393224 | tf_op jit(solution)/shard_map/ppermute | solution.py:40
  14.4 3.9 %collective-permute-done.4.refs_2_.refs_4_ = bf16[64,1024]{1,0:T(8,128)(2,1)S(1)} collective-permute-done((bf16[64,1024]{1,0:T(8,128)(2,1)S(1)}, bf16[64,1024]{1,0:T(8,128)(2,1)S(1)}, u32[]{:S(2)}, u32[]{:S(2)}) %collective-permute-start.4) | collective-permute-done | bytes 131104 | tf_op jit(solution)/shard_map/ppermute | solution.py:40
  18.2 0.5 project_kv.4
  18.7 0.7 collective-permute-done.6.refs_3_.refs_7_
  19.5 0.6 project_kv.5
  20.1 1.7 %collective-permute-start.10 = (bf16[128,512]{1,0:T(8,128)(2,1)S(1)}, bf16[128,512]{1,0:T(8,128)(2,1)S(1)}, u32[]{:S(2)}, u32[]{:S(2)}) collective-permute-start(bf16[128,512]{1,0:T(8,128)(2,1)S(1)} %get-tuple-element.51.refs_0_), channel_id=1, source_target_pairs={{0,8},{1,9},{2,10},{3,11},{4,12},{5,13},{6,14},{7,15},{8,16},{9,17... | collective-permute-start | bytes 393224 | tf_op jit(solution)/shard_map/ppermute | solution.py:40
  21.8 3.3 %collective-permute-start.9 = (bf16[128,512]{1,0:T(8,128)(2,1)S(1)}, bf16[128,512]{1,0:T(8,128)(2,1)S(1)}, u32[]{:S(2)}, u32[]{:S(2)}) collective-permute-start(bf16[128,512]{1,0:T(8,128)(2,1)S(1)} %get-tuple-element.51.refs_0_), channel_id=1, source_target_pairs={{0,16},{1,17},{2,18},{3,19},{4,20},{5,21},{6,22},{7,23},{8,24},{9,... | collective-permute-start | bytes 393224 | tf_op jit(solution)/shard_map/ppermute | solution.py:40
  25.1 0.7 collective-permute-start.8
  25.8 4.7 %collective-permute-start.7 = (bf16[128,512]{1,0:T(8,128)(2,1)S(1)}, bf16[128,512]{1,0:T(8,128)(2,1)S(1)}, u32[]{:S(2)}, u32[]{:S(2)}) collective-permute-start(bf16[128,512]{1,0:T(8,128)(2,1)S(1)} %get-tuple-element.51.refs_0_), channel_id=1, source_target_pairs={{0,4},{1,5},{2,6},{3,7},{4,0},{5,1},{6,2},{7,3},{8,12},{9,13},{10,... | collective-permute-start | bytes 393224 | tf_op jit(solution)/shard_map/ppermute | solution.py:40
  30.5 1.4 %project_q.2.q = bf16[128,1024]{1,0:T(8,128)(2,1)S(1)} custom-call(bf16[64,1024]{1,0:T(8,128)(2,1)S(1)} %collective-permute-done.refs_0_, bf16[64,1024]{1,0:T(8,128)(2,1)S(1)} %collective-permute-done.1.refs_1_, bf16[64,1024]{1,0:T(8,128)(2,1)S(1)} %get-tuple-element.43.refs_0_.refs_2_.a, bf16[64,1024]{1,0:T(8,128)(2,1)S(1)} %collective-permute-done.2.refs_1_.refs_3_, ...), custom_call_target="tpu_custom_call" | custom-call | flops 5673741824 | bytes 9585152 | tf_op jit(solution)/shard_map/project_q/pallas_call | solution.py:47
  32.0 2.5 %collective-permute-start.13 = (bf16[128,512]{1,0:T(8,128)(2,1)S(1)}, bf16[128,512]{1,0:T(8,128)(2,1)S(1)}, u32[]{:S(2)}, u32[]{:S(2)}) collective-permute-start(bf16[128,512]{1,0:T(8,128)(2,1)S(1)} %collective-permute-done.10.refs_3_), channel_id=1, source_target_pairs={{0,4},{1,5},{2,6},{3,7},{4,0},{5,1},{6,2},{7,3},{8,12},{9,13},{10,... | collective-permute-start | bytes 393224 | tf_op jit(solution)/shard_map/ppermute | solution.py:40
  34.6 0.4 collective-permute-start.11
  35.0 0.5 collective-permute-done.13.refs_7_
  35.5 0.4 collective-permute-done.12.refs_6_
  36.0 2.5 %attend_and_project.2 = (bf16[128,512]{1,0:T(8,128)(2,1)S(1)}, bf16[128,512]{1,0:T(8,128)(2,1)S(1)}, bf16[128,512]{1,0:T(8,128)(2,1)S(1)}, bf16[128,512]{1,0:T(8,128)(2,1)S(1)}, bf16[128,1024]{1,0:T(8,128)(2,1)S(1)}) custom-call(bf16[128,1024]{1,0:T(8,128)(2,1)S(1)} %project_q.2.q, s32[64,1]{1,0:T(8,128)S(1)} %iota_add_fusion.qpos, s32[1,512]{1,0:T(1,128)S(1)} %bitcast.3, ...), custom_call_target="tpu_custom_call" | custom-call | flops 6076395008 | bytes 9701632 | tf_op jit(solution)/shard_map/attend_and_project/pallas_call | solution.py:47
  38.6 2.3 %collective-permute-start.15 = (bf16[128,512]{1,0:T(8,128)(2,1)S(1)}, bf16[128,512]{1,0:T(8,128)(2,1)S(1)}, u32[]{:S(2)}, u32[]{:S(2)}) collective-permute-start(bf16[128,512]{1,0:T(8,128)(2,1)S(1)} %get-tuple-element.58), channel_id=1, source_target_pairs={{0,1},{1,2},{2,3},{3,0},{4,5},{5,6},{6,7},{7,4},{8,9},{9,10},{10,1... | collective-permute-start | bytes 393224 | tf_op jit(solution)/shard_map/ppermute | solution.py:40
  40.9 0.4 collective-permute-start.16
  41.4 0.8 project_out.1
  42.2 1.8 %collective-permute-start.21 = (bf16[128,512]{1,0:T(8,128)(2,1)S(1)}, bf16[128,512]{1,0:T(8,128)(2,1)S(1)}, u32[]{:S(2)}, u32[]{:S(2)}) collective-permute-start(bf16[128,512]{1,0:T(8,128)(2,1)S(1)} %get-tuple-element.62), channel_id=1, source_target_pairs={{0,2},{1,3},{2,0},{3,1},{4,6},{5,7},{6,4},{7,5},{8,10},{9,11},{10,... | collective-permute-start | bytes 393224 | tf_op jit(solution)/shard_map/ppermute | solution.py:40
  43.9 0.9 collective-permute-done.14.refs_0_
  44.9 1.8 %collective-permute-start.23 = (bf16[128,512]{1,0:T(8,128)(2,1)S(1)}, bf16[128,512]{1,0:T(8,128)(2,1)S(1)}, u32[]{:S(2)}, u32[]{:S(2)}) collective-permute-start(bf16[128,512]{1,0:T(8,128)(2,1)S(1)} %get-tuple-element.64), channel_id=1, source_target_pairs={{0,3},{1,0},{2,1},{3,2},{4,7},{5,4},{6,5},{7,6},{8,11},{9,8},{10,9... | collective-permute-start | bytes 393224 | tf_op jit(solution)/shard_map/ppermute | solution.py:40
  46.6 1.4 %collective-permute-done.15.refs_1_ = bf16[128,512]{1,0:T(8,128)(2,1)S(1)} collective-permute-done((bf16[128,512]{1,0:T(8,128)(2,1)S(1)}, bf16[128,512]{1,0:T(8,128)(2,1)S(1)}, u32[]{:S(2)}, u32[]{:S(2)}) %collective-permute-start.15) | collective-permute-done | bytes 131104 | tf_op jit(solution)/shard_map/ppermute | solution.py:40
  48.1 2.6 %collective-permute-start.17 = (bf16[128,512]{1,0:T(8,128)(2,1)S(1)}, bf16[128,512]{1,0:T(8,128)(2,1)S(1)}, u32[]{:S(2)}, u32[]{:S(2)}) collective-permute-start(bf16[128,512]{1,0:T(8,128)(2,1)S(1)} %add_parts.2), channel_id=1, source_target_pairs={{0,96},{1,97},{2,98},{3,99},{4,100},{5,101},{6,102},{7,103},{8,104... | collective-permute-start | bytes 393224 | tf_op jit(solution)/shard_map/ppermute | solution.py:40
  50.8 2.6 %collective-permute-done.22.refs_1_ = bf16[128,512]{1,0:T(8,128)(2,1)S(1)} collective-permute-done((bf16[128,512]{1,0:T(8,128)(2,1)S(1)}, bf16[128,512]{1,0:T(8,128)(2,1)S(1)}, u32[]{:S(2)}, u32[]{:S(2)}) %collective-permute-start.22) | collective-permute-done | bytes 131104 | tf_op jit(solution)/shard_map/ppermute | solution.py:40
  53.5 2.6 %collective-permute-start.24 = (bf16[128,512]{1,0:T(8,128)(2,1)S(1)}, bf16[128,512]{1,0:T(8,128)(2,1)S(1)}, u32[]{:S(2)}, u32[]{:S(2)}) collective-permute-start(bf16[128,512]{1,0:T(8,128)(2,1)S(1)} %add_parts.3), channel_id=1, source_target_pairs={{0,96},{1,97},{2,98},{3,99},{4,100},{5,101},{6,102},{7,103},{8,104... | collective-permute-start | bytes 393224 | tf_op jit(solution)/shard_map/ppermute | solution.py:40
  56.0 0.5 collective-permute-start.20
  56.5 1.7 %collective-permute-start.19 = (bf16[128,512]{1,0:T(8,128)(2,1)S(1)}, bf16[128,512]{1,0:T(8,128)(2,1)S(1)}, u32[]{:S(2)}, u32[]{:S(2)}) collective-permute-start(bf16[128,512]{1,0:T(8,128)(2,1)S(1)} %collective-permute-done.17.refs_0_), channel_id=1, source_target_pairs={{0,3},{1,0},{2,1},{3,2},{4,7},{5,4},{6,5},{7,6},{8,11},{9,8},{10,9... | collective-permute-start | bytes 393224 | tf_op jit(solution)/shard_map/ppermute | solution.py:40
  58.2 0.4 collective-permute-start.18
  59.0 1.6 %collective-permute-start.27 = (bf16[128,512]{1,0:T(8,128)(2,1)S(1)}, bf16[128,512]{1,0:T(8,128)(2,1)S(1)}, u32[]{:S(2)}, u32[]{:S(2)}) collective-permute-start(bf16[128,512]{1,0:T(8,128)(2,1)S(1)} %collective-permute-done.24.refs_0_.refs_4_), channel_id=1, source_target_pairs={{0,2},{1,3},{2,0},{3,1},{4,6},{5,7},{6,4},{7,5},{8,10},{9,11},{10,... | collective-permute-start | bytes 393224 | tf_op jit(solution)/shard_map/ppermute | solution.py:40
  60.6 2.0 %collective-permute-start.26 = (bf16[128,512]{1,0:T(8,128)(2,1)S(1)}, bf16[128,512]{1,0:T(8,128)(2,1)S(1)}, u32[]{:S(2)}, u32[]{:S(2)}) collective-permute-start(bf16[128,512]{1,0:T(8,128)(2,1)S(1)} %collective-permute-done.24.refs_0_.refs_4_), channel_id=1, source_target_pairs={{0,3},{1,0},{2,1},{3,2},{4,7},{5,4},{6,5},{7,6},{8,11},{9,8},{10,9... | collective-permute-start | bytes 393224 | tf_op jit(solution)/shard_map/ppermute | solution.py:40
  62.6 2.0 %collective-permute-done.19.refs_2_ = bf16[128,512]{1,0:T(8,128)(2,1)S(1)} collective-permute-done((bf16[128,512]{1,0:T(8,128)(2,1)S(1)}, bf16[128,512]{1,0:T(8,128)(2,1)S(1)}, u32[]{:S(2)}, u32[]{:S(2)}) %collective-permute-start.19) | collective-permute-done | bytes 131104 | tf_op jit(solution)/shard_map/ppermute | solution.py:40
  64.6 1.2 %collective-permute-done.18.refs_1_ = bf16[128,512]{1,0:T(8,128)(2,1)S(1)} collective-permute-done((bf16[128,512]{1,0:T(8,128)(2,1)S(1)}, bf16[128,512]{1,0:T(8,128)(2,1)S(1)}, u32[]{:S(2)}, u32[]{:S(2)}) %collective-permute-start.18) | collective-permute-done | bytes 131104 | tf_op jit(solution)/shard_map/ppermute | solution.py:40
  65.8 0.5 project_kv.6
  66.3 0.7 collective-permute-done.27.refs_3_.refs_7_
  67.0 2.6 %collective-permute-done.26.refs_2_.refs_6_ = bf16[128,512]{1,0:T(8,128)(2,1)S(1)} collective-permute-done((bf16[128,512]{1,0:T(8,128)(2,1)S(1)}, bf16[128,512]{1,0:T(8,128)(2,1)S(1)}, u32[]{:S(2)}, u32[]{:S(2)}) %collective-permute-start.26) | collective-permute-done | bytes 131104 | tf_op jit(solution)/shard_map/ppermute | solution.py:40
  69.6 1.3 %collective-permute-done.25.refs_1_.refs_5_ = bf16[128,512]{1,0:T(8,128)(2,1)S(1)} collective-permute-done((bf16[128,512]{1,0:T(8,128)(2,1)S(1)}, bf16[128,512]{1,0:T(8,128)(2,1)S(1)}, u32[]{:S(2)}, u32[]{:S(2)}) %collective-permute-start.25) | collective-permute-done | bytes 131104 | tf_op jit(solution)/shard_map/ppermute | solution.py:40
  70.8 0.6 project_kv.7
  71.4 0.7 collective-permute-start.31
  72.1 2.5 %collective-permute-start.30 = (bf16[128,512]{1,0:T(8,128)(2,1)S(1)}, bf16[128,512]{1,0:T(8,128)(2,1)S(1)}, u32[]{:S(2)}, u32[]{:S(2)}) collective-permute-start(bf16[128,512]{1,0:T(8,128)(2,1)S(1)} %get-tuple-element.69.refs_0_), channel_id=1, source_target_pairs={{0,16},{1,17},{2,18},{3,19},{4,20},{5,21},{6,22},{7,23},{8,24},{9,... | collective-permute-start | bytes 393224 | tf_op jit(solution)/shard_map/ppermute | solution.py:40
  74.6 0.6 collective-permute-start.29
  75.2 2.2 %collective-permute-start.28 = (bf16[128,512]{1,0:T(8,128)(2,1)S(1)}, bf16[128,512]{1,0:T(8,128)(2,1)S(1)}, u32[]{:S(2)}, u32[]{:S(2)}) collective-permute-start(bf16[128,512]{1,0:T(8,128)(2,1)S(1)} %get-tuple-element.69.refs_0_), channel_id=1, source_target_pairs={{0,4},{1,5},{2,6},{3,7},{4,0},{5,1},{6,2},{7,3},{8,12},{9,13},{10,... | collective-permute-start | bytes 393224 | tf_op jit(solution)/shard_map/ppermute | solution.py:40
  77.3 1.4 %project_q.3.q = bf16[128,1024]{1,0:T(8,128)(2,1)S(1)} custom-call(bf16[128,512]{1,0:T(8,128)(2,1)S(1)} %collective-permute-done.17.refs_0_, bf16[128,512]{1,0:T(8,128)(2,1)S(1)} %collective-permute-done.18.refs_1_, bf16[128,512]{1,0:T(8,128)(2,1)S(1)} %collective-permute-done.19.refs_2_, bf16[128,512]{1,0:T(8,128)(2,1)S(1)} %collective-permute-done.20.refs_3_, ...), custom_call_target="tpu_custom_call" | custom-call | flops 5673741824 | bytes 9585152 | tf_op jit(solution)/shard_map/project_q/pallas_call | solution.py:47
  78.7 0.7 collective-permute-done.29.refs_1_
  79.4 2.6 %collective-permute-start.32 = (bf16[128,512]{1,0:T(8,128)(2,1)S(1)}, bf16[128,512]{1,0:T(8,128)(2,1)S(1)}, u32[]{:S(2)}, u32[]{:S(2)}) collective-permute-start(bf16[128,512]{1,0:T(8,128)(2,1)S(1)} %collective-permute-done.29.refs_1_), channel_id=1, source_target_pairs={{0,4},{1,5},{2,6},{3,7},{4,0},{5,1},{6,2},{7,3},{8,12},{9,13},{10,... | collective-permute-start | bytes 393224 | tf_op jit(solution)/shard_map/ppermute | solution.py:40
  82.1 0.4 collective-permute-start.33
  82.5 0.8 collective-permute-done.34.refs_7_
  83.5 3.2 %attend_and_project.3 = (bf16[64,1024]{1,0:T(8,128)(2,1)S(1)}, bf16[64,1024]{1,0:T(8,128)(2,1)S(1)}, bf16[64,1024]{1,0:T(8,128)(2,1)S(1)}, bf16[64,1024]{1,0:T(8...) custom-call(bf16[128,1024]{1,0:T(8,128)(2,1)S(1)} %project_q.3.q, ...), custom_call_target="tpu_custom_call" | custom-call | flops 6076395008 | bytes 9701632 | tf_op jit(solution)/shard_map/attend_and_project/pallas_call | solution.py:47
  86.7 0.4 collective-permute-start.38
  87.1 2.4 %collective-permute-start.39 = (bf16[64,1024]{1,0:T(8,128)(2,1)S(1)}, bf16[64,1024]{1,0:T(8,128)(2,1)S(1)}, u32[]{:S(2)}, u32[]{:S(2)}) collective-permute-start(bf16[64,1024]{1,0:T(8,128)(2,1)S(1)} %get-tuple-element.78), channel_id=1, source_target_pairs={{0,1},{1,2},{2,3},{3,0},{4,5},{5,6},{6,7},{7,4},{8,9},{9,10},{10,1... | collective-permute-start | bytes 393224 | tf_op jit(solution)/shard_map/ppermute | solution.py:40
  89.8 1.6 %collective-permute-start.35 = (bf16[64,1024]{1,0:T(8,128)(2,1)S(1)}, bf16[64,1024]{1,0:T(8,128)(2,1)S(1)}, u32[]{:S(2)}, u32[]{:S(2)}) collective-permute-start(bf16[64,1024]{1,0:T(8,128)(2,1)S(1)} %get-tuple-element.73), channel_id=1, source_target_pairs={{0,2},{1,3},{2,0},{3,1},{4,6},{5,7},{6,4},{7,5},{8,10},{9,11},{10,... | collective-permute-start | bytes 393224 | tf_op jit(solution)/shard_map/ppermute | solution.py:40
  91.4 1.6 %collective-permute-done.38.refs_0_ = bf16[64,1024]{1,0:T(8,128)(2,1)S(1)} collective-permute-done((bf16[64,1024]{1,0:T(8,128)(2,1)S(1)}, bf16[64,1024]{1,0:T(8,128)(2,1)S(1)}, u32[]{:S(2)}, u32[]{:S(2)}) %collective-permute-start.38) | collective-permute-done | bytes 131104 | tf_op jit(solution)/shard_map/ppermute | solution.py:40
  93.0 2.2 %collective-permute-start.37 = (bf16[64,1024]{1,0:T(8,128)(2,1)S(1)}, bf16[64,1024]{1,0:T(8,128)(2,1)S(1)}, u32[]{:S(2)}, u32[]{:S(2)}) collective-permute-start(bf16[64,1024]{1,0:T(8,128)(2,1)S(1)} %get-tuple-element.75), channel_id=1, source_target_pairs={{0,3},{1,0},{2,1},{3,2},{4,7},{5,4},{6,5},{7,6},{8,11},{9,8},{10,9... | collective-permute-start | bytes 393224 | tf_op jit(solution)/shard_map/ppermute | solution.py:40
  95.2 1.9 %collective-permute-done.39.refs_1_ = bf16[64,1024]{1,0:T(8,128)(2,1)S(1)} collective-permute-done((bf16[64,1024]{1,0:T(8,128)(2,1)S(1)}, bf16[64,1024]{1,0:T(8,128)(2,1)S(1)}, u32[]{:S(2)}, u32[]{:S(2)}) %collective-permute-start.39) | collective-permute-done | bytes 131104 | tf_op jit(solution)/shard_map/ppermute | solution.py:40
  97.3 1.4 %collective-permute-done.35.refs_0_ = bf16[64,1024]{1,0:T(8,128)(2,1)S(1)} collective-permute-done((bf16[64,1024]{1,0:T(8,128)(2,1)S(1)}, bf16[64,1024]{1,0:T(8,128)(2,1)S(1)}, u32[]{:S(2)}, u32[]{:S(2)}) %collective-permute-start.35) | collective-permute-done | bytes 131104 | tf_op jit(solution)/shard_map/ppermute | solution.py:40
  98.7 3.4 %collective-permute-done.36.refs_1_ = bf16[64,1024]{1,0:T(8,128)(2,1)S(1)} collective-permute-done((bf16[64,1024]{1,0:T(8,128)(2,1)S(1)}, bf16[64,1024]{1,0:T(8,128)(2,1)S(1)}, u32[]{:S(2)}, u32[]{:S(2)}) %collective-permute-start.36) | collective-permute-done | bytes 131104 | tf_op jit(solution)/shard_map/ppermute | solution.py:40
  102.1 0.8 finish.1
  (73 shorter events, 2.4 us)
Async XLA Ops:
  0.0 12.4 %copy-start.2 = (bf16[1,4096]{1,0:T(2,128)(2,1)S(1)}, bf16[1,4096]{1,0:T(2,128)(2,1)}, u32[]{:S(2)}) copy-start(bf16[1,4096]{1,0:T(2,128)(2,1)} %g) | copy-start | bytes 24580
  1.0 17.2 %copy-start = (bf16[1,4096,256]{2,1,0:T(8,128)(2,1)S(1)}, bf16[1,4096,256]{2,1,0:T(8,128)(2,1)}, u32[]{:S(2)}) copy-start(bf16[1,4096,256]{2,1,0:T(8,128)(2,1)} %refs_5_.7) | copy-start | bytes 6291460
  1.0 17.7 %collective-permute-start.2 = (bf16[64,1024]{1,0:T(8,128)(2,1)S(1)}, bf16[64,1024]{1,0:T(8,128)(2,1)S(1)}, u32[]{:S(2)}, u32[]{:S(2)}) collective-permute-start(bf16[64,1024]{1,0:T(8,128)(2,1)S(1)} %get-tuple-element.43.refs_0_.refs_2_.a), channel_id=1, source_target_pairs={{0,2},{1,3},{2,0},{3,1},{4,6},{5,7},{6,4},{7,5},{8,10},{9,11},{10,... | collective-permute-start | bytes 393224 | tf_op jit(solution)/shard_map/ppermute | solution.py:40
  4.8 8.1 %collective-permute-start.1 = (bf16[64,1024]{1,0:T(8,128)(2,1)S(1)}, bf16[64,1024]{1,0:T(8,128)(2,1)S(1)}, u32[]{:S(2)}, u32[]{:S(2)}) collective-permute-start(bf16[64,1024]{1,0:T(8,128)(2,1)S(1)} %get-tuple-element.43.refs_0_.refs_2_.a), channel_id=1, source_target_pairs={{0,3},{1,0},{2,1},{3,2},{4,7},{5,4},{6,5},{7,6},{8,11},{9,8},{10,9... | collective-permute-start | bytes 393224 | tf_op jit(solution)/shard_map/ppermute | solution.py:40
  5.6 8.6 %collective-permute-start = (bf16[64,1024]{1,0:T(8,128)(2,1)S(1)}, bf16[64,1024]{1,0:T(8,128)(2,1)S(1)}, u32[]{:S(2)}, u32[]{:S(2)}) collective-permute-start(bf16[64,1024]{1,0:T(8,128)(2,1)S(1)} %get-tuple-element.43.refs_0_.refs_2_.a), channel_id=1, source_target_pairs={{0,1},{1,2},{2,3},{3,0},{4,5},{5,6},{6,7},{7,4},{8,9},{9,10},{10,1... | collective-permute-start | bytes 393224 | tf_op jit(solution)/shard_map/ppermute | solution.py:40
  6.3 3.8 %collective-permute-start.3 = (bf16[64,1024]{1,0:T(8,128)(2,1)S(1)}, bf16[64,1024]{1,0:T(8,128)(2,1)S(1)}, u32[]{:S(2)}, u32[]{:S(2)}) collective-permute-start(bf16[64,1024]{1,0:T(8,128)(2,1)S(1)} %get-tuple-element.44), channel_id=1, source_target_pairs={{0,32},{1,33},{2,34},{3,35},{4,36},{5,37},{6,38},{7,39},{8,40},{9,... | collective-permute-start | bytes 393224 | tf_op jit(solution)/shard_map/ppermute | solution.py:40
  7.7 10.5 %copy-start.1 = (bf16[1,4096,256]{2,1,0:T(8,128)(2,1)S(1)}, bf16[1,4096,256]{2,1,0:T(8,128)(2,1)}, u32[]{:S(2)}) copy-start(bf16[1,4096,256]{2,1,0:T(8,128)(2,1)} %refs_6_.7) | copy-start | bytes 6291460
  10.1 4.2 %collective-permute-start.5 = (bf16[64,1024]{1,0:T(8,128)(2,1)S(1)}, bf16[64,1024]{1,0:T(8,128)(2,1)S(1)}, u32[]{:S(2)}, u32[]{:S(2)}) collective-permute-start(bf16[64,1024]{1,0:T(8,128)(2,1)S(1)} %collective-permute-done.3.refs_2_.refs_6_.b), channel_id=1, source_target_pairs={{0,3},{1,0},{2,1},{3,2},{4,7},{5,4},{6,5},{7,6},{8,11},{9,8},{10,9... | collective-permute-start | bytes 393224 | tf_op jit(solution)/shard_map/ppermute | solution.py:40
  12.4 5.8 %collective-permute-start.4 = (bf16[64,1024]{1,0:T(8,128)(2,1)S(1)}, bf16[64,1024]{1,0:T(8,128)(2,1)S(1)}, u32[]{:S(2)}, u32[]{:S(2)}) collective-permute-start(bf16[64,1024]{1,0:T(8,128)(2,1)S(1)} %collective-permute-done.3.refs_2_.refs_6_.b), channel_id=1, source_target_pairs={{0,1},{1,2},{2,3},{3,0},{4,5},{5,6},{6,7},{7,4},{8,9},{9,10},{10,1... | collective-permute-start | bytes 393224 | tf_op jit(solution)/shard_map/ppermute | solution.py:40
  12.8 17.7 %slice-start.2 = ((s8[8388608]{0:T(1024)(128)(4,1)}), s8[4194304]{0:T(1024)(128)(4,1)S(1)}, s32[]{:S(2)}) async-start(s8[8388608]{0:T(1024)(128)(4,1)} %bitcast.5), calls=%async_computation.2 | async-start | bytes 8388608
  12.9 17.6 %slice-start.3 = ((s8[8388608]{0:T(1024)(128)(4,1)}), s8[4194304]{0:T(1024)(128)(4,1)S(1)}, s32[]{:S(2)}) async-start(s8[8388608]{0:T(1024)(128)(4,1)} %bitcast.5), calls=%async_computation.3 | async-start | bytes 8388608
  13.0 6.5 %collective-permute-start.6 = (bf16[64,1024]{1,0:T(8,128)(2,1)S(1)}, bf16[64,1024]{1,0:T(8,128)(2,1)S(1)}, u32[]{:S(2)}, u32[]{:S(2)}) collective-permute-start(bf16[64,1024]{1,0:T(8,128)(2,1)S(1)} %collective-permute-done.3.refs_2_.refs_6_.b), channel_id=1, source_target_pairs={{0,2},{1,3},{2,0},{3,1},{4,6},{5,7},{6,4},{7,5},{8,10},{9,11},{10,... | collective-permute-start | bytes 393224 | tf_op jit(solution)/shard_map/ppermute | solution.py:40
  19.5 16.6 %slice-start = ((s8[8388608]{0:T(1024)(128)(4,1)}), s8[4194304]{0:T(1024)(128)(4,1)S(1)}, s32[]{:S(2)}) async-start(s8[8388608]{0:T(1024)(128)(4,1)} %bitcast.1), calls=%async_computation | async-start | bytes 8388608
  20.1 11.9 %collective-permute-start.10 = (bf16[128,512]{1,0:T(8,128)(2,1)S(1)}, bf16[128,512]{1,0:T(8,128)(2,1)S(1)}, u32[]{:S(2)}, u32[]{:S(2)}) collective-permute-start(bf16[128,512]{1,0:T(8,128)(2,1)S(1)} %get-tuple-element.51.refs_0_), channel_id=1, source_target_pairs={{0,8},{1,9},{2,10},{3,11},{4,12},{5,13},{6,14},{7,15},{8,16},{9,17... | collective-permute-start | bytes 393224 | tf_op jit(solution)/shard_map/ppermute | solution.py:40
  21.8 12.7 %collective-permute-start.9 = (bf16[128,512]{1,0:T(8,128)(2,1)S(1)}, bf16[128,512]{1,0:T(8,128)(2,1)S(1)}, u32[]{:S(2)}, u32[]{:S(2)}) collective-permute-start(bf16[128,512]{1,0:T(8,128)(2,1)S(1)} %get-tuple-element.51.refs_0_), channel_id=1, source_target_pairs={{0,16},{1,17},{2,18},{3,19},{4,20},{5,21},{6,22},{7,23},{8,24},{9,... | collective-permute-start | bytes 393224 | tf_op jit(solution)/shard_map/ppermute | solution.py:40
  25.1 6.9 %collective-permute-start.8 = (bf16[128,512]{1,0:T(8,128)(2,1)S(1)}, bf16[128,512]{1,0:T(8,128)(2,1)S(1)}, u32[]{:S(2)}, u32[]{:S(2)}) collective-permute-start(bf16[128,512]{1,0:T(8,128)(2,1)S(1)} %get-tuple-element.51.refs_0_), channel_id=1, source_target_pairs={{0,24},{1,25},{2,26},{3,27},{4,28},{5,29},{6,30},{7,31},{8,0},{9,1... | collective-permute-start | bytes 393224 | tf_op jit(solution)/shard_map/ppermute | solution.py:40
  25.8 6.2 %collective-permute-start.7 = (bf16[128,512]{1,0:T(8,128)(2,1)S(1)}, bf16[128,512]{1,0:T(8,128)(2,1)S(1)}, u32[]{:S(2)}, u32[]{:S(2)}) collective-permute-start(bf16[128,512]{1,0:T(8,128)(2,1)S(1)} %get-tuple-element.51.refs_0_), channel_id=1, source_target_pairs={{0,4},{1,5},{2,6},{3,7},{4,0},{5,1},{6,2},{7,3},{8,12},{9,13},{10,... | collective-permute-start | bytes 393224 | tf_op jit(solution)/shard_map/ppermute | solution.py:40
  30.5 5.5 %slice-start.1 = ((s8[8388608]{0:T(1024)(128)(4,1)}), s8[4194304]{0:T(1024)(128)(4,1)S(1)}, s32[]{:S(2)}) async-start(s8[8388608]{0:T(1024)(128)(4,1)} %bitcast.1), calls=%async_computation.1 | async-start | bytes 8388608
  32.0 3.5 %collective-permute-start.13 = (bf16[128,512]{1,0:T(8,128)(2,1)S(1)}, bf16[128,512]{1,0:T(8,128)(2,1)S(1)}, u32[]{:S(2)}, u32[]{:S(2)}) collective-permute-start(bf16[128,512]{1,0:T(8,128)(2,1)S(1)} %collective-permute-done.10.refs_3_), channel_id=1, source_target_pairs={{0,4},{1,5},{2,6},{3,7},{4,0},{5,1},{6,2},{7,3},{8,12},{9,13},{10,... | collective-permute-start | bytes 393224 | tf_op jit(solution)/shard_map/ppermute | solution.py:40
  34.5 1.3 %collective-permute-start.12 = (bf16[128,512]{1,0:T(8,128)(2,1)S(1)}, bf16[128,512]{1,0:T(8,128)(2,1)S(1)}, u32[]{:S(2)}, u32[]{:S(2)}) collective-permute-start(bf16[128,512]{1,0:T(8,128)(2,1)S(1)} %collective-permute-done.9.refs_2_), channel_id=1, source_target_pairs={{0,4},{1,5},{2,6},{3,7},{4,0},{5,1},{6,2},{7,3},{8,12},{9,13},{10,... | collective-permute-start | bytes 393224 | tf_op jit(solution)/shard_map/ppermute | solution.py:40
  34.6 1.4 %collective-permute-start.11 = (bf16[128,512]{1,0:T(8,128)(2,1)S(1)}, bf16[128,512]{1,0:T(8,128)(2,1)S(1)}, u32[]{:S(2)}, u32[]{:S(2)}) collective-permute-start(bf16[128,512]{1,0:T(8,128)(2,1)S(1)} %collective-permute-done.8.refs_1_), channel_id=1, source_target_pairs={{0,4},{1,5},{2,6},{3,7},{4,0},{5,1},{6,2},{7,3},{8,12},{9,13},{10,... | collective-permute-start | bytes 393224 | tf_op jit(solution)/shard_map/ppermute | solution.py:40
  38.5 6.4 %collective-permute-start.14 = (bf16[128,512]{1,0:T(8,128)(2,1)S(1)}, bf16[128,512]{1,0:T(8,128)(2,1)S(1)}, u32[]{:S(2)}, u32[]{:S(2)}) collective-permute-start(bf16[128,512]{1,0:T(8,128)(2,1)S(1)} %get-tuple-element.57), channel_id=1, source_target_pairs={{0,2},{1,3},{2,0},{3,1},{4,6},{5,7},{6,4},{7,5},{8,10},{9,11},{10,... | collective-permute-start | bytes 393224 | tf_op jit(solution)/shard_map/ppermute | solution.py:40
  38.6 9.5 %collective-permute-start.15 = (bf16[128,512]{1,0:T(8,128)(2,1)S(1)}, bf16[128,512]{1,0:T(8,128)(2,1)S(1)}, u32[]{:S(2)}, u32[]{:S(2)}) collective-permute-start(bf16[128,512]{1,0:T(8,128)(2,1)S(1)} %get-tuple-element.58), channel_id=1, source_target_pairs={{0,1},{1,2},{2,3},{3,0},{4,5},{5,6},{6,7},{7,4},{8,9},{9,10},{10,1... | collective-permute-start | bytes 393224 | tf_op jit(solution)/shard_map/ppermute | solution.py:40
  40.9 7.1 %collective-permute-start.16 = (bf16[128,512]{1,0:T(8,128)(2,1)S(1)}, bf16[128,512]{1,0:T(8,128)(2,1)S(1)}, u32[]{:S(2)}, u32[]{:S(2)}) collective-permute-start(bf16[128,512]{1,0:T(8,128)(2,1)S(1)} %get-tuple-element.59), channel_id=1, source_target_pairs={{0,3},{1,0},{2,1},{3,2},{4,7},{5,4},{6,5},{7,6},{8,11},{9,8},{10,9... | collective-permute-start | bytes 393224 | tf_op jit(solution)/shard_map/ppermute | solution.py:40
  42.2 8.6 %collective-permute-start.21 = (bf16[128,512]{1,0:T(8,128)(2,1)S(1)}, bf16[128,512]{1,0:T(8,128)(2,1)S(1)}, u32[]{:S(2)}, u32[]{:S(2)}) collective-permute-start(bf16[128,512]{1,0:T(8,128)(2,1)S(1)} %get-tuple-element.62), channel_id=1, source_target_pairs={{0,2},{1,3},{2,0},{3,1},{4,6},{5,7},{6,4},{7,5},{8,10},{9,11},{10,... | collective-permute-start | bytes 393224 | tf_op jit(solution)/shard_map/ppermute | solution.py:40
  43.9 9.4 %collective-permute-start.22 = (bf16[128,512]{1,0:T(8,128)(2,1)S(1)}, bf16[128,512]{1,0:T(8,128)(2,1)S(1)}, u32[]{:S(2)}, u32[]{:S(2)}) collective-permute-start(bf16[128,512]{1,0:T(8,128)(2,1)S(1)} %get-tuple-element.63), channel_id=1, source_target_pairs={{0,1},{1,2},{2,3},{3,0},{4,5},{5,6},{6,7},{7,4},{8,9},{9,10},{10,1... | collective-permute-start | bytes 393224 | tf_op jit(solution)/shard_map/ppermute | solution.py:40
  44.9 8.5 %collective-permute-start.23 = (bf16[128,512]{1,0:T(8,128)(2,1)S(1)}, bf16[128,512]{1,0:T(8,128)(2,1)S(1)}, u32[]{:S(2)}, u32[]{:S(2)}) collective-permute-start(bf16[128,512]{1,0:T(8,128)(2,1)S(1)} %get-tuple-element.64), channel_id=1, source_target_pairs={{0,3},{1,0},{2,1},{3,2},{4,7},{5,4},{6,5},{7,6},{8,11},{9,8},{10,9... | collective-permute-start | bytes 393224 | tf_op jit(solution)/shard_map/ppermute | solution.py:40
  48.1 7.9 %collective-permute-start.17 = (bf16[128,512]{1,0:T(8,128)(2,1)S(1)}, bf16[128,512]{1,0:T(8,128)(2,1)S(1)}, u32[]{:S(2)}, u32[]{:S(2)}) collective-permute-start(bf16[128,512]{1,0:T(8,128)(2,1)S(1)} %add_parts.2), channel_id=1, source_target_pairs={{0,96},{1,97},{2,98},{3,99},{4,100},{5,101},{6,102},{7,103},{8,104... | collective-permute-start | bytes 393224 | tf_op jit(solution)/shard_map/ppermute | solution.py:40
  53.5 5.5 %collective-permute-start.24 = (bf16[128,512]{1,0:T(8,128)(2,1)S(1)}, bf16[128,512]{1,0:T(8,128)(2,1)S(1)}, u32[]{:S(2)}, u32[]{:S(2)}) collective-permute-start(bf16[128,512]{1,0:T(8,128)(2,1)S(1)} %add_parts.3), channel_id=1, source_target_pairs={{0,96},{1,97},{2,98},{3,99},{4,100},{5,101},{6,102},{7,103},{8,104... | collective-permute-start | bytes 393224 | tf_op jit(solution)/shard_map/ppermute | solution.py:40
  56.0 6.6 %collective-permute-start.20 = (bf16[128,512]{1,0:T(8,128)(2,1)S(1)}, bf16[128,512]{1,0:T(8,128)(2,1)S(1)}, u32[]{:S(2)}, u32[]{:S(2)}) collective-permute-start(bf16[128,512]{1,0:T(8,128)(2,1)S(1)} %collective-permute-done.17.refs_0_), channel_id=1, source_target_pairs={{0,2},{1,3},{2,0},{3,1},{4,6},{5,7},{6,4},{7,5},{8,10},{9,11},{10,... | collective-permute-start | bytes 393224 | tf_op jit(solution)/shard_map/ppermute | solution.py:40
  56.5 8.1 %collective-permute-start.19 = (bf16[128,512]{1,0:T(8,128)(2,1)S(1)}, bf16[128,512]{1,0:T(8,128)(2,1)S(1)}, u32[]{:S(2)}, u32[]{:S(2)}) collective-permute-start(bf16[128,512]{1,0:T(8,128)(2,1)S(1)} %collective-permute-done.17.refs_0_), channel_id=1, source_target_pairs={{0,3},{1,0},{2,1},{3,2},{4,7},{5,4},{6,5},{7,6},{8,11},{9,8},{10,9... | collective-permute-start | bytes 393224 | tf_op jit(solution)/shard_map/ppermute | solution.py:40
  58.2 7.6 %collective-permute-start.18 = (bf16[128,512]{1,0:T(8,128)(2,1)S(1)}, bf16[128,512]{1,0:T(8,128)(2,1)S(1)}, u32[]{:S(2)}, u32[]{:S(2)}) collective-permute-start(bf16[128,512]{1,0:T(8,128)(2,1)S(1)} %collective-permute-done.17.refs_0_), channel_id=1, source_target_pairs={{0,1},{1,2},{2,3},{3,0},{4,5},{5,6},{6,7},{7,4},{8,9},{9,10},{10,1... | collective-permute-start | bytes 393224 | tf_op jit(solution)/shard_map/ppermute | solution.py:40
  59.0 8.0 %collective-permute-start.27 = (bf16[128,512]{1,0:T(8,128)(2,1)S(1)}, bf16[128,512]{1,0:T(8,128)(2,1)S(1)}, u32[]{:S(2)}, u32[]{:S(2)}) collective-permute-start(bf16[128,512]{1,0:T(8,128)(2,1)S(1)} %collective-permute-done.24.refs_0_.refs_4_), channel_id=1, source_target_pairs={{0,2},{1,3},{2,0},{3,1},{4,6},{5,7},{6,4},{7,5},{8,10},{9,11},{10,... | collective-permute-start | bytes 393224 | tf_op jit(solution)/shard_map/ppermute | solution.py:40
  60.6 9.0 %collective-permute-start.26 = (bf16[128,512]{1,0:T(8,128)(2,1)S(1)}, bf16[128,512]{1,0:T(8,128)(2,1)S(1)}, u32[]{:S(2)}, u32[]{:S(2)}) collective-permute-start(bf16[128,512]{1,0:T(8,128)(2,1)S(1)} %collective-permute-done.24.refs_0_.refs_4_), channel_id=1, source_target_pairs={{0,3},{1,0},{2,1},{3,2},{4,7},{5,4},{6,5},{7,6},{8,11},{9,8},{10,9... | collective-permute-start | bytes 393224 | tf_op jit(solution)/shard_map/ppermute | solution.py:40
  62.6 8.2 %collective-permute-start.25 = (bf16[128,512]{1,0:T(8,128)(2,1)S(1)}, bf16[128,512]{1,0:T(8,128)(2,1)S(1)}, u32[]{:S(2)}, u32[]{:S(2)}) collective-permute-start(bf16[128,512]{1,0:T(8,128)(2,1)S(1)} %collective-permute-done.24.refs_0_.refs_4_), channel_id=1, source_target_pairs={{0,1},{1,2},{2,3},{3,0},{4,5},{5,6},{6,7},{7,4},{8,9},{9,10},{10,1... | collective-permute-start | bytes 393224 | tf_op jit(solution)/shard_map/ppermute | solution.py:40
  71.4 10.6 %collective-permute-start.31 = (bf16[128,512]{1,0:T(8,128)(2,1)S(1)}, bf16[128,512]{1,0:T(8,128)(2,1)S(1)}, u32[]{:S(2)}, u32[]{:S(2)}) collective-permute-start(bf16[128,512]{1,0:T(8,128)(2,1)S(1)} %get-tuple-element.69.refs_0_), channel_id=1, source_target_pairs={{0,8},{1,9},{2,10},{3,11},{4,12},{5,13},{6,14},{7,15},{8,16},{9,17... | collective-permute-start | bytes 393224 | tf_op jit(solution)/shard_map/ppermute | solution.py:40
  72.1 10.0 %collective-permute-start.30 = (bf16[128,512]{1,0:T(8,128)(2,1)S(1)}, bf16[128,512]{1,0:T(8,128)(2,1)S(1)}, u32[]{:S(2)}, u32[]{:S(2)}) collective-permute-start(bf16[128,512]{1,0:T(8,128)(2,1)S(1)} %get-tuple-element.69.refs_0_), channel_id=1, source_target_pairs={{0,16},{1,17},{2,18},{3,19},{4,20},{5,21},{6,22},{7,23},{8,24},{9,... | collective-permute-start | bytes 393224 | tf_op jit(solution)/shard_map/ppermute | solution.py:40
  74.6 4.8 %collective-permute-start.29 = (bf16[128,512]{1,0:T(8,128)(2,1)S(1)}, bf16[128,512]{1,0:T(8,128)(2,1)S(1)}, u32[]{:S(2)}, u32[]{:S(2)}) collective-permute-start(bf16[128,512]{1,0:T(8,128)(2,1)S(1)} %get-tuple-element.69.refs_0_), channel_id=1, source_target_pairs={{0,24},{1,25},{2,26},{3,27},{4,28},{5,29},{6,30},{7,31},{8,0},{9,1... | collective-permute-start | bytes 393224 | tf_op jit(solution)/shard_map/ppermute | solution.py:40
  75.2 4.3 %collective-permute-start.28 = (bf16[128,512]{1,0:T(8,128)(2,1)S(1)}, bf16[128,512]{1,0:T(8,128)(2,1)S(1)}, u32[]{:S(2)}, u32[]{:S(2)}) collective-permute-start(bf16[128,512]{1,0:T(8,128)(2,1)S(1)} %get-tuple-element.69.refs_0_), channel_id=1, source_target_pairs={{0,4},{1,5},{2,6},{3,7},{4,0},{5,1},{6,2},{7,3},{8,12},{9,13},{10,... | collective-permute-start | bytes 393224 | tf_op jit(solution)/shard_map/ppermute | solution.py:40
  79.4 4.1 %collective-permute-start.32 = (bf16[128,512]{1,0:T(8,128)(2,1)S(1)}, bf16[128,512]{1,0:T(8,128)(2,1)S(1)}, u32[]{:S(2)}, u32[]{:S(2)}) collective-permute-start(bf16[128,512]{1,0:T(8,128)(2,1)S(1)} %collective-permute-done.29.refs_1_), channel_id=1, source_target_pairs={{0,4},{1,5},{2,6},{3,7},{4,0},{5,1},{6,2},{7,3},{8,12},{9,13},{10,... | collective-permute-start | bytes 393224 | tf_op jit(solution)/shard_map/ppermute | solution.py:40
  82.0 1.3 %collective-permute-start.34 = (bf16[128,512]{1,0:T(8,128)(2,1)S(1)}, bf16[128,512]{1,0:T(8,128)(2,1)S(1)}, u32[]{:S(2)}, u32[]{:S(2)}) collective-permute-start(bf16[128,512]{1,0:T(8,128)(2,1)S(1)} %collective-permute-done.31.refs_3_), channel_id=1, source_target_pairs={{0,4},{1,5},{2,6},{3,7},{4,0},{5,1},{6,2},{7,3},{8,12},{9,13},{10,... | collective-permute-start | bytes 393224 | tf_op jit(solution)/shard_map/ppermute | solution.py:40
  82.1 1.4 %collective-permute-start.33 = (bf16[128,512]{1,0:T(8,128)(2,1)S(1)}, bf16[128,512]{1,0:T(8,128)(2,1)S(1)}, u32[]{:S(2)}, u32[]{:S(2)}) collective-permute-start(bf16[128,512]{1,0:T(8,128)(2,1)S(1)} %collective-permute-done.30.refs_2_), channel_id=1, source_target_pairs={{0,4},{1,5},{2,6},{3,7},{4,0},{5,1},{6,2},{7,3},{8,12},{9,13},{10,... | collective-permute-start | bytes 393224 | tf_op jit(solution)/shard_map/ppermute | solution.py:40
  86.7 6.3 %collective-permute-start.38 = (bf16[64,1024]{1,0:T(8,128)(2,1)S(1)}, bf16[64,1024]{1,0:T(8,128)(2,1)S(1)}, u32[]{:S(2)}, u32[]{:S(2)}) collective-permute-start(bf16[64,1024]{1,0:T(8,128)(2,1)S(1)} %get-tuple-element.77), channel_id=1, source_target_pairs={{0,2},{1,3},{2,0},{3,1},{4,6},{5,7},{6,4},{7,5},{8,10},{9,11},{10,... | collective-permute-start | bytes 393224 | tf_op jit(solution)/shard_map/ppermute | solution.py:40
  87.1 10.0 %collective-permute-start.39 = (bf16[64,1024]{1,0:T(8,128)(2,1)S(1)}, bf16[64,1024]{1,0:T(8,128)(2,1)S(1)}, u32[]{:S(2)}, u32[]{:S(2)}) collective-permute-start(bf16[64,1024]{1,0:T(8,128)(2,1)S(1)} %get-tuple-element.78), channel_id=1, source_target_pairs={{0,1},{1,2},{2,3},{3,0},{4,5},{5,6},{6,7},{7,4},{8,9},{9,10},{10,1... | collective-permute-start | bytes 393224 | tf_op jit(solution)/shard_map/ppermute | solution.py:40
  89.5 7.6 %collective-permute-start.40 = (bf16[64,1024]{1,0:T(8,128)(2,1)S(1)}, bf16[64,1024]{1,0:T(8,128)(2,1)S(1)}, u32[]{:S(2)}, u32[]{:S(2)}) collective-permute-start(bf16[64,1024]{1,0:T(8,128)(2,1)S(1)} %get-tuple-element.79), channel_id=1, source_target_pairs={{0,3},{1,0},{2,1},{3,2},{4,7},{5,4},{6,5},{7,6},{8,11},{9,8},{10,9... | collective-permute-start | bytes 393224 | tf_op jit(solution)/shard_map/ppermute | solution.py:40
  89.8 8.9 %collective-permute-start.35 = (bf16[64,1024]{1,0:T(8,128)(2,1)S(1)}, bf16[64,1024]{1,0:T(8,128)(2,1)S(1)}, u32[]{:S(2)}, u32[]{:S(2)}) collective-permute-start(bf16[64,1024]{1,0:T(8,128)(2,1)S(1)} %get-tuple-element.73), channel_id=1, source_target_pairs={{0,2},{1,3},{2,0},{3,1},{4,6},{5,7},{6,4},{7,5},{8,10},{9,11},{10,... | collective-permute-start | bytes 393224 | tf_op jit(solution)/shard_map/ppermute | solution.py:40
  91.4 10.7 %collective-permute-start.36 = (bf16[64,1024]{1,0:T(8,128)(2,1)S(1)}, bf16[64,1024]{1,0:T(8,128)(2,1)S(1)}, u32[]{:S(2)}, u32[]{:S(2)}) collective-permute-start(bf16[64,1024]{1,0:T(8,128)(2,1)S(1)} %get-tuple-element.74), channel_id=1, source_target_pairs={{0,1},{1,2},{2,3},{3,0},{4,5},{5,6},{6,7},{7,4},{8,9},{9,10},{10,1... | collective-permute-start | bytes 393224 | tf_op jit(solution)/shard_map/ppermute | solution.py:40
  93.0 9.0 %collective-permute-start.37 = (bf16[64,1024]{1,0:T(8,128)(2,1)S(1)}, bf16[64,1024]{1,0:T(8,128)(2,1)S(1)}, u32[]{:S(2)}, u32[]{:S(2)}) collective-permute-start(bf16[64,1024]{1,0:T(8,128)(2,1)S(1)} %get-tuple-element.75), channel_id=1, source_target_pairs={{0,3},{1,0},{2,1},{3,2},{4,7},{5,4},{6,5},{7,6},{8,11},{9,8},{10,9... | collective-permute-start | bytes 393224 | tf_op jit(solution)/shard_map/ppermute | solution.py:40
  97.2 4.9 %collective-permute-start.41 = (bf16[64,1024]{1,0:T(8,128)(2,1)S(1)}, bf16[64,1024]{1,0:T(8,128)(2,1)S(1)}, u32[]{:S(2)}, u32[]{:S(2)}) collective-permute-start(bf16[64,1024]{1,0:T(8,128)(2,1)S(1)} %last_cross.1), channel_id=1, source_target_pairs={{0,32},{1,33},{2,34},{3,35},{4,36},{5,37},{6,38},{7,39},{8,40},{9,... | collective-permute-start | bytes 393224 | tf_op jit(solution)/shard_map/ppermute | solution.py:40

commit v7 on v6

--- a/solution.py
+++ b/solution.py
@@ -9,15 +9,15 @@
 
 HS = 128
 EPS = 1e-05
-CHUNKS = 2
+CHUNKS = (512, 512)
 SMALL = 10 * 1024 * 1024
 SHIFTS = (2, 1, 3, 0)
 ORDER = (0, 1, 3, 2)
-Z_ORDER = (3, 2, 1)
+Z_ORDER = (3, 1, 2)
 FLOPS_PER_US = 1_150_000_000
 BESIDE_GAIN = 3
-BESIDE_FIRST, BESIDE_KV, BESIDE_Q, BESIDE_MIX = 5, 2, 4, 4
-DIAG = False
+BESIDE_FIRST, BESIDE_KV, BESIDE_Q, BESIDE_MIX = 5, 2, 4, 8
+DIAG = (0, 1)
 AXES = ("section", "ctx", "tp")
 
 
@@ -375,7 +375,7 @@
     core = ctx % 2
     half = tokens.shape[1]
     width = tokens.shape[2]
-    chunk = width // CHUNKS
+    starts = [sum(CHUNKS[:c]) for c in range(len(CHUNKS))]
 
     local = lax.iota(jnp.int32, half)
 
@@ -430,37 +430,38 @@
     pieces = [(s, 0, [own_from[s], other_from[s]]) for s in (1, 3, 0, 2)]
     carry = project_kv(pieces[:2], width, gain, wk, wv, None, None)
     kv, r = project_kv(pieces[2:], width, gain, wk, wv, carry, rope)
-    chunked = [[(c * chunk, s, 0, 2 * half) for s in SHIFTS] for c in range(CHUNKS)]
+    chunked = [[(at, s, 0, 2 * half) for s in SHIFTS] for at in starts]
     got, attended = mix(
         kv,
         lambda: project_q(pieces, width, gain, wq, r, rope),
         w_out,
-        chunk,
+        CHUNKS[0],
         0,
         chunked[0],
     )
-    got += project_out(attended, w_out, chunk, sum(chunked[1:], []))
+    for c in range(1, len(CHUNKS)):
+        got += project_out(attended, w_out, CHUNKS[c], chunked[c])
     x0 = stacked(own, other)
     sums = []
-    for c in range(CHUNKS):
+    for c in range(len(CHUNKS)):
         parts = []
         for s, block in zip(SHIFTS, got[c * n_tp : (c + 1) * n_tp]):
             parts.append(send(block, by_tp=s) if s else block)
-        sums.append(add_parts(x0, c * chunk, parts))
+        sums.append(add_parts(x0, starts[c], parts))
 
     rope = tuple(swapped(t) for t in rope)
     carry = None
     every = []
     came = []
-    for c in range(CHUNKS):
-        last = c == CHUNKS - 1
+    for c in range(len(CHUNKS)):
+        last = c == len(CHUNKS) - 1
         came.append(send(sums[c], next_layer=True))
         x_from = {0: came[c]}
-        if DIAG:
+        if c in DIAG:
             x_from[2] = send(sums[c], next_layer=True, by_tp=2)
-        for s in (1, 3) if DIAG else (3, 1, 2):
+        for s in (1, 3) if c in DIAG else (3, 1, 2):
             x_from[s] = send(came[c], by_tp=s)
-        pieces = [(s, c * chunk, [x_from[s]]) for s in ORDER]
+        pieces = [(s, starts[c], [x_from[s]]) for s in ORDER]
         every += pieces
         carry = project_kv(pieces, width, gain, wk, wv, carry, rope if last else None)
     kv, r = carry

time: 103 us -> 103 us (level)
  starting transfers between devices: 57.1 us -> 53.8 us
  waiting for transfers between devices: 31.1 us -> 34 us
    ppermute x42, starting transfers between devices: 57.1 us -> 53.8 us  [send(): return lax.ppermute(block, AXES, route)]
    ppermute x42, waiting for transfers between devices: 31.1 us -> 34 us  [send(): return lax.ppermute(block, AXES, route)]
  transfers between devices with their start and end apart: 42 -> 42, of which waited for: 23 -> 22; matrix products, arithmetic and copies ran while one was open for 1% -> 1% of each run, Pallas kernels for 5% -> 5%
where the time goes in v7:
time: 103 us
  starting transfers between devices  53.8 us (52%)
  waiting for transfers between devices  34 us (33%)
  Pallas kernels  13.4 us (13%)
    ppermute x42, starting transfers between devices, send(): return lax.ppermute(block, AXES, route)  53.8 us
    ppermute x42, waiting for transfers between devices, send(): return lax.ppermute(block, AXES, route)  34 us
    pallas_call x16, Pallas kernels, in_vmem(): pl.pallas_call(kernel, in_specs=specs, out_specs=[pl.BlockSpec(memory_spa...  13.4 us
  transfers between devices with their start and end apart: 42, of which 22 were waited for; matrix products, arithmetic and copies ran while one was open for 1% of the time, Pallas kernels for 5%

profile of v7, /device:TPU:1, one launch (start us, length us, event | category | flops | bytes accessed | tf_op | source)
XLA Modules:
  0.0 102.5 jit_solution(15539405454598704151)
XLA Ops:
  0.0 1.0 rows_of_segments.1
  1.0 3.8 %collective-permute-start.2 = (bf16[64,1024]{1,0:T(8,128)(2,1)S(1)}, bf16[64,1024]{1,0:T(8,128)(2,1)S(1)}, u32[]{:S(2)}, u32[]{:S(2)}) collective-permute-start(bf16[64,1024]{1,0:T(8,128)(2,1)S(1)} %get-tuple-element.43.refs_0_.refs_2_.a), channel_id=1, source_target_pairs={{0,2},{1,3},{2,0},{3,1},{4,6},{5,7},{6,4},{7,5},{8,10},{9,11},{10,... | collective-permute-start | bytes 393224 | tf_op jit(solution)/shard_map/ppermute | solution.py:40
  4.8 0.8 collective-permute-start.1
  5.6 0.7 collective-permute-start
  6.3 1.2 %collective-permute-start.3 = (bf16[64,1024]{1,0:T(8,128)(2,1)S(1)}, bf16[64,1024]{1,0:T(8,128)(2,1)S(1)}, u32[]{:S(2)}, u32[]{:S(2)}) collective-permute-start(bf16[64,1024]{1,0:T(8,128)(2,1)S(1)} %get-tuple-element.44), channel_id=1, source_target_pairs={{0,32},{1,33},{2,34},{3,35},{4,36},{5,37},{6,38},{7,39},{8,40},{9,... | collective-permute-start | bytes 393224 | tf_op jit(solution)/shard_map/ppermute | solution.py:40
  7.8 2.4 %collective-permute-done.3.refs_2_.refs_6_.b = bf16[64,1024]{1,0:T(8,128)(2,1)S(1)} collective-permute-done((bf16[64,1024]{1,0:T(8,128)(2,1)S(1)}, bf16[64,1024]{1,0:T(8,128)(2,1)S(1)}, u32[]{:S(2)}, u32[]{:S(2)}) %collective-permute-start.3) | collective-permute-done | bytes 131104 | tf_op jit(solution)/shard_map/ppermute | solution.py:40
  10.1 2.3 %collective-permute-start.5 = (bf16[64,1024]{1,0:T(8,128)(2,1)S(1)}, bf16[64,1024]{1,0:T(8,128)(2,1)S(1)}, u32[]{:S(2)}, u32[]{:S(2)}) collective-permute-start(bf16[64,1024]{1,0:T(8,128)(2,1)S(1)} %collective-permute-done.3.refs_2_.refs_6_.b), channel_id=1, source_target_pairs={{0,3},{1,0},{2,1},{3,2},{4,7},{5,4},{6,5},{7,6},{8,11},{9,8},{10,9... | collective-permute-start | bytes 393224 | tf_op jit(solution)/shard_map/ppermute | solution.py:40
  12.4 0.3 fusion.5
  13.0 1.3 %collective-permute-start.6 = (bf16[64,1024]{1,0:T(8,128)(2,1)S(1)}, bf16[64,1024]{1,0:T(8,128)(2,1)S(1)}, u32[]{:S(2)}, u32[]{:S(2)}) collective-permute-start(bf16[64,1024]{1,0:T(8,128)(2,1)S(1)} %collective-permute-done.3.refs_2_.refs_6_.b), channel_id=1, source_target_pairs={{0,2},{1,3},{2,0},{3,1},{4,6},{5,7},{6,4},{7,5},{8,10},{9,11},{10,... | collective-permute-start | bytes 393224 | tf_op jit(solution)/shard_map/ppermute | solution.py:40
  14.4 3.9 %collective-permute-done.4.refs_2_.refs_4_ = bf16[64,1024]{1,0:T(8,128)(2,1)S(1)} collective-permute-done((bf16[64,1024]{1,0:T(8,128)(2,1)S(1)}, bf16[64,1024]{1,0:T(8,128)(2,1)S(1)}, u32[]{:S(2)}, u32[]{:S(2)}) %collective-permute-start.4) | collective-permute-done | bytes 131104 | tf_op jit(solution)/shard_map/ppermute | solution.py:40
  18.2 0.5 project_kv.4
  18.7 0.7 collective-permute-done.6.refs_3_.refs_7_
  19.5 0.6 project_kv.5
  20.1 3.7 %collective-permute-start.10 = (bf16[128,512]{1,0:T(8,128)(2,1)S(1)}, bf16[128,512]{1,0:T(8,128)(2,1)S(1)}, u32[]{:S(2)}, u32[]{:S(2)}) collective-permute-start(bf16[128,512]{1,0:T(8,128)(2,1)S(1)} %get-tuple-element.51.refs_0_), channel_id=1, source_target_pairs={{0,16},{1,17},{2,18},{3,19},{4,20},{5,21},{6,22},{7,23},{8,24},{9,... | collective-permute-start | bytes 393224 | tf_op jit(solution)/shard_map/ppermute | solution.py:40
  23.7 0.7 collective-permute-start.9
  24.5 1.9 %collective-permute-start.8 = (bf16[128,512]{1,0:T(8,128)(2,1)S(1)}, bf16[128,512]{1,0:T(8,128)(2,1)S(1)}, u32[]{:S(2)}, u32[]{:S(2)}) collective-permute-start(bf16[128,512]{1,0:T(8,128)(2,1)S(1)} %get-tuple-element.51.refs_0_), channel_id=1, source_target_pairs={{0,24},{1,25},{2,26},{3,27},{4,28},{5,29},{6,30},{7,31},{8,0},{9,1... | collective-permute-start | bytes 393224 | tf_op jit(solution)/shard_map/ppermute | solution.py:40
  26.4 4.7 %collective-permute-start.7 = (bf16[128,512]{1,0:T(8,128)(2,1)S(1)}, bf16[128,512]{1,0:T(8,128)(2,1)S(1)}, u32[]{:S(2)}, u32[]{:S(2)}) collective-permute-start(bf16[128,512]{1,0:T(8,128)(2,1)S(1)} %get-tuple-element.51.refs_0_), channel_id=1, source_target_pairs={{0,4},{1,5},{2,6},{3,7},{4,0},{5,1},{6,2},{7,3},{8,12},{9,13},{10,... | collective-permute-start | bytes 393224 | tf_op jit(solution)/shard_map/ppermute | solution.py:40
  31.1 1.4 %project_q.2.q = bf16[128,1024]{1,0:T(8,128)(2,1)S(1)} custom-call(bf16[64,1024]{1,0:T(8,128)(2,1)S(1)} %collective-permute-done.refs_0_, bf16[64,1024]{1,0:T(8,128)(2,1)S(1)} %collective-permute-done.1.refs_1_, bf16[64,1024]{1,0:T(8,128)(2,1)S(1)} %get-tuple-element.43.refs_0_.refs_2_.a, bf16[64,1024]{1,0:T(8,128)(2,1)S(1)} %collective-permute-done.2.refs_1_.refs_3_, ...), custom_call_target="tpu_custom_call" | custom-call | flops 5673741824 | bytes 9585152 | tf_op jit(solution)/shard_map/project_q/pallas_call | solution.py:47
  32.6 1.3 %collective-permute-start.13 = (bf16[128,512]{1,0:T(8,128)(2,1)S(1)}, bf16[128,512]{1,0:T(8,128)(2,1)S(1)}, u32[]{:S(2)}, u32[]{:S(2)}) collective-permute-start(bf16[128,512]{1,0:T(8,128)(2,1)S(1)} %collective-permute-done.10.refs_3_), channel_id=1, source_target_pairs={{0,4},{1,5},{2,6},{3,7},{4,0},{5,1},{6,2},{7,3},{8,12},{9,13},{10,... | collective-permute-start | bytes 393224 | tf_op jit(solution)/shard_map/ppermute | solution.py:40
  34.1 0.3 collective-permute-start.11
  34.4 0.5 collective-permute-done.13.refs_7_
  34.9 0.4 collective-permute-done.12.refs_6_
  35.4 2.5 %attend_and_project.2 = (bf16[128,512]{1,0:T(8,128)(2,1)S(1)}, bf16[128,512]{1,0:T(8,128)(2,1)S(1)}, bf16[128,512]{1,0:T(8,128)(2,1)S(1)}, bf16[128,512]{1,0:T(8,128)(2,1)S(1)}, bf16[128,1024]{1,0:T(8,128)(2,1)S(1)}) custom-call(bf16[128,1024]{1,0:T(8,128)(2,1)S(1)} %project_q.2.q, s32[64,1]{1,0:T(8,128)S(1)} %iota_add_fusion.qpos, s32[1,512]{1,0:T(1,128)S(1)} %bitcast.3, ...), custom_call_target="tpu_custom_call" | custom-call | flops 10676395008 | bytes 9701632 | tf_op jit(solution)/shard_map/attend_and_project/pallas_call | solution.py:47
  38.0 2.3 %collective-permute-start.15 = (bf16[128,512]{1,0:T(8,128)(2,1)S(1)}, bf16[128,512]{1,0:T(8,128)(2,1)S(1)}, u32[]{:S(2)}, u32[]{:S(2)}) collective-permute-start(bf16[128,512]{1,0:T(8,128)(2,1)S(1)} %get-tuple-element.58), channel_id=1, source_target_pairs={{0,1},{1,2},{2,3},{3,0},{4,5},{5,6},{6,7},{7,4},{8,9},{9,10},{10,1... | collective-permute-start | bytes 393224 | tf_op jit(solution)/shard_map/ppermute | solution.py:40
  40.3 0.4 collective-permute-start.16
  40.8 0.8 project_out.1
  41.6 1.8 %collective-permute-start.21 = (bf16[128,512]{1,0:T(8,128)(2,1)S(1)}, bf16[128,512]{1,0:T(8,128)(2,1)S(1)}, u32[]{:S(2)}, u32[]{:S(2)}) collective-permute-start(bf16[128,512]{1,0:T(8,128)(2,1)S(1)} %get-tuple-element.62), channel_id=1, source_target_pairs={{0,2},{1,3},{2,0},{3,1},{4,6},{5,7},{6,4},{7,5},{8,10},{9,11},{10,... | collective-permute-start | bytes 393224 | tf_op jit(solution)/shard_map/ppermute | solution.py:40
  43.3 0.9 collective-permute-done.14.refs_0_
  44.3 1.7 %collective-permute-start.23 = (bf16[128,512]{1,0:T(8,128)(2,1)S(1)}, bf16[128,512]{1,0:T(8,128)(2,1)S(1)}, u32[]{:S(2)}, u32[]{:S(2)}) collective-permute-start(bf16[128,512]{1,0:T(8,128)(2,1)S(1)} %get-tuple-element.64), channel_id=1, source_target_pairs={{0,3},{1,0},{2,1},{3,2},{4,7},{5,4},{6,5},{7,6},{8,11},{9,8},{10,9... | collective-permute-start | bytes 393224 | tf_op jit(solution)/shard_map/ppermute | solution.py:40
  46.0 1.4 %collective-permute-done.15.refs_1_ = bf16[128,512]{1,0:T(8,128)(2,1)S(1)} collective-permute-done((bf16[128,512]{1,0:T(8,128)(2,1)S(1)}, bf16[128,512]{1,0:T(8,128)(2,1)S(1)}, u32[]{:S(2)}, u32[]{:S(2)}) %collective-permute-start.15) | collective-permute-done | bytes 131104 | tf_op jit(solution)/shard_map/ppermute | solution.py:40
  47.5 2.6 %collective-permute-start.17 = (bf16[128,512]{1,0:T(8,128)(2,1)S(1)}, bf16[128,512]{1,0:T(8,128)(2,1)S(1)}, u32[]{:S(2)}, u32[]{:S(2)}) collective-permute-start(bf16[128,512]{1,0:T(8,128)(2,1)S(1)} %add_parts.2), channel_id=1, source_target_pairs={{0,96},{1,97},{2,98},{3,99},{4,100},{5,101},{6,102},{7,103},{8,104... | collective-permute-start | bytes 393224 | tf_op jit(solution)/shard_map/ppermute | solution.py:40
  50.2 0.4 collective-permute-start.20
  50.6 2.2 %collective-permute-done.22.refs_1_ = bf16[128,512]{1,0:T(8,128)(2,1)S(1)} collective-permute-done((bf16[128,512]{1,0:T(8,128)(2,1)S(1)}, bf16[128,512]{1,0:T(8,128)(2,1)S(1)}, u32[]{:S(2)}, u32[]{:S(2)}) %collective-permute-start.22) | collective-permute-done | bytes 131104 | tf_op jit(solution)/shard_map/ppermute | solution.py:40
  52.9 2.6 %collective-permute-start.24 = (bf16[128,512]{1,0:T(8,128)(2,1)S(1)}, bf16[128,512]{1,0:T(8,128)(2,1)S(1)}, u32[]{:S(2)}, u32[]{:S(2)}) collective-permute-start(bf16[128,512]{1,0:T(8,128)(2,1)S(1)} %add_parts.3), channel_id=1, source_target_pairs={{0,96},{1,97},{2,98},{3,99},{4,100},{5,101},{6,102},{7,103},{8,104... | collective-permute-start | bytes 393224 | tf_op jit(solution)/shard_map/ppermute | solution.py:40
  55.5 2.0 %collective-permute-start.19 = (bf16[128,512]{1,0:T(8,128)(2,1)S(1)}, bf16[128,512]{1,0:T(8,128)(2,1)S(1)}, u32[]{:S(2)}, u32[]{:S(2)}) collective-permute-start(bf16[128,512]{1,0:T(8,128)(2,1)S(1)} %collective-permute-done.17.refs_0_), channel_id=1, source_target_pairs={{0,3},{1,0},{2,1},{3,2},{4,7},{5,4},{6,5},{7,6},{8,11},{9,8},{10,9... | collective-permute-start | bytes 393224 | tf_op jit(solution)/shard_map/ppermute | solution.py:40
  57.5 1.8 %collective-permute-start.27 = (bf16[128,512]{1,0:T(8,128)(2,1)S(1)}, bf16[128,512]{1,0:T(8,128)(2,1)S(1)}, u32[]{:S(2)}, u32[]{:S(2)}) collective-permute-start(bf16[128,512]{1,0:T(8,128)(2,1)S(1)} %add_parts.3), channel_id=1, source_target_pairs={{0,98},{1,99},{2,96},{3,97},{4,102},{5,103},{6,100},{7,101},{8,106... | collective-permute-start | bytes 393224 | tf_op jit(solution)/shard_map/ppermute | solution.py:40
  59.3 0.6 collective-permute-done.24.refs_0_.refs_4_
  59.9 1.9 %collective-permute-start.26 = (bf16[128,512]{1,0:T(8,128)(2,1)S(1)}, bf16[128,512]{1,0:T(8,128)(2,1)S(1)}, u32[]{:S(2)}, u32[]{:S(2)}) collective-permute-start(bf16[128,512]{1,0:T(8,128)(2,1)S(1)} %collective-permute-done.24.refs_0_.refs_4_), channel_id=1, source_target_pairs={{0,3},{1,0},{2,1},{3,2},{4,7},{5,4},{6,5},{7,6},{8,11},{9,8},{10,9... | collective-permute-start | bytes 393224 | tf_op jit(solution)/shard_map/ppermute | solution.py:40
  61.8 0.7 collective-permute-done.18.refs_1_
  62.5 0.5 project_kv.6
  63.0 2.2 %collective-permute-done.27.refs_3_.refs_7_ = bf16[128,512]{1,0:T(8,128)(2,1)S(1)} collective-permute-done((bf16[128,512]{1,0:T(8,128)(2,1)S(1)}, bf16[128,512]{1,0:T(8,128)(2,1)S(1)}, u32[]{:S(2)}, u32[]{:S(2)}) %collective-permute-start.27) | collective-permute-done | bytes 131104 | tf_op jit(solution)/shard_map/ppermute | solution.py:40
  65.1 0.2 collective-permute-done.26.refs_2_.refs_6_
  65.4 4.6 %collective-permute-done.25.refs_1_.refs_5_ = bf16[128,512]{1,0:T(8,128)(2,1)S(1)} collective-permute-done((bf16[128,512]{1,0:T(8,128)(2,1)S(1)}, bf16[128,512]{1,0:T(8,128)(2,1)S(1)}, u32[]{:S(2)}, u32[]{:S(2)}) %collective-permute-start.25) | collective-permute-done | bytes 131104 | tf_op jit(solution)/shard_map/ppermute | solution.py:40
  69.9 0.6 project_kv.7
  70.5 1.5 %collective-permute-start.31 = (bf16[128,512]{1,0:T(8,128)(2,1)S(1)}, bf16[128,512]{1,0:T(8,128)(2,1)S(1)}, u32[]{:S(2)}, u32[]{:S(2)}) collective-permute-start(bf16[128,512]{1,0:T(8,128)(2,1)S(1)} %get-tuple-element.69.refs_0_), channel_id=1, source_target_pairs={{0,16},{1,17},{2,18},{3,19},{4,20},{5,21},{6,22},{7,23},{8,24},{9,... | collective-permute-start | bytes 393224 | tf_op jit(solution)/shard_map/ppermute | solution.py:40
  72.0 2.4 %collective-permute-start.30 = (bf16[128,512]{1,0:T(8,128)(2,1)S(1)}, bf16[128,512]{1,0:T(8,128)(2,1)S(1)}, u32[]{:S(2)}, u32[]{:S(2)}) collective-permute-start(bf16[128,512]{1,0:T(8,128)(2,1)S(1)} %get-tuple-element.69.refs_0_), channel_id=1, source_target_pairs={{0,8},{1,9},{2,10},{3,11},{4,12},{5,13},{6,14},{7,15},{8,16},{9,17... | collective-permute-start | bytes 393224 | tf_op jit(solution)/shard_map/ppermute | solution.py:40
  74.3 0.3 collective-permute-start.29
  74.7 1.6 %collective-permute-start.28 = (bf16[128,512]{1,0:T(8,128)(2,1)S(1)}, bf16[128,512]{1,0:T(8,128)(2,1)S(1)}, u32[]{:S(2)}, u32[]{:S(2)}) collective-permute-start(bf16[128,512]{1,0:T(8,128)(2,1)S(1)} %get-tuple-element.69.refs_0_), channel_id=1, source_target_pairs={{0,4},{1,5},{2,6},{3,7},{4,0},{5,1},{6,2},{7,3},{8,12},{9,13},{10,... | collective-permute-start | bytes 393224 | tf_op jit(solution)/shard_map/ppermute | solution.py:40
  76.2 1.4 %project_q.3.q = bf16[128,1024]{1,0:T(8,128)(2,1)S(1)} custom-call(bf16[128,512]{1,0:T(8,128)(2,1)S(1)} %collective-permute-done.17.refs_0_, bf16[128,512]{1,0:T(8,128)(2,1)S(1)} %collective-permute-done.18.refs_1_, bf16[128,512]{1,0:T(8,128)(2,1)S(1)} %collective-permute-done.19.refs_2_, bf16[128,512]{1,0:T(8,128)(2,1)S(1)} %collective-permute-done.20.refs_3_, ...), custom_call_target="tpu_custom_call" | custom-call | flops 5673741824 | bytes 9585152 | tf_op jit(solution)/shard_map/project_q/pallas_call | solution.py:47
  77.6 2.4 %collective-permute-done.29.refs_1_ = bf16[128,512]{1,0:T(8,128)(2,1)S(1)} collective-permute-done((bf16[128,512]{1,0:T(8,128)(2,1)S(1)}, bf16[128,512]{1,0:T(8,128)(2,1)S(1)}, u32[]{:S(2)}, u32[]{:S(2)}) %collective-permute-start.29) | collective-permute-done | bytes 131104 | tf_op jit(solution)/shard_map/ppermute | solution.py:40
  80.0 1.6 %collective-permute-start.32 = (bf16[128,512]{1,0:T(8,128)(2,1)S(1)}, bf16[128,512]{1,0:T(8,128)(2,1)S(1)}, u32[]{:S(2)}, u32[]{:S(2)}) collective-permute-start(bf16[128,512]{1,0:T(8,128)(2,1)S(1)} %collective-permute-done.29.refs_1_), channel_id=1, source_target_pairs={{0,4},{1,5},{2,6},{3,7},{4,0},{5,1},{6,2},{7,3},{8,12},{9,13},{10,... | collective-permute-start | bytes 393224 | tf_op jit(solution)/shard_map/ppermute | solution.py:40
  81.7 0.4 collective-permute-start.33
  82.2 0.8 collective-permute-done.34.refs_7_
  83.1 3.2 %attend_and_project.3 = (bf16[64,1024]{1,0:T(8,128)(2,1)S(1)}, bf16[64,1024]{1,0:T(8,128)(2,1)S(1)}, bf16[64,1024]{1,0:T(8,128)(2,1)S(1)}, bf16[64,1024]{1,0:T(8...) custom-call(bf16[128,1024]{1,0:T(8,128)(2,1)S(1)} %project_q.3.q, ...), custom_call_target="tpu_custom_call" | custom-call | flops 10676395008 | bytes 9701632 | tf_op jit(solution)/shard_map/attend_and_project/pallas_call | solution.py:47
  86.3 0.4 collective-permute-start.38
  86.7 0.7 collective-permute-start.39
  87.4 2.0 %collective-permute-start.40 = (bf16[64,1024]{1,0:T(8,128)(2,1)S(1)}, bf16[64,1024]{1,0:T(8,128)(2,1)S(1)}, u32[]{:S(2)}, u32[]{:S(2)}) collective-permute-start(bf16[64,1024]{1,0:T(8,128)(2,1)S(1)} %get-tuple-element.79), channel_id=1, source_target_pairs={{0,3},{1,0},{2,1},{3,2},{4,7},{5,4},{6,5},{7,6},{8,11},{9,8},{10,9... | collective-permute-start | bytes 393224 | tf_op jit(solution)/shard_map/ppermute | solution.py:40
  89.4 1.5 %collective-permute-start.35 = (bf16[64,1024]{1,0:T(8,128)(2,1)S(1)}, bf16[64,1024]{1,0:T(8,128)(2,1)S(1)}, u32[]{:S(2)}, u32[]{:S(2)}) collective-permute-start(bf16[64,1024]{1,0:T(8,128)(2,1)S(1)} %get-tuple-element.73), channel_id=1, source_target_pairs={{0,2},{1,3},{2,0},{3,1},{4,6},{5,7},{6,4},{7,5},{8,10},{9,11},{10,... | collective-permute-start | bytes 393224 | tf_op jit(solution)/shard_map/ppermute | solution.py:40
  90.9 1.8 %collective-permute-done.38.refs_0_ = bf16[64,1024]{1,0:T(8,128)(2,1)S(1)} collective-permute-done((bf16[64,1024]{1,0:T(8,128)(2,1)S(1)}, bf16[64,1024]{1,0:T(8,128)(2,1)S(1)}, u32[]{:S(2)}, u32[]{:S(2)}) %collective-permute-start.38) | collective-permute-done | bytes 131104 | tf_op jit(solution)/shard_map/ppermute | solution.py:40
  92.7 0.9 collective-permute-start.37
  93.6 3.1 %collective-permute-done.39.refs_1_ = bf16[64,1024]{1,0:T(8,128)(2,1)S(1)} collective-permute-done((bf16[64,1024]{1,0:T(8,128)(2,1)S(1)}, bf16[64,1024]{1,0:T(8,128)(2,1)S(1)}, u32[]{:S(2)}, u32[]{:S(2)}) %collective-permute-start.39) | collective-permute-done | bytes 131104 | tf_op jit(solution)/shard_map/ppermute | solution.py:40
  96.9 1.4 %collective-permute-done.35.refs_0_ = bf16[64,1024]{1,0:T(8,128)(2,1)S(1)} collective-permute-done((bf16[64,1024]{1,0:T(8,128)(2,1)S(1)}, bf16[64,1024]{1,0:T(8,128)(2,1)S(1)}, u32[]{:S(2)}, u32[]{:S(2)}) %collective-permute-start.35) | collective-permute-done | bytes 131104 | tf_op jit(solution)/shard_map/ppermute | solution.py:40
  98.3 3.4 %collective-permute-done.36.refs_1_ = bf16[64,1024]{1,0:T(8,128)(2,1)S(1)} collective-permute-done((bf16[64,1024]{1,0:T(8,128)(2,1)S(1)}, bf16[64,1024]{1,0:T(8,128)(2,1)S(1)}, u32[]{:S(2)}, u32[]{:S(2)}) %collective-permute-start.36) | collective-permute-done | bytes 131104 | tf_op jit(solution)/shard_map/ppermute | solution.py:40
  101.7 0.8 finish.1
  (73 shorter events, 2.0 us)
Async XLA Ops:
  0.0 12.4 %copy-start.2 = (bf16[1,4096]{1,0:T(2,128)(2,1)S(1)}, bf16[1,4096]{1,0:T(2,128)(2,1)}, u32[]{:S(2)}) copy-start(bf16[1,4096]{1,0:T(2,128)(2,1)} %g) | copy-start | bytes 24580
  1.0 17.2 %copy-start = (bf16[1,4096,256]{2,1,0:T(8,128)(2,1)S(1)}, bf16[1,4096,256]{2,1,0:T(8,128)(2,1)}, u32[]{:S(2)}) copy-start(bf16[1,4096,256]{2,1,0:T(8,128)(2,1)} %refs_5_.7) | copy-start | bytes 6291460
  1.0 17.7 %collective-permute-start.2 = (bf16[64,1024]{1,0:T(8,128)(2,1)S(1)}, bf16[64,1024]{1,0:T(8,128)(2,1)S(1)}, u32[]{:S(2)}, u32[]{:S(2)}) collective-permute-start(bf16[64,1024]{1,0:T(8,128)(2,1)S(1)} %get-tuple-element.43.refs_0_.refs_2_.a), channel_id=1, source_target_pairs={{0,2},{1,3},{2,0},{3,1},{4,6},{5,7},{6,4},{7,5},{8,10},{9,11},{10,... | collective-permute-start | bytes 393224 | tf_op jit(solution)/shard_map/ppermute | solution.py:40
  4.8 8.1 %collective-permute-start.1 = (bf16[64,1024]{1,0:T(8,128)(2,1)S(1)}, bf16[64,1024]{1,0:T(8,128)(2,1)S(1)}, u32[]{:S(2)}, u32[]{:S(2)}) collective-permute-start(bf16[64,1024]{1,0:T(8,128)(2,1)S(1)} %get-tuple-element.43.refs_0_.refs_2_.a), channel_id=1, source_target_pairs={{0,3},{1,0},{2,1},{3,2},{4,7},{5,4},{6,5},{7,6},{8,11},{9,8},{10,9... | collective-permute-start | bytes 393224 | tf_op jit(solution)/shard_map/ppermute | solution.py:40
  5.6 8.6 %collective-permute-start = (bf16[64,1024]{1,0:T(8,128)(2,1)S(1)}, bf16[64,1024]{1,0:T(8,128)(2,1)S(1)}, u32[]{:S(2)}, u32[]{:S(2)}) collective-permute-start(bf16[64,1024]{1,0:T(8,128)(2,1)S(1)} %get-tuple-element.43.refs_0_.refs_2_.a), channel_id=1, source_target_pairs={{0,1},{1,2},{2,3},{3,0},{4,5},{5,6},{6,7},{7,4},{8,9},{9,10},{10,1... | collective-permute-start | bytes 393224 | tf_op jit(solution)/shard_map/ppermute | solution.py:40
  6.3 3.8 %collective-permute-start.3 = (bf16[64,1024]{1,0:T(8,128)(2,1)S(1)}, bf16[64,1024]{1,0:T(8,128)(2,1)S(1)}, u32[]{:S(2)}, u32[]{:S(2)}) collective-permute-start(bf16[64,1024]{1,0:T(8,128)(2,1)S(1)} %get-tuple-element.44), channel_id=1, source_target_pairs={{0,32},{1,33},{2,34},{3,35},{4,36},{5,37},{6,38},{7,39},{8,40},{9,... | collective-permute-start | bytes 393224 | tf_op jit(solution)/shard_map/ppermute | solution.py:40
  7.7 10.5 %copy-start.1 = (bf16[1,4096,256]{2,1,0:T(8,128)(2,1)S(1)}, bf16[1,4096,256]{2,1,0:T(8,128)(2,1)}, u32[]{:S(2)}) copy-start(bf16[1,4096,256]{2,1,0:T(8,128)(2,1)} %refs_6_.7) | copy-start | bytes 6291460
  10.1 4.2 %collective-permute-start.5 = (bf16[64,1024]{1,0:T(8,128)(2,1)S(1)}, bf16[64,1024]{1,0:T(8,128)(2,1)S(1)}, u32[]{:S(2)}, u32[]{:S(2)}) collective-permute-start(bf16[64,1024]{1,0:T(8,128)(2,1)S(1)} %collective-permute-done.3.refs_2_.refs_6_.b), channel_id=1, source_target_pairs={{0,3},{1,0},{2,1},{3,2},{4,7},{5,4},{6,5},{7,6},{8,11},{9,8},{10,9... | collective-permute-start | bytes 393224 | tf_op jit(solution)/shard_map/ppermute | solution.py:40
  12.4 5.8 %collective-permute-start.4 = (bf16[64,1024]{1,0:T(8,128)(2,1)S(1)}, bf16[64,1024]{1,0:T(8,128)(2,1)S(1)}, u32[]{:S(2)}, u32[]{:S(2)}) collective-permute-start(bf16[64,1024]{1,0:T(8,128)(2,1)S(1)} %collective-permute-done.3.refs_2_.refs_6_.b), channel_id=1, source_target_pairs={{0,1},{1,2},{2,3},{3,0},{4,5},{5,6},{6,7},{7,4},{8,9},{9,10},{10,1... | collective-permute-start | bytes 393224 | tf_op jit(solution)/shard_map/ppermute | solution.py:40
  12.8 18.3 %slice-start.2 = ((s8[8388608]{0:T(1024)(128)(4,1)}), s8[4194304]{0:T(1024)(128)(4,1)S(1)}, s32[]{:S(2)}) async-start(s8[8388608]{0:T(1024)(128)(4,1)} %bitcast.5), calls=%async_computation.2 | async-start | bytes 8388608
  12.9 18.2 %slice-start.3 = ((s8[8388608]{0:T(1024)(128)(4,1)}), s8[4194304]{0:T(1024)(128)(4,1)S(1)}, s32[]{:S(2)}) async-start(s8[8388608]{0:T(1024)(128)(4,1)} %bitcast.5), calls=%async_computation.3 | async-start | bytes 8388608
  13.0 6.5 %collective-permute-start.6 = (bf16[64,1024]{1,0:T(8,128)(2,1)S(1)}, bf16[64,1024]{1,0:T(8,128)(2,1)S(1)}, u32[]{:S(2)}, u32[]{:S(2)}) collective-permute-start(bf16[64,1024]{1,0:T(8,128)(2,1)S(1)} %collective-permute-done.3.refs_2_.refs_6_.b), channel_id=1, source_target_pairs={{0,2},{1,3},{2,0},{3,1},{4,6},{5,7},{6,4},{7,5},{8,10},{9,11},{10,... | collective-permute-start | bytes 393224 | tf_op jit(solution)/shard_map/ppermute | solution.py:40
  19.5 16.0 %slice-start = ((s8[8388608]{0:T(1024)(128)(4,1)}), s8[4194304]{0:T(1024)(128)(4,1)S(1)}, s32[]{:S(2)}) async-start(s8[8388608]{0:T(1024)(128)(4,1)} %bitcast.1), calls=%async_computation | async-start | bytes 8388608
  20.1 12.5 %collective-permute-start.10 = (bf16[128,512]{1,0:T(8,128)(2,1)S(1)}, bf16[128,512]{1,0:T(8,128)(2,1)S(1)}, u32[]{:S(2)}, u32[]{:S(2)}) collective-permute-start(bf16[128,512]{1,0:T(8,128)(2,1)S(1)} %get-tuple-element.51.refs_0_), channel_id=1, source_target_pairs={{0,16},{1,17},{2,18},{3,19},{4,20},{5,21},{6,22},{7,23},{8,24},{9,... | collective-permute-start | bytes 393224 | tf_op jit(solution)/shard_map/ppermute | solution.py:40
  23.7 10.1 %collective-permute-start.9 = (bf16[128,512]{1,0:T(8,128)(2,1)S(1)}, bf16[128,512]{1,0:T(8,128)(2,1)S(1)}, u32[]{:S(2)}, u32[]{:S(2)}) collective-permute-start(bf16[128,512]{1,0:T(8,128)(2,1)S(1)} %get-tuple-element.51.refs_0_), channel_id=1, source_target_pairs={{0,8},{1,9},{2,10},{3,11},{4,12},{5,13},{6,14},{7,15},{8,16},{9,17... | collective-permute-start | bytes 393224 | tf_op jit(solution)/shard_map/ppermute | solution.py:40
  24.5 8.1 %collective-permute-start.8 = (bf16[128,512]{1,0:T(8,128)(2,1)S(1)}, bf16[128,512]{1,0:T(8,128)(2,1)S(1)}, u32[]{:S(2)}, u32[]{:S(2)}) collective-permute-start(bf16[128,512]{1,0:T(8,128)(2,1)S(1)} %get-tuple-element.51.refs_0_), channel_id=1, source_target_pairs={{0,24},{1,25},{2,26},{3,27},{4,28},{5,29},{6,30},{7,31},{8,0},{9,1... | collective-permute-start | bytes 393224 | tf_op jit(solution)/shard_map/ppermute | solution.py:40
  26.4 6.1 %collective-permute-start.7 = (bf16[128,512]{1,0:T(8,128)(2,1)S(1)}, bf16[128,512]{1,0:T(8,128)(2,1)S(1)}, u32[]{:S(2)}, u32[]{:S(2)}) collective-permute-start(bf16[128,512]{1,0:T(8,128)(2,1)S(1)} %get-tuple-element.51.refs_0_), channel_id=1, source_target_pairs={{0,4},{1,5},{2,6},{3,7},{4,0},{5,1},{6,2},{7,3},{8,12},{9,13},{10,... | collective-permute-start | bytes 393224 | tf_op jit(solution)/shard_map/ppermute | solution.py:40
  31.1 4.3 %slice-start.1 = ((s8[8388608]{0:T(1024)(128)(4,1)}), s8[4194304]{0:T(1024)(128)(4,1)S(1)}, s32[]{:S(2)}) async-start(s8[8388608]{0:T(1024)(128)(4,1)} %bitcast.1), calls=%async_computation.1 | async-start | bytes 8388608
  32.6 2.3 %collective-permute-start.13 = (bf16[128,512]{1,0:T(8,128)(2,1)S(1)}, bf16[128,512]{1,0:T(8,128)(2,1)S(1)}, u32[]{:S(2)}, u32[]{:S(2)}) collective-permute-start(bf16[128,512]{1,0:T(8,128)(2,1)S(1)} %collective-permute-done.10.refs_3_), channel_id=1, source_target_pairs={{0,4},{1,5},{2,6},{3,7},{4,0},{5,1},{6,2},{7,3},{8,12},{9,13},{10,... | collective-permute-start | bytes 393224 | tf_op jit(solution)/shard_map/ppermute | solution.py:40
  33.9 1.3 %collective-permute-start.12 = (bf16[128,512]{1,0:T(8,128)(2,1)S(1)}, bf16[128,512]{1,0:T(8,128)(2,1)S(1)}, u32[]{:S(2)}, u32[]{:S(2)}) collective-permute-start(bf16[128,512]{1,0:T(8,128)(2,1)S(1)} %collective-permute-done.9.refs_2_), channel_id=1, source_target_pairs={{0,4},{1,5},{2,6},{3,7},{4,0},{5,1},{6,2},{7,3},{8,12},{9,13},{10,... | collective-permute-start | bytes 393224 | tf_op jit(solution)/shard_map/ppermute | solution.py:40
  34.1 1.4 %collective-permute-start.11 = (bf16[128,512]{1,0:T(8,128)(2,1)S(1)}, bf16[128,512]{1,0:T(8,128)(2,1)S(1)}, u32[]{:S(2)}, u32[]{:S(2)}) collective-permute-start(bf16[128,512]{1,0:T(8,128)(2,1)S(1)} %collective-permute-done.8.refs_1_), channel_id=1, source_target_pairs={{0,4},{1,5},{2,6},{3,7},{4,0},{5,1},{6,2},{7,3},{8,12},{9,13},{10,... | collective-permute-start | bytes 393224 | tf_op jit(solution)/shard_map/ppermute | solution.py:40
  37.9 6.4 %collective-permute-start.14 = (bf16[128,512]{1,0:T(8,128)(2,1)S(1)}, bf16[128,512]{1,0:T(8,128)(2,1)S(1)}, u32[]{:S(2)}, u32[]{:S(2)}) collective-permute-start(bf16[128,512]{1,0:T(8,128)(2,1)S(1)} %get-tuple-element.57), channel_id=1, source_target_pairs={{0,2},{1,3},{2,0},{3,1},{4,6},{5,7},{6,4},{7,5},{8,10},{9,11},{10,... | collective-permute-start | bytes 393224 | tf_op jit(solution)/shard_map/ppermute | solution.py:40
  38.0 9.5 %collective-permute-start.15 = (bf16[128,512]{1,0:T(8,128)(2,1)S(1)}, bf16[128,512]{1,0:T(8,128)(2,1)S(1)}, u32[]{:S(2)}, u32[]{:S(2)}) collective-permute-start(bf16[128,512]{1,0:T(8,128)(2,1)S(1)} %get-tuple-element.58), channel_id=1, source_target_pairs={{0,1},{1,2},{2,3},{3,0},{4,5},{5,6},{6,7},{7,4},{8,9},{9,10},{10,1... | collective-permute-start | bytes 393224 | tf_op jit(solution)/shard_map/ppermute | solution.py:40
  40.3 7.1 %collective-permute-start.16 = (bf16[128,512]{1,0:T(8,128)(2,1)S(1)}, bf16[128,512]{1,0:T(8,128)(2,1)S(1)}, u32[]{:S(2)}, u32[]{:S(2)}) collective-permute-start(bf16[128,512]{1,0:T(8,128)(2,1)S(1)} %get-tuple-element.59), channel_id=1, source_target_pairs={{0,3},{1,0},{2,1},{3,2},{4,7},{5,4},{6,5},{7,6},{8,11},{9,8},{10,9... | collective-permute-start | bytes 393224 | tf_op jit(solution)/shard_map/ppermute | solution.py:40
  41.6 9.0 %collective-permute-start.21 = (bf16[128,512]{1,0:T(8,128)(2,1)S(1)}, bf16[128,512]{1,0:T(8,128)(2,1)S(1)}, u32[]{:S(2)}, u32[]{:S(2)}) collective-permute-start(bf16[128,512]{1,0:T(8,128)(2,1)S(1)} %get-tuple-element.62), channel_id=1, source_target_pairs={{0,2},{1,3},{2,0},{3,1},{4,6},{5,7},{6,4},{7,5},{8,10},{9,11},{10,... | collective-permute-start | bytes 393224 | tf_op jit(solution)/shard_map/ppermute | solution.py:40
  43.3 9.4 %collective-permute-start.22 = (bf16[128,512]{1,0:T(8,128)(2,1)S(1)}, bf16[128,512]{1,0:T(8,128)(2,1)S(1)}, u32[]{:S(2)}, u32[]{:S(2)}) collective-permute-start(bf16[128,512]{1,0:T(8,128)(2,1)S(1)} %get-tuple-element.63), channel_id=1, source_target_pairs={{0,1},{1,2},{2,3},{3,0},{4,5},{5,6},{6,7},{7,4},{8,9},{9,10},{10,1... | collective-permute-start | bytes 393224 | tf_op jit(solution)/shard_map/ppermute | solution.py:40
  44.3 8.5 %collective-permute-start.23 = (bf16[128,512]{1,0:T(8,128)(2,1)S(1)}, bf16[128,512]{1,0:T(8,128)(2,1)S(1)}, u32[]{:S(2)}, u32[]{:S(2)}) collective-permute-start(bf16[128,512]{1,0:T(8,128)(2,1)S(1)} %get-tuple-element.64), channel_id=1, source_target_pairs={{0,3},{1,0},{2,1},{3,2},{4,7},{5,4},{6,5},{7,6},{8,11},{9,8},{10,9... | collective-permute-start | bytes 393224 | tf_op jit(solution)/shard_map/ppermute | solution.py:40
  47.5 7.9 %collective-permute-start.17 = (bf16[128,512]{1,0:T(8,128)(2,1)S(1)}, bf16[128,512]{1,0:T(8,128)(2,1)S(1)}, u32[]{:S(2)}, u32[]{:S(2)}) collective-permute-start(bf16[128,512]{1,0:T(8,128)(2,1)S(1)} %add_parts.2), channel_id=1, source_target_pairs={{0,96},{1,97},{2,98},{3,99},{4,100},{5,101},{6,102},{7,103},{8,104... | collective-permute-start | bytes 393224 | tf_op jit(solution)/shard_map/ppermute | solution.py:40
  50.2 11.5 %collective-permute-start.20 = (bf16[128,512]{1,0:T(8,128)(2,1)S(1)}, bf16[128,512]{1,0:T(8,128)(2,1)S(1)}, u32[]{:S(2)}, u32[]{:S(2)}) collective-permute-start(bf16[128,512]{1,0:T(8,128)(2,1)S(1)} %add_parts.2), channel_id=1, source_target_pairs={{0,98},{1,99},{2,96},{3,97},{4,102},{5,103},{6,100},{7,101},{8,106... | collective-permute-start | bytes 393224 | tf_op jit(solution)/shard_map/ppermute | solution.py:40
  52.9 7.0 %collective-permute-start.24 = (bf16[128,512]{1,0:T(8,128)(2,1)S(1)}, bf16[128,512]{1,0:T(8,128)(2,1)S(1)}, u32[]{:S(2)}, u32[]{:S(2)}) collective-permute-start(bf16[128,512]{1,0:T(8,128)(2,1)S(1)} %add_parts.3), channel_id=1, source_target_pairs={{0,96},{1,97},{2,98},{3,99},{4,100},{5,101},{6,102},{7,103},{8,104... | collective-permute-start | bytes 393224 | tf_op jit(solution)/shard_map/ppermute | solution.py:40
  55.5 6.3 %collective-permute-start.19 = (bf16[128,512]{1,0:T(8,128)(2,1)S(1)}, bf16[128,512]{1,0:T(8,128)(2,1)S(1)}, u32[]{:S(2)}, u32[]{:S(2)}) collective-permute-start(bf16[128,512]{1,0:T(8,128)(2,1)S(1)} %collective-permute-done.17.refs_0_), channel_id=1, source_target_pairs={{0,3},{1,0},{2,1},{3,2},{4,7},{5,4},{6,5},{7,6},{8,11},{9,8},{10,9... | collective-permute-start | bytes 393224 | tf_op jit(solution)/shard_map/ppermute | solution.py:40
  57.5 5.0 %collective-permute-start.18 = (bf16[128,512]{1,0:T(8,128)(2,1)S(1)}, bf16[128,512]{1,0:T(8,128)(2,1)S(1)}, u32[]{:S(2)}, u32[]{:S(2)}) collective-permute-start(bf16[128,512]{1,0:T(8,128)(2,1)S(1)} %collective-permute-done.17.refs_0_), channel_id=1, source_target_pairs={{0,1},{1,2},{2,3},{3,0},{4,5},{5,6},{6,7},{7,4},{8,9},{9,10},{10,1... | collective-permute-start | bytes 393224 | tf_op jit(solution)/shard_map/ppermute | solution.py:40
  57.5 7.7 %collective-permute-start.27 = (bf16[128,512]{1,0:T(8,128)(2,1)S(1)}, bf16[128,512]{1,0:T(8,128)(2,1)S(1)}, u32[]{:S(2)}, u32[]{:S(2)}) collective-permute-start(bf16[128,512]{1,0:T(8,128)(2,1)S(1)} %add_parts.3), channel_id=1, source_target_pairs={{0,98},{1,99},{2,96},{3,97},{4,102},{5,103},{6,100},{7,101},{8,106... | collective-permute-start | bytes 393224 | tf_op jit(solution)/shard_map/ppermute | solution.py:40
  59.9 5.5 %collective-permute-start.26 = (bf16[128,512]{1,0:T(8,128)(2,1)S(1)}, bf16[128,512]{1,0:T(8,128)(2,1)S(1)}, u32[]{:S(2)}, u32[]{:S(2)}) collective-permute-start(bf16[128,512]{1,0:T(8,128)(2,1)S(1)} %collective-permute-done.24.refs_0_.refs_4_), channel_id=1, source_target_pairs={{0,3},{1,0},{2,1},{3,2},{4,7},{5,4},{6,5},{7,6},{8,11},{9,8},{10,9... | collective-permute-start | bytes 393224 | tf_op jit(solution)/shard_map/ppermute | solution.py:40
  61.8 8.2 %collective-permute-start.25 = (bf16[128,512]{1,0:T(8,128)(2,1)S(1)}, bf16[128,512]{1,0:T(8,128)(2,1)S(1)}, u32[]{:S(2)}, u32[]{:S(2)}) collective-permute-start(bf16[128,512]{1,0:T(8,128)(2,1)S(1)} %collective-permute-done.24.refs_0_.refs_4_), channel_id=1, source_target_pairs={{0,1},{1,2},{2,3},{3,0},{4,5},{5,6},{6,7},{7,4},{8,9},{9,10},{10,1... | collective-permute-start | bytes 393224 | tf_op jit(solution)/shard_map/ppermute | solution.py:40
  70.5 11.1 %collective-permute-start.31 = (bf16[128,512]{1,0:T(8,128)(2,1)S(1)}, bf16[128,512]{1,0:T(8,128)(2,1)S(1)}, u32[]{:S(2)}, u32[]{:S(2)}) collective-permute-start(bf16[128,512]{1,0:T(8,128)(2,1)S(1)} %get-tuple-element.69.refs_0_), channel_id=1, source_target_pairs={{0,16},{1,17},{2,18},{3,19},{4,20},{5,21},{6,22},{7,23},{8,24},{9,... | collective-permute-start | bytes 393224 | tf_op jit(solution)/shard_map/ppermute | solution.py:40
  72.0 9.7 %collective-permute-start.30 = (bf16[128,512]{1,0:T(8,128)(2,1)S(1)}, bf16[128,512]{1,0:T(8,128)(2,1)S(1)}, u32[]{:S(2)}, u32[]{:S(2)}) collective-permute-start(bf16[128,512]{1,0:T(8,128)(2,1)S(1)} %get-tuple-element.69.refs_0_), channel_id=1, source_target_pairs={{0,8},{1,9},{2,10},{3,11},{4,12},{5,13},{6,14},{7,15},{8,16},{9,17... | collective-permute-start | bytes 393224 | tf_op jit(solution)/shard_map/ppermute | solution.py:40
  74.3 5.6 %collective-permute-start.29 = (bf16[128,512]{1,0:T(8,128)(2,1)S(1)}, bf16[128,512]{1,0:T(8,128)(2,1)S(1)}, u32[]{:S(2)}, u32[]{:S(2)}) collective-permute-start(bf16[128,512]{1,0:T(8,128)(2,1)S(1)} %get-tuple-element.69.refs_0_), channel_id=1, source_target_pairs={{0,24},{1,25},{2,26},{3,27},{4,28},{5,29},{6,30},{7,31},{8,0},{9,1... | collective-permute-start | bytes 393224 | tf_op jit(solution)/shard_map/ppermute | solution.py:40
  74.7 5.3 %collective-permute-start.28 = (bf16[128,512]{1,0:T(8,128)(2,1)S(1)}, bf16[128,512]{1,0:T(8,128)(2,1)S(1)}, u32[]{:S(2)}, u32[]{:S(2)}) collective-permute-start(bf16[128,512]{1,0:T(8,128)(2,1)S(1)} %get-tuple-element.69.refs_0_), channel_id=1, source_target_pairs={{0,4},{1,5},{2,6},{3,7},{4,0},{5,1},{6,2},{7,3},{8,12},{9,13},{10,... | collective-permute-start | bytes 393224 | tf_op jit(solution)/shard_map/ppermute | solution.py:40
  80.0 3.2 %collective-permute-start.32 = (bf16[128,512]{1,0:T(8,128)(2,1)S(1)}, bf16[128,512]{1,0:T(8,128)(2,1)S(1)}, u32[]{:S(2)}, u32[]{:S(2)}) collective-permute-start(bf16[128,512]{1,0:T(8,128)(2,1)S(1)} %collective-permute-done.29.refs_1_), channel_id=1, source_target_pairs={{0,4},{1,5},{2,6},{3,7},{4,0},{5,1},{6,2},{7,3},{8,12},{9,13},{10,... | collective-permute-start | bytes 393224 | tf_op jit(solution)/shard_map/ppermute | solution.py:40
  81.6 1.3 %collective-permute-start.34 = (bf16[128,512]{1,0:T(8,128)(2,1)S(1)}, bf16[128,512]{1,0:T(8,128)(2,1)S(1)}, u32[]{:S(2)}, u32[]{:S(2)}) collective-permute-start(bf16[128,512]{1,0:T(8,128)(2,1)S(1)} %collective-permute-done.31.refs_3_), channel_id=1, source_target_pairs={{0,4},{1,5},{2,6},{3,7},{4,0},{5,1},{6,2},{7,3},{8,12},{9,13},{10,... | collective-permute-start | bytes 393224 | tf_op jit(solution)/shard_map/ppermute | solution.py:40
  81.7 1.4 %collective-permute-start.33 = (bf16[128,512]{1,0:T(8,128)(2,1)S(1)}, bf16[128,512]{1,0:T(8,128)(2,1)S(1)}, u32[]{:S(2)}, u32[]{:S(2)}) collective-permute-start(bf16[128,512]{1,0:T(8,128)(2,1)S(1)} %collective-permute-done.30.refs_2_), channel_id=1, source_target_pairs={{0,4},{1,5},{2,6},{3,7},{4,0},{5,1},{6,2},{7,3},{8,12},{9,13},{10,... | collective-permute-start | bytes 393224 | tf_op jit(solution)/shard_map/ppermute | solution.py:40
  86.3 6.3 %collective-permute-start.38 = (bf16[64,1024]{1,0:T(8,128)(2,1)S(1)}, bf16[64,1024]{1,0:T(8,128)(2,1)S(1)}, u32[]{:S(2)}, u32[]{:S(2)}) collective-permute-start(bf16[64,1024]{1,0:T(8,128)(2,1)S(1)} %get-tuple-element.77), channel_id=1, source_target_pairs={{0,2},{1,3},{2,0},{3,1},{4,6},{5,7},{6,4},{7,5},{8,10},{9,11},{10,... | collective-permute-start | bytes 393224 | tf_op jit(solution)/shard_map/ppermute | solution.py:40
  86.7 10.0 %collective-permute-start.39 = (bf16[64,1024]{1,0:T(8,128)(2,1)S(1)}, bf16[64,1024]{1,0:T(8,128)(2,1)S(1)}, u32[]{:S(2)}, u32[]{:S(2)}) collective-permute-start(bf16[64,1024]{1,0:T(8,128)(2,1)S(1)} %get-tuple-element.78), channel_id=1, source_target_pairs={{0,1},{1,2},{2,3},{3,0},{4,5},{5,6},{6,7},{7,4},{8,9},{9,10},{10,1... | collective-permute-start | bytes 393224 | tf_op jit(solution)/shard_map/ppermute | solution.py:40
  87.4 9.3 %collective-permute-start.40 = (bf16[64,1024]{1,0:T(8,128)(2,1)S(1)}, bf16[64,1024]{1,0:T(8,128)(2,1)S(1)}, u32[]{:S(2)}, u32[]{:S(2)}) collective-permute-start(bf16[64,1024]{1,0:T(8,128)(2,1)S(1)} %get-tuple-element.79), channel_id=1, source_target_pairs={{0,3},{1,0},{2,1},{3,2},{4,7},{5,4},{6,5},{7,6},{8,11},{9,8},{10,9... | collective-permute-start | bytes 393224 | tf_op jit(solution)/shard_map/ppermute | solution.py:40
  89.4 8.9 %collective-permute-start.35 = (bf16[64,1024]{1,0:T(8,128)(2,1)S(1)}, bf16[64,1024]{1,0:T(8,128)(2,1)S(1)}, u32[]{:S(2)}, u32[]{:S(2)}) collective-permute-start(bf16[64,1024]{1,0:T(8,128)(2,1)S(1)} %get-tuple-element.73), channel_id=1, source_target_pairs={{0,2},{1,3},{2,0},{3,1},{4,6},{5,7},{6,4},{7,5},{8,10},{9,11},{10,... | collective-permute-start | bytes 393224 | tf_op jit(solution)/shard_map/ppermute | solution.py:40
  90.9 10.8 %collective-permute-start.36 = (bf16[64,1024]{1,0:T(8,128)(2,1)S(1)}, bf16[64,1024]{1,0:T(8,128)(2,1)S(1)}, u32[]{:S(2)}, u32[]{:S(2)}) collective-permute-start(bf16[64,1024]{1,0:T(8,128)(2,1)S(1)} %get-tuple-element.74), channel_id=1, source_target_pairs={{0,1},{1,2},{2,3},{3,0},{4,5},{5,6},{6,7},{7,4},{8,9},{9,10},{10,1... | collective-permute-start | bytes 393224 | tf_op jit(solution)/shard_map/ppermute | solution.py:40
  92.7 9.0 %collective-permute-start.37 = (bf16[64,1024]{1,0:T(8,128)(2,1)S(1)}, bf16[64,1024]{1,0:T(8,128)(2,1)S(1)}, u32[]{:S(2)}, u32[]{:S(2)}) collective-permute-start(bf16[64,1024]{1,0:T(8,128)(2,1)S(1)} %get-tuple-element.75), channel_id=1, source_target_pairs={{0,3},{1,0},{2,1},{3,2},{4,7},{5,4},{6,5},{7,6},{8,11},{9,8},{10,9... | collective-permute-start | bytes 393224 | tf_op jit(solution)/shard_map/ppermute | solution.py:40
  96.8 4.9 %collective-permute-start.41 = (bf16[64,1024]{1,0:T(8,128)(2,1)S(1)}, bf16[64,1024]{1,0:T(8,128)(2,1)S(1)}, u32[]{:S(2)}, u32[]{:S(2)}) collective-permute-start(bf16[64,1024]{1,0:T(8,128)(2,1)S(1)} %last_cross.1), channel_id=1, source_target_pairs={{0,32},{1,33},{2,34},{3,35},{4,36},{5,37},{6,38},{7,39},{8,40},{9,... | collective-permute-start | bytes 393224 | tf_op jit(solution)/shard_map/ppermute | solution.py:40

commit v8 on v7

--- a/solution.py
+++ b/solution.py
@@ -427,9 +427,8 @@
     rope = tables(positions_of)
     other_from = {s: send(other, by_tp=s) for s in (3, 1, 2)}
     own_from[0], other_from[0] = own, other
-    pieces = [(s, 0, [own_from[s], other_from[s]]) for s in (1, 3, 0, 2)]
-    carry = project_kv(pieces[:2], width, gain, wk, wv, None, None)
-    kv, r = project_kv(pieces[2:], width, gain, wk, wv, carry, rope)
+    pieces = [(s, 0, [own_from[s], other_from[s]]) for s in (0, 1, 3, 2)]
+    kv, r = project_kv(pieces, width, gain, wk, wv, None, rope)
     chunked = [[(at, s, 0, 2 * half) for s in SHIFTS] for at in starts]
     got, attended = mix(
         kv,

time: 103 us -> 101 us (0.981)
  starting transfers between devices: 53.8 us -> 51.5 us
  waiting for transfers between devices: 34 us -> 35.2 us
    ppermute x42, starting transfers between devices: 53.8 us -> 51.5 us  [send(): return lax.ppermute(block, AXES, route)]
    ppermute x42, waiting for transfers between devices: 34 us -> 35.2 us  [send(): return lax.ppermute(block, AXES, route)]
    pallas_call x16 -> x15, Pallas kernels: 13.4 us -> 13.2 us  [in_vmem(): pl.pallas_call(kernel, in_specs=specs, out_specs=[pl.BlockSpec(memory_spa...]
  transfers between devices with their start and end apart: 42 -> 42, of which waited for: 22 -> 22; matrix products, arithmetic and copies ran while one was open for 1% -> 1% of each run, Pallas kernels for 5% -> 4%
where the time goes in v8:
time: 101 us
  starting transfers between devices  51.5 us (51%)
  waiting for transfers between devices  35.2 us (35%)
  Pallas kernels  13.2 us (13%)
    ppermute x42, starting transfers between devices, send(): return lax.ppermute(block, AXES, route)  51.5 us
    ppermute x42, waiting for transfers between devices, send(): return lax.ppermute(block, AXES, route)  35.2 us
    pallas_call x15, Pallas kernels, in_vmem(): pl.pallas_call(kernel, in_specs=specs, out_specs=[pl.BlockSpec(memory_spa...  13.2 us
  transfers between devices with their start and end apart: 42, of which 22 were waited for; matrix products, arithmetic and copies ran while one was open for 1% of the time, Pallas kernels for 4%

profile of v8, /device:TPU:1, one launch (start us, length us, event | category | flops | bytes accessed | tf_op | source)
XLA Modules:
  0.0 101.1 jit_solution(17380388202431661366)
XLA Ops:
  0.0 1.0 rows_of_segments.1
  1.0 3.8 %collective-permute-start.2 = (bf16[64,1024]{1,0:T(8,128)(2,1)S(1)}, bf16[64,1024]{1,0:T(8,128)(2,1)S(1)}, u32[]{:S(2)}, u32[]{:S(2)}) collective-permute-start(bf16[64,1024]{1,0:T(8,128)(2,1)S(1)} %get-tuple-element.41.refs_0_.a), channel_id=1, source_target_pairs={{0,2},{1,3},{2,0},{3,1},{4,6},{5,7},{6,4},{7,5},{8,10},{9,11},{10,... | collective-permute-start | bytes 393224 | tf_op jit(solution)/shard_map/ppermute | solution.py:40
  4.8 0.8 collective-permute-start.1
  5.6 0.7 collective-permute-start
  6.3 1.2 %collective-permute-start.3 = (bf16[64,1024]{1,0:T(8,128)(2,1)S(1)}, bf16[64,1024]{1,0:T(8,128)(2,1)S(1)}, u32[]{:S(2)}, u32[]{:S(2)}) collective-permute-start(bf16[64,1024]{1,0:T(8,128)(2,1)S(1)} %get-tuple-element.42), channel_id=1, source_target_pairs={{0,32},{1,33},{2,34},{3,35},{4,36},{5,37},{6,38},{7,39},{8,40},{9,... | collective-permute-start | bytes 393224 | tf_op jit(solution)/shard_map/ppermute | solution.py:40
  7.8 2.4 %collective-permute-done.3.refs_4_.b = bf16[64,1024]{1,0:T(8,128)(2,1)S(1)} collective-permute-done((bf16[64,1024]{1,0:T(8,128)(2,1)S(1)}, bf16[64,1024]{1,0:T(8,128)(2,1)S(1)}, u32[]{:S(2)}, u32[]{:S(2)}) %collective-permute-start.3) | collective-permute-done | bytes 131104 | tf_op jit(solution)/shard_map/ppermute | solution.py:40
  10.1 1.0 %collective-permute-start.6 = (bf16[64,1024]{1,0:T(8,128)(2,1)S(1)}, bf16[64,1024]{1,0:T(8,128)(2,1)S(1)}, u32[]{:S(2)}, u32[]{:S(2)}) collective-permute-start(bf16[64,1024]{1,0:T(8,128)(2,1)S(1)} %collective-permute-done.3.refs_4_.b), channel_id=1, source_target_pairs={{0,2},{1,3},{2,0},{3,1},{4,6},{5,7},{6,4},{7,5},{8,10},{9,11},{10,... | collective-permute-start | bytes 393224 | tf_op jit(solution)/shard_map/ppermute | solution.py:40
  11.1 2.1 %collective-permute-start.5 = (bf16[64,1024]{1,0:T(8,128)(2,1)S(1)}, bf16[64,1024]{1,0:T(8,128)(2,1)S(1)}, u32[]{:S(2)}, u32[]{:S(2)}) collective-permute-start(bf16[64,1024]{1,0:T(8,128)(2,1)S(1)} %collective-permute-done.3.refs_4_.b), channel_id=1, source_target_pairs={{0,3},{1,0},{2,1},{3,2},{4,7},{5,4},{6,5},{7,6},{8,11},{9,8},{10,9... | collective-permute-start | bytes 393224 | tf_op jit(solution)/shard_map/ppermute | solution.py:40
  13.2 0.3 fusion.5
  13.9 1.6 %collective-permute-done.6.refs_7_ = bf16[64,1024]{1,0:T(8,128)(2,1)S(1)} collective-permute-done((bf16[64,1024]{1,0:T(8,128)(2,1)S(1)}, bf16[64,1024]{1,0:T(8,128)(2,1)S(1)}, u32[]{:S(2)}, u32[]{:S(2)}) %collective-permute-start.6) | collective-permute-done | bytes 131104 | tf_op jit(solution)/shard_map/ppermute | solution.py:40
  15.4 1.3 %collective-permute-done.5.refs_6_ = bf16[64,1024]{1,0:T(8,128)(2,1)S(1)} collective-permute-done((bf16[64,1024]{1,0:T(8,128)(2,1)S(1)}, bf16[64,1024]{1,0:T(8,128)(2,1)S(1)}, u32[]{:S(2)}, u32[]{:S(2)}) %collective-permute-start.5) | collective-permute-done | bytes 131104 | tf_op jit(solution)/shard_map/ppermute | solution.py:40
  16.7 3.3 %collective-permute-done.4.refs_5_ = bf16[64,1024]{1,0:T(8,128)(2,1)S(1)} collective-permute-done((bf16[64,1024]{1,0:T(8,128)(2,1)S(1)}, bf16[64,1024]{1,0:T(8,128)(2,1)S(1)}, u32[]{:S(2)}, u32[]{:S(2)}) %collective-permute-start.4) | collective-permute-done | bytes 131104 | tf_op jit(solution)/shard_map/ppermute | solution.py:40
  20.0 0.9 project_kv.3
  20.9 3.7 %collective-permute-start.10 = (bf16[128,512]{1,0:T(8,128)(2,1)S(1)}, bf16[128,512]{1,0:T(8,128)(2,1)S(1)}, u32[]{:S(2)}, u32[]{:S(2)}) collective-permute-start(bf16[128,512]{1,0:T(8,128)(2,1)S(1)} %get-tuple-element.47.refs_0_), channel_id=1, source_target_pairs={{0,16},{1,17},{2,18},{3,19},{4,20},{5,21},{6,22},{7,23},{8,24},{9,... | collective-permute-start | bytes 393224 | tf_op jit(solution)/shard_map/ppermute | solution.py:40
  24.6 0.7 collective-permute-start.9
  25.3 1.9 %collective-permute-start.8 = (bf16[128,512]{1,0:T(8,128)(2,1)S(1)}, bf16[128,512]{1,0:T(8,128)(2,1)S(1)}, u32[]{:S(2)}, u32[]{:S(2)}) collective-permute-start(bf16[128,512]{1,0:T(8,128)(2,1)S(1)} %get-tuple-element.47.refs_0_), channel_id=1, source_target_pairs={{0,24},{1,25},{2,26},{3,27},{4,28},{5,29},{6,30},{7,31},{8,0},{9,1... | collective-permute-start | bytes 393224 | tf_op jit(solution)/shard_map/ppermute | solution.py:40
  27.3 3.6 %collective-permute-start.7 = (bf16[128,512]{1,0:T(8,128)(2,1)S(1)}, bf16[128,512]{1,0:T(8,128)(2,1)S(1)}, u32[]{:S(2)}, u32[]{:S(2)}) collective-permute-start(bf16[128,512]{1,0:T(8,128)(2,1)S(1)} %get-tuple-element.47.refs_0_), channel_id=1, source_target_pairs={{0,4},{1,5},{2,6},{3,7},{4,0},{5,1},{6,2},{7,3},{8,12},{9,13},{10,... | collective-permute-start | bytes 393224 | tf_op jit(solution)/shard_map/ppermute | solution.py:40
  30.8 1.4 %project_q.2.q = bf16[128,1024]{1,0:T(8,128)(2,1)S(1)} custom-call(bf16[64,1024]{1,0:T(8,128)(2,1)S(1)} %get-tuple-element.41.refs_0_.a, bf16[64,1024]{1,0:T(8,128)(2,1)S(1)} %collective-permute-done.refs_1_, bf16[64,1024]{1,0:T(8,128)(2,1)S(1)} %collective-permute-done.1.refs_2_, bf16[64,1024]{1,0:T(8,128)(2,1)S(1)} %collective-permute-done.2.refs_3_, ...), custom_call_target="tpu_custom_call" | custom-call | flops 5673741824 | bytes 9585152 | tf_op jit(solution)/shard_map/project_q/pallas_call | solution.py:47
  32.3 1.3 %collective-permute-start.13 = (bf16[128,512]{1,0:T(8,128)(2,1)S(1)}, bf16[128,512]{1,0:T(8,128)(2,1)S(1)}, u32[]{:S(2)}, u32[]{:S(2)}) collective-permute-start(bf16[128,512]{1,0:T(8,128)(2,1)S(1)} %collective-permute-done.10.refs_3_), channel_id=1, source_target_pairs={{0,4},{1,5},{2,6},{3,7},{4,0},{5,1},{6,2},{7,3},{8,12},{9,13},{10,... | collective-permute-start | bytes 393224 | tf_op jit(solution)/shard_map/ppermute | solution.py:40
  33.8 0.3 collective-permute-start.11
  34.1 0.5 collective-permute-done.13.refs_7_
  34.6 0.4 collective-permute-done.12.refs_6_
  34.9 0.2 collective-permute-done.11.refs_5_
  35.1 2.5 %attend_and_project.2 = (bf16[128,512]{1,0:T(8,128)(2,1)S(1)}, bf16[128,512]{1,0:T(8,128)(2,1)S(1)}, bf16[128,512]{1,0:T(8,128)(2,1)S(1)}, bf16[128,512]{1,0:T(8,128)(2,1)S(1)}, bf16[128,1024]{1,0:T(8,128)(2,1)S(1)}) custom-call(bf16[128,1024]{1,0:T(8,128)(2,1)S(1)} %project_q.2.q, s32[64,1]{1,0:T(8,128)S(1)} %iota_add_fusion.qpos, s32[1,512]{1,0:T(1,128)S(1)} %bitcast.3, ...), custom_call_target="tpu_custom_call" | custom-call | flops 10676395008 | bytes 9701632 | tf_op jit(solution)/shard_map/attend_and_project/pallas_call | solution.py:47
  37.6 0.4 collective-permute-start.14
  38.2 2.5 %collective-permute-start.16 = (bf16[128,512]{1,0:T(8,128)(2,1)S(1)}, bf16[128,512]{1,0:T(8,128)(2,1)S(1)}, u32[]{:S(2)}, u32[]{:S(2)}) collective-permute-start(bf16[128,512]{1,0:T(8,128)(2,1)S(1)} %get-tuple-element.55), channel_id=1, source_target_pairs={{0,3},{1,0},{2,1},{3,2},{4,7},{5,4},{6,5},{7,6},{8,11},{9,8},{10,9... | collective-permute-start | bytes 393224 | tf_op jit(solution)/shard_map/ppermute | solution.py:40
  40.8 0.8 project_out.1
  41.5 1.5 %collective-permute-start.21 = (bf16[128,512]{1,0:T(8,128)(2,1)S(1)}, bf16[128,512]{1,0:T(8,128)(2,1)S(1)}, u32[]{:S(2)}, u32[]{:S(2)}) collective-permute-start(bf16[128,512]{1,0:T(8,128)(2,1)S(1)} %get-tuple-element.58), channel_id=1, source_target_pairs={{0,2},{1,3},{2,0},{3,1},{4,6},{5,7},{6,4},{7,5},{8,10},{9,11},{10,... | collective-permute-start | bytes 393224 | tf_op jit(solution)/shard_map/ppermute | solution.py:40
  43.0 0.9 collective-permute-done.14.refs_0_
  44.0 1.7 %collective-permute-start.23 = (bf16[128,512]{1,0:T(8,128)(2,1)S(1)}, bf16[128,512]{1,0:T(8,128)(2,1)S(1)}, u32[]{:S(2)}, u32[]{:S(2)}) collective-permute-start(bf16[128,512]{1,0:T(8,128)(2,1)S(1)} %get-tuple-element.60), channel_id=1, source_target_pairs={{0,3},{1,0},{2,1},{3,2},{4,7},{5,4},{6,5},{7,6},{8,11},{9,8},{10,9... | collective-permute-start | bytes 393224 | tf_op jit(solution)/shard_map/ppermute | solution.py:40
  45.7 2.3 %collective-permute-done.15.refs_1_ = bf16[128,512]{1,0:T(8,128)(2,1)S(1)} collective-permute-done((bf16[128,512]{1,0:T(8,128)(2,1)S(1)}, bf16[128,512]{1,0:T(8,128)(2,1)S(1)}, u32[]{:S(2)}, u32[]{:S(2)}) %collective-permute-start.15) | collective-permute-done | bytes 131104 | tf_op jit(solution)/shard_map/ppermute | solution.py:40
  48.1 2.6 %collective-permute-start.17 = (bf16[128,512]{1,0:T(8,128)(2,1)S(1)}, bf16[128,512]{1,0:T(8,128)(2,1)S(1)}, u32[]{:S(2)}, u32[]{:S(2)}) collective-permute-start(bf16[128,512]{1,0:T(8,128)(2,1)S(1)} %add_parts.2), channel_id=1, source_target_pairs={{0,96},{1,97},{2,98},{3,99},{4,100},{5,101},{6,102},{7,103},{8,104... | collective-permute-start | bytes 393224 | tf_op jit(solution)/shard_map/ppermute | solution.py:40
  50.9 2.0 %collective-permute-done.22.refs_1_ = bf16[128,512]{1,0:T(8,128)(2,1)S(1)} collective-permute-done((bf16[128,512]{1,0:T(8,128)(2,1)S(1)}, bf16[128,512]{1,0:T(8,128)(2,1)S(1)}, u32[]{:S(2)}, u32[]{:S(2)}) %collective-permute-start.22) | collective-permute-done | bytes 131104 | tf_op jit(solution)/shard_map/ppermute | solution.py:40
  53.0 2.6 %collective-permute-start.24 = (bf16[128,512]{1,0:T(8,128)(2,1)S(1)}, bf16[128,512]{1,0:T(8,128)(2,1)S(1)}, u32[]{:S(2)}, u32[]{:S(2)}) collective-permute-start(bf16[128,512]{1,0:T(8,128)(2,1)S(1)} %add_parts.3), channel_id=1, source_target_pairs={{0,96},{1,97},{2,98},{3,99},{4,100},{5,101},{6,102},{7,103},{8,104... | collective-permute-start | bytes 393224 | tf_op jit(solution)/shard_map/ppermute | solution.py:40
  55.6 1.5 %collective-permute-start.18 = (bf16[128,512]{1,0:T(8,128)(2,1)S(1)}, bf16[128,512]{1,0:T(8,128)(2,1)S(1)}, u32[]{:S(2)}, u32[]{:S(2)}) collective-permute-start(bf16[128,512]{1,0:T(8,128)(2,1)S(1)} %collective-permute-done.17.refs_0_), channel_id=1, source_target_pairs={{0,1},{1,2},{2,3},{3,0},{4,5},{5,6},{6,7},{7,4},{8,9},{9,10},{10,1... | collective-permute-start | bytes 393224 | tf_op jit(solution)/shard_map/ppermute | solution.py:40
  57.0 0.7 collective-permute-start.27
  57.8 2.0 %collective-permute-done.24.refs_0_.refs_4_ = bf16[128,512]{1,0:T(8,128)(2,1)S(1)} collective-permute-done((bf16[128,512]{1,0:T(8,128)(2,1)S(1)}, bf16[128,512]{1,0:T(8,128)(2,1)S(1)}, u32[]{:S(2)}, u32[]{:S(2)}) %collective-permute-start.24) | collective-permute-done | bytes 131104 | tf_op jit(solution)/shard_map/ppermute | solution.py:40
  59.9 1.3 %collective-permute-start.25 = (bf16[128,512]{1,0:T(8,128)(2,1)S(1)}, bf16[128,512]{1,0:T(8,128)(2,1)S(1)}, u32[]{:S(2)}, u32[]{:S(2)}) collective-permute-start(bf16[128,512]{1,0:T(8,128)(2,1)S(1)} %collective-permute-done.24.refs_0_.refs_4_), channel_id=1, source_target_pairs={{0,1},{1,2},{2,3},{3,0},{4,5},{5,6},{6,7},{7,4},{8,9},{9,10},{10,1... | collective-permute-start | bytes 393224 | tf_op jit(solution)/shard_map/ppermute | solution.py:40
  61.3 2.4 %collective-permute-done.19.refs_2_ = bf16[128,512]{1,0:T(8,128)(2,1)S(1)} collective-permute-done((bf16[128,512]{1,0:T(8,128)(2,1)S(1)}, bf16[128,512]{1,0:T(8,128)(2,1)S(1)}, u32[]{:S(2)}, u32[]{:S(2)}) %collective-permute-start.19) | collective-permute-done | bytes 131104 | tf_op jit(solution)/shard_map/ppermute | solution.py:40
  63.7 0.5 project_kv.4
  64.2 0.4 collective-permute-done.27.refs_3_.refs_7_
  64.6 0.9 collective-permute-done.26.refs_2_.refs_6_
  65.5 3.1 %collective-permute-done.25.refs_1_.refs_5_ = bf16[128,512]{1,0:T(8,128)(2,1)S(1)} collective-permute-done((bf16[128,512]{1,0:T(8,128)(2,1)S(1)}, bf16[128,512]{1,0:T(8,128)(2,1)S(1)}, u32[]{:S(2)}, u32[]{:S(2)}) %collective-permute-start.25) | collective-permute-done | bytes 131104 | tf_op jit(solution)/shard_map/ppermute | solution.py:40
  68.6 0.6 project_kv.5
  69.1 1.5 %collective-permute-start.31 = (bf16[128,512]{1,0:T(8,128)(2,1)S(1)}, bf16[128,512]{1,0:T(8,128)(2,1)S(1)}, u32[]{:S(2)}, u32[]{:S(2)}) collective-permute-start(bf16[128,512]{1,0:T(8,128)(2,1)S(1)} %get-tuple-element.65.refs_0_), channel_id=1, source_target_pairs={{0,16},{1,17},{2,18},{3,19},{4,20},{5,21},{6,22},{7,23},{8,24},{9,... | collective-permute-start | bytes 393224 | tf_op jit(solution)/shard_map/ppermute | solution.py:40
  70.6 2.4 %collective-permute-start.30 = (bf16[128,512]{1,0:T(8,128)(2,1)S(1)}, bf16[128,512]{1,0:T(8,128)(2,1)S(1)}, u32[]{:S(2)}, u32[]{:S(2)}) collective-permute-start(bf16[128,512]{1,0:T(8,128)(2,1)S(1)} %get-tuple-element.65.refs_0_), channel_id=1, source_target_pairs={{0,8},{1,9},{2,10},{3,11},{4,12},{5,13},{6,14},{7,15},{8,16},{9,17... | collective-permute-start | bytes 393224 | tf_op jit(solution)/shard_map/ppermute | solution.py:40
  73.0 0.3 collective-permute-start.29
  73.3 2.4 %collective-permute-start.28 = (bf16[128,512]{1,0:T(8,128)(2,1)S(1)}, bf16[128,512]{1,0:T(8,128)(2,1)S(1)}, u32[]{:S(2)}, u32[]{:S(2)}) collective-permute-start(bf16[128,512]{1,0:T(8,128)(2,1)S(1)} %get-tuple-element.65.refs_0_), channel_id=1, source_target_pairs={{0,4},{1,5},{2,6},{3,7},{4,0},{5,1},{6,2},{7,3},{8,12},{9,13},{10,... | collective-permute-start | bytes 393224 | tf_op jit(solution)/shard_map/ppermute | solution.py:40
  75.7 1.4 %project_q.3.q = bf16[128,1024]{1,0:T(8,128)(2,1)S(1)} custom-call(bf16[128,512]{1,0:T(8,128)(2,1)S(1)} %collective-permute-done.17.refs_0_, bf16[128,512]{1,0:T(8,128)(2,1)S(1)} %collective-permute-done.18.refs_1_, bf16[128,512]{1,0:T(8,128)(2,1)S(1)} %collective-permute-done.19.refs_2_, bf16[128,512]{1,0:T(8,128)(2,1)S(1)} %collective-permute-done.20.refs_3_, ...), custom_call_target="tpu_custom_call" | custom-call | flops 5673741824 | bytes 9585152 | tf_op jit(solution)/shard_map/project_q/pallas_call | solution.py:47
  77.1 1.0 collective-permute-done.29.refs_1_
  78.0 2.3 %collective-permute-start.32 = (bf16[128,512]{1,0:T(8,128)(2,1)S(1)}, bf16[128,512]{1,0:T(8,128)(2,1)S(1)}, u32[]{:S(2)}, u32[]{:S(2)}) collective-permute-start(bf16[128,512]{1,0:T(8,128)(2,1)S(1)} %collective-permute-done.29.refs_1_), channel_id=1, source_target_pairs={{0,4},{1,5},{2,6},{3,7},{4,0},{5,1},{6,2},{7,3},{8,12},{9,13},{10,... | collective-permute-start | bytes 393224 | tf_op jit(solution)/shard_map/ppermute | solution.py:40
  80.4 0.4 collective-permute-start.33
  80.8 0.8 collective-permute-done.34.refs_7_
  81.8 3.2 %attend_and_project.3 = (bf16[64,1024]{1,0:T(8,128)(2,1)S(1)}, bf16[64,1024]{1,0:T(8,128)(2,1)S(1)}, bf16[64,1024]{1,0:T(8,128)(2,1)S(1)}, bf16[64,1024]{1,0:T(8...) custom-call(bf16[128,1024]{1,0:T(8,128)(2,1)S(1)} %project_q.3.q, ...), custom_call_target="tpu_custom_call" | custom-call | flops 10676395008 | bytes 9701632 | tf_op jit(solution)/shard_map/attend_and_project/pallas_call | solution.py:47
  85.0 0.3 collective-permute-start.38
  85.3 0.9 collective-permute-start.39
  86.1 1.8 %collective-permute-start.40 = (bf16[64,1024]{1,0:T(8,128)(2,1)S(1)}, bf16[64,1024]{1,0:T(8,128)(2,1)S(1)}, u32[]{:S(2)}, u32[]{:S(2)}) collective-permute-start(bf16[64,1024]{1,0:T(8,128)(2,1)S(1)} %get-tuple-element.75), channel_id=1, source_target_pairs={{0,3},{1,0},{2,1},{3,2},{4,7},{5,4},{6,5},{7,6},{8,11},{9,8},{10,9... | collective-permute-start | bytes 393224 | tf_op jit(solution)/shard_map/ppermute | solution.py:40
  88.0 1.6 %collective-permute-start.35 = (bf16[64,1024]{1,0:T(8,128)(2,1)S(1)}, bf16[64,1024]{1,0:T(8,128)(2,1)S(1)}, u32[]{:S(2)}, u32[]{:S(2)}) collective-permute-start(bf16[64,1024]{1,0:T(8,128)(2,1)S(1)} %get-tuple-element.69), channel_id=1, source_target_pairs={{0,2},{1,3},{2,0},{3,1},{4,6},{5,7},{6,4},{7,5},{8,10},{9,11},{10,... | collective-permute-start | bytes 393224 | tf_op jit(solution)/shard_map/ppermute | solution.py:40
  89.6 1.8 %collective-permute-done.38.refs_0_ = bf16[64,1024]{1,0:T(8,128)(2,1)S(1)} collective-permute-done((bf16[64,1024]{1,0:T(8,128)(2,1)S(1)}, bf16[64,1024]{1,0:T(8,128)(2,1)S(1)}, u32[]{:S(2)}, u32[]{:S(2)}) %collective-permute-start.38) | collective-permute-done | bytes 131104 | tf_op jit(solution)/shard_map/ppermute | solution.py:40
  91.4 0.9 collective-permute-start.37
  92.3 2.9 %collective-permute-done.39.refs_1_ = bf16[64,1024]{1,0:T(8,128)(2,1)S(1)} collective-permute-done((bf16[64,1024]{1,0:T(8,128)(2,1)S(1)}, bf16[64,1024]{1,0:T(8,128)(2,1)S(1)}, u32[]{:S(2)}, u32[]{:S(2)}) %collective-permute-start.39) | collective-permute-done | bytes 131104 | tf_op jit(solution)/shard_map/ppermute | solution.py:40
  95.4 1.6 %collective-permute-done.35.refs_0_ = bf16[64,1024]{1,0:T(8,128)(2,1)S(1)} collective-permute-done((bf16[64,1024]{1,0:T(8,128)(2,1)S(1)}, bf16[64,1024]{1,0:T(8,128)(2,1)S(1)}, u32[]{:S(2)}, u32[]{:S(2)}) %collective-permute-start.35) | collective-permute-done | bytes 131104 | tf_op jit(solution)/shard_map/ppermute | solution.py:40
  97.0 3.3 %collective-permute-done.36.refs_1_ = bf16[64,1024]{1,0:T(8,128)(2,1)S(1)} collective-permute-done((bf16[64,1024]{1,0:T(8,128)(2,1)S(1)}, bf16[64,1024]{1,0:T(8,128)(2,1)S(1)}, u32[]{:S(2)}, u32[]{:S(2)}) %collective-permute-start.36) | collective-permute-done | bytes 131104 | tf_op jit(solution)/shard_map/ppermute | solution.py:40
  100.3 0.8 finish.1
  (72 shorter events, 2.0 us)
Async XLA Ops:
  0.0 13.2 %copy-start.2 = (bf16[1,4096]{1,0:T(2,128)(2,1)S(1)}, bf16[1,4096]{1,0:T(2,128)(2,1)}, u32[]{:S(2)}) copy-start(bf16[1,4096]{1,0:T(2,128)(2,1)} %g) | copy-start | bytes 24580
  1.0 19.0 %copy-start = (bf16[1,4096,256]{2,1,0:T(8,128)(2,1)S(1)}, bf16[1,4096,256]{2,1,0:T(8,128)(2,1)}, u32[]{:S(2)}) copy-start(bf16[1,4096,256]{2,1,0:T(8,128)(2,1)} %refs_5_.3) | copy-start | bytes 6291460
  1.0 12.5 %collective-permute-start.2 = (bf16[64,1024]{1,0:T(8,128)(2,1)S(1)}, bf16[64,1024]{1,0:T(8,128)(2,1)S(1)}, u32[]{:S(2)}, u32[]{:S(2)}) collective-permute-start(bf16[64,1024]{1,0:T(8,128)(2,1)S(1)} %get-tuple-element.41.refs_0_.a), channel_id=1, source_target_pairs={{0,2},{1,3},{2,0},{3,1},{4,6},{5,7},{6,4},{7,5},{8,10},{9,11},{10,... | collective-permute-start | bytes 393224 | tf_op jit(solution)/shard_map/ppermute | solution.py:40
  4.8 9.0 %collective-permute-start.1 = (bf16[64,1024]{1,0:T(8,128)(2,1)S(1)}, bf16[64,1024]{1,0:T(8,128)(2,1)S(1)}, u32[]{:S(2)}, u32[]{:S(2)}) collective-permute-start(bf16[64,1024]{1,0:T(8,128)(2,1)S(1)} %get-tuple-element.41.refs_0_.a), channel_id=1, source_target_pairs={{0,3},{1,0},{2,1},{3,2},{4,7},{5,4},{6,5},{7,6},{8,11},{9,8},{10,9... | collective-permute-start | bytes 393224 | tf_op jit(solution)/shard_map/ppermute | solution.py:40
  5.6 8.2 %collective-permute-start = (bf16[64,1024]{1,0:T(8,128)(2,1)S(1)}, bf16[64,1024]{1,0:T(8,128)(2,1)S(1)}, u32[]{:S(2)}, u32[]{:S(2)}) collective-permute-start(bf16[64,1024]{1,0:T(8,128)(2,1)S(1)} %get-tuple-element.41.refs_0_.a), channel_id=1, source_target_pairs={{0,1},{1,2},{2,3},{3,0},{4,5},{5,6},{6,7},{7,4},{8,9},{9,10},{10,1... | collective-permute-start | bytes 393224 | tf_op jit(solution)/shard_map/ppermute | solution.py:40
  6.3 3.8 %collective-permute-start.3 = (bf16[64,1024]{1,0:T(8,128)(2,1)S(1)}, bf16[64,1024]{1,0:T(8,128)(2,1)S(1)}, u32[]{:S(2)}, u32[]{:S(2)}) collective-permute-start(bf16[64,1024]{1,0:T(8,128)(2,1)S(1)} %get-tuple-element.42), channel_id=1, source_target_pairs={{0,32},{1,33},{2,34},{3,35},{4,36},{5,37},{6,38},{7,39},{8,40},{9,... | collective-permute-start | bytes 393224 | tf_op jit(solution)/shard_map/ppermute | solution.py:40
  7.7 12.3 %copy-start.1 = (bf16[1,4096,256]{2,1,0:T(8,128)(2,1)S(1)}, bf16[1,4096,256]{2,1,0:T(8,128)(2,1)}, u32[]{:S(2)}) copy-start(bf16[1,4096,256]{2,1,0:T(8,128)(2,1)} %refs_6_.3) | copy-start | bytes 6291460
  10.1 5.3 %collective-permute-start.6 = (bf16[64,1024]{1,0:T(8,128)(2,1)S(1)}, bf16[64,1024]{1,0:T(8,128)(2,1)S(1)}, u32[]{:S(2)}, u32[]{:S(2)}) collective-permute-start(bf16[64,1024]{1,0:T(8,128)(2,1)S(1)} %collective-permute-done.3.refs_4_.b), channel_id=1, source_target_pairs={{0,2},{1,3},{2,0},{3,1},{4,6},{5,7},{6,4},{7,5},{8,10},{9,11},{10,... | collective-permute-start | bytes 393224 | tf_op jit(solution)/shard_map/ppermute | solution.py:40
  11.1 5.6 %collective-permute-start.5 = (bf16[64,1024]{1,0:T(8,128)(2,1)S(1)}, bf16[64,1024]{1,0:T(8,128)(2,1)S(1)}, u32[]{:S(2)}, u32[]{:S(2)}) collective-permute-start(bf16[64,1024]{1,0:T(8,128)(2,1)S(1)} %collective-permute-done.3.refs_4_.b), channel_id=1, source_target_pairs={{0,3},{1,0},{2,1},{3,2},{4,7},{5,4},{6,5},{7,6},{8,11},{9,8},{10,9... | collective-permute-start | bytes 393224 | tf_op jit(solution)/shard_map/ppermute | solution.py:40
  13.2 17.6 %slice-start.2 = ((s8[8388608]{0:T(1024)(128)(4,1)}), s8[4194304]{0:T(1024)(128)(4,1)S(1)}, s32[]{:S(2)}) async-start(s8[8388608]{0:T(1024)(128)(4,1)} %bitcast.5), calls=%async_computation.2 | async-start | bytes 8388608
  13.2 17.6 %slice-start.3 = ((s8[8388608]{0:T(1024)(128)(4,1)}), s8[4194304]{0:T(1024)(128)(4,1)S(1)}, s32[]{:S(2)}) async-start(s8[8388608]{0:T(1024)(128)(4,1)} %bitcast.5), calls=%async_computation.3 | async-start | bytes 8388608
  13.6 6.5 %collective-permute-start.4 = (bf16[64,1024]{1,0:T(8,128)(2,1)S(1)}, bf16[64,1024]{1,0:T(8,128)(2,1)S(1)}, u32[]{:S(2)}, u32[]{:S(2)}) collective-permute-start(bf16[64,1024]{1,0:T(8,128)(2,1)S(1)} %collective-permute-done.3.refs_4_.b), channel_id=1, source_target_pairs={{0,1},{1,2},{2,3},{3,0},{4,5},{5,6},{6,7},{7,4},{8,9},{9,10},{10,1... | collective-permute-start | bytes 393224 | tf_op jit(solution)/shard_map/ppermute | solution.py:40
  20.0 15.1 %slice-start = ((s8[8388608]{0:T(1024)(128)(4,1)}), s8[4194304]{0:T(1024)(128)(4,1)S(1)}, s32[]{:S(2)}) async-start(s8[8388608]{0:T(1024)(128)(4,1)} %bitcast.1), calls=%async_computation | async-start | bytes 8388608
  20.9 11.4 %collective-permute-start.10 = (bf16[128,512]{1,0:T(8,128)(2,1)S(1)}, bf16[128,512]{1,0:T(8,128)(2,1)S(1)}, u32[]{:S(2)}, u32[]{:S(2)}) collective-permute-start(bf16[128,512]{1,0:T(8,128)(2,1)S(1)} %get-tuple-element.47.refs_0_), channel_id=1, source_target_pairs={{0,16},{1,17},{2,18},{3,19},{4,20},{5,21},{6,22},{7,23},{8,24},{9,... | collective-permute-start | bytes 393224 | tf_op jit(solution)/shard_map/ppermute | solution.py:40
  24.6 9.0 %collective-permute-start.9 = (bf16[128,512]{1,0:T(8,128)(2,1)S(1)}, bf16[128,512]{1,0:T(8,128)(2,1)S(1)}, u32[]{:S(2)}, u32[]{:S(2)}) collective-permute-start(bf16[128,512]{1,0:T(8,128)(2,1)S(1)} %get-tuple-element.47.refs_0_), channel_id=1, source_target_pairs={{0,8},{1,9},{2,10},{3,11},{4,12},{5,13},{6,14},{7,15},{8,16},{9,17... | collective-permute-start | bytes 393224 | tf_op jit(solution)/shard_map/ppermute | solution.py:40
  25.3 6.9 %collective-permute-start.8 = (bf16[128,512]{1,0:T(8,128)(2,1)S(1)}, bf16[128,512]{1,0:T(8,128)(2,1)S(1)}, u32[]{:S(2)}, u32[]{:S(2)}) collective-permute-start(bf16[128,512]{1,0:T(8,128)(2,1)S(1)} %get-tuple-element.47.refs_0_), channel_id=1, source_target_pairs={{0,24},{1,25},{2,26},{3,27},{4,28},{5,29},{6,30},{7,31},{8,0},{9,1... | collective-permute-start | bytes 393224 | tf_op jit(solution)/shard_map/ppermute | solution.py:40
  27.3 5.0 %collective-permute-start.7 = (bf16[128,512]{1,0:T(8,128)(2,1)S(1)}, bf16[128,512]{1,0:T(8,128)(2,1)S(1)}, u32[]{:S(2)}, u32[]{:S(2)}) collective-permute-start(bf16[128,512]{1,0:T(8,128)(2,1)S(1)} %get-tuple-element.47.refs_0_), channel_id=1, source_target_pairs={{0,4},{1,5},{2,6},{3,7},{4,0},{5,1},{6,2},{7,3},{8,12},{9,13},{10,... | collective-permute-start | bytes 393224 | tf_op jit(solution)/shard_map/ppermute | solution.py:40
  30.8 4.3 %slice-start.1 = ((s8[8388608]{0:T(1024)(128)(4,1)}), s8[4194304]{0:T(1024)(128)(4,1)S(1)}, s32[]{:S(2)}) async-start(s8[8388608]{0:T(1024)(128)(4,1)} %bitcast.1), calls=%async_computation.1 | async-start | bytes 8388608
  32.3 2.3 %collective-permute-start.13 = (bf16[128,512]{1,0:T(8,128)(2,1)S(1)}, bf16[128,512]{1,0:T(8,128)(2,1)S(1)}, u32[]{:S(2)}, u32[]{:S(2)}) collective-permute-start(bf16[128,512]{1,0:T(8,128)(2,1)S(1)} %collective-permute-done.10.refs_3_), channel_id=1, source_target_pairs={{0,4},{1,5},{2,6},{3,7},{4,0},{5,1},{6,2},{7,3},{8,12},{9,13},{10,... | collective-permute-start | bytes 393224 | tf_op jit(solution)/shard_map/ppermute | solution.py:40
  33.6 1.3 %collective-permute-start.12 = (bf16[128,512]{1,0:T(8,128)(2,1)S(1)}, bf16[128,512]{1,0:T(8,128)(2,1)S(1)}, u32[]{:S(2)}, u32[]{:S(2)}) collective-permute-start(bf16[128,512]{1,0:T(8,128)(2,1)S(1)} %collective-permute-done.9.refs_2_), channel_id=1, source_target_pairs={{0,4},{1,5},{2,6},{3,7},{4,0},{5,1},{6,2},{7,3},{8,12},{9,13},{10,... | collective-permute-start | bytes 393224 | tf_op jit(solution)/shard_map/ppermute | solution.py:40
  33.8 1.4 %collective-permute-start.11 = (bf16[128,512]{1,0:T(8,128)(2,1)S(1)}, bf16[128,512]{1,0:T(8,128)(2,1)S(1)}, u32[]{:S(2)}, u32[]{:S(2)}) collective-permute-start(bf16[128,512]{1,0:T(8,128)(2,1)S(1)} %collective-permute-done.8.refs_1_), channel_id=1, source_target_pairs={{0,4},{1,5},{2,6},{3,7},{4,0},{5,1},{6,2},{7,3},{8,12},{9,13},{10,... | collective-permute-start | bytes 393224 | tf_op jit(solution)/shard_map/ppermute | solution.py:40
  37.6 6.4 %collective-permute-start.14 = (bf16[128,512]{1,0:T(8,128)(2,1)S(1)}, bf16[128,512]{1,0:T(8,128)(2,1)S(1)}, u32[]{:S(2)}, u32[]{:S(2)}) collective-permute-start(bf16[128,512]{1,0:T(8,128)(2,1)S(1)} %get-tuple-element.53), channel_id=1, source_target_pairs={{0,2},{1,3},{2,0},{3,1},{4,6},{5,7},{6,4},{7,5},{8,10},{9,11},{10,... | collective-permute-start | bytes 393224 | tf_op jit(solution)/shard_map/ppermute | solution.py:40
  38.0 10.0 %collective-permute-start.15 = (bf16[128,512]{1,0:T(8,128)(2,1)S(1)}, bf16[128,512]{1,0:T(8,128)(2,1)S(1)}, u32[]{:S(2)}, u32[]{:S(2)}) collective-permute-start(bf16[128,512]{1,0:T(8,128)(2,1)S(1)} %get-tuple-element.54), channel_id=1, source_target_pairs={{0,1},{1,2},{2,3},{3,0},{4,5},{5,6},{6,7},{7,4},{8,9},{9,10},{10,1... | collective-permute-start | bytes 393224 | tf_op jit(solution)/shard_map/ppermute | solution.py:40
  38.2 9.8 %collective-permute-start.16 = (bf16[128,512]{1,0:T(8,128)(2,1)S(1)}, bf16[128,512]{1,0:T(8,128)(2,1)S(1)}, u32[]{:S(2)}, u32[]{:S(2)}) collective-permute-start(bf16[128,512]{1,0:T(8,128)(2,1)S(1)} %get-tuple-element.55), channel_id=1, source_target_pairs={{0,3},{1,0},{2,1},{3,2},{4,7},{5,4},{6,5},{7,6},{8,11},{9,8},{10,9... | collective-permute-start | bytes 393224 | tf_op jit(solution)/shard_map/ppermute | solution.py:40
  41.5 9.4 %collective-permute-start.21 = (bf16[128,512]{1,0:T(8,128)(2,1)S(1)}, bf16[128,512]{1,0:T(8,128)(2,1)S(1)}, u32[]{:S(2)}, u32[]{:S(2)}) collective-permute-start(bf16[128,512]{1,0:T(8,128)(2,1)S(1)} %get-tuple-element.58), channel_id=1, source_target_pairs={{0,2},{1,3},{2,0},{3,1},{4,6},{5,7},{6,4},{7,5},{8,10},{9,11},{10,... | collective-permute-start | bytes 393224 | tf_op jit(solution)/shard_map/ppermute | solution.py:40
  43.0 9.9 %collective-permute-start.22 = (bf16[128,512]{1,0:T(8,128)(2,1)S(1)}, bf16[128,512]{1,0:T(8,128)(2,1)S(1)}, u32[]{:S(2)}, u32[]{:S(2)}) collective-permute-start(bf16[128,512]{1,0:T(8,128)(2,1)S(1)} %get-tuple-element.59), channel_id=1, source_target_pairs={{0,1},{1,2},{2,3},{3,0},{4,5},{5,6},{6,7},{7,4},{8,9},{9,10},{10,1... | collective-permute-start | bytes 393224 | tf_op jit(solution)/shard_map/ppermute | solution.py:40
  44.0 8.9 %collective-permute-start.23 = (bf16[128,512]{1,0:T(8,128)(2,1)S(1)}, bf16[128,512]{1,0:T(8,128)(2,1)S(1)}, u32[]{:S(2)}, u32[]{:S(2)}) collective-permute-start(bf16[128,512]{1,0:T(8,128)(2,1)S(1)} %get-tuple-element.60), channel_id=1, source_target_pairs={{0,3},{1,0},{2,1},{3,2},{4,7},{5,4},{6,5},{7,6},{8,11},{9,8},{10,9... | collective-permute-start | bytes 393224 | tf_op jit(solution)/shard_map/ppermute | solution.py:40
  48.1 7.5 %collective-permute-start.17 = (bf16[128,512]{1,0:T(8,128)(2,1)S(1)}, bf16[128,512]{1,0:T(8,128)(2,1)S(1)}, u32[]{:S(2)}, u32[]{:S(2)}) collective-permute-start(bf16[128,512]{1,0:T(8,128)(2,1)S(1)} %add_parts.2), channel_id=1, source_target_pairs={{0,96},{1,97},{2,98},{3,99},{4,100},{5,101},{6,102},{7,103},{8,104... | collective-permute-start | bytes 393224 | tf_op jit(solution)/shard_map/ppermute | solution.py:40
  50.8 9.2 %collective-permute-start.20 = (bf16[128,512]{1,0:T(8,128)(2,1)S(1)}, bf16[128,512]{1,0:T(8,128)(2,1)S(1)}, u32[]{:S(2)}, u32[]{:S(2)}) collective-permute-start(bf16[128,512]{1,0:T(8,128)(2,1)S(1)} %add_parts.2), channel_id=1, source_target_pairs={{0,98},{1,99},{2,96},{3,97},{4,102},{5,103},{6,100},{7,101},{8,106... | collective-permute-start | bytes 393224 | tf_op jit(solution)/shard_map/ppermute | solution.py:40
  53.0 6.8 %collective-permute-start.24 = (bf16[128,512]{1,0:T(8,128)(2,1)S(1)}, bf16[128,512]{1,0:T(8,128)(2,1)S(1)}, u32[]{:S(2)}, u32[]{:S(2)}) collective-permute-start(bf16[128,512]{1,0:T(8,128)(2,1)S(1)} %add_parts.3), channel_id=1, source_target_pairs={{0,96},{1,97},{2,98},{3,99},{4,100},{5,101},{6,102},{7,103},{8,104... | collective-permute-start | bytes 393224 | tf_op jit(solution)/shard_map/ppermute | solution.py:40
  55.6 8.1 %collective-permute-start.19 = (bf16[128,512]{1,0:T(8,128)(2,1)S(1)}, bf16[128,512]{1,0:T(8,128)(2,1)S(1)}, u32[]{:S(2)}, u32[]{:S(2)}) collective-permute-start(bf16[128,512]{1,0:T(8,128)(2,1)S(1)} %collective-permute-done.17.refs_0_), channel_id=1, source_target_pairs={{0,3},{1,0},{2,1},{3,2},{4,7},{5,4},{6,5},{7,6},{8,11},{9,8},{10,9... | collective-permute-start | bytes 393224 | tf_op jit(solution)/shard_map/ppermute | solution.py:40
  55.6 8.1 %collective-permute-start.18 = (bf16[128,512]{1,0:T(8,128)(2,1)S(1)}, bf16[128,512]{1,0:T(8,128)(2,1)S(1)}, u32[]{:S(2)}, u32[]{:S(2)}) collective-permute-start(bf16[128,512]{1,0:T(8,128)(2,1)S(1)} %collective-permute-done.17.refs_0_), channel_id=1, source_target_pairs={{0,1},{1,2},{2,3},{3,0},{4,5},{5,6},{6,7},{7,4},{8,9},{9,10},{10,1... | collective-permute-start | bytes 393224 | tf_op jit(solution)/shard_map/ppermute | solution.py:40
  57.0 7.6 %collective-permute-start.27 = (bf16[128,512]{1,0:T(8,128)(2,1)S(1)}, bf16[128,512]{1,0:T(8,128)(2,1)S(1)}, u32[]{:S(2)}, u32[]{:S(2)}) collective-permute-start(bf16[128,512]{1,0:T(8,128)(2,1)S(1)} %add_parts.3), channel_id=1, source_target_pairs={{0,98},{1,99},{2,96},{3,97},{4,102},{5,103},{6,100},{7,101},{8,106... | collective-permute-start | bytes 393224 | tf_op jit(solution)/shard_map/ppermute | solution.py:40
  59.8 5.7 %collective-permute-start.26 = (bf16[128,512]{1,0:T(8,128)(2,1)S(1)}, bf16[128,512]{1,0:T(8,128)(2,1)S(1)}, u32[]{:S(2)}, u32[]{:S(2)}) collective-permute-start(bf16[128,512]{1,0:T(8,128)(2,1)S(1)} %collective-permute-done.24.refs_0_.refs_4_), channel_id=1, source_target_pairs={{0,3},{1,0},{2,1},{3,2},{4,7},{5,4},{6,5},{7,6},{8,11},{9,8},{10,9... | collective-permute-start | bytes 393224 | tf_op jit(solution)/shard_map/ppermute | solution.py:40
  59.9 8.6 %collective-permute-start.25 = (bf16[128,512]{1,0:T(8,128)(2,1)S(1)}, bf16[128,512]{1,0:T(8,128)(2,1)S(1)}, u32[]{:S(2)}, u32[]{:S(2)}) collective-permute-start(bf16[128,512]{1,0:T(8,128)(2,1)S(1)} %collective-permute-done.24.refs_0_.refs_4_), channel_id=1, source_target_pairs={{0,1},{1,2},{2,3},{3,0},{4,5},{5,6},{6,7},{7,4},{8,9},{9,10},{10,1... | collective-permute-start | bytes 393224 | tf_op jit(solution)/shard_map/ppermute | solution.py:40
  69.1 11.2 %collective-permute-start.31 = (bf16[128,512]{1,0:T(8,128)(2,1)S(1)}, bf16[128,512]{1,0:T(8,128)(2,1)S(1)}, u32[]{:S(2)}, u32[]{:S(2)}) collective-permute-start(bf16[128,512]{1,0:T(8,128)(2,1)S(1)} %get-tuple-element.65.refs_0_), channel_id=1, source_target_pairs={{0,16},{1,17},{2,18},{3,19},{4,20},{5,21},{6,22},{7,23},{8,24},{9,... | collective-permute-start | bytes 393224 | tf_op jit(solution)/shard_map/ppermute | solution.py:40
  70.6 9.8 %collective-permute-start.30 = (bf16[128,512]{1,0:T(8,128)(2,1)S(1)}, bf16[128,512]{1,0:T(8,128)(2,1)S(1)}, u32[]{:S(2)}, u32[]{:S(2)}) collective-permute-start(bf16[128,512]{1,0:T(8,128)(2,1)S(1)} %get-tuple-element.65.refs_0_), channel_id=1, source_target_pairs={{0,8},{1,9},{2,10},{3,11},{4,12},{5,13},{6,14},{7,15},{8,16},{9,17... | collective-permute-start | bytes 393224 | tf_op jit(solution)/shard_map/ppermute | solution.py:40
  73.0 5.1 %collective-permute-start.29 = (bf16[128,512]{1,0:T(8,128)(2,1)S(1)}, bf16[128,512]{1,0:T(8,128)(2,1)S(1)}, u32[]{:S(2)}, u32[]{:S(2)}) collective-permute-start(bf16[128,512]{1,0:T(8,128)(2,1)S(1)} %get-tuple-element.65.refs_0_), channel_id=1, source_target_pairs={{0,24},{1,25},{2,26},{3,27},{4,28},{5,29},{6,30},{7,31},{8,0},{9,1... | collective-permute-start | bytes 393224 | tf_op jit(solution)/shard_map/ppermute | solution.py:40
  73.3 4.8 %collective-permute-start.28 = (bf16[128,512]{1,0:T(8,128)(2,1)S(1)}, bf16[128,512]{1,0:T(8,128)(2,1)S(1)}, u32[]{:S(2)}, u32[]{:S(2)}) collective-permute-start(bf16[128,512]{1,0:T(8,128)(2,1)S(1)} %get-tuple-element.65.refs_0_), channel_id=1, source_target_pairs={{0,4},{1,5},{2,6},{3,7},{4,0},{5,1},{6,2},{7,3},{8,12},{9,13},{10,... | collective-permute-start | bytes 393224 | tf_op jit(solution)/shard_map/ppermute | solution.py:40
  78.0 3.8 %collective-permute-start.32 = (bf16[128,512]{1,0:T(8,128)(2,1)S(1)}, bf16[128,512]{1,0:T(8,128)(2,1)S(1)}, u32[]{:S(2)}, u32[]{:S(2)}) collective-permute-start(bf16[128,512]{1,0:T(8,128)(2,1)S(1)} %collective-permute-done.29.refs_1_), channel_id=1, source_target_pairs={{0,4},{1,5},{2,6},{3,7},{4,0},{5,1},{6,2},{7,3},{8,12},{9,13},{10,... | collective-permute-start | bytes 393224 | tf_op jit(solution)/shard_map/ppermute | solution.py:40
  80.3 1.3 %collective-permute-start.34 = (bf16[128,512]{1,0:T(8,128)(2,1)S(1)}, bf16[128,512]{1,0:T(8,128)(2,1)S(1)}, u32[]{:S(2)}, u32[]{:S(2)}) collective-permute-start(bf16[128,512]{1,0:T(8,128)(2,1)S(1)} %collective-permute-done.31.refs_3_), channel_id=1, source_target_pairs={{0,4},{1,5},{2,6},{3,7},{4,0},{5,1},{6,2},{7,3},{8,12},{9,13},{10,... | collective-permute-start | bytes 393224 | tf_op jit(solution)/shard_map/ppermute | solution.py:40
  80.4 1.4 %collective-permute-start.33 = (bf16[128,512]{1,0:T(8,128)(2,1)S(1)}, bf16[128,512]{1,0:T(8,128)(2,1)S(1)}, u32[]{:S(2)}, u32[]{:S(2)}) collective-permute-start(bf16[128,512]{1,0:T(8,128)(2,1)S(1)} %collective-permute-done.30.refs_2_), channel_id=1, source_target_pairs={{0,4},{1,5},{2,6},{3,7},{4,0},{5,1},{6,2},{7,3},{8,12},{9,13},{10,... | collective-permute-start | bytes 393224 | tf_op jit(solution)/shard_map/ppermute | solution.py:40
  85.0 6.3 %collective-permute-start.38 = (bf16[64,1024]{1,0:T(8,128)(2,1)S(1)}, bf16[64,1024]{1,0:T(8,128)(2,1)S(1)}, u32[]{:S(2)}, u32[]{:S(2)}) collective-permute-start(bf16[64,1024]{1,0:T(8,128)(2,1)S(1)} %get-tuple-element.73), channel_id=1, source_target_pairs={{0,2},{1,3},{2,0},{3,1},{4,6},{5,7},{6,4},{7,5},{8,10},{9,11},{10,... | collective-permute-start | bytes 393224 | tf_op jit(solution)/shard_map/ppermute | solution.py:40
  85.3 9.9 %collective-permute-start.39 = (bf16[64,1024]{1,0:T(8,128)(2,1)S(1)}, bf16[64,1024]{1,0:T(8,128)(2,1)S(1)}, u32[]{:S(2)}, u32[]{:S(2)}) collective-permute-start(bf16[64,1024]{1,0:T(8,128)(2,1)S(1)} %get-tuple-element.74), channel_id=1, source_target_pairs={{0,1},{1,2},{2,3},{3,0},{4,5},{5,6},{6,7},{7,4},{8,9},{9,10},{10,1... | collective-permute-start | bytes 393224 | tf_op jit(solution)/shard_map/ppermute | solution.py:40
  86.1 9.1 %collective-permute-start.40 = (bf16[64,1024]{1,0:T(8,128)(2,1)S(1)}, bf16[64,1024]{1,0:T(8,128)(2,1)S(1)}, u32[]{:S(2)}, u32[]{:S(2)}) collective-permute-start(bf16[64,1024]{1,0:T(8,128)(2,1)S(1)} %get-tuple-element.75), channel_id=1, source_target_pairs={{0,3},{1,0},{2,1},{3,2},{4,7},{5,4},{6,5},{7,6},{8,11},{9,8},{10,9... | collective-permute-start | bytes 393224 | tf_op jit(solution)/shard_map/ppermute | solution.py:40
  88.0 9.0 %collective-permute-start.35 = (bf16[64,1024]{1,0:T(8,128)(2,1)S(1)}, bf16[64,1024]{1,0:T(8,128)(2,1)S(1)}, u32[]{:S(2)}, u32[]{:S(2)}) collective-permute-start(bf16[64,1024]{1,0:T(8,128)(2,1)S(1)} %get-tuple-element.69), channel_id=1, source_target_pairs={{0,2},{1,3},{2,0},{3,1},{4,6},{5,7},{6,4},{7,5},{8,10},{9,11},{10,... | collective-permute-start | bytes 393224 | tf_op jit(solution)/shard_map/ppermute | solution.py:40
  89.6 10.7 %collective-permute-start.36 = (bf16[64,1024]{1,0:T(8,128)(2,1)S(1)}, bf16[64,1024]{1,0:T(8,128)(2,1)S(1)}, u32[]{:S(2)}, u32[]{:S(2)}) collective-permute-start(bf16[64,1024]{1,0:T(8,128)(2,1)S(1)} %get-tuple-element.70), channel_id=1, source_target_pairs={{0,1},{1,2},{2,3},{3,0},{4,5},{5,6},{6,7},{7,4},{8,9},{9,10},{10,1... | collective-permute-start | bytes 393224 | tf_op jit(solution)/shard_map/ppermute | solution.py:40
  91.4 9.0 %collective-permute-start.37 = (bf16[64,1024]{1,0:T(8,128)(2,1)S(1)}, bf16[64,1024]{1,0:T(8,128)(2,1)S(1)}, u32[]{:S(2)}, u32[]{:S(2)}) collective-permute-start(bf16[64,1024]{1,0:T(8,128)(2,1)S(1)} %get-tuple-element.71), channel_id=1, source_target_pairs={{0,3},{1,0},{2,1},{3,2},{4,7},{5,4},{6,5},{7,6},{8,11},{9,8},{10,9... | collective-permute-start | bytes 393224 | tf_op jit(solution)/shard_map/ppermute | solution.py:40
  95.3 5.0 %collective-permute-start.41 = (bf16[64,1024]{1,0:T(8,128)(2,1)S(1)}, bf16[64,1024]{1,0:T(8,128)(2,1)S(1)}, u32[]{:S(2)}, u32[]{:S(2)}) collective-permute-start(bf16[64,1024]{1,0:T(8,128)(2,1)S(1)} %last_cross.1), channel_id=1, source_target_pairs={{0,32},{1,33},{2,34},{3,35},{4,36},{5,37},{6,38},{7,39},{8,40},{9,... | collective-permute-start | bytes 393224 | tf_op jit(solution)/shard_map/ppermute | solution.py:40

commit v9 on v8

--- a/solution.py
+++ b/solution.py
@@ -12,7 +12,7 @@
 CHUNKS = (512, 512)
 SMALL = 10 * 1024 * 1024
 SHIFTS = (2, 1, 3, 0)
-ORDER = (0, 1, 3, 2)
+ORDER = (2, 0, 3, 1)
 Z_ORDER = (3, 1, 2)
 FLOPS_PER_US = 1_150_000_000
 BESIDE_GAIN = 3

time: 101 us -> 101 us (level)
  waiting for transfers between devices: 35.2 us -> 32.5 us
  starting transfers between devices: 51.5 us -> 54 us
    ppermute x42, waiting for transfers between devices: 35.2 us -> 32.5 us  [send(): return lax.ppermute(block, AXES, route)]
    ppermute x42, starting transfers between devices: 51.5 us -> 54 us  [send(): return lax.ppermute(block, AXES, route)]
  transfers between devices with their start and end apart: 42 -> 42, of which waited for: 22 -> 21; matrix products, arithmetic and copies ran while one was open for 1% -> 1% of each run, Pallas kernels for 4% -> 4%
where the time goes in v9:
time: 101 us
  starting transfers between devices  54 us (53%)
  waiting for transfers between devices  32.5 us (32%)
  Pallas kernels  13.2 us (13%)
    ppermute x42, starting transfers between devices, send(): return lax.ppermute(block, AXES, route)  54 us
    ppermute x42, waiting for transfers between devices, send(): return lax.ppermute(block, AXES, route)  32.5 us
    pallas_call x15, Pallas kernels, in_vmem(): pl.pallas_call(kernel, in_specs=specs, out_specs=[pl.BlockSpec(memory_spa...  13.2 us
  transfers between devices with their start and end apart: 42, of which 21 were waited for; matrix products, arithmetic and copies ran while one was open for 1% of the time, Pallas kernels for 4%

profile of v9, /device:TPU:1, one launch (start us, length us, event | category | flops | bytes accessed | tf_op | source)
XLA Modules:
  0.0 100.9 jit_solution(2096678925902102939)
XLA Ops:
  0.0 1.0 rows_of_segments.1
  1.0 3.8 %collective-permute-start.2 = (bf16[64,1024]{1,0:T(8,128)(2,1)S(1)}, bf16[64,1024]{1,0:T(8,128)(2,1)S(1)}, u32[]{:S(2)}, u32[]{:S(2)}) collective-permute-start(bf16[64,1024]{1,0:T(8,128)(2,1)S(1)} %get-tuple-element.41.refs_0_.a), channel_id=1, source_target_pairs={{0,2},{1,3},{2,0},{3,1},{4,6},{5,7},{6,4},{7,5},{8,10},{9,11},{10,... | collective-permute-start | bytes 393224 | tf_op jit(solution)/shard_map/ppermute | solution.py:40
  4.8 0.8 collective-permute-start.1
  5.6 0.7 collective-permute-start
  6.3 1.2 %collective-permute-start.3 = (bf16[64,1024]{1,0:T(8,128)(2,1)S(1)}, bf16[64,1024]{1,0:T(8,128)(2,1)S(1)}, u32[]{:S(2)}, u32[]{:S(2)}) collective-permute-start(bf16[64,1024]{1,0:T(8,128)(2,1)S(1)} %get-tuple-element.42), channel_id=1, source_target_pairs={{0,32},{1,33},{2,34},{3,35},{4,36},{5,37},{6,38},{7,39},{8,40},{9,... | collective-permute-start | bytes 393224 | tf_op jit(solution)/shard_map/ppermute | solution.py:40
  7.8 2.4 %collective-permute-done.3.refs_4_.b = bf16[64,1024]{1,0:T(8,128)(2,1)S(1)} collective-permute-done((bf16[64,1024]{1,0:T(8,128)(2,1)S(1)}, bf16[64,1024]{1,0:T(8,128)(2,1)S(1)}, u32[]{:S(2)}, u32[]{:S(2)}) %collective-permute-start.3) | collective-permute-done | bytes 131104 | tf_op jit(solution)/shard_map/ppermute | solution.py:40
  10.1 1.0 %collective-permute-start.6 = (bf16[64,1024]{1,0:T(8,128)(2,1)S(1)}, bf16[64,1024]{1,0:T(8,128)(2,1)S(1)}, u32[]{:S(2)}, u32[]{:S(2)}) collective-permute-start(bf16[64,1024]{1,0:T(8,128)(2,1)S(1)} %collective-permute-done.3.refs_4_.b), channel_id=1, source_target_pairs={{0,2},{1,3},{2,0},{3,1},{4,6},{5,7},{6,4},{7,5},{8,10},{9,11},{10,... | collective-permute-start | bytes 393224 | tf_op jit(solution)/shard_map/ppermute | solution.py:40
  11.1 2.1 %collective-permute-start.5 = (bf16[64,1024]{1,0:T(8,128)(2,1)S(1)}, bf16[64,1024]{1,0:T(8,128)(2,1)S(1)}, u32[]{:S(2)}, u32[]{:S(2)}) collective-permute-start(bf16[64,1024]{1,0:T(8,128)(2,1)S(1)} %collective-permute-done.3.refs_4_.b), channel_id=1, source_target_pairs={{0,3},{1,0},{2,1},{3,2},{4,7},{5,4},{6,5},{7,6},{8,11},{9,8},{10,9... | collective-permute-start | bytes 393224 | tf_op jit(solution)/shard_map/ppermute | solution.py:40
  13.2 0.3 fusion.5
  13.9 1.6 %collective-permute-done.6.refs_7_ = bf16[64,1024]{1,0:T(8,128)(2,1)S(1)} collective-permute-done((bf16[64,1024]{1,0:T(8,128)(2,1)S(1)}, bf16[64,1024]{1,0:T(8,128)(2,1)S(1)}, u32[]{:S(2)}, u32[]{:S(2)}) %collective-permute-start.6) | collective-permute-done | bytes 131104 | tf_op jit(solution)/shard_map/ppermute | solution.py:40
  15.4 1.3 %collective-permute-done.5.refs_6_ = bf16[64,1024]{1,0:T(8,128)(2,1)S(1)} collective-permute-done((bf16[64,1024]{1,0:T(8,128)(2,1)S(1)}, bf16[64,1024]{1,0:T(8,128)(2,1)S(1)}, u32[]{:S(2)}, u32[]{:S(2)}) %collective-permute-start.5) | collective-permute-done | bytes 131104 | tf_op jit(solution)/shard_map/ppermute | solution.py:40
  16.7 3.3 %collective-permute-done.4.refs_5_ = bf16[64,1024]{1,0:T(8,128)(2,1)S(1)} collective-permute-done((bf16[64,1024]{1,0:T(8,128)(2,1)S(1)}, bf16[64,1024]{1,0:T(8,128)(2,1)S(1)}, u32[]{:S(2)}, u32[]{:S(2)}) %collective-permute-start.4) | collective-permute-done | bytes 131104 | tf_op jit(solution)/shard_map/ppermute | solution.py:40
  20.0 0.9 project_kv.3
  20.9 3.7 %collective-permute-start.10 = (bf16[128,512]{1,0:T(8,128)(2,1)S(1)}, bf16[128,512]{1,0:T(8,128)(2,1)S(1)}, u32[]{:S(2)}, u32[]{:S(2)}) collective-permute-start(bf16[128,512]{1,0:T(8,128)(2,1)S(1)} %get-tuple-element.47.refs_0_), channel_id=1, source_target_pairs={{0,16},{1,17},{2,18},{3,19},{4,20},{5,21},{6,22},{7,23},{8,24},{9,... | collective-permute-start | bytes 393224 | tf_op jit(solution)/shard_map/ppermute | solution.py:40
  24.6 0.7 collective-permute-start.9
  25.3 1.9 %collective-permute-start.8 = (bf16[128,512]{1,0:T(8,128)(2,1)S(1)}, bf16[128,512]{1,0:T(8,128)(2,1)S(1)}, u32[]{:S(2)}, u32[]{:S(2)}) collective-permute-start(bf16[128,512]{1,0:T(8,128)(2,1)S(1)} %get-tuple-element.47.refs_0_), channel_id=1, source_target_pairs={{0,24},{1,25},{2,26},{3,27},{4,28},{5,29},{6,30},{7,31},{8,0},{9,1... | collective-permute-start | bytes 393224 | tf_op jit(solution)/shard_map/ppermute | solution.py:40
  27.3 3.6 %collective-permute-start.7 = (bf16[128,512]{1,0:T(8,128)(2,1)S(1)}, bf16[128,512]{1,0:T(8,128)(2,1)S(1)}, u32[]{:S(2)}, u32[]{:S(2)}) collective-permute-start(bf16[128,512]{1,0:T(8,128)(2,1)S(1)} %get-tuple-element.47.refs_0_), channel_id=1, source_target_pairs={{0,4},{1,5},{2,6},{3,7},{4,0},{5,1},{6,2},{7,3},{8,12},{9,13},{10,... | collective-permute-start | bytes 393224 | tf_op jit(solution)/shard_map/ppermute | solution.py:40
  30.8 1.4 %project_q.2.q = bf16[128,1024]{1,0:T(8,128)(2,1)S(1)} custom-call(bf16[64,1024]{1,0:T(8,128)(2,1)S(1)} %get-tuple-element.41.refs_0_.a, bf16[64,1024]{1,0:T(8,128)(2,1)S(1)} %collective-permute-done.refs_1_, bf16[64,1024]{1,0:T(8,128)(2,1)S(1)} %collective-permute-done.1.refs_2_, bf16[64,1024]{1,0:T(8,128)(2,1)S(1)} %collective-permute-done.2.refs_3_, ...), custom_call_target="tpu_custom_call" | custom-call | flops 5673741824 | bytes 9585152 | tf_op jit(solution)/shard_map/project_q/pallas_call | solution.py:47
  32.3 1.3 %collective-permute-start.13 = (bf16[128,512]{1,0:T(8,128)(2,1)S(1)}, bf16[128,512]{1,0:T(8,128)(2,1)S(1)}, u32[]{:S(2)}, u32[]{:S(2)}) collective-permute-start(bf16[128,512]{1,0:T(8,128)(2,1)S(1)} %collective-permute-done.10.refs_3_), channel_id=1, source_target_pairs={{0,4},{1,5},{2,6},{3,7},{4,0},{5,1},{6,2},{7,3},{8,12},{9,13},{10,... | collective-permute-start | bytes 393224 | tf_op jit(solution)/shard_map/ppermute | solution.py:40
  33.6 0.2 collective-permute-start.12
  33.8 0.3 collective-permute-start.11
  34.1 0.5 collective-permute-done.13.refs_7_
  34.6 0.4 collective-permute-done.12.refs_6_
  34.9 0.2 collective-permute-done.11.refs_5_
  35.1 2.5 %attend_and_project.2 = (bf16[128,512]{1,0:T(8,128)(2,1)S(1)}, bf16[128,512]{1,0:T(8,128)(2,1)S(1)}, bf16[128,512]{1,0:T(8,128)(2,1)S(1)}, bf16[128,512]{1,0:T(8,128)(2,1)S(1)}, bf16[128,1024]{1,0:T(8,128)(2,1)S(1)}) custom-call(bf16[128,1024]{1,0:T(8,128)(2,1)S(1)} %project_q.2.q, s32[64,1]{1,0:T(8,128)S(1)} %iota_add_fusion.qpos, s32[1,512]{1,0:T(1,128)S(1)} %bitcast.3, ...), custom_call_target="tpu_custom_call" | custom-call | flops 10676395008 | bytes 9701632 | tf_op jit(solution)/shard_map/attend_and_project/pallas_call | solution.py:47
  37.6 0.4 collective-permute-start.14
  38.2 2.5 %collective-permute-start.16 = (bf16[128,512]{1,0:T(8,128)(2,1)S(1)}, bf16[128,512]{1,0:T(8,128)(2,1)S(1)}, u32[]{:S(2)}, u32[]{:S(2)}) collective-permute-start(bf16[128,512]{1,0:T(8,128)(2,1)S(1)} %get-tuple-element.55), channel_id=1, source_target_pairs={{0,3},{1,0},{2,1},{3,2},{4,7},{5,4},{6,5},{7,6},{8,11},{9,8},{10,9... | collective-permute-start | bytes 393224 | tf_op jit(solution)/shard_map/ppermute | solution.py:40
  40.8 0.8 project_out.1
  41.5 1.5 %collective-permute-start.21 = (bf16[128,512]{1,0:T(8,128)(2,1)S(1)}, bf16[128,512]{1,0:T(8,128)(2,1)S(1)}, u32[]{:S(2)}, u32[]{:S(2)}) collective-permute-start(bf16[128,512]{1,0:T(8,128)(2,1)S(1)} %get-tuple-element.58), channel_id=1, source_target_pairs={{0,2},{1,3},{2,0},{3,1},{4,6},{5,7},{6,4},{7,5},{8,10},{9,11},{10,... | collective-permute-start | bytes 393224 | tf_op jit(solution)/shard_map/ppermute | solution.py:40
  43.0 0.9 collective-permute-done.14.refs_0_
  44.0 1.7 %collective-permute-start.23 = (bf16[128,512]{1,0:T(8,128)(2,1)S(1)}, bf16[128,512]{1,0:T(8,128)(2,1)S(1)}, u32[]{:S(2)}, u32[]{:S(2)}) collective-permute-start(bf16[128,512]{1,0:T(8,128)(2,1)S(1)} %get-tuple-element.60), channel_id=1, source_target_pairs={{0,3},{1,0},{2,1},{3,2},{4,7},{5,4},{6,5},{7,6},{8,11},{9,8},{10,9... | collective-permute-start | bytes 393224 | tf_op jit(solution)/shard_map/ppermute | solution.py:40
  45.7 2.3 %collective-permute-done.15.refs_1_ = bf16[128,512]{1,0:T(8,128)(2,1)S(1)} collective-permute-done((bf16[128,512]{1,0:T(8,128)(2,1)S(1)}, bf16[128,512]{1,0:T(8,128)(2,1)S(1)}, u32[]{:S(2)}, u32[]{:S(2)}) %collective-permute-start.15) | collective-permute-done | bytes 131104 | tf_op jit(solution)/shard_map/ppermute | solution.py:40
  48.1 2.6 %collective-permute-start.18 = (bf16[128,512]{1,0:T(8,128)(2,1)S(1)}, bf16[128,512]{1,0:T(8,128)(2,1)S(1)}, u32[]{:S(2)}, u32[]{:S(2)}) collective-permute-start(bf16[128,512]{1,0:T(8,128)(2,1)S(1)} %add_parts.2), channel_id=1, source_target_pairs={{0,96},{1,97},{2,98},{3,99},{4,100},{5,101},{6,102},{7,103},{8,104... | collective-permute-start | bytes 393224 | tf_op jit(solution)/shard_map/ppermute | solution.py:40
  50.8 0.2 collective-permute-start.17
  50.9 2.0 %collective-permute-done.22.refs_1_ = bf16[128,512]{1,0:T(8,128)(2,1)S(1)} collective-permute-done((bf16[128,512]{1,0:T(8,128)(2,1)S(1)}, bf16[128,512]{1,0:T(8,128)(2,1)S(1)}, u32[]{:S(2)}, u32[]{:S(2)}) %collective-permute-start.22) | collective-permute-done | bytes 131104 | tf_op jit(solution)/shard_map/ppermute | solution.py:40
  53.0 2.6 %collective-permute-start.25 = (bf16[128,512]{1,0:T(8,128)(2,1)S(1)}, bf16[128,512]{1,0:T(8,128)(2,1)S(1)}, u32[]{:S(2)}, u32[]{:S(2)}) collective-permute-start(bf16[128,512]{1,0:T(8,128)(2,1)S(1)} %add_parts.3), channel_id=1, source_target_pairs={{0,96},{1,97},{2,98},{3,99},{4,100},{5,101},{6,102},{7,103},{8,104... | collective-permute-start | bytes 393224 | tf_op jit(solution)/shard_map/ppermute | solution.py:40
  55.6 2.7 %collective-permute-start.19 = (bf16[128,512]{1,0:T(8,128)(2,1)S(1)}, bf16[128,512]{1,0:T(8,128)(2,1)S(1)}, u32[]{:S(2)}, u32[]{:S(2)}) collective-permute-start(bf16[128,512]{1,0:T(8,128)(2,1)S(1)} %collective-permute-done.18.refs_1_), channel_id=1, source_target_pairs={{0,3},{1,0},{2,1},{3,2},{4,7},{5,4},{6,5},{7,6},{8,11},{9,8},{10,9... | collective-permute-start | bytes 393224 | tf_op jit(solution)/shard_map/ppermute | solution.py:40
  58.3 1.5 %collective-permute-done.25.refs_1_.refs_5_ = bf16[128,512]{1,0:T(8,128)(2,1)S(1)} collective-permute-done((bf16[128,512]{1,0:T(8,128)(2,1)S(1)}, bf16[128,512]{1,0:T(8,128)(2,1)S(1)}, u32[]{:S(2)}, u32[]{:S(2)}) %collective-permute-start.25) | collective-permute-done | bytes 131104 | tf_op jit(solution)/shard_map/ppermute | solution.py:40
  59.8 2.7 %collective-permute-start.26 = (bf16[128,512]{1,0:T(8,128)(2,1)S(1)}, bf16[128,512]{1,0:T(8,128)(2,1)S(1)}, u32[]{:S(2)}, u32[]{:S(2)}) collective-permute-start(bf16[128,512]{1,0:T(8,128)(2,1)S(1)} %collective-permute-done.25.refs_1_.refs_5_), channel_id=1, source_target_pairs={{0,3},{1,0},{2,1},{3,2},{4,7},{5,4},{6,5},{7,6},{8,11},{9,8},{10,9... | collective-permute-start | bytes 393224 | tf_op jit(solution)/shard_map/ppermute | solution.py:40
  62.6 0.5 project_kv.4
  63.1 2.7 %collective-permute-done.24.refs_0_.refs_4_ = bf16[128,512]{1,0:T(8,128)(2,1)S(1)} collective-permute-done((bf16[128,512]{1,0:T(8,128)(2,1)S(1)}, bf16[128,512]{1,0:T(8,128)(2,1)S(1)}, u32[]{:S(2)}, u32[]{:S(2)}) %collective-permute-start.24) | collective-permute-done | bytes 131104 | tf_op jit(solution)/shard_map/ppermute | solution.py:40
  65.8 2.5 %collective-permute-done.27.refs_3_.refs_7_ = bf16[128,512]{1,0:T(8,128)(2,1)S(1)} collective-permute-done((bf16[128,512]{1,0:T(8,128)(2,1)S(1)}, bf16[128,512]{1,0:T(8,128)(2,1)S(1)}, u32[]{:S(2)}, u32[]{:S(2)}) %collective-permute-start.27) | collective-permute-done | bytes 131104 | tf_op jit(solution)/shard_map/ppermute | solution.py:40
  68.3 0.6 project_kv.5
  68.9 1.5 %collective-permute-start.31 = (bf16[128,512]{1,0:T(8,128)(2,1)S(1)}, bf16[128,512]{1,0:T(8,128)(2,1)S(1)}, u32[]{:S(2)}, u32[]{:S(2)}) collective-permute-start(bf16[128,512]{1,0:T(8,128)(2,1)S(1)} %get-tuple-element.65.refs_0_), channel_id=1, source_target_pairs={{0,16},{1,17},{2,18},{3,19},{4,20},{5,21},{6,22},{7,23},{8,24},{9,... | collective-permute-start | bytes 393224 | tf_op jit(solution)/shard_map/ppermute | solution.py:40
  70.3 2.3 %collective-permute-start.30 = (bf16[128,512]{1,0:T(8,128)(2,1)S(1)}, bf16[128,512]{1,0:T(8,128)(2,1)S(1)}, u32[]{:S(2)}, u32[]{:S(2)}) collective-permute-start(bf16[128,512]{1,0:T(8,128)(2,1)S(1)} %get-tuple-element.65.refs_0_), channel_id=1, source_target_pairs={{0,8},{1,9},{2,10},{3,11},{4,12},{5,13},{6,14},{7,15},{8,16},{9,17... | collective-permute-start | bytes 393224 | tf_op jit(solution)/shard_map/ppermute | solution.py:40
  72.7 0.3 collective-permute-start.29
  73.0 2.3 %collective-permute-start.28 = (bf16[128,512]{1,0:T(8,128)(2,1)S(1)}, bf16[128,512]{1,0:T(8,128)(2,1)S(1)}, u32[]{:S(2)}, u32[]{:S(2)}) collective-permute-start(bf16[128,512]{1,0:T(8,128)(2,1)S(1)} %get-tuple-element.65.refs_0_), channel_id=1, source_target_pairs={{0,4},{1,5},{2,6},{3,7},{4,0},{5,1},{6,2},{7,3},{8,12},{9,13},{10,... | collective-permute-start | bytes 393224 | tf_op jit(solution)/shard_map/ppermute | solution.py:40
  75.3 1.4 %project_q.3.q = bf16[128,1024]{1,0:T(8,128)(2,1)S(1)} custom-call(bf16[128,512]{1,0:T(8,128)(2,1)S(1)} %collective-permute-done.17.refs_0_, bf16[128,512]{1,0:T(8,128)(2,1)S(1)} %collective-permute-done.18.refs_1_, bf16[128,512]{1,0:T(8,128)(2,1)S(1)} %collective-permute-done.19.refs_2_, bf16[128,512]{1,0:T(8,128)(2,1)S(1)} %collective-permute-done.20.refs_3_, ...), custom_call_target="tpu_custom_call" | custom-call | flops 5673741824 | bytes 9585152 | tf_op jit(solution)/shard_map/project_q/pallas_call | solution.py:47
  76.7 1.2 %collective-permute-done.29.refs_1_ = bf16[128,512]{1,0:T(8,128)(2,1)S(1)} collective-permute-done((bf16[128,512]{1,0:T(8,128)(2,1)S(1)}, bf16[128,512]{1,0:T(8,128)(2,1)S(1)}, u32[]{:S(2)}, u32[]{:S(2)}) %collective-permute-start.29) | collective-permute-done | bytes 131104 | tf_op jit(solution)/shard_map/ppermute | solution.py:40
  77.8 2.1 %collective-permute-start.32 = (bf16[128,512]{1,0:T(8,128)(2,1)S(1)}, bf16[128,512]{1,0:T(8,128)(2,1)S(1)}, u32[]{:S(2)}, u32[]{:S(2)}) collective-permute-start(bf16[128,512]{1,0:T(8,128)(2,1)S(1)} %collective-permute-done.29.refs_1_), channel_id=1, source_target_pairs={{0,4},{1,5},{2,6},{3,7},{4,0},{5,1},{6,2},{7,3},{8,12},{9,13},{10,... | collective-permute-start | bytes 393224 | tf_op jit(solution)/shard_map/ppermute | solution.py:40
  80.1 0.4 collective-permute-start.33
  80.5 0.8 collective-permute-done.34.refs_7_
  81.3 0.2 collective-permute-done.33.refs_6_
  81.5 3.2 %attend_and_project.3 = (bf16[64,1024]{1,0:T(8,128)(2,1)S(1)}, bf16[64,1024]{1,0:T(8,128)(2,1)S(1)}, bf16[64,1024]{1,0:T(8,128)(2,1)S(1)}, bf16[64,1024]{1,0:T(8...) custom-call(bf16[128,1024]{1,0:T(8,128)(2,1)S(1)} %project_q.3.q, ...), custom_call_target="tpu_custom_call" | custom-call | flops 10676395008 | bytes 9701632 | tf_op jit(solution)/shard_map/attend_and_project/pallas_call | solution.py:47
  84.7 0.3 collective-permute-start.38
  85.0 2.0 %collective-permute-start.39 = (bf16[64,1024]{1,0:T(8,128)(2,1)S(1)}, bf16[64,1024]{1,0:T(8,128)(2,1)S(1)}, u32[]{:S(2)}, u32[]{:S(2)}) collective-permute-start(bf16[64,1024]{1,0:T(8,128)(2,1)S(1)} %get-tuple-element.74), channel_id=1, source_target_pairs={{0,1},{1,2},{2,3},{3,0},{4,5},{5,6},{6,7},{7,4},{8,9},{9,10},{10,1... | collective-permute-start | bytes 393224 | tf_op jit(solution)/shard_map/ppermute | solution.py:40
  87.1 0.6 collective-permute-start.40
  87.7 1.5 %collective-permute-start.35 = (bf16[64,1024]{1,0:T(8,128)(2,1)S(1)}, bf16[64,1024]{1,0:T(8,128)(2,1)S(1)}, u32[]{:S(2)}, u32[]{:S(2)}) collective-permute-start(bf16[64,1024]{1,0:T(8,128)(2,1)S(1)} %get-tuple-element.69), channel_id=1, source_target_pairs={{0,2},{1,3},{2,0},{3,1},{4,6},{5,7},{6,4},{7,5},{8,10},{9,11},{10,... | collective-permute-start | bytes 393224 | tf_op jit(solution)/shard_map/ppermute | solution.py:40
  89.4 1.6 %collective-permute-done.38.refs_0_ = bf16[64,1024]{1,0:T(8,128)(2,1)S(1)} collective-permute-done((bf16[64,1024]{1,0:T(8,128)(2,1)S(1)}, bf16[64,1024]{1,0:T(8,128)(2,1)S(1)}, u32[]{:S(2)}, u32[]{:S(2)}) %collective-permute-start.38) | collective-permute-done | bytes 131104 | tf_op jit(solution)/shard_map/ppermute | solution.py:40
  91.0 1.7 %collective-permute-start.37 = (bf16[64,1024]{1,0:T(8,128)(2,1)S(1)}, bf16[64,1024]{1,0:T(8,128)(2,1)S(1)}, u32[]{:S(2)}, u32[]{:S(2)}) collective-permute-start(bf16[64,1024]{1,0:T(8,128)(2,1)S(1)} %get-tuple-element.71), channel_id=1, source_target_pairs={{0,3},{1,0},{2,1},{3,2},{4,7},{5,4},{6,5},{7,6},{8,11},{9,8},{10,9... | collective-permute-start | bytes 393224 | tf_op jit(solution)/shard_map/ppermute | solution.py:40
  92.8 2.3 %collective-permute-done.39.refs_1_ = bf16[64,1024]{1,0:T(8,128)(2,1)S(1)} collective-permute-done((bf16[64,1024]{1,0:T(8,128)(2,1)S(1)}, bf16[64,1024]{1,0:T(8,128)(2,1)S(1)}, u32[]{:S(2)}, u32[]{:S(2)}) %collective-permute-start.39) | collective-permute-done | bytes 131104 | tf_op jit(solution)/shard_map/ppermute | solution.py:40
  95.3 1.4 %collective-permute-done.35.refs_0_ = bf16[64,1024]{1,0:T(8,128)(2,1)S(1)} collective-permute-done((bf16[64,1024]{1,0:T(8,128)(2,1)S(1)}, bf16[64,1024]{1,0:T(8,128)(2,1)S(1)}, u32[]{:S(2)}, u32[]{:S(2)}) %collective-permute-start.35) | collective-permute-done | bytes 131104 | tf_op jit(solution)/shard_map/ppermute | solution.py:40
  96.7 3.4 %collective-permute-done.36.refs_1_ = bf16[64,1024]{1,0:T(8,128)(2,1)S(1)} collective-permute-done((bf16[64,1024]{1,0:T(8,128)(2,1)S(1)}, bf16[64,1024]{1,0:T(8,128)(2,1)S(1)}, u32[]{:S(2)}, u32[]{:S(2)}) %collective-permute-start.36) | collective-permute-done | bytes 131104 | tf_op jit(solution)/shard_map/ppermute | solution.py:40
  100.1 0.8 finish.1
  (72 shorter events, 1.7 us)
Async XLA Ops:
  0.0 13.2 %copy-start.2 = (bf16[1,4096]{1,0:T(2,128)(2,1)S(1)}, bf16[1,4096]{1,0:T(2,128)(2,1)}, u32[]{:S(2)}) copy-start(bf16[1,4096]{1,0:T(2,128)(2,1)} %g) | copy-start | bytes 24580
  1.0 19.0 %copy-start = (bf16[1,4096,256]{2,1,0:T(8,128)(2,1)S(1)}, bf16[1,4096,256]{2,1,0:T(8,128)(2,1)}, u32[]{:S(2)}) copy-start(bf16[1,4096,256]{2,1,0:T(8,128)(2,1)} %refs_5_.3) | copy-start | bytes 6291460
  1.0 12.5 %collective-permute-start.2 = (bf16[64,1024]{1,0:T(8,128)(2,1)S(1)}, bf16[64,1024]{1,0:T(8,128)(2,1)S(1)}, u32[]{:S(2)}, u32[]{:S(2)}) collective-permute-start(bf16[64,1024]{1,0:T(8,128)(2,1)S(1)} %get-tuple-element.41.refs_0_.a), channel_id=1, source_target_pairs={{0,2},{1,3},{2,0},{3,1},{4,6},{5,7},{6,4},{7,5},{8,10},{9,11},{10,... | collective-permute-start | bytes 393224 | tf_op jit(solution)/shard_map/ppermute | solution.py:40
  4.8 9.0 %collective-permute-start.1 = (bf16[64,1024]{1,0:T(8,128)(2,1)S(1)}, bf16[64,1024]{1,0:T(8,128)(2,1)S(1)}, u32[]{:S(2)}, u32[]{:S(2)}) collective-permute-start(bf16[64,1024]{1,0:T(8,128)(2,1)S(1)} %get-tuple-element.41.refs_0_.a), channel_id=1, source_target_pairs={{0,3},{1,0},{2,1},{3,2},{4,7},{5,4},{6,5},{7,6},{8,11},{9,8},{10,9... | collective-permute-start | bytes 393224 | tf_op jit(solution)/shard_map/ppermute | solution.py:40
  5.6 8.2 %collective-permute-start = (bf16[64,1024]{1,0:T(8,128)(2,1)S(1)}, bf16[64,1024]{1,0:T(8,128)(2,1)S(1)}, u32[]{:S(2)}, u32[]{:S(2)}) collective-permute-start(bf16[64,1024]{1,0:T(8,128)(2,1)S(1)} %get-tuple-element.41.refs_0_.a), channel_id=1, source_target_pairs={{0,1},{1,2},{2,3},{3,0},{4,5},{5,6},{6,7},{7,4},{8,9},{9,10},{10,1... | collective-permute-start | bytes 393224 | tf_op jit(solution)/shard_map/ppermute | solution.py:40
  6.3 3.8 %collective-permute-start.3 = (bf16[64,1024]{1,0:T(8,128)(2,1)S(1)}, bf16[64,1024]{1,0:T(8,128)(2,1)S(1)}, u32[]{:S(2)}, u32[]{:S(2)}) collective-permute-start(bf16[64,1024]{1,0:T(8,128)(2,1)S(1)} %get-tuple-element.42), channel_id=1, source_target_pairs={{0,32},{1,33},{2,34},{3,35},{4,36},{5,37},{6,38},{7,39},{8,40},{9,... | collective-permute-start | bytes 393224 | tf_op jit(solution)/shard_map/ppermute | solution.py:40
  7.7 12.3 %copy-start.1 = (bf16[1,4096,256]{2,1,0:T(8,128)(2,1)S(1)}, bf16[1,4096,256]{2,1,0:T(8,128)(2,1)}, u32[]{:S(2)}) copy-start(bf16[1,4096,256]{2,1,0:T(8,128)(2,1)} %refs_6_.3) | copy-start | bytes 6291460
  10.1 5.3 %collective-permute-start.6 = (bf16[64,1024]{1,0:T(8,128)(2,1)S(1)}, bf16[64,1024]{1,0:T(8,128)(2,1)S(1)}, u32[]{:S(2)}, u32[]{:S(2)}) collective-permute-start(bf16[64,1024]{1,0:T(8,128)(2,1)S(1)} %collective-permute-done.3.refs_4_.b), channel_id=1, source_target_pairs={{0,2},{1,3},{2,0},{3,1},{4,6},{5,7},{6,4},{7,5},{8,10},{9,11},{10,... | collective-permute-start | bytes 393224 | tf_op jit(solution)/shard_map/ppermute | solution.py:40
  11.1 5.6 %collective-permute-start.5 = (bf16[64,1024]{1,0:T(8,128)(2,1)S(1)}, bf16[64,1024]{1,0:T(8,128)(2,1)S(1)}, u32[]{:S(2)}, u32[]{:S(2)}) collective-permute-start(bf16[64,1024]{1,0:T(8,128)(2,1)S(1)} %collective-permute-done.3.refs_4_.b), channel_id=1, source_target_pairs={{0,3},{1,0},{2,1},{3,2},{4,7},{5,4},{6,5},{7,6},{8,11},{9,8},{10,9... | collective-permute-start | bytes 393224 | tf_op jit(solution)/shard_map/ppermute | solution.py:40
  13.2 17.6 %slice-start.2 = ((s8[8388608]{0:T(1024)(128)(4,1)}), s8[4194304]{0:T(1024)(128)(4,1)S(1)}, s32[]{:S(2)}) async-start(s8[8388608]{0:T(1024)(128)(4,1)} %bitcast.5), calls=%async_computation.2 | async-start | bytes 8388608
  13.2 17.6 %slice-start.3 = ((s8[8388608]{0:T(1024)(128)(4,1)}), s8[4194304]{0:T(1024)(128)(4,1)S(1)}, s32[]{:S(2)}) async-start(s8[8388608]{0:T(1024)(128)(4,1)} %bitcast.5), calls=%async_computation.3 | async-start | bytes 8388608
  13.6 6.5 %collective-permute-start.4 = (bf16[64,1024]{1,0:T(8,128)(2,1)S(1)}, bf16[64,1024]{1,0:T(8,128)(2,1)S(1)}, u32[]{:S(2)}, u32[]{:S(2)}) collective-permute-start(bf16[64,1024]{1,0:T(8,128)(2,1)S(1)} %collective-permute-done.3.refs_4_.b), channel_id=1, source_target_pairs={{0,1},{1,2},{2,3},{3,0},{4,5},{5,6},{6,7},{7,4},{8,9},{9,10},{10,1... | collective-permute-start | bytes 393224 | tf_op jit(solution)/shard_map/ppermute | solution.py:40
  20.0 15.1 %slice-start = ((s8[8388608]{0:T(1024)(128)(4,1)}), s8[4194304]{0:T(1024)(128)(4,1)S(1)}, s32[]{:S(2)}) async-start(s8[8388608]{0:T(1024)(128)(4,1)} %bitcast.1), calls=%async_computation | async-start | bytes 8388608
  20.9 11.4 %collective-permute-start.10 = (bf16[128,512]{1,0:T(8,128)(2,1)S(1)}, bf16[128,512]{1,0:T(8,128)(2,1)S(1)}, u32[]{:S(2)}, u32[]{:S(2)}) collective-permute-start(bf16[128,512]{1,0:T(8,128)(2,1)S(1)} %get-tuple-element.47.refs_0_), channel_id=1, source_target_pairs={{0,16},{1,17},{2,18},{3,19},{4,20},{5,21},{6,22},{7,23},{8,24},{9,... | collective-permute-start | bytes 393224 | tf_op jit(solution)/shard_map/ppermute | solution.py:40
  24.6 9.0 %collective-permute-start.9 = (bf16[128,512]{1,0:T(8,128)(2,1)S(1)}, bf16[128,512]{1,0:T(8,128)(2,1)S(1)}, u32[]{:S(2)}, u32[]{:S(2)}) collective-permute-start(bf16[128,512]{1,0:T(8,128)(2,1)S(1)} %get-tuple-element.47.refs_0_), channel_id=1, source_target_pairs={{0,8},{1,9},{2,10},{3,11},{4,12},{5,13},{6,14},{7,15},{8,16},{9,17... | collective-permute-start | bytes 393224 | tf_op jit(solution)/shard_map/ppermute | solution.py:40
  25.3 6.9 %collective-permute-start.8 = (bf16[128,512]{1,0:T(8,128)(2,1)S(1)}, bf16[128,512]{1,0:T(8,128)(2,1)S(1)}, u32[]{:S(2)}, u32[]{:S(2)}) collective-permute-start(bf16[128,512]{1,0:T(8,128)(2,1)S(1)} %get-tuple-element.47.refs_0_), channel_id=1, source_target_pairs={{0,24},{1,25},{2,26},{3,27},{4,28},{5,29},{6,30},{7,31},{8,0},{9,1... | collective-permute-start | bytes 393224 | tf_op jit(solution)/shard_map/ppermute | solution.py:40
  27.3 5.0 %collective-permute-start.7 = (bf16[128,512]{1,0:T(8,128)(2,1)S(1)}, bf16[128,512]{1,0:T(8,128)(2,1)S(1)}, u32[]{:S(2)}, u32[]{:S(2)}) collective-permute-start(bf16[128,512]{1,0:T(8,128)(2,1)S(1)} %get-tuple-element.47.refs_0_), channel_id=1, source_target_pairs={{0,4},{1,5},{2,6},{3,7},{4,0},{5,1},{6,2},{7,3},{8,12},{9,13},{10,... | collective-permute-start | bytes 393224 | tf_op jit(solution)/shard_map/ppermute | solution.py:40
  30.8 4.3 %slice-start.1 = ((s8[8388608]{0:T(1024)(128)(4,1)}), s8[4194304]{0:T(1024)(128)(4,1)S(1)}, s32[]{:S(2)}) async-start(s8[8388608]{0:T(1024)(128)(4,1)} %bitcast.1), calls=%async_computation.1 | async-start | bytes 8388608
  32.3 2.3 %collective-permute-start.13 = (bf16[128,512]{1,0:T(8,128)(2,1)S(1)}, bf16[128,512]{1,0:T(8,128)(2,1)S(1)}, u32[]{:S(2)}, u32[]{:S(2)}) collective-permute-start(bf16[128,512]{1,0:T(8,128)(2,1)S(1)} %collective-permute-done.10.refs_3_), channel_id=1, source_target_pairs={{0,4},{1,5},{2,6},{3,7},{4,0},{5,1},{6,2},{7,3},{8,12},{9,13},{10,... | collective-permute-start | bytes 393224 | tf_op jit(solution)/shard_map/ppermute | solution.py:40
  33.6 1.3 %collective-permute-start.12 = (bf16[128,512]{1,0:T(8,128)(2,1)S(1)}, bf16[128,512]{1,0:T(8,128)(2,1)S(1)}, u32[]{:S(2)}, u32[]{:S(2)}) collective-permute-start(bf16[128,512]{1,0:T(8,128)(2,1)S(1)} %collective-permute-done.9.refs_2_), channel_id=1, source_target_pairs={{0,4},{1,5},{2,6},{3,7},{4,0},{5,1},{6,2},{7,3},{8,12},{9,13},{10,... | collective-permute-start | bytes 393224 | tf_op jit(solution)/shard_map/ppermute | solution.py:40
  33.8 1.4 %collective-permute-start.11 = (bf16[128,512]{1,0:T(8,128)(2,1)S(1)}, bf16[128,512]{1,0:T(8,128)(2,1)S(1)}, u32[]{:S(2)}, u32[]{:S(2)}) collective-permute-start(bf16[128,512]{1,0:T(8,128)(2,1)S(1)} %collective-permute-done.8.refs_1_), channel_id=1, source_target_pairs={{0,4},{1,5},{2,6},{3,7},{4,0},{5,1},{6,2},{7,3},{8,12},{9,13},{10,... | collective-permute-start | bytes 393224 | tf_op jit(solution)/shard_map/ppermute | solution.py:40
  37.6 6.4 %collective-permute-start.14 = (bf16[128,512]{1,0:T(8,128)(2,1)S(1)}, bf16[128,512]{1,0:T(8,128)(2,1)S(1)}, u32[]{:S(2)}, u32[]{:S(2)}) collective-permute-start(bf16[128,512]{1,0:T(8,128)(2,1)S(1)} %get-tuple-element.53), channel_id=1, source_target_pairs={{0,2},{1,3},{2,0},{3,1},{4,6},{5,7},{6,4},{7,5},{8,10},{9,11},{10,... | collective-permute-start | bytes 393224 | tf_op jit(solution)/shard_map/ppermute | solution.py:40
  38.0 10.0 %collective-permute-start.15 = (bf16[128,512]{1,0:T(8,128)(2,1)S(1)}, bf16[128,512]{1,0:T(8,128)(2,1)S(1)}, u32[]{:S(2)}, u32[]{:S(2)}) collective-permute-start(bf16[128,512]{1,0:T(8,128)(2,1)S(1)} %get-tuple-element.54), channel_id=1, source_target_pairs={{0,1},{1,2},{2,3},{3,0},{4,5},{5,6},{6,7},{7,4},{8,9},{9,10},{10,1... | collective-permute-start | bytes 393224 | tf_op jit(solution)/shard_map/ppermute | solution.py:40
  38.2 9.8 %collective-permute-start.16 = (bf16[128,512]{1,0:T(8,128)(2,1)S(1)}, bf16[128,512]{1,0:T(8,128)(2,1)S(1)}, u32[]{:S(2)}, u32[]{:S(2)}) collective-permute-start(bf16[128,512]{1,0:T(8,128)(2,1)S(1)} %get-tuple-element.55), channel_id=1, source_target_pairs={{0,3},{1,0},{2,1},{3,2},{4,7},{5,4},{6,5},{7,6},{8,11},{9,8},{10,9... | collective-permute-start | bytes 393224 | tf_op jit(solution)/shard_map/ppermute | solution.py:40
  41.5 9.4 %collective-permute-start.21 = (bf16[128,512]{1,0:T(8,128)(2,1)S(1)}, bf16[128,512]{1,0:T(8,128)(2,1)S(1)}, u32[]{:S(2)}, u32[]{:S(2)}) collective-permute-start(bf16[128,512]{1,0:T(8,128)(2,1)S(1)} %get-tuple-element.58), channel_id=1, source_target_pairs={{0,2},{1,3},{2,0},{3,1},{4,6},{5,7},{6,4},{7,5},{8,10},{9,11},{10,... | collective-permute-start | bytes 393224 | tf_op jit(solution)/shard_map/ppermute | solution.py:40
  43.0 9.9 %collective-permute-start.22 = (bf16[128,512]{1,0:T(8,128)(2,1)S(1)}, bf16[128,512]{1,0:T(8,128)(2,1)S(1)}, u32[]{:S(2)}, u32[]{:S(2)}) collective-permute-start(bf16[128,512]{1,0:T(8,128)(2,1)S(1)} %get-tuple-element.59), channel_id=1, source_target_pairs={{0,1},{1,2},{2,3},{3,0},{4,5},{5,6},{6,7},{7,4},{8,9},{9,10},{10,1... | collective-permute-start | bytes 393224 | tf_op jit(solution)/shard_map/ppermute | solution.py:40
  44.0 8.9 %collective-permute-start.23 = (bf16[128,512]{1,0:T(8,128)(2,1)S(1)}, bf16[128,512]{1,0:T(8,128)(2,1)S(1)}, u32[]{:S(2)}, u32[]{:S(2)}) collective-permute-start(bf16[128,512]{1,0:T(8,128)(2,1)S(1)} %get-tuple-element.60), channel_id=1, source_target_pairs={{0,3},{1,0},{2,1},{3,2},{4,7},{5,4},{6,5},{7,6},{8,11},{9,8},{10,9... | collective-permute-start | bytes 393224 | tf_op jit(solution)/shard_map/ppermute | solution.py:40
  48.1 7.5 %collective-permute-start.18 = (bf16[128,512]{1,0:T(8,128)(2,1)S(1)}, bf16[128,512]{1,0:T(8,128)(2,1)S(1)}, u32[]{:S(2)}, u32[]{:S(2)}) collective-permute-start(bf16[128,512]{1,0:T(8,128)(2,1)S(1)} %add_parts.2), channel_id=1, source_target_pairs={{0,96},{1,97},{2,98},{3,99},{4,100},{5,101},{6,102},{7,103},{8,104... | collective-permute-start | bytes 393224 | tf_op jit(solution)/shard_map/ppermute | solution.py:40
  50.8 9.0 %collective-permute-start.17 = (bf16[128,512]{1,0:T(8,128)(2,1)S(1)}, bf16[128,512]{1,0:T(8,128)(2,1)S(1)}, u32[]{:S(2)}, u32[]{:S(2)}) collective-permute-start(bf16[128,512]{1,0:T(8,128)(2,1)S(1)} %add_parts.2), channel_id=1, source_target_pairs={{0,98},{1,99},{2,96},{3,97},{4,102},{5,103},{6,100},{7,101},{8,106... | collective-permute-start | bytes 393224 | tf_op jit(solution)/shard_map/ppermute | solution.py:40
  53.0 6.8 %collective-permute-start.25 = (bf16[128,512]{1,0:T(8,128)(2,1)S(1)}, bf16[128,512]{1,0:T(8,128)(2,1)S(1)}, u32[]{:S(2)}, u32[]{:S(2)}) collective-permute-start(bf16[128,512]{1,0:T(8,128)(2,1)S(1)} %add_parts.3), channel_id=1, source_target_pairs={{0,96},{1,97},{2,98},{3,99},{4,100},{5,101},{6,102},{7,103},{8,104... | collective-permute-start | bytes 393224 | tf_op jit(solution)/shard_map/ppermute | solution.py:40
  55.6 7.0 %collective-permute-start.20 = (bf16[128,512]{1,0:T(8,128)(2,1)S(1)}, bf16[128,512]{1,0:T(8,128)(2,1)S(1)}, u32[]{:S(2)}, u32[]{:S(2)}) collective-permute-start(bf16[128,512]{1,0:T(8,128)(2,1)S(1)} %collective-permute-done.18.refs_1_), channel_id=1, source_target_pairs={{0,1},{1,2},{2,3},{3,0},{4,5},{5,6},{6,7},{7,4},{8,9},{9,10},{10,1... | collective-permute-start | bytes 393224 | tf_op jit(solution)/shard_map/ppermute | solution.py:40
  55.6 7.0 %collective-permute-start.19 = (bf16[128,512]{1,0:T(8,128)(2,1)S(1)}, bf16[128,512]{1,0:T(8,128)(2,1)S(1)}, u32[]{:S(2)}, u32[]{:S(2)}) collective-permute-start(bf16[128,512]{1,0:T(8,128)(2,1)S(1)} %collective-permute-done.18.refs_1_), channel_id=1, source_target_pairs={{0,3},{1,0},{2,1},{3,2},{4,7},{5,4},{6,5},{7,6},{8,11},{9,8},{10,9... | collective-permute-start | bytes 393224 | tf_op jit(solution)/shard_map/ppermute | solution.py:40
  58.2 7.5 %collective-permute-start.24 = (bf16[128,512]{1,0:T(8,128)(2,1)S(1)}, bf16[128,512]{1,0:T(8,128)(2,1)S(1)}, u32[]{:S(2)}, u32[]{:S(2)}) collective-permute-start(bf16[128,512]{1,0:T(8,128)(2,1)S(1)} %add_parts.3), channel_id=1, source_target_pairs={{0,98},{1,99},{2,96},{3,97},{4,102},{5,103},{6,100},{7,101},{8,106... | collective-permute-start | bytes 393224 | tf_op jit(solution)/shard_map/ppermute | solution.py:40
  59.8 8.5 %collective-permute-start.27 = (bf16[128,512]{1,0:T(8,128)(2,1)S(1)}, bf16[128,512]{1,0:T(8,128)(2,1)S(1)}, u32[]{:S(2)}, u32[]{:S(2)}) collective-permute-start(bf16[128,512]{1,0:T(8,128)(2,1)S(1)} %collective-permute-done.25.refs_1_.refs_5_), channel_id=1, source_target_pairs={{0,1},{1,2},{2,3},{3,0},{4,5},{5,6},{6,7},{7,4},{8,9},{9,10},{10,1... | collective-permute-start | bytes 393224 | tf_op jit(solution)/shard_map/ppermute | solution.py:40
  59.8 8.5 %collective-permute-start.26 = (bf16[128,512]{1,0:T(8,128)(2,1)S(1)}, bf16[128,512]{1,0:T(8,128)(2,1)S(1)}, u32[]{:S(2)}, u32[]{:S(2)}) collective-permute-start(bf16[128,512]{1,0:T(8,128)(2,1)S(1)} %collective-permute-done.25.refs_1_.refs_5_), channel_id=1, source_target_pairs={{0,3},{1,0},{2,1},{3,2},{4,7},{5,4},{6,5},{7,6},{8,11},{9,8},{10,9... | collective-permute-start | bytes 393224 | tf_op jit(solution)/shard_map/ppermute | solution.py:40
  68.9 11.1 %collective-permute-start.31 = (bf16[128,512]{1,0:T(8,128)(2,1)S(1)}, bf16[128,512]{1,0:T(8,128)(2,1)S(1)}, u32[]{:S(2)}, u32[]{:S(2)}) collective-permute-start(bf16[128,512]{1,0:T(8,128)(2,1)S(1)} %get-tuple-element.65.refs_0_), channel_id=1, source_target_pairs={{0,16},{1,17},{2,18},{3,19},{4,20},{5,21},{6,22},{7,23},{8,24},{9,... | collective-permute-start | bytes 393224 | tf_op jit(solution)/shard_map/ppermute | solution.py:40
  70.3 9.7 %collective-permute-start.30 = (bf16[128,512]{1,0:T(8,128)(2,1)S(1)}, bf16[128,512]{1,0:T(8,128)(2,1)S(1)}, u32[]{:S(2)}, u32[]{:S(2)}) collective-permute-start(bf16[128,512]{1,0:T(8,128)(2,1)S(1)} %get-tuple-element.65.refs_0_), channel_id=1, source_target_pairs={{0,8},{1,9},{2,10},{3,11},{4,12},{5,13},{6,14},{7,15},{8,16},{9,17... | collective-permute-start | bytes 393224 | tf_op jit(solution)/shard_map/ppermute | solution.py:40
  72.7 5.2 %collective-permute-start.29 = (bf16[128,512]{1,0:T(8,128)(2,1)S(1)}, bf16[128,512]{1,0:T(8,128)(2,1)S(1)}, u32[]{:S(2)}, u32[]{:S(2)}) collective-permute-start(bf16[128,512]{1,0:T(8,128)(2,1)S(1)} %get-tuple-element.65.refs_0_), channel_id=1, source_target_pairs={{0,24},{1,25},{2,26},{3,27},{4,28},{5,29},{6,30},{7,31},{8,0},{9,1... | collective-permute-start | bytes 393224 | tf_op jit(solution)/shard_map/ppermute | solution.py:40
  73.0 4.8 %collective-permute-start.28 = (bf16[128,512]{1,0:T(8,128)(2,1)S(1)}, bf16[128,512]{1,0:T(8,128)(2,1)S(1)}, u32[]{:S(2)}, u32[]{:S(2)}) collective-permute-start(bf16[128,512]{1,0:T(8,128)(2,1)S(1)} %get-tuple-element.65.refs_0_), channel_id=1, source_target_pairs={{0,4},{1,5},{2,6},{3,7},{4,0},{5,1},{6,2},{7,3},{8,12},{9,13},{10,... | collective-permute-start | bytes 393224 | tf_op jit(solution)/shard_map/ppermute | solution.py:40
  77.8 3.7 %collective-permute-start.32 = (bf16[128,512]{1,0:T(8,128)(2,1)S(1)}, bf16[128,512]{1,0:T(8,128)(2,1)S(1)}, u32[]{:S(2)}, u32[]{:S(2)}) collective-permute-start(bf16[128,512]{1,0:T(8,128)(2,1)S(1)} %collective-permute-done.29.refs_1_), channel_id=1, source_target_pairs={{0,4},{1,5},{2,6},{3,7},{4,0},{5,1},{6,2},{7,3},{8,12},{9,13},{10,... | collective-permute-start | bytes 393224 | tf_op jit(solution)/shard_map/ppermute | solution.py:40
  80.0 1.3 %collective-permute-start.34 = (bf16[128,512]{1,0:T(8,128)(2,1)S(1)}, bf16[128,512]{1,0:T(8,128)(2,1)S(1)}, u32[]{:S(2)}, u32[]{:S(2)}) collective-permute-start(bf16[128,512]{1,0:T(8,128)(2,1)S(1)} %collective-permute-done.31.refs_3_), channel_id=1, source_target_pairs={{0,4},{1,5},{2,6},{3,7},{4,0},{5,1},{6,2},{7,3},{8,12},{9,13},{10,... | collective-permute-start | bytes 393224 | tf_op jit(solution)/shard_map/ppermute | solution.py:40
  80.1 1.4 %collective-permute-start.33 = (bf16[128,512]{1,0:T(8,128)(2,1)S(1)}, bf16[128,512]{1,0:T(8,128)(2,1)S(1)}, u32[]{:S(2)}, u32[]{:S(2)}) collective-permute-start(bf16[128,512]{1,0:T(8,128)(2,1)S(1)} %collective-permute-done.30.refs_2_), channel_id=1, source_target_pairs={{0,4},{1,5},{2,6},{3,7},{4,0},{5,1},{6,2},{7,3},{8,12},{9,13},{10,... | collective-permute-start | bytes 393224 | tf_op jit(solution)/shard_map/ppermute | solution.py:40
  84.7 6.3 %collective-permute-start.38 = (bf16[64,1024]{1,0:T(8,128)(2,1)S(1)}, bf16[64,1024]{1,0:T(8,128)(2,1)S(1)}, u32[]{:S(2)}, u32[]{:S(2)}) collective-permute-start(bf16[64,1024]{1,0:T(8,128)(2,1)S(1)} %get-tuple-element.73), channel_id=1, source_target_pairs={{0,2},{1,3},{2,0},{3,1},{4,6},{5,7},{6,4},{7,5},{8,10},{9,11},{10,... | collective-permute-start | bytes 393224 | tf_op jit(solution)/shard_map/ppermute | solution.py:40
  85.0 10.0 %collective-permute-start.39 = (bf16[64,1024]{1,0:T(8,128)(2,1)S(1)}, bf16[64,1024]{1,0:T(8,128)(2,1)S(1)}, u32[]{:S(2)}, u32[]{:S(2)}) collective-permute-start(bf16[64,1024]{1,0:T(8,128)(2,1)S(1)} %get-tuple-element.74), channel_id=1, source_target_pairs={{0,1},{1,2},{2,3},{3,0},{4,5},{5,6},{6,7},{7,4},{8,9},{9,10},{10,1... | collective-permute-start | bytes 393224 | tf_op jit(solution)/shard_map/ppermute | solution.py:40
  87.1 8.0 %collective-permute-start.40 = (bf16[64,1024]{1,0:T(8,128)(2,1)S(1)}, bf16[64,1024]{1,0:T(8,128)(2,1)S(1)}, u32[]{:S(2)}, u32[]{:S(2)}) collective-permute-start(bf16[64,1024]{1,0:T(8,128)(2,1)S(1)} %get-tuple-element.75), channel_id=1, source_target_pairs={{0,3},{1,0},{2,1},{3,2},{4,7},{5,4},{6,5},{7,6},{8,11},{9,8},{10,9... | collective-permute-start | bytes 393224 | tf_op jit(solution)/shard_map/ppermute | solution.py:40
  87.7 9.0 %collective-permute-start.35 = (bf16[64,1024]{1,0:T(8,128)(2,1)S(1)}, bf16[64,1024]{1,0:T(8,128)(2,1)S(1)}, u32[]{:S(2)}, u32[]{:S(2)}) collective-permute-start(bf16[64,1024]{1,0:T(8,128)(2,1)S(1)} %get-tuple-element.69), channel_id=1, source_target_pairs={{0,2},{1,3},{2,0},{3,1},{4,6},{5,7},{6,4},{7,5},{8,10},{9,11},{10,... | collective-permute-start | bytes 393224 | tf_op jit(solution)/shard_map/ppermute | solution.py:40
  89.3 10.8 %collective-permute-start.36 = (bf16[64,1024]{1,0:T(8,128)(2,1)S(1)}, bf16[64,1024]{1,0:T(8,128)(2,1)S(1)}, u32[]{:S(2)}, u32[]{:S(2)}) collective-permute-start(bf16[64,1024]{1,0:T(8,128)(2,1)S(1)} %get-tuple-element.70), channel_id=1, source_target_pairs={{0,1},{1,2},{2,3},{3,0},{4,5},{5,6},{6,7},{7,4},{8,9},{9,10},{10,1... | collective-permute-start | bytes 393224 | tf_op jit(solution)/shard_map/ppermute | solution.py:40
  91.0 9.0 %collective-permute-start.37 = (bf16[64,1024]{1,0:T(8,128)(2,1)S(1)}, bf16[64,1024]{1,0:T(8,128)(2,1)S(1)}, u32[]{:S(2)}, u32[]{:S(2)}) collective-permute-start(bf16[64,1024]{1,0:T(8,128)(2,1)S(1)} %get-tuple-element.71), channel_id=1, source_target_pairs={{0,3},{1,0},{2,1},{3,2},{4,7},{5,4},{6,5},{7,6},{8,11},{9,8},{10,9... | collective-permute-start | bytes 393224 | tf_op jit(solution)/shard_map/ppermute | solution.py:40
  95.2 4.9 %collective-permute-start.41 = (bf16[64,1024]{1,0:T(8,128)(2,1)S(1)}, bf16[64,1024]{1,0:T(8,128)(2,1)S(1)}, u32[]{:S(2)}, u32[]{:S(2)}) collective-permute-start(bf16[64,1024]{1,0:T(8,128)(2,1)S(1)} %last_cross.1), channel_id=1, source_target_pairs={{0,32},{1,33},{2,34},{3,35},{4,36},{5,37},{6,38},{7,39},{8,40},{9,... | collective-permute-start | bytes 393224 | tf_op jit(solution)/shard_map/ppermute | solution.py:40
